TPU v7x, 512 devices: a whole 4x8x8 slice. The times are simulated.
512 devices in a mesh: gx: 16 (over x, z_hi), gy: 32 (over y, z_lo, core).
Axes of the slice: x: 4, y: 8, z: 8 (z_hi: 4, z_lo: 2; z = z_hi * 2 + z_lo), core: 2. Of those that a mesh axis runs over, the one named last changes fastest.
Arguments:
- right_sides: float32 [65536, 64], P(('gx', 'gy')), may hold values from -6 to 6
- factor_u: float32 [8, 65536, 128], P(None, ('gx', 'gy')), may hold values from -6 to 6
- factor_v: float32 [8, 65536, 128], P(None, ('gx', 'gy')), may hold values from -1 to 1, as said below
Outputs:
- solution: float32 [65536, 64], P(('gx', 'gy'))
Inputs may be any that keep to these rules, and one draw needn't show every extreme that they name: `factor_v`: entries of level k are independent with standard deviation 0.02 / sqrt(2**(k + 1) * 128).
All inputs are finite; a program needn't handle non-finite values.
Results may differ from a plain program's by a relative error of at most 0.0001.
Values sent between devices are 32-bit elements; how exact they have to be, the bound alone decides.
No kernel may reach another device: no remote copies, remote signals or barrier semaphores. Data moves between devices by JAX's collectives and lax.ppermute only.
A program may use at most 64 MiB of HBM per device.

v0:
```python
import jax
import jax.numpy as jnp
from jax import lax
from jax.sharding import PartitionSpec as P


def partner(value, axis, distance):
    mask = 2**distance
    pairs = [(source, source ^ mask) for source in range(lax.axis_size(axis))]
    return lax.ppermute(value, axis, pairs)


def combine_peer(partial_value, peer_bit, gy_bits):
    if peer_bit < gy_bits:
        return partner(partial_value, "gy", peer_bit)
    return partner(partial_value, "gx", peer_bit - gy_bits)


def group_sum(partial_value, upper_bit, gy_bits):
    bit_list = list(range(upper_bit))
    for peer_bit in bit_list:
        partial_value = partial_value + combine_peer(partial_value, peer_bit, gy_bits)
    return partial_value


def invert_coupling(matrix, rank):
    highest = lax.Precision.HIGHEST
    identity = jnp.eye(rank, dtype=jnp.float32)
    inverse = identity
    for sweep in range(7):
        product = jnp.dot(matrix, inverse, precision=highest)
        inverse = jnp.dot(inverse, 2.0 * identity - product, precision=highest)
    return inverse


def solve_node(summed, sibling, second_side, rank):
    highest = lax.Precision.HIGHEST
    own_gram, own_proj = (summed[:, :rank], summed[:, rank:])
    sib_gram, sib_proj = (sibling[:, :rank], sibling[:, rank:])
    gram_first = jnp.where(second_side, sib_gram, own_gram)
    gram_second = jnp.where(second_side, own_gram, sib_gram)
    proj_first = jnp.where(second_side, sib_proj, own_proj)
    proj_second = jnp.where(second_side, own_proj, sib_proj)
    schur = jnp.eye(rank, dtype=jnp.float32) - jnp.dot(gram_first, gram_second, precision=highest)
    inverse = invert_coupling(schur, rank)
    shifted = proj_first - jnp.dot(gram_first, proj_second, precision=highest)
    z_second = jnp.dot(inverse, shifted, precision=highest)
    z_first = proj_second - jnp.dot(gram_second, z_second, precision=highest)
    own_z = jnp.where(second_side, z_second, z_first)
    sib_z = jnp.where(second_side, z_first, z_second)
    return (own_z, sib_z)


def shards(right_sides, factor_u, factor_v):
    highest = lax.Precision.HIGHEST
    gy_bits = lax.axis_size("gy").bit_length() - 1
    levels = factor_u.shape[0]
    rank = factor_u.shape[2]
    nrhs_cols = right_sides.shape[1]
    linear = lax.axis_index("gx") * lax.axis_size("gy") + lax.axis_index("gy")
    solution = right_sides
    carried = [factor_u[level] for level in range(levels)]
    for level in range(levels):
        rest = jnp.concatenate([solution] + carried[level + 1 :], axis=1)
        left = carried[level]
        second_side = linear >> level + 1 & 1 == 1
        operands = jnp.concatenate([left, rest], axis=1)
        local = lax.dot_general(
            factor_v[level], operands, (((0,), (0,)), ((), ())), precision=highest
        )
        summed = group_sum(local, level + 1, gy_bits)
        sibling = combine_peer(summed, level + 1, gy_bits)
        own_z, sib_z = solve_node(summed, sibling, second_side, rank)
        rest = rest - jnp.dot(left, own_z, precision=highest)
        solution = rest[:, :nrhs_cols]
        newer = [
            rest[:, nrhs_cols + rank * j : nrhs_cols + rank * (j + 1)]
            for j in range(levels - level - 1)
        ]
        carried = carried[: level + 1] + newer
    return solution


def solution(mesh):
    placed = (P(("gx", "gy"), None), P(None, ("gx", "gy"), None), P(None, ("gx", "gy"), None))
    return jax.shard_map(
        shards, mesh=mesh, in_specs=placed, out_specs=P(("gx", "gy"), None), check_vma=False
    )
```

profile of v0, /device:TPU:28, one launch (start us, length us, event | category | flops | bytes accessed | tf_op | source)
XLA Modules:
  0.0 542.9 jit_solution(4207964483118634628)
XLA Ops:
  12.5 12.9 %collective-permute-done.1 = f32[128,1088]{0,1:T(8,128)S(1)} collective-permute-done((f32[128,1088]{0,1:T(8,128)S(1)}, f32[128,1088]{0,1:T(8,128)S(1)}, u32[]{:S(2)}, u32[]{:S(2)}) %collective-permute-start.1) | collective-permute-done | bytes 557088 | tf_op jit(solution)/shard_map/ppermute | solution.py:10
  39.7 11.5 %collective-permute-done.3 = f32[128,960]{0,1:T(8,128)S(1)} collective-permute-done((f32[128,960]{0,1:T(8,128)S(1)}, f32[128,960]{0,1:T(8,128)S(1)}, u32[]{:S(2)}, u32[]{:S(2)}) %collective-permute-start.3) | collective-permute-done | bytes 491552 | tf_op jit(solution)/shard_map/ppermute | solution.py:10
  53.7 12.0 %collective-permute-done.4 = f32[128,960]{0,1:T(8,128)S(1)} collective-permute-done((f32[128,960]{0,1:T(8,128)S(1)}, f32[128,960]{0,1:T(8,128)S(1)}, u32[]{:S(2)}, u32[]{:S(2)}) %collective-permute-start.4) | collective-permute-done | bytes 491552 | tf_op jit(solution)/shard_map/ppermute | solution.py:10
  78.8 10.1 %collective-permute-done.6 = f32[128,832]{0,1:T(8,128)S(1)} collective-permute-done((f32[128,832]{0,1:T(8,128)S(1)}, f32[128,832]{0,1:T(8,128)S(1)}, u32[]{:S(2)}, u32[]{:S(2)}) %collective-permute-start.6) | collective-permute-done | bytes 426016 | tf_op jit(solution)/shard_map/ppermute | solution.py:10
  91.3 10.6 %collective-permute-done.7 = f32[128,832]{0,1:T(8,128)S(1)} collective-permute-done((f32[128,832]{0,1:T(8,128)S(1)}, f32[128,832]{0,1:T(8,128)S(1)}, u32[]{:S(2)}, u32[]{:S(2)}) %collective-permute-start.7) | collective-permute-done | bytes 426016 | tf_op jit(solution)/shard_map/ppermute | solution.py:10
  104.4 19.5 %collective-permute-done.8 = f32[128,832]{0,1:T(8,128)S(1)} collective-permute-done((f32[128,832]{0,1:T(8,128)S(1)}, f32[128,832]{0,1:T(8,128)S(1)}, u32[]{:S(2)}, u32[]{:S(2)}) %collective-permute-start.8) | collective-permute-done | bytes 426016 | tf_op jit(solution)/shard_map/ppermute | solution.py:10
  136.6 8.7 %collective-permute-done.10 = f32[128,704]{0,1:T(8,128)S(1)} collective-permute-done((f32[128,704]{0,1:T(8,128)S(1)}, f32[128,704]{0,1:T(8,128)S(1)}, u32[]{:S(2)}, u32[]{:S(2)}) %collective-permute-start.10) | collective-permute-done | bytes 360480 | tf_op jit(solution)/shard_map/ppermute | solution.py:10
  147.3 9.6 %collective-permute-done.11 = f32[128,704]{0,1:T(8,128)S(1)} collective-permute-done((f32[128,704]{0,1:T(8,128)S(1)}, f32[128,704]{0,1:T(8,128)S(1)}, u32[]{:S(2)}, u32[]{:S(2)}) %collective-permute-start.11) | collective-permute-done | bytes 360480 | tf_op jit(solution)/shard_map/ppermute | solution.py:10
  158.9 17.3 %collective-permute-done.12 = f32[128,704]{0,1:T(8,128)S(1)} collective-permute-done((f32[128,704]{0,1:T(8,128)S(1)}, f32[128,704]{0,1:T(8,128)S(1)}, u32[]{:S(2)}, u32[]{:S(2)}) %collective-permute-start.12) | collective-permute-done | bytes 360480 | tf_op jit(solution)/shard_map/ppermute | solution.py:10
  181.4 18.2 %collective-permute-done.13 = f32[128,704]{0,1:T(8,128)S(1)} collective-permute-done((f32[128,704]{0,1:T(8,128)S(1)}, f32[128,704]{0,1:T(8,128)S(1)}, u32[]{:S(2)}, u32[]{:S(2)}) %collective-permute-start.13) | collective-permute-done | bytes 360480 | tf_op jit(solution)/shard_map/ppermute | solution.py:10
  212.0 7.3 %collective-permute-done.15 = f32[128,576]{0,1:T(8,128)S(1)} collective-permute-done((f32[128,576]{0,1:T(8,128)S(1)}, f32[128,576]{0,1:T(8,128)S(1)}, u32[]{:S(2)}, u32[]{:S(2)}) %collective-permute-start.15) | collective-permute-done | bytes 294944 | tf_op jit(solution)/shard_map/ppermute | solution.py:10
  221.2 8.2 %collective-permute-done.16 = f32[128,576]{0,1:T(8,128)S(1)} collective-permute-done((f32[128,576]{0,1:T(8,128)S(1)}, f32[128,576]{0,1:T(8,128)S(1)}, u32[]{:S(2)}, u32[]{:S(2)}) %collective-permute-start.16) | collective-permute-done | bytes 294944 | tf_op jit(solution)/shard_map/ppermute | solution.py:10
  231.4 14.5 %collective-permute-done.17 = f32[128,576]{0,1:T(8,128)S(1)} collective-permute-done((f32[128,576]{0,1:T(8,128)S(1)}, f32[128,576]{0,1:T(8,128)S(1)}, u32[]{:S(2)}, u32[]{:S(2)}) %collective-permute-start.17) | collective-permute-done | bytes 294944 | tf_op jit(solution)/shard_map/ppermute | solution.py:10
  250.9 15.7 %collective-permute-done.18 = f32[128,576]{0,1:T(8,128)S(1)} collective-permute-done((f32[128,576]{0,1:T(8,128)S(1)}, f32[128,576]{0,1:T(8,128)S(1)}, u32[]{:S(2)}, u32[]{:S(2)}) %collective-permute-start.18) | collective-permute-done | bytes 294944 | tf_op jit(solution)/shard_map/ppermute | solution.py:10
  273.0 13.3 %collective-permute-done.19 = f32[128,576]{0,1:T(8,128)S(1)} collective-permute-done((f32[128,576]{0,1:T(8,128)S(1)}, f32[128,576]{0,1:T(8,128)S(1)}, u32[]{:S(2)}, u32[]{:S(2)}) %collective-permute-start.19) | collective-permute-done | bytes 294944 | tf_op jit(solution)/shard_map/ppermute | solution.py:10
  314.9 11.7 %collective-permute-done.23 = f32[128,448]{0,1:T(8,128)S(1)} collective-permute-done((f32[128,448]{0,1:T(8,128)S(1)}, f32[128,448]{0,1:T(8,128)S(1)}, u32[]{:S(2)}, u32[]{:S(2)}) %collective-permute-start.23) | collective-permute-done | bytes 229408 | tf_op jit(solution)/shard_map/ppermute | solution.py:10
  331.4 12.9 %collective-permute-done.24 = f32[128,448]{0,1:T(8,128)S(1)} collective-permute-done((f32[128,448]{0,1:T(8,128)S(1)}, f32[128,448]{0,1:T(8,128)S(1)}, u32[]{:S(2)}, u32[]{:S(2)}) %collective-permute-start.24) | collective-permute-done | bytes 229408 | tf_op jit(solution)/shard_map/ppermute | solution.py:10
  349.3 10.7 %collective-permute-done.25 = f32[128,448]{0,1:T(8,128)S(1)} collective-permute-done((f32[128,448]{0,1:T(8,128)S(1)}, f32[128,448]{0,1:T(8,128)S(1)}, u32[]{:S(2)}, u32[]{:S(2)}) %collective-permute-start.25) | collective-permute-done | bytes 229408 | tf_op jit(solution)/shard_map/ppermute | solution.py:10
  360.0 8.5 %collective-permute-start.26 = (f32[128,448]{0,1:T(8,128)S(1)}, f32[128,448]{0,1:T(8,128)S(1)}, u32[]{:S(2)}, u32[]{:S(2)}) collective-permute-start(f32[128,448]{0,1:T(8,128)S(1)} %add.132), channel_id=1, source_target_pairs={{0,64},{32,96},{64,0},{96,32},{128,192},{160,224},{192,128},{224,1... | collective-permute-start | bytes 688136 | tf_op jit(solution)/shard_map/ppermute | solution.py:10
  368.5 10.2 %collective-permute-done.26 = f32[128,448]{0,1:T(8,128)S(1)} collective-permute-done((f32[128,448]{0,1:T(8,128)S(1)}, f32[128,448]{0,1:T(8,128)S(1)}, u32[]{:S(2)}, u32[]{:S(2)}) %collective-permute-start.26) | collective-permute-done | bytes 229408 | tf_op jit(solution)/shard_map/ppermute | solution.py:10
  404.2 8.9 %collective-permute-done.30 = f32[128,320]{0,1:T(8,128)S(1)} collective-permute-done((f32[128,320]{0,1:T(8,128)S(1)}, f32[128,320]{0,1:T(8,128)S(1)}, u32[]{:S(2)}, u32[]{:S(2)}) %collective-permute-start.30) | collective-permute-done | bytes 163872 | tf_op jit(solution)/shard_map/ppermute | solution.py:10
  418.0 9.6 %collective-permute-done.31 = f32[128,320]{0,1:T(8,128)S(1)} collective-permute-done((f32[128,320]{0,1:T(8,128)S(1)}, f32[128,320]{0,1:T(8,128)S(1)}, u32[]{:S(2)}, u32[]{:S(2)}) %collective-permute-start.31) | collective-permute-done | bytes 163872 | tf_op jit(solution)/shard_map/ppermute | solution.py:10
  432.8 7.9 %collective-permute-done.32 = f32[128,320]{0,1:T(8,128)S(1)} collective-permute-done((f32[128,320]{0,1:T(8,128)S(1)}, f32[128,320]{0,1:T(8,128)S(1)}, u32[]{:S(2)}, u32[]{:S(2)}) %collective-permute-start.32) | collective-permute-done | bytes 163872 | tf_op jit(solution)/shard_map/ppermute | solution.py:10
  445.4 10.0 %collective-permute-done.33 = f32[128,320]{0,1:T(8,128)S(1)} collective-permute-done((f32[128,320]{0,1:T(8,128)S(1)}, f32[128,320]{0,1:T(8,128)S(1)}, u32[]{:S(2)}, u32[]{:S(2)}) %collective-permute-start.33) | collective-permute-done | bytes 163872 | tf_op jit(solution)/shard_map/ppermute | solution.py:10
  (301 shorter events, 261.2 us)
Async XLA Ops:
  8.2 17.2 %collective-permute-start.1 = (f32[128,1088]{0,1:T(8,128)S(1)}, f32[128,1088]{0,1:T(8,128)S(1)}, u32[]{:S(2)}, u32[]{:S(2)}) collective-permute-start(f32[128,1088]{0,1:T(8,128)S(1)} %add.112), channel_id=1, source_target_pairs={{0,2},{1,3},{2,0},{3,1},{4,6},{5,7},{6,4},{7,5},{8,10},{9,11},{10,... | collective-permute-start | bytes 1671176 | tf_op jit(solution)/shard_map/ppermute | solution.py:10
  36.1 15.2 %collective-permute-start.3 = (f32[128,960]{0,1:T(8,128)S(1)}, f32[128,960]{0,1:T(8,128)S(1)}, u32[]{:S(2)}, u32[]{:S(2)}) collective-permute-start(f32[128,960]{0,1:T(8,128)S(1)} %add.113), channel_id=1, source_target_pairs={{0,2},{1,3},{2,0},{3,1},{4,6},{5,7},{6,4},{7,5},{8,10},{9,11},{10,... | collective-permute-start | bytes 1474568 | tf_op jit(solution)/shard_map/ppermute | solution.py:10
  51.3 14.3 %collective-permute-start.4 = (f32[128,960]{0,1:T(8,128)S(1)}, f32[128,960]{0,1:T(8,128)S(1)}, u32[]{:S(2)}, u32[]{:S(2)}) collective-permute-start(f32[128,960]{0,1:T(8,128)S(1)} %add.114), channel_id=1, source_target_pairs={{0,4},{1,5},{2,6},{3,7},{4,0},{5,1},{6,2},{7,3},{8,12},{9,13},{10,... | collective-permute-start | bytes 1474568 | tf_op jit(solution)/shard_map/ppermute | solution.py:10
  75.2 13.8 %collective-permute-start.6 = (f32[128,832]{0,1:T(8,128)S(1)}, f32[128,832]{0,1:T(8,128)S(1)}, u32[]{:S(2)}, u32[]{:S(2)}) collective-permute-start(f32[128,832]{0,1:T(8,128)S(1)} %add.115), channel_id=1, source_target_pairs={{0,2},{1,3},{2,0},{3,1},{4,6},{5,7},{6,4},{7,5},{8,10},{9,11},{10,... | collective-permute-start | bytes 1277960 | tf_op jit(solution)/shard_map/ppermute | solution.py:10
  89.0 12.9 %collective-permute-start.7 = (f32[128,832]{0,1:T(8,128)S(1)}, f32[128,832]{0,1:T(8,128)S(1)}, u32[]{:S(2)}, u32[]{:S(2)}) collective-permute-start(f32[128,832]{0,1:T(8,128)S(1)} %add.116), channel_id=1, source_target_pairs={{0,4},{1,5},{2,6},{3,7},{4,0},{5,1},{6,2},{7,3},{8,12},{9,13},{10,... | collective-permute-start | bytes 1277960 | tf_op jit(solution)/shard_map/ppermute | solution.py:10
  101.9 21.9 %collective-permute-start.8 = (f32[128,832]{0,1:T(8,128)S(1)}, f32[128,832]{0,1:T(8,128)S(1)}, u32[]{:S(2)}, u32[]{:S(2)}) collective-permute-start(f32[128,832]{0,1:T(8,128)S(1)} %add.117), channel_id=1, source_target_pairs={{0,8},{1,9},{2,10},{3,11},{4,12},{5,13},{6,14},{7,15},{8,0},{9,1},... | collective-permute-start | bytes 1277960 | tf_op jit(solution)/shard_map/ppermute | solution.py:10
  133.0 12.3 %collective-permute-start.10 = (f32[128,704]{0,1:T(8,128)S(1)}, f32[128,704]{0,1:T(8,128)S(1)}, u32[]{:S(2)}, u32[]{:S(2)}) collective-permute-start(f32[128,704]{0,1:T(8,128)S(1)} %add.118), channel_id=1, source_target_pairs={{0,2},{1,3},{2,0},{3,1},{4,6},{5,7},{6,4},{7,5},{8,10},{9,11},{10,... | collective-permute-start | bytes 1081352 | tf_op jit(solution)/shard_map/ppermute | solution.py:10
  145.4 11.5 %collective-permute-start.11 = (f32[128,704]{0,1:T(8,128)S(1)}, f32[128,704]{0,1:T(8,128)S(1)}, u32[]{:S(2)}, u32[]{:S(2)}) collective-permute-start(f32[128,704]{0,1:T(8,128)S(1)} %add.119), channel_id=1, source_target_pairs={{0,4},{1,5},{2,6},{3,7},{4,0},{5,1},{6,2},{7,3},{8,12},{9,13},{10,... | collective-permute-start | bytes 1081352 | tf_op jit(solution)/shard_map/ppermute | solution.py:10
  156.9 19.2 %collective-permute-start.12 = (f32[128,704]{0,1:T(8,128)S(1)}, f32[128,704]{0,1:T(8,128)S(1)}, u32[]{:S(2)}, u32[]{:S(2)}) collective-permute-start(f32[128,704]{0,1:T(8,128)S(1)} %add.120), channel_id=1, source_target_pairs={{0,8},{1,9},{2,10},{3,11},{4,12},{5,13},{6,14},{7,15},{8,0},{9,1},... | collective-permute-start | bytes 1081352 | tf_op jit(solution)/shard_map/ppermute | solution.py:10
  176.2 23.3 %collective-permute-start.13 = (f32[128,704]{0,1:T(8,128)S(1)}, f32[128,704]{0,1:T(8,128)S(1)}, u32[]{:S(2)}, u32[]{:S(2)}) collective-permute-start(f32[128,704]{0,1:T(8,128)S(1)} %add.121), channel_id=1, source_target_pairs={{0,16},{1,17},{2,18},{3,19},{4,20},{5,21},{6,22},{7,23},{8,24},{9,... | collective-permute-start | bytes 1081352 | tf_op jit(solution)/shard_map/ppermute | solution.py:10
  208.3 10.9 %collective-permute-start.15 = (f32[128,576]{0,1:T(8,128)S(1)}, f32[128,576]{0,1:T(8,128)S(1)}, u32[]{:S(2)}, u32[]{:S(2)}) collective-permute-start(f32[128,576]{0,1:T(8,128)S(1)} %add.122), channel_id=1, source_target_pairs={{0,2},{1,3},{2,0},{3,1},{4,6},{5,7},{6,4},{7,5},{8,10},{9,11},{10,... | collective-permute-start | bytes 884744 | tf_op jit(solution)/shard_map/ppermute | solution.py:10
  229.5 16.4 %collective-permute-start.17 = (f32[128,576]{0,1:T(8,128)S(1)}, f32[128,576]{0,1:T(8,128)S(1)}, u32[]{:S(2)}, u32[]{:S(2)}) collective-permute-start(f32[128,576]{0,1:T(8,128)S(1)} %add.124), channel_id=1, source_target_pairs={{0,8},{1,9},{2,10},{3,11},{4,12},{5,13},{6,14},{7,15},{8,0},{9,1},... | collective-permute-start | bytes 884744 | tf_op jit(solution)/shard_map/ppermute | solution.py:10
  245.9 20.7 %collective-permute-start.18 = (f32[128,576]{0,1:T(8,128)S(1)}, f32[128,576]{0,1:T(8,128)S(1)}, u32[]{:S(2)}, u32[]{:S(2)}) collective-permute-start(f32[128,576]{0,1:T(8,128)S(1)} %add.125), channel_id=1, source_target_pairs={{0,16},{1,17},{2,18},{3,19},{4,20},{5,21},{6,22},{7,23},{8,24},{9,... | collective-permute-start | bytes 884744 | tf_op jit(solution)/shard_map/ppermute | solution.py:10
  266.6 19.6 %collective-permute-start.19 = (f32[128,576]{0,1:T(8,128)S(1)}, f32[128,576]{0,1:T(8,128)S(1)}, u32[]{:S(2)}, u32[]{:S(2)}) collective-permute-start(f32[128,576]{0,1:T(8,128)S(1)} %add.126), channel_id=1, source_target_pairs={{0,32},{32,0},{64,96},{96,64},{128,160},{160,128},{192,224},{224,1... | collective-permute-start | bytes 884744 | tf_op jit(solution)/shard_map/ppermute | solution.py:10
  312.9 13.6 %collective-permute-start.23 = (f32[128,448]{0,1:T(8,128)S(1)}, f32[128,448]{0,1:T(8,128)S(1)}, u32[]{:S(2)}, u32[]{:S(2)}) collective-permute-start(f32[128,448]{0,1:T(8,128)S(1)} %add.129), channel_id=1, source_target_pairs={{0,8},{1,9},{2,10},{3,11},{4,12},{5,13},{6,14},{7,15},{8,0},{9,1},... | collective-permute-start | bytes 688136 | tf_op jit(solution)/shard_map/ppermute | solution.py:10
  326.6 17.8 %collective-permute-start.24 = (f32[128,448]{0,1:T(8,128)S(1)}, f32[128,448]{0,1:T(8,128)S(1)}, u32[]{:S(2)}, u32[]{:S(2)}) collective-permute-start(f32[128,448]{0,1:T(8,128)S(1)} %add.130), channel_id=1, source_target_pairs={{0,16},{1,17},{2,18},{3,19},{4,20},{5,21},{6,22},{7,23},{8,24},{9,... | collective-permute-start | bytes 688136 | tf_op jit(solution)/shard_map/ppermute | solution.py:10
  344.4 15.6 %collective-permute-start.25 = (f32[128,448]{0,1:T(8,128)S(1)}, f32[128,448]{0,1:T(8,128)S(1)}, u32[]{:S(2)}, u32[]{:S(2)}) collective-permute-start(f32[128,448]{0,1:T(8,128)S(1)} %add.131), channel_id=1, source_target_pairs={{0,32},{32,0},{64,96},{96,64},{128,160},{160,128},{192,224},{224,1... | collective-permute-start | bytes 688136 | tf_op jit(solution)/shard_map/ppermute | solution.py:10
  360.0 18.7 %collective-permute-start.26 = (f32[128,448]{0,1:T(8,128)S(1)}, f32[128,448]{0,1:T(8,128)S(1)}, u32[]{:S(2)}, u32[]{:S(2)}) collective-permute-start(f32[128,448]{0,1:T(8,128)S(1)} %add.132), channel_id=1, source_target_pairs={{0,64},{32,96},{64,0},{96,32},{128,192},{160,224},{192,128},{224,1... | collective-permute-start | bytes 688136 | tf_op jit(solution)/shard_map/ppermute | solution.py:10
  402.3 10.8 %collective-permute-start.30 = (f32[128,320]{0,1:T(8,128)S(1)}, f32[128,320]{0,1:T(8,128)S(1)}, u32[]{:S(2)}, u32[]{:S(2)}) collective-permute-start(f32[128,320]{0,1:T(8,128)S(1)} %add.135), channel_id=1, source_target_pairs={{0,8},{1,9},{2,10},{3,11},{4,12},{5,13},{6,14},{7,15},{8,0},{9,1},... | collective-permute-start | bytes 491528 | tf_op jit(solution)/shard_map/ppermute | solution.py:10
  413.1 14.6 %collective-permute-start.31 = (f32[128,320]{0,1:T(8,128)S(1)}, f32[128,320]{0,1:T(8,128)S(1)}, u32[]{:S(2)}, u32[]{:S(2)}) collective-permute-start(f32[128,320]{0,1:T(8,128)S(1)} %add.136), channel_id=1, source_target_pairs={{0,16},{1,17},{2,18},{3,19},{4,20},{5,21},{6,22},{7,23},{8,24},{9,... | collective-permute-start | bytes 491528 | tf_op jit(solution)/shard_map/ppermute | solution.py:10
  427.6 13.0 %collective-permute-start.32 = (f32[128,320]{0,1:T(8,128)S(1)}, f32[128,320]{0,1:T(8,128)S(1)}, u32[]{:S(2)}, u32[]{:S(2)}) collective-permute-start(f32[128,320]{0,1:T(8,128)S(1)} %add.137), channel_id=1, source_target_pairs={{0,32},{32,0},{64,96},{96,64},{128,160},{160,128},{192,224},{224,1... | collective-permute-start | bytes 491528 | tf_op jit(solution)/shard_map/ppermute | solution.py:10
  440.7 14.8 %collective-permute-start.33 = (f32[128,320]{0,1:T(8,128)S(1)}, f32[128,320]{0,1:T(8,128)S(1)}, u32[]{:S(2)}, u32[]{:S(2)}) collective-permute-start(f32[128,320]{0,1:T(8,128)S(1)} %add.138), channel_id=1, source_target_pairs={{0,64},{32,96},{64,0},{96,32},{128,192},{160,224},{192,128},{224,1... | collective-permute-start | bytes 491528 | tf_op jit(solution)/shard_map/ppermute | solution.py:10
  492.4 11.1 %collective-permute-start.39 = (f32[128,192]{0,1:T(8,128)S(1)}, f32[128,192]{0,1:T(8,128)S(1)}, u32[]{:S(2)}, u32[]{:S(2)}) collective-permute-start(f32[128,192]{0,1:T(8,128)S(1)} %add.143), channel_id=1, source_target_pairs={{0,16},{1,17},{2,18},{3,19},{4,20},{5,21},{6,22},{7,23},{8,24},{9,... | collective-permute-start | bytes 294920 | tf_op jit(solution)/shard_map/ppermute | solution.py:10
  511.3 11.5 %collective-permute-start.41 = (f32[128,192]{0,1:T(8,128)S(1)}, f32[128,192]{0,1:T(8,128)S(1)}, u32[]{:S(2)}, u32[]{:S(2)}) collective-permute-start(f32[128,192]{0,1:T(8,128)S(1)} %add.145), channel_id=1, source_target_pairs={{0,64},{32,96},{64,0},{96,32},{128,192},{160,224},{192,128},{224,1... | collective-permute-start | bytes 294920 | tf_op jit(solution)/shard_map/ppermute | solution.py:10
  (22 other events, 126.1 us)
where the time goes:
time: 544 us; the launch traced here: 543 us
  waiting for transfers between devices  358 us (66%)
  starting transfers between devices  137 us (25%)
  matrix products  41.4 us (8%)
    ppermute x44, waiting for transfers between devices, partner(): return lax.ppermute(value, axis, pairs)  358 us
    ppermute x44, starting transfers between devices, partner(): return lax.ppermute(value, axis, pairs)  137 us
    dot_general x56, matrix products, invert_coupling(): product = jnp.dot(matrix, inverse, precision=highest)  11.2 us
    dot_general x56, matrix products, invert_coupling(): inverse = jnp.dot(inverse, 2.0 * identity - product, precision=highest)  11.2 us
  transfers between devices with their start and end apart: 44, of which 44 were waited for; matrix products, arithmetic and copies ran while one was open for 0% of the time, Pallas kernels for 0%

commit v1 on v0

v1 whole, which is shorter than its diff:
```python
import jax
import jax.numpy as jnp
from jax import lax
from jax.sharding import PartitionSpec as P

HIGHEST = lax.Precision.HIGHEST


def dot(a, b):
    return jnp.dot(a, b, precision=HIGHEST)


def partner(value, bit, gy_bits):
    axis, shift = ("gy", bit) if bit < gy_bits else ("gx", bit - gy_bits)
    mask = 1 << shift
    return lax.ppermute(value, axis, [(s, s ^ mask) for s in range(lax.axis_size(axis))])


def groups_of(count, size):
    return [list(range(i, i + size)) for i in range(0, count, size)]


def inverse_of(error):
    rank = error.shape[0]
    total = jnp.eye(rank, dtype=jnp.float32) + error
    power = error
    for step in range(6):
        power = dot(power, power)
        total = total + dot(total, power)
    return total


def solve_own(gram_own, gram_sib, proj_own, proj_sib):
    inverse = inverse_of(dot(gram_own, gram_sib))
    return dot(proj_sib - dot(proj_own, gram_sib), inverse)


def chip_halves(core, mine, other):
    first = jnp.where(core == 0, mine, other)
    second = jnp.where(core == 0, other, mine)
    return jnp.concatenate([first, second], axis=0)


def shards(right_sides, factor_u, factor_v):
    gy_size = lax.axis_size("gy")
    gy_bits = gy_size.bit_length() - 1
    levels, rows, rank = factor_u.shape
    gy = lax.axis_index("gy")
    core = gy & 1
    pairs = groups_of(gy_size, 2)
    quads = groups_of(gy_size, 4)
    same_core = [list(range(c, gy_size, 2)) for c in range(2)]
    chips = gy_size // 2

    carried = jnp.concatenate(
        [factor_u[j].T for j in range(levels)] + [right_sides.T], axis=0
    )

    for level in range(gy_bits - 2):
        local = dot(carried, factor_v[level])
        half = (local.shape[0] - rank) // 2
        keep = lax.dynamic_slice_in_dim(local, rank + core * half, half, 0)
        give = lax.dynamic_slice_in_dim(local, rank + (1 - core) * half, half, 0)
        gram = local[:rank]
        summed = jnp.concatenate([gram, keep], axis=0) + partner(
            jnp.concatenate([gram, give], axis=0), 0, gy_bits
        )
        for bit in range(1, level + 1):
            summed = summed + partner(summed, bit, gy_bits)
        sibling = partner(summed, level + 1, gy_bits)
        part = solve_own(summed[:rank], sibling[:rank], summed[rank:], sibling[rank:])
        z = lax.all_gather(part, "gy", axis_index_groups=pairs, axis=0, tiled=True)
        carried = carried[rank:] - dot(z, carried[:rank])

    level = gy_bits - 2
    local = dot(carried, factor_v[level])
    half = local.shape[0] // 2
    keep = lax.dynamic_slice_in_dim(local, core * half, half, 0)
    give = lax.dynamic_slice_in_dim(local, (1 - core) * half, half, 0)
    chip_sum = keep + partner(give, 0, gy_bits)
    share = -(-half // (8 * chips)) * 8
    chip_sum = jnp.pad(chip_sum, ((0, share * chips - half), (0, 0)))
    pieces = lax.all_to_all(
        chip_sum.reshape(chips, share, rank), "gy", 0, 0, axis_index_groups=same_core
    )
    both = pieces.reshape(2, chips // 2, share, rank).sum(axis=1)
    everyone = jnp.broadcast_to(both, (chips, 2, share, rank))
    gathered = lax.all_to_all(everyone, "gy", 0, 0, axis_index_groups=same_core)
    second_side = (gy >> (gy_bits - 1)) & 1 == 1
    first = gathered[:, 0].reshape(chips * share, rank)[:half]
    second = gathered[:, 1].reshape(chips * share, rank)[:half]
    own = jnp.where(second_side, second, first)
    sib = jnp.where(second_side, first, second)
    other = partner(jnp.concatenate([own, sib], axis=0), 0, gy_bits)
    own = chip_halves(core, own, other[:half])
    sib = chip_halves(core, sib, other[half:])
    z = solve_own(own[:rank], sib[:rank], own[rank:], sib[rank:])
    carried = carried[rank:] - dot(z, carried[:rank])

    level = gy_bits - 1
    count = levels - level
    width = carried.shape[0]
    state = jnp.concatenate([dot(carried, factor_v[j]) for j in range(level, levels)], axis=0)
    half = count * width // 2
    keep = lax.dynamic_slice_in_dim(state, core * half, half, 0)
    give = lax.dynamic_slice_in_dim(state, (1 - core) * half, half, 0)
    chip_sum = keep + partner(give, 0, gy_bits)
    share = half // chips
    pieces = lax.all_to_all(
        chip_sum.reshape(chips, share, rank), "gy", 0, 0, axis_index_groups=same_core
    )
    piece = pieces.sum(axis=0)
    both = jnp.stack([piece, partner(piece, level + 1, gy_bits)])
    everyone = jnp.broadcast_to(both, (chips, 2, share, rank))
    gathered = lax.all_to_all(everyone, "gy", 0, 0, axis_index_groups=same_core)
    own = gathered[:, 0].reshape(half, rank)
    sib = gathered[:, 1].reshape(half, rank)
    other = partner(jnp.concatenate([own, sib], axis=0), 0, gy_bits)
    own = chip_halves(core, own, other[:half])
    sib = chip_halves(core, sib, other[half:])

    while True:
        own = own.reshape(count, width, rank)
        sib = sib.reshape(count, width, rank)
        gram_own = own[0, :rank]
        z = solve_own(gram_own, sib[0, :rank], own[0, rank:], sib[0, rank:])
        if count > 1:
            z_sib = own[0, rank:] - dot(z, gram_own)
            z_both = jnp.concatenate([z, z_sib], axis=1)
            node = []
            for j in range(1, count):
                left = jnp.concatenate([own[j, :rank], sib[j, :rank]], axis=0)
                node.append(own[j, rank:] + sib[j, rank:] - dot(z_both, left))
        carried = carried[rank:] - dot(z, carried[:rank])
        if count == 1:
            break
        level, count, width = level + 1, count - 1, width - rank
        own = jnp.concatenate(node, axis=0)
        total = own.shape[0]
        if total > 1024:
            quarter = total // 4
            part = lax.dynamic_slice_in_dim(own, (gy & 3) * quarter, quarter, 0)
            sib = lax.all_gather(
                partner(part, level + 1, gy_bits), "gy", axis_index_groups=quads, axis=0, tiled=True
            )
        elif total > 512:
            part = lax.dynamic_slice_in_dim(own, core * (total // 2), total // 2, 0)
            sib = lax.all_gather(
                partner(part, level + 1, gy_bits), "gy", axis_index_groups=pairs, axis=0, tiled=True
            )
        else:
            sib = partner(own, level + 1, gy_bits)
    return carried.T


def solution(mesh):
    placed = (P(("gx", "gy"), None), P(None, ("gx", "gy"), None), P(None, ("gx", "gy"), None))
    return jax.shard_map(
        shards, mesh=mesh, in_specs=placed, out_specs=P(("gx", "gy"), None), check_vma=False
    )
```

time: 544 us -> 288 us (0.53)
  the two profiles are of different devices: /device:TPU:28 before, /device:TPU:1 now
where the time goes in v1:
time: 288 us; the launch traced here: 287 us
  blocking collectives  89.7 us (31%)
  waiting for transfers between devices  85.3 us (30%)
  starting transfers between devices  66.7 us (23%)
  matrix products  37.5 us (13%)
  local copies, waits for them, and re-layouts  3.55 us (1%)
    ppermute x17, waiting for transfers between devices, partner(): lax.ppermute(value, axis, [(s, s ^ mask) for s in range(lax.axis_size(axi...  73.4 us
    ppermute x17, starting transfers between devices, partner(): lax.ppermute(value, axis, [(s, s ^ mask) for s in range(lax.axis_size(axi...  63.1 us
    dot_general x145, matrix products, dot(): return jnp.dot(a, b, precision=HIGHEST)  37.5 us
    all_to_all x2, blocking collectives, shards(): lax.all_to_all(chip_sum.reshape(chips, share, rank), 'gy', 0, 0, axis_ind...  34.7 us
    all_to_all x1, blocking collectives, shards(): gathered = lax.all_to_all(everyone, 'gy', 0, 0, axis_index_groups=same_core)  31.4 us
    all_gather x2, blocking collectives, shards(): lax.all_gather(partner(part, level + 1, gy_bits), 'gy', axis_index_groups...  14.5 us
    all_to_all x1, waiting for transfers between devices, shards(): gathered = lax.all_to_all(everyone, 'gy', 0, 0, axis_index_groups=same_core)  11.9 us
    all_gather x3, blocking collectives, shards(): z = lax.all_gather(part, 'gy', axis_index_groups=pairs, axis=0, tiled=True)  9.03 us
  transfers between devices with their start and end apart: 18, of which 18 were waited for; matrix products, arithmetic and copies ran while one was open for 0% of the time, Pallas kernels for 0%

profile of v1, /device:TPU:1, one launch (start us, length us, event | category | flops | bytes accessed | tf_op | source)
XLA Modules:
  0.0 286.7 jit_solution(7955748867320170426)
XLA Ops:
  3.1 8.8 %collective-permute-start = (f32[608,128]{1,0:T(8,128)S(1)}, f32[608,128]{1,0:T(8,128)S(1)}, u32[]{:S(2)}, u32[]{:S(2)}) collective-permute-start(f32[608,128]{1,0:T(8,128)S(1)} %pad_maximum_fusion.6), channel_id=1, source_target_pairs={{0,1},{1,0},{2,3},{3,2},{4,5},{5,4},{6,7},{7,6},{8,9},{9,8},{10,11... | collective-permute-start | bytes 933896 | tf_op jit(solution)/shard_map/ppermute | solution.py:16
  15.1 8.5 %collective-permute-done.1 = f32[608,128]{1,0:T(8,128)S(1)} collective-permute-done((f32[608,128]{1,0:T(8,128)S(1)}, f32[608,128]{1,0:T(8,128)S(1)}, u32[]{:S(2)}, u32[]{:S(2)}) %collective-permute-start.1) | collective-permute-done | bytes 311328 | tf_op jit(solution)/shard_map/ppermute | solution.py:16
  27.1 3.0 %all_gather.15 = f32[960,128]{1,0:T(8,128)S(1)} all-gather(f32[480,128]{1,0:T(8,128)S(1)} %fusion.14), channel_id=1, replica_groups={{0,1},{2,3},{4,5},{6,7},{8,9},{10,11},{12,13},{14,15},{16,17},{18,19},{..., dimensions={0}, use_global_device_ids=true | all-gather | bytes 737280 | tf_op jit(solution)/shard_map/all_gather | solution.py:72
  37.6 7.8 %collective-permute-done.3 = f32[544,128]{1,0:T(8,128)S(1)} collective-permute-done((f32[544,128]{1,0:T(8,128)S(1)}, f32[544,128]{1,0:T(8,128)S(1)}, u32[]{:S(2)}, u32[]{:S(2)}) %collective-permute-start.3) | collective-permute-done | bytes 278560 | tf_op jit(solution)/shard_map/ppermute | solution.py:16
  47.4 6.9 %collective-permute-done.4 = f32[544,128]{1,0:T(8,128)S(1)} collective-permute-done((f32[544,128]{1,0:T(8,128)S(1)}, f32[544,128]{1,0:T(8,128)S(1)}, u32[]{:S(2)}, u32[]{:S(2)}) %collective-permute-start.4) | collective-permute-done | bytes 278560 | tf_op jit(solution)/shard_map/ppermute | solution.py:16
  57.7 3.9 %all_gather.16 = f32[832,128]{1,0:T(8,128)S(1)} all-gather(f32[416,128]{1,0:T(8,128)S(1)} %fusion.20), channel_id=1, replica_groups={{0,1},{2,3},{4,5},{6,7},{8,9},{10,11},{12,13},{14,15},{16,17},{18,19},{..., dimensions={0}, use_global_device_ids=true | all-gather | bytes 638976 | tf_op jit(solution)/shard_map/all_gather | solution.py:72
  68.0 7.1 %collective-permute-done.6 = f32[480,128]{1,0:T(8,128)S(1)} collective-permute-done((f32[480,128]{1,0:T(8,128)S(1)}, f32[480,128]{1,0:T(8,128)S(1)}, u32[]{:S(2)}, u32[]{:S(2)}) %collective-permute-start.6) | collective-permute-done | bytes 245792 | tf_op jit(solution)/shard_map/ppermute | solution.py:16
  77.1 6.2 %collective-permute-done.7 = f32[480,128]{1,0:T(8,128)S(1)} collective-permute-done((f32[480,128]{1,0:T(8,128)S(1)}, f32[480,128]{1,0:T(8,128)S(1)}, u32[]{:S(2)}, u32[]{:S(2)}) %collective-permute-start.7) | collective-permute-done | bytes 245792 | tf_op jit(solution)/shard_map/ppermute | solution.py:16
  85.2 13.7 %collective-permute-done.8 = f32[480,128]{1,0:T(8,128)S(1)} collective-permute-done((f32[480,128]{1,0:T(8,128)S(1)}, f32[480,128]{1,0:T(8,128)S(1)}, u32[]{:S(2)}, u32[]{:S(2)}) %collective-permute-start.8) | collective-permute-done | bytes 245792 | tf_op jit(solution)/shard_map/ppermute | solution.py:16
  108.8 13.1 %all_to_all.20 = f32[16,24,128]{2,1,0:T(8,128)S(1)} all-to-all(f32[16,24,128]{2,1,0:T(8,128)S(1)} %bitcast.459), channel_id=1, replica_groups={{0,2,4,6,8,10,12,14,16,18,20,22,24,26,28,30},{1,3,5,7,9,11,13,15,17,19,..., dimensions={0} | all-to-all | bytes 393216 | tf_op jit(solution)/shard_map/all_to_all | solution.py:83
  122.7 3.6 %all-to-all-start.1 = ((f32[16,2,24,128]{3,2,1,0:T(8,128)}), f32[16,2,24,128]{3,2,1,0:T(8,128)S(1)}, u32[]{:S(2)}, u32[]{:S(2)}) async-start(f32[16,2,24,128]{3,2,1,0:T(8,128)} %broadcast_in_dim.6), calls=%async_computation.1 | async-start | bytes 786432 | tf_op jit(solution)/shard_map/all_to_all | solution.py:88
  126.2 11.9 %all-to-all-done.1 = f32[16,2,24,128]{3,2,1,0:T(8,128)S(1)} async-done(((f32[16,2,24,128]{3,2,1,0:T(8,128)}), f32[16,2,24,128]{3,2,1,0:T(8,128)S(1)}, u32[]{:S(2)}, u32[]{:S(2)}) %all-to-all-start.1) | async-done | bytes 393248 | tf_op jit(solution)/shard_map/all_to_all | solution.py:88
  138.2 5.7 %collective-permute-start.10 = (f32[704,128]{1,0:T(8,128)S(1)}, f32[704,128]{1,0:T(8,128)S(1)}, u32[]{:S(2)}, u32[]{:S(2)}) collective-permute-start(f32[704,128]{1,0:T(8,128)S(1)} %pad_maximum_fusion.11), channel_id=1, source_target_pairs={{0,1},{1,0},{2,3},{3,2},{4,5},{5,4},{6,7},{7,6},{8,9},{9,8},{10,11... | collective-permute-start | bytes 1081352 | tf_op jit(solution)/shard_map/ppermute | solution.py:16
  154.9 21.6 %all_to_all.21 = f32[16,72,128]{2,1,0:T(8,128)S(1)} all-to-all(f32[16,72,128]{2,1,0:T(8,128)S(1)} %bitcast.448), channel_id=1, replica_groups={{0,2,4,6,8,10,12,14,16,18,20,22,24,26,28,30},{1,3,5,7,9,11,13,15,17,19,..., dimensions={0} | all-to-all | bytes 1179648 | tf_op jit(solution)/shard_map/all_to_all | solution.py:109
  176.6 5.8 %collective-permute-start.12 = (f32[72,128]{1,0:T(8,128)S(1)}, f32[72,128]{1,0:T(8,128)S(1)}, u32[]{:S(2)}, u32[]{:S(2)}) collective-permute-start(f32[72,128]{1,0:T(8,128)S(1)} %reduce_sum.19), channel_id=1, source_target_pairs={{0,32},{32,0},{64,96},{96,64},{128,160},{160,128},{192,224},{224,1... | collective-permute-start | bytes 110600 | tf_op jit(solution)/shard_map/ppermute | solution.py:16
  184.2 31.4 %all_to_all.22 = f32[16,2,72,128]{3,2,1,0:T(8,128)S(1)} all-to-all(f32[16,2,72,128]{3,2,1,0:T(8,128)S(1)} %broadcast_in_dim.7), channel_id=1, replica_groups={{0,2,4,6,8,10,12,14,16,18,20,22,24,26,28,30},{1,3,5,7,9,11,13,15,17,19,..., dimensions={0} | all-to-all | bytes 2359296 | tf_op jit(solution)/shard_map/all_to_all | solution.py:115
  216.8 6.2 %collective-permute-start.13 = (f32[2304,128]{1,0:T(8,128)}, f32[2304,128]{1,0:T(8,128)S(1)}, u32[]{:S(2)}, u32[]{:S(2)}) collective-permute-start(f32[2304,128]{1,0:T(8,128)} %pad_maximum_fusion.1), channel_id=1, source_target_pairs={{0,1},{1,0},{2,3},{3,2},{4,5},{5,4},{6,7},{7,6},{8,9},{9,8},{10,11... | collective-permute-start | bytes 3538952 | tf_op jit(solution)/shard_map/ppermute | solution.py:16
  223.0 2.7 collective-permute-done.13
  231.8 8.2 %collective-permute-start.14 = (f32[336,128]{1,0:T(8,128)S(1)}, f32[336,128]{1,0:T(8,128)S(1)}, u32[]{:S(2)}, u32[]{:S(2)}) collective-permute-start(f32[336,128]{1,0:T(8,128)S(1)} %constant_dynamic-slice_fusion), channel_id=1, source_target_pairs={{0,64},{32,96},{64,0},{96,32},{128,192},{160,224},{192,128},{224,1... | collective-permute-start | bytes 516104 | tf_op jit(solution)/shard_map/ppermute | solution.py:16
  240.1 4.4 %collective-permute-done.14 = f32[336,128]{1,0:T(8,128)S(1)} collective-permute-done((f32[336,128]{1,0:T(8,128)S(1)}, f32[336,128]{1,0:T(8,128)S(1)}, u32[]{:S(2)}, u32[]{:S(2)}) %collective-permute-start.14) | collective-permute-done | bytes 172064 | tf_op jit(solution)/shard_map/ppermute | solution.py:16
  244.5 11.9 %all_gather.18 = f32[1344,128]{1,0:T(8,128)S(1)} all-gather(f32[336,128]{1,0:T(8,128)S(1)} %collective-permute-done.14), channel_id=1, replica_groups={{0,1,2,3},{4,5,6,7},{8,9,10,11},{12,13,14,15},{16,17,18,19},{20,21,22,2..., dimensions={0}, use_global_device_ids=true | all-gather | bytes 860160 | tf_op jit(solution)/shard_map/all_gather | solution.py:143
  261.3 3.1 %collective-permute-start.15 = (f32[320,128]{1,0:T(8,128)S(1)}, f32[320,128]{1,0:T(8,128)S(1)}, u32[]{:S(2)}, u32[]{:S(2)}) collective-permute-start(f32[320,128]{1,0:T(8,128)S(1)} %fusion.28), channel_id=1, source_target_pairs={{0,128},{32,160},{64,192},{96,224},{128,0},{160,32},{192,64},{224,... | collective-permute-start | bytes 491528 | tf_op jit(solution)/shard_map/ppermute | solution.py:16
  264.5 4.4 %collective-permute-done.15 = f32[320,128]{1,0:T(8,128)S(1)} collective-permute-done((f32[320,128]{1,0:T(8,128)S(1)}, f32[320,128]{1,0:T(8,128)S(1)}, u32[]{:S(2)}, u32[]{:S(2)}) %collective-permute-start.15) | collective-permute-done | bytes 163872 | tf_op jit(solution)/shard_map/ppermute | solution.py:16
  275.3 4.7 %collective-permute-start.16 = (f32[192,128]{1,0:T(8,128)S(1)}, f32[192,128]{1,0:T(8,128)S(1)}, u32[]{:S(2)}, u32[]{:S(2)}) collective-permute-start(f32[192,128]{1,0:T(8,128)S(1)} %fusion.60), channel_id=1, source_target_pairs={{0,256},{32,288},{64,320},{96,352},{128,384},{160,416},{192,448},{... | collective-permute-start | bytes 294920 | tf_op jit(solution)/shard_map/ppermute | solution.py:16
  (231 shorter events, 80.3 us)
Async XLA Ops:
  1.3 0.8 copy-start.1
  1.4 1.1 copy-start
  3.1 10.0 %collective-permute-start = (f32[608,128]{1,0:T(8,128)S(1)}, f32[608,128]{1,0:T(8,128)S(1)}, u32[]{:S(2)}, u32[]{:S(2)}) collective-permute-start(f32[608,128]{1,0:T(8,128)S(1)} %pad_maximum_fusion.6), channel_id=1, source_target_pairs={{0,1},{1,0},{2,3},{3,2},{4,5},{5,4},{6,7},{7,6},{8,9},{9,8},{10,11... | collective-permute-start | bytes 933896 | tf_op jit(solution)/shard_map/ppermute | solution.py:16
  13.2 10.5 %collective-permute-start.1 = (f32[608,128]{1,0:T(8,128)S(1)}, f32[608,128]{1,0:T(8,128)S(1)}, u32[]{:S(2)}, u32[]{:S(2)}) collective-permute-start(f32[608,128]{1,0:T(8,128)S(1)} %fusion.1), channel_id=1, source_target_pairs={{0,2},{1,3},{2,0},{3,1},{4,6},{5,7},{6,4},{7,5},{8,10},{9,11},{10,... | collective-permute-start | bytes 933896 | tf_op jit(solution)/shard_map/ppermute | solution.py:16
  32.1 3.5 %collective-permute-start.2 = (f32[544,128]{1,0:T(8,128)S(1)}, f32[544,128]{1,0:T(8,128)S(1)}, u32[]{:S(2)}, u32[]{:S(2)}) collective-permute-start(f32[544,128]{1,0:T(8,128)S(1)} %pad_maximum_fusion.9), channel_id=1, source_target_pairs={{0,1},{1,0},{2,3},{3,2},{4,5},{5,4},{6,7},{7,6},{8,9},{9,8},{10,11... | collective-permute-start | bytes 835592 | tf_op jit(solution)/shard_map/ppermute | solution.py:16
  35.6 9.8 %collective-permute-start.3 = (f32[544,128]{1,0:T(8,128)S(1)}, f32[544,128]{1,0:T(8,128)S(1)}, u32[]{:S(2)}, u32[]{:S(2)}) collective-permute-start(f32[544,128]{1,0:T(8,128)S(1)} %fusion.8), channel_id=1, source_target_pairs={{0,2},{1,3},{2,0},{3,1},{4,6},{5,7},{6,4},{7,5},{8,10},{9,11},{10,... | collective-permute-start | bytes 835592 | tf_op jit(solution)/shard_map/ppermute | solution.py:16
  45.4 8.8 %collective-permute-start.4 = (f32[544,128]{1,0:T(8,128)S(1)}, f32[544,128]{1,0:T(8,128)S(1)}, u32[]{:S(2)}, u32[]{:S(2)}) collective-permute-start(f32[544,128]{1,0:T(8,128)S(1)} %add.313), channel_id=1, source_target_pairs={{0,4},{1,5},{2,6},{3,7},{4,0},{5,1},{6,2},{7,3},{8,12},{9,13},{10,... | collective-permute-start | bytes 835592 | tf_op jit(solution)/shard_map/ppermute | solution.py:16
  62.6 3.4 %collective-permute-start.5 = (f32[480,128]{1,0:T(8,128)S(1)}, f32[480,128]{1,0:T(8,128)S(1)}, u32[]{:S(2)}, u32[]{:S(2)}) collective-permute-start(f32[480,128]{1,0:T(8,128)S(1)} %pad_maximum_fusion.13), channel_id=1, source_target_pairs={{0,1},{1,0},{2,3},{3,2},{4,5},{5,4},{6,7},{7,6},{8,9},{9,8},{10,11... | collective-permute-start | bytes 737288 | tf_op jit(solution)/shard_map/ppermute | solution.py:16
  66.0 9.1 %collective-permute-start.6 = (f32[480,128]{1,0:T(8,128)S(1)}, f32[480,128]{1,0:T(8,128)S(1)}, u32[]{:S(2)}, u32[]{:S(2)}) collective-permute-start(f32[480,128]{1,0:T(8,128)S(1)} %fusion.11), channel_id=1, source_target_pairs={{0,2},{1,3},{2,0},{3,1},{4,6},{5,7},{6,4},{7,5},{8,10},{9,11},{10,... | collective-permute-start | bytes 737288 | tf_op jit(solution)/shard_map/ppermute | solution.py:16
  75.1 8.1 %collective-permute-start.7 = (f32[480,128]{1,0:T(8,128)S(1)}, f32[480,128]{1,0:T(8,128)S(1)}, u32[]{:S(2)}, u32[]{:S(2)}) collective-permute-start(f32[480,128]{1,0:T(8,128)S(1)} %add.326), channel_id=1, source_target_pairs={{0,4},{1,5},{2,6},{3,7},{4,0},{5,1},{6,2},{7,3},{8,12},{9,13},{10,... | collective-permute-start | bytes 737288 | tf_op jit(solution)/shard_map/ppermute | solution.py:16
  83.3 15.7 %collective-permute-start.8 = (f32[480,128]{1,0:T(8,128)S(1)}, f32[480,128]{1,0:T(8,128)S(1)}, u32[]{:S(2)}, u32[]{:S(2)}) collective-permute-start(f32[480,128]{1,0:T(8,128)S(1)} %add.327), channel_id=1, source_target_pairs={{0,8},{1,9},{2,10},{3,11},{4,12},{5,13},{6,14},{7,15},{8,0},{9,1},... | collective-permute-start | bytes 737288 | tf_op jit(solution)/shard_map/ppermute | solution.py:16
  105.4 3.3 %collective-permute-start.9 = (f32[352,128]{1,0:T(8,128)S(1)}, f32[352,128]{1,0:T(8,128)S(1)}, u32[]{:S(2)}, u32[]{:S(2)}) collective-permute-start(f32[352,128]{1,0:T(8,128)S(1)} %constant_dynamic-slice_fusion.2), channel_id=1, source_target_pairs={{0,1},{1,0},{2,3},{3,2},{4,5},{5,4},{6,7},{7,6},{8,9},{9,8},{10,11... | collective-permute-start | bytes 540680 | tf_op jit(solution)/shard_map/ppermute | solution.py:16
  122.7 15.5 %all-to-all-start.1 = ((f32[16,2,24,128]{3,2,1,0:T(8,128)}), f32[16,2,24,128]{3,2,1,0:T(8,128)S(1)}, u32[]{:S(2)}, u32[]{:S(2)}) async-start(f32[16,2,24,128]{3,2,1,0:T(8,128)} %broadcast_in_dim.6), calls=%async_computation.1 | async-start | bytes 786432 | tf_op jit(solution)/shard_map/all_to_all | solution.py:88
  138.2 7.0 %collective-permute-start.10 = (f32[704,128]{1,0:T(8,128)S(1)}, f32[704,128]{1,0:T(8,128)S(1)}, u32[]{:S(2)}, u32[]{:S(2)}) collective-permute-start(f32[704,128]{1,0:T(8,128)S(1)} %pad_maximum_fusion.11), channel_id=1, source_target_pairs={{0,1},{1,0},{2,3},{3,2},{4,5},{5,4},{6,7},{7,6},{8,9},{9,8},{10,11... | collective-permute-start | bytes 1081352 | tf_op jit(solution)/shard_map/ppermute | solution.py:16
  150.9 3.9 %collective-permute-start.11 = (f32[1152,128]{1,0:T(8,128)S(1)}, f32[1152,128]{1,0:T(8,128)S(1)}, u32[]{:S(2)}, u32[]{:S(2)}) collective-permute-start(f32[1152,128]{1,0:T(8,128)S(1)} %constant_dynamic-slice_fusion.1), channel_id=1, source_target_pairs={{0,1},{1,0},{2,3},{3,2},{4,5},{5,4},{6,7},{7,6},{8,9},{9,8},{10,11... | collective-permute-start | bytes 1769480 | tf_op jit(solution)/shard_map/ppermute | solution.py:16
  176.6 7.5 %collective-permute-start.12 = (f32[72,128]{1,0:T(8,128)S(1)}, f32[72,128]{1,0:T(8,128)S(1)}, u32[]{:S(2)}, u32[]{:S(2)}) collective-permute-start(f32[72,128]{1,0:T(8,128)S(1)} %reduce_sum.19), channel_id=1, source_target_pairs={{0,32},{32,0},{64,96},{96,64},{128,160},{160,128},{192,224},{224,1... | collective-permute-start | bytes 110600 | tf_op jit(solution)/shard_map/ppermute | solution.py:16
  216.8 8.9 %collective-permute-start.13 = (f32[2304,128]{1,0:T(8,128)}, f32[2304,128]{1,0:T(8,128)S(1)}, u32[]{:S(2)}, u32[]{:S(2)}) collective-permute-start(f32[2304,128]{1,0:T(8,128)} %pad_maximum_fusion.1), channel_id=1, source_target_pairs={{0,1},{1,0},{2,3},{3,2},{4,5},{5,4},{6,7},{7,6},{8,9},{9,8},{10,11... | collective-permute-start | bytes 3538952 | tf_op jit(solution)/shard_map/ppermute | solution.py:16
  231.8 12.6 %collective-permute-start.14 = (f32[336,128]{1,0:T(8,128)S(1)}, f32[336,128]{1,0:T(8,128)S(1)}, u32[]{:S(2)}, u32[]{:S(2)}) collective-permute-start(f32[336,128]{1,0:T(8,128)S(1)} %constant_dynamic-slice_fusion), channel_id=1, source_target_pairs={{0,64},{32,96},{64,0},{96,32},{128,192},{160,224},{192,128},{224,1... | collective-permute-start | bytes 516104 | tf_op jit(solution)/shard_map/ppermute | solution.py:16
  261.3 7.5 %collective-permute-start.15 = (f32[320,128]{1,0:T(8,128)S(1)}, f32[320,128]{1,0:T(8,128)S(1)}, u32[]{:S(2)}, u32[]{:S(2)}) collective-permute-start(f32[320,128]{1,0:T(8,128)S(1)} %fusion.28), channel_id=1, source_target_pairs={{0,128},{32,160},{64,192},{96,224},{128,0},{160,32},{192,64},{224,... | collective-permute-start | bytes 491528 | tf_op jit(solution)/shard_map/ppermute | solution.py:16
  275.3 7.4 %collective-permute-start.16 = (f32[192,128]{1,0:T(8,128)S(1)}, f32[192,128]{1,0:T(8,128)S(1)}, u32[]{:S(2)}, u32[]{:S(2)}) collective-permute-start(f32[192,128]{1,0:T(8,128)S(1)} %fusion.60), channel_id=1, source_target_pairs={{0,256},{32,288},{64,320},{96,352},{128,384},{160,416},{192,448},{... | collective-permute-start | bytes 294920 | tf_op jit(solution)/shard_map/ppermute | solution.py:16

commit v2 on v0

v2 whole, which is shorter than its diff:
```python
import functools

import jax
import jax.numpy as jnp
from jax import lax
from jax.experimental import pallas as pl
from jax.experimental.pallas import tpu as pltpu
from jax.sharding import PartitionSpec as P

VMEM_BYTES = 40 * 2**20


def dot(a, b):
    return jnp.dot(a, b, precision=lax.Precision.HIGH)


def split(value):
    high = value.astype(jnp.bfloat16)
    low = (value - high.astype(jnp.float32)).astype(jnp.bfloat16)
    return high, low


def dot_split(a, b):
    def part(x, y):
        return jnp.dot(x, y, preferred_element_type=jnp.float32)

    return part(a[0], b[0]) + (part(a[0], b[1]) + part(a[1], b[0]))


def kdot(a, b):
    return dot_split(split(a), split(b))


def inverse_of(error):
    total = jnp.eye(error.shape[0], dtype=jnp.float32) + error
    power = error
    for step in range(6):
        parts = split(power)
        power = dot_split(parts, parts)
        total = total + kdot(total, power)
    return total


def solve_own(gram_own, gram_sib, proj_own, proj_sib):
    inverse = inverse_of(kdot(gram_own, gram_sib))
    return kdot(proj_sib - kdot(proj_own, gram_sib), inverse)


def leaf_kernel(own, sib, z_out):
    rank = own.shape[1]
    z_out[...] = solve_own(own[:rank], sib[:rank], own[rank:], sib[rank:])


def node_kernel(count, own, sib, ops_own, ops_sib, sums, z_out, node_out):
    rank = own.shape[1]
    width = own.shape[0] - rank
    gram_own = own[:rank]
    proj_own = own[rank:]
    z = solve_own(gram_own, sib[:rank], proj_own, sib[rank:])
    z_out[...] = z
    z_sib = proj_own - kdot(z, gram_own)
    z_both = split(jnp.concatenate([z, z_sib], axis=1))
    for j in range(count):
        at = slice(j * rank, (j + 1) * rank)
        left = split(jnp.concatenate([ops_own[at], ops_sib[at]], axis=0))
        rows = slice(j * width, (j + 1) * width)
        node_out[rows] = sums[rows] - dot_split(z_both, left)


def call(kernel, outs, *args):
    flops = 2 * 3 * 128 * 128 * (sum(a.shape[0] for a in args) + 14 * 128)
    return pl.pallas_call(
        kernel,
        out_shape=[jax.ShapeDtypeStruct(o, jnp.float32) for o in outs],
        compiler_params=pltpu.CompilerParams(vmem_limit_bytes=VMEM_BYTES),
        cost_estimate=pl.CostEstimate(
            flops=flops, bytes_accessed=4 * sum(a.size for a in args), transcendentals=0
        ),
    )(*args)


def solve_leaf(own, sib):
    rank = own.shape[1]
    return call(leaf_kernel, [(own.shape[0] - rank, rank)], own, sib)[0]


def solve_node(own, sib, ops_own, ops_sib, sums):
    rank = own.shape[1]
    count = ops_own.shape[0] // rank
    outs = [(own.shape[0] - rank, rank), sums.shape]
    return call(functools.partial(node_kernel, count), outs, own, sib, ops_own, ops_sib, sums)


def partner(value, bit, gy_bits):
    axis, shift = ("gy", bit) if bit < gy_bits else ("gx", bit - gy_bits)
    mask = 1 << shift
    return lax.ppermute(value, axis, [(s, s ^ mask) for s in range(lax.axis_size(axis))])


def groups_of(count, size):
    return [list(range(i, i + size)) for i in range(0, count, size)]


def chip_groups(count, chips):
    size = 2 * chips
    return [
        list(range(start + c, start + size, 2)) for start in range(0, count, size) for c in range(2)
    ]


def pad_rows(value, rows):
    return jnp.pad(value, ((0, rows - value.shape[0]), (0, 0)))


def up8(value):
    return -(-value // 8) * 8


def reduce_shares(both, sums, chips, groups):
    rank = both.shape[1]
    share_both = up8(-(-both.shape[0] // chips))
    share_sums = up8(-(-sums.shape[0] // chips))
    sent = jnp.concatenate(
        [
            pad_rows(both, share_both * chips).reshape(chips, share_both, rank),
            pad_rows(sums, share_sums * chips).reshape(chips, share_sums, rank),
        ],
        axis=1,
    )
    pieces = lax.all_to_all(sent, "gy", 0, 0, axis_index_groups=groups)
    return pieces, share_both


def gather_shares(first, second, sums, rows_both, rows_sums, chips, groups):
    rank = sums.shape[1]
    n = first.shape[0]
    share = jnp.concatenate([first, second, sums], axis=0)
    out = lax.all_to_all(
        jnp.broadcast_to(share, (chips,) + share.shape), "gy", 0, 0, axis_index_groups=groups
    )
    return (
        out[:, :n].reshape(-1, rank)[:rows_both],
        out[:, n : 2 * n].reshape(-1, rank)[:rows_both],
        out[:, 2 * n :].reshape(-1, rank)[:rows_sums],
    )


def half_of(value, core):
    rows = value.shape[0] // 2
    return lax.dynamic_slice_in_dim(value, core * rows, rows, 0)


def from_cores(gathered, at, rows, size):
    return [gathered[c * size + at : c * size + at + rows] for c in range(2)]


def shards(right_sides, factor_u, factor_v):
    gy_size = lax.axis_size("gy")
    gy_bits = gy_size.bit_length() - 1
    levels, _, rank = factor_u.shape
    gy = lax.axis_index("gy")
    core = gy & 1
    pairs = groups_of(gy_size, 2)
    quads = groups_of(gy_size, 4)

    carried = jnp.concatenate([factor_u[j].T for j in range(levels)] + [right_sides.T], axis=0)

    for level in (0, 2):
        lower = dot(carried, factor_v[level])
        upper = dot(carried, factor_v[level + 1])
        shared = 2 * rank
        rest = (carried.shape[0] - shared) // 2

        def rows_for(side):
            both = [lower[:shared], half_of(lower[shared:], side), upper[:rank]]
            sums = [upper[rank:shared], half_of(upper[shared:], side)]
            return jnp.concatenate(both + sums, axis=0)

        chip = rows_for(core) + partner(rows_for(1 - core), 0, gy_bits)
        top = shared + rest
        n_both = top + rank
        n_sums = rank + rest
        if level == 0:
            near = partner(chip, 1, gy_bits)
            own, sib = chip[:n_both], near[:n_both]
            sums = chip[n_both:] + near[n_both:]
        else:
            chips = 8
            groups = chip_groups(gy_size, chips)
            pieces, share = reduce_shares(chip[:n_both], chip[n_both:], chips, groups)
            side_sums = pieces.reshape((2, chips // 2) + pieces.shape[1:]).sum(axis=1)
            first, second, sums = gather_shares(
                side_sums[0, :share],
                side_sums[1, :share],
                side_sums[0, share:] + side_sums[1, share:],
                n_both,
                n_sums,
                chips,
                groups,
            )
            second_side = (gy >> (level + 1)) & 1 == 1
            own = jnp.where(second_side, second, first)
            sib = jnp.where(second_side, first, second)
        z_low, node = solve_node(own[:top], sib[:top], own[top:], sib[top:], sums)
        z_up = solve_leaf(node, partner(node, level + 2, gy_bits))
        halves = lax.all_gather(
            jnp.concatenate([z_low[rank:], z_up], axis=0),
            "gy",
            axis_index_groups=pairs,
            axis=0,
            tiled=True,
        )
        z_rest = jnp.concatenate(
            [
                jnp.concatenate(from_cores(halves, 0, rest, 2 * rest), axis=0),
                jnp.concatenate(from_cores(halves, rest, rest, 2 * rest), axis=0),
            ],
            axis=1,
        )
        left = carried[:rank]
        next_left = carried[rank:shared] - dot(z_low[:rank], left)
        carried = carried[shared:] - dot(z_rest, jnp.concatenate([left, next_left], axis=0))

    level = gy_bits - 1
    count = levels - level
    width = carried.shape[0]
    first = dot(carried, factor_v[level])
    higher = [dot(carried, factor_v[j]) for j in range(level + 1, levels)]
    both = jnp.concatenate([first] + [h[:rank] for h in higher], axis=0)
    sums = jnp.concatenate([h[rank:] for h in higher], axis=0)
    n_both = both.shape[0] // 2
    n_sums = sums.shape[0] // 2

    def state_for(side):
        return jnp.concatenate([half_of(both, side), half_of(sums, side)], axis=0)

    chip = state_for(core) + partner(state_for(1 - core), 0, gy_bits)
    chips = gy_size // 2
    groups = chip_groups(gy_size, chips)
    pieces, share = reduce_shares(chip[:n_both], chip[n_both:], chips, groups)
    piece = pieces.sum(axis=0)
    near = partner(piece, level + 1, gy_bits)
    mine = jnp.concatenate(
        gather_shares(
            piece[:share], near[:share], piece[share:] + near[share:], n_both, n_sums, chips, groups
        ),
        axis=0,
    )
    other = partner(mine, 0, gy_bits)
    front = jnp.where(core == 0, mine, other)
    back = jnp.where(core == 0, other, mine)

    def joined(at, rows):
        return jnp.concatenate([front[at : at + rows], back[at : at + rows]], axis=0)

    own = joined(0, n_both)
    sib = joined(n_both, n_both)
    sums = joined(2 * n_both, n_sums)
    z, node = solve_node(own[:width], sib[:width], own[width:], sib[width:], sums)
    carried = carried[rank:] - dot(z, carried[:rank])

    while True:
        level, count, width = level + 1, count - 1, width - rank
        total = node.shape[0]
        if total > 1024:
            quarter = total // 4
            part = lax.dynamic_slice_in_dim(node, (gy & 3) * quarter, quarter, 0)
            near = lax.all_gather(
                partner(part, level + 1, gy_bits), "gy", axis_index_groups=quads, axis=0, tiled=True
            )
        elif total > 512:
            near = lax.all_gather(
                partner(half_of(node, core), level + 1, gy_bits),
                "gy",
                axis_index_groups=pairs,
                axis=0,
                tiled=True,
            )
        else:
            near = partner(node, level + 1, gy_bits)
        if count == 1:
            z = solve_leaf(node, near)
            return (carried[rank:] - dot(z, carried[:rank])).T
        node = node.reshape(count, width, rank)
        near = near.reshape(count, width, rank)
        ops_own = node[1:, :rank].reshape(-1, rank)
        ops_sib = near[1:, :rank].reshape(-1, rank)
        sums = (node[1:, rank:] + near[1:, rank:]).reshape(-1, rank)
        z, node = solve_node(node[0], near[0], ops_own, ops_sib, sums)
        carried = carried[rank:] - dot(z, carried[:rank])


def solution(mesh):
    placed = (P(("gx", "gy"), None), P(None, ("gx", "gy"), None), P(None, ("gx", "gy"), None))
    return jax.shard_map(
        shards, mesh=mesh, in_specs=placed, out_specs=P(("gx", "gy"), None), check_vma=False
    )
```

time: 544 us -> 258 us (0.47)
  the two profiles are of different devices: /device:TPU:28 before, /device:TPU:1 now
where the time goes in v2:
time: 258 us; the launch traced here: 257 us
  blocking collectives  91.3 us (35%)
  waiting for transfers between devices  75.5 us (29%)
  starting transfers between devices  51.7 us (20%)
  Pallas kernels  16.7 us (6%)
  local copies, waits for them, and re-layouts  13.7 us (5%)
  matrix products  6.08 us (2%)
    ppermute x11, waiting for transfers between devices, partner(): lax.ppermute(value, axis, [(s, s ^ mask) for s in range(lax.axis_size(axi...  53.1 us
    ppermute x11, starting transfers between devices, partner(): lax.ppermute(value, axis, [(s, s ^ mask) for s in range(lax.axis_size(axi...  47.9 us
    all_to_all x2, blocking collectives, reduce_shares(): pieces = lax.all_to_all(sent, 'gy', 0, 0, axis_index_groups=groups)  42.7 us
    all_to_all x1, blocking collectives, gather_shares(): lax.all_to_all(jnp.broadcast_to(share, (chips,) + share.shape), 'gy', 0,...  25.9 us
    all_to_all x1, waiting for transfers between devices, gather_shares(): lax.all_to_all(jnp.broadcast_to(share, (chips,) + share.shape), 'gy', 0,...  22.4 us
    pallas_call x8, Pallas kernels, call(): pl.pallas_call(kernel, out_shape=[jax.ShapeDtypeStruct(o, jnp.float32) fo...  16.7 us
    all_gather x1, blocking collectives, shards(): lax.all_gather(partner(part, level + 1, gy_bits), 'gy', axis_index_groups...  11.6 us
    all_gather x2, blocking collectives, shards(): lax.all_gather(jnp.concatenate([z_low[rank:], z_up], axis=0), 'gy', axis_...  8.39 us
  transfers between devices with their start and end apart: 12, of which 12 were waited for; matrix products, arithmetic and copies ran while one was open for 1% of the time, Pallas kernels for 0%

profile of v2, /device:TPU:1, one launch (start us, length us, event | category | flops | bytes accessed | tf_op | source)
XLA Modules:
  0.0 257.2 jit_solution(14042675408659914923)
XLA Ops:
  5.7 8.8 %collective-permute-start = (f32[1344,128]{1,0:T(8,128)S(1)}, f32[1344,128]{1,0:T(8,128)S(1)}, u32[]{:S(2)}, u32[]{:S(2)}) collective-permute-start(f32[1344,128]{1,0:T(8,128)S(1)} %fusion.10), channel_id=1, source_target_pairs={{0,1},{1,0},{2,3},{3,2},{4,5},{5,4},{6,7},{7,6},{8,9},{9,8},{10,11... | collective-permute-start | bytes 2064392 | tf_op jit(solution)/shard_map/ppermute | solution.py:97
  18.3 16.6 %collective-permute-done.1 = f32[1344,128]{1,0:T(8,128)S(1)} collective-permute-done((f32[1344,128]{1,0:T(8,128)S(1)}, f32[1344,128]{1,0:T(8,128)S(1)}, u32[]{:S(2)}, u32[]{:S(2)}) %collective-permute-start.1) | collective-permute-done | bytes 688160 | tf_op jit(solution)/shard_map/ppermute | solution.py:97
  35.0 2.4 shard_map.37
  40.4 5.8 %collective-permute-done.2.sib = f32[544,128]{1,0:T(8,128)S(1)} collective-permute-done((f32[544,128]{1,0:T(8,128)S(1)}, f32[544,128]{1,0:T(8,128)S(1)}, u32[]{:S(2)}, u32[]{:S(2)}) %collective-permute-start.2) | collective-permute-done | bytes 278560 | tf_op jit(solution)/shard_map/ppermute | solution.py:97
  48.0 4.2 %all_gather.12 = f32[1664,128]{1,0:T(8,128)S(1)} all-gather(f32[832,128]{1,0:T(8,128)S(1)} %pad_maximum_fusion.15), channel_id=1, replica_groups={{0,1},{2,3},{4,5},{6,7},{8,9},{10,11},{12,13},{14,15},{16,17},{18,19},{..., dimensions={0}, use_global_device_ids=true | all-gather | bytes 1277952 | tf_op jit(solution)/shard_map/all_gather | solution.py:206
  60.1 18.1 %all_to_all.20 = f32[8,144,128]{2,1,0:T(8,128)S(1)} all-to-all(f32[8,144,128]{2,1,0:T(8,128)S(1)} %pad_maximum_fusion.12), channel_id=1, replica_groups={{0,2,4,6,8,10,12,14},{1,3,5,7,9,11,13,15},{16,18,20,22,24,26,28,30},{17..., dimensions={0} | all-to-all | bytes 1179648 | tf_op jit(solution)/shard_map/all_to_all | solution.py:130
  79.4 3.7 %all-to-all-start.1 = ((f32[8,232,128]{2,1,0:T(8,128)}), f32[8,232,128]{2,1,0:T(8,128)S(1)}, u32[]{:S(2)}, u32[]{:S(2)}) async-start(f32[8,232,128]{2,1,0:T(8,128)} %broadcast_in_dim.6), calls=%async_computation.1 | async-start | bytes 1900544 | tf_op jit(solution)/shard_map/all_to_all | solution.py:138
  83.1 22.4 %all-to-all-done.1 = f32[8,232,128]{2,1,0:T(8,128)S(1)} async-done(((f32[8,232,128]{2,1,0:T(8,128)}), f32[8,232,128]{2,1,0:T(8,128)S(1)}, u32[]{:S(2)}, u32[]{:S(2)}) %all-to-all-start.1) | async-done | bytes 950304 | tf_op jit(solution)/shard_map/all_to_all | solution.py:138
  108.0 3.2 %collective-permute-start.4 = (f32[416,128]{1,0:T(8,128)S(1)}, f32[416,128]{1,0:T(8,128)S(1)}, u32[]{:S(2)}, u32[]{:S(2)}) collective-permute-start(f32[416,128]{1,0:T(8,128)S(1)} %get-tuple-element.18.own), channel_id=1, source_target_pairs={{0,16},{1,17},{2,18},{3,19},{4,20},{5,21},{6,22},{7,23},{8,24},{9,... | collective-permute-start | bytes 638984 | tf_op jit(solution)/shard_map/ppermute | solution.py:97
  111.4 11.6 %collective-permute-done.4.sib = f32[416,128]{1,0:T(8,128)S(1)} collective-permute-done((f32[416,128]{1,0:T(8,128)S(1)}, f32[416,128]{1,0:T(8,128)S(1)}, u32[]{:S(2)}, u32[]{:S(2)}) %collective-permute-start.4) | collective-permute-done | bytes 213024 | tf_op jit(solution)/shard_map/ppermute | solution.py:97
  124.7 4.2 %all_gather.13 = f32[1152,128]{1,0:T(8,128)S(1)} all-gather(f32[576,128]{1,0:T(8,128)S(1)} %pad_maximum_fusion.18), channel_id=1, replica_groups={{0,1},{2,3},{4,5},{6,7},{8,9},{10,11},{12,13},{14,15},{16,17},{18,19},{..., dimensions={0}, use_global_device_ids=true | all-gather | bytes 884736 | tf_op jit(solution)/shard_map/all_gather | solution.py:206
  139.6 24.6 %all_to_all.21 = f32[16,80,128]{2,1,0:T(8,128)S(1)} all-to-all(f32[16,80,128]{2,1,0:T(8,128)S(1)} %pad_maximum_fusion.11), channel_id=1, replica_groups={{0,2,4,6,8,10,12,14,16,18,20,22,24,26,28,30},{1,3,5,7,9,11,13,15,17,19,..., dimensions={0} | all-to-all | bytes 1310720 | tf_op jit(solution)/shard_map/all_to_all | solution.py:130
  164.3 5.3 %collective-permute-start.6 = (f32[80,128]{1,0:T(8,128)S(1)}, f32[80,128]{1,0:T(8,128)S(1)}, u32[]{:S(2)}, u32[]{:S(2)}) collective-permute-start(f32[80,128]{1,0:T(8,128)S(1)} %reduce_sum.19), channel_id=1, source_target_pairs={{0,32},{32,0},{64,96},{96,64},{128,160},{160,128},{192,224},{224,1... | collective-permute-start | bytes 122888 | tf_op jit(solution)/shard_map/ppermute | solution.py:97
  171.2 25.9 %all_to_all.22 = f32[16,112,128]{2,1,0:T(8,128)S(1)} all-to-all(f32[16,112,128]{2,1,0:T(8,128)S(1)} %broadcast_in_dim.7), channel_id=1, replica_groups={{0,2,4,6,8,10,12,14,16,18,20,22,24,26,28,30},{1,3,5,7,9,11,13,15,17,19,..., dimensions={0} | all-to-all | bytes 1835008 | tf_op jit(solution)/shard_map/all_to_all | solution.py:138
  197.2 6.4 %collective-permute-start.7 = (f32[1632,128]{1,0:T(8,128)S(1)}, f32[1632,128]{1,0:T(8,128)S(1)}, u32[]{:S(2)}, u32[]{:S(2)}) collective-permute-start(f32[1632,128]{1,0:T(8,128)S(1)} %pad_maximum_fusion.4), channel_id=1, source_target_pairs={{0,1},{1,0},{2,3},{3,2},{4,5},{5,4},{6,7},{7,6},{8,9},{9,8},{10,11... | collective-permute-start | bytes 2506760 | tf_op jit(solution)/shard_map/ppermute | solution.py:97
  205.8 2.7 %shard_map.41 = (f32[448,128]{1,0:T(8,128)S(1)}, f32[1344,128]{1,0:T(8,128)S(1)}) custom-call(f32[576,128]{1,0:T(8,128)S(1)} %pad_maximum_fusion.17.own, f32[576,128]{1,0:T(8,128)S(1)} %pad_maximum_fusion.16.sib, f32[384,128]{1,0:T(8,128)S(1)} %get-tuple-element.36.ops_own, f32[384,128]{1,0:T(8,128)S(1)} %get-tuple-element.35.ops_sib, ...), custom_call_target="tpu_custom_call" | custom-call | flops 497025024 | bytes 1671168 | tf_op jit(solution)/shard_map/pallas_call | solution.py:72
  208.6 8.2 %collective-permute-start.8 = (f32[336,128]{1,0:T(8,128)S(1)}, f32[336,128]{1,0:T(8,128)S(1)}, u32[]{:S(2)}, u32[]{:S(2)}) collective-permute-start(f32[336,128]{1,0:T(8,128)S(1)} %constant_dynamic-slice_fusion.1), channel_id=1, source_target_pairs={{0,64},{32,96},{64,0},{96,32},{128,192},{160,224},{192,128},{224,1... | collective-permute-start | bytes 516104 | tf_op jit(solution)/shard_map/ppermute | solution.py:97
  217.0 4.2 %collective-permute-done.8 = f32[336,128]{1,0:T(8,128)S(1)} collective-permute-done((f32[336,128]{1,0:T(8,128)S(1)}, f32[336,128]{1,0:T(8,128)S(1)}, u32[]{:S(2)}, u32[]{:S(2)}) %collective-permute-start.8) | collective-permute-done | bytes 172064 | tf_op jit(solution)/shard_map/ppermute | solution.py:97
  221.2 11.6 %all_gather.14 = f32[1344,128]{1,0:T(8,128)S(1)} all-gather(f32[336,128]{1,0:T(8,128)S(1)} %collective-permute-done.8), channel_id=1, replica_groups={{0,1,2,3},{4,5,6,7},{8,9,10,11},{12,13,14,15},{16,17,18,19},{20,21,22,2..., dimensions={0}, use_global_device_ids=true | all-gather | bytes 860160 | tf_op jit(solution)/shard_map/all_gather | solution.py:268
  235.2 3.1 %collective-permute-start.9 = (f32[320,128]{1,0:T(8,128)S(1)}, f32[320,128]{1,0:T(8,128)S(1)}, u32[]{:S(2)}, u32[]{:S(2)}) collective-permute-start(f32[320,128]{1,0:T(8,128)S(1)} %get-tuple-element.63), channel_id=1, source_target_pairs={{0,128},{32,160},{64,192},{96,224},{128,0},{160,32},{192,64},{224,... | collective-permute-start | bytes 491528 | tf_op jit(solution)/shard_map/ppermute | solution.py:97
  238.5 4.2 %collective-permute-done.9 = f32[320,128]{1,0:T(8,128)S(1)} collective-permute-done((f32[320,128]{1,0:T(8,128)S(1)}, f32[320,128]{1,0:T(8,128)S(1)}, u32[]{:S(2)}, u32[]{:S(2)}) %collective-permute-start.9) | collective-permute-done | bytes 163872 | tf_op jit(solution)/shard_map/ppermute | solution.py:97
  242.7 2.6 %all_gather.15 = f32[640,128]{1,0:T(8,128)S(1)} all-gather(f32[320,128]{1,0:T(8,128)S(1)} %collective-permute-done.9), channel_id=1, replica_groups={{0,1},{2,3},{4,5},{6,7},{8,9},{10,11},{12,13},{14,15},{16,17},{18,19},{..., dimensions={0}, use_global_device_ids=true | all-gather | bytes 491520 | tf_op jit(solution)/shard_map/all_gather | solution.py:272
  247.5 4.6 %collective-permute-start.10 = (f32[192,128]{1,0:T(8,128)S(1)}, f32[192,128]{1,0:T(8,128)S(1)}, u32[]{:S(2)}, u32[]{:S(2)}) collective-permute-start(f32[192,128]{1,0:T(8,128)S(1)} %get-tuple-element.24.own), channel_id=1, source_target_pairs={{0,256},{32,288},{64,320},{96,352},{128,384},{160,416},{192,448},{... | collective-permute-start | bytes 294920 | tf_op jit(solution)/shard_map/ppermute | solution.py:97
  252.3 2.5 collective-permute-done.10.sib
  (165 shorter events, 49.2 us)
Async XLA Ops:
  2.0 1.1 copy-start.6
  2.0 0.8 copy-start.7
  3.8 0.8 copy-start.2
  4.6 1.0 slice-start.1
  5.7 10.5 %collective-permute-start = (f32[1344,128]{1,0:T(8,128)S(1)}, f32[1344,128]{1,0:T(8,128)S(1)}, u32[]{:S(2)}, u32[]{:S(2)}) collective-permute-start(f32[1344,128]{1,0:T(8,128)S(1)} %fusion.10), channel_id=1, source_target_pairs={{0,1},{1,0},{2,3},{3,2},{4,5},{5,4},{6,7},{7,6},{8,9},{9,8},{10,11... | collective-permute-start | bytes 2064392 | tf_op jit(solution)/shard_map/ppermute | solution.py:97
  16.4 18.5 %collective-permute-start.1 = (f32[1344,128]{1,0:T(8,128)S(1)}, f32[1344,128]{1,0:T(8,128)S(1)}, u32[]{:S(2)}, u32[]{:S(2)}) collective-permute-start(f32[1344,128]{1,0:T(8,128)S(1)} %fusion.9), channel_id=1, source_target_pairs={{0,2},{1,3},{2,0},{3,1},{4,6},{5,7},{6,4},{7,5},{8,10},{9,11},{10,... | collective-permute-start | bytes 2064392 | tf_op jit(solution)/shard_map/ppermute | solution.py:97
  37.4 8.8 %collective-permute-start.2 = (f32[544,128]{1,0:T(8,128)S(1)}, f32[544,128]{1,0:T(8,128)S(1)}, u32[]{:S(2)}, u32[]{:S(2)}) collective-permute-start(f32[544,128]{1,0:T(8,128)S(1)} %get-tuple-element.16.own), channel_id=1, source_target_pairs={{0,4},{1,5},{2,6},{3,7},{4,0},{5,1},{6,2},{7,3},{8,12},{9,13},{10,... | collective-permute-start | bytes 835592 | tf_op jit(solution)/shard_map/ppermute | solution.py:97
  52.8 58.4 %copy-start = (f32[832,128]{1,0:T(8,128)}, f32[832,128]{1,0:T(8,128)S(1)}, u32[]{:S(2)}) copy-start(f32[832,128]{1,0:T(8,128)S(1)} %convolution_subtract_fusion) | copy-start | bytes 1277956
  54.2 1.0 slice-start.2
  55.3 3.9 %collective-permute-start.3 = (f32[1088,128]{1,0:T(8,128)S(1)}, f32[1088,128]{1,0:T(8,128)S(1)}, u32[]{:S(2)}, u32[]{:S(2)}) collective-permute-start(f32[1088,128]{1,0:T(8,128)S(1)} %fusion.20), channel_id=1, source_target_pairs={{0,1},{1,0},{2,3},{3,2},{4,5},{5,4},{6,7},{7,6},{8,9},{9,8},{10,11... | collective-permute-start | bytes 1671176 | tf_op jit(solution)/shard_map/ppermute | solution.py:97
  79.4 26.1 %all-to-all-start.1 = ((f32[8,232,128]{2,1,0:T(8,128)}), f32[8,232,128]{2,1,0:T(8,128)S(1)}, u32[]{:S(2)}, u32[]{:S(2)}) async-start(f32[8,232,128]{2,1,0:T(8,128)} %broadcast_in_dim.6), calls=%async_computation.1 | async-start | bytes 1900544 | tf_op jit(solution)/shard_map/all_to_all | solution.py:138
  108.0 15.0 %collective-permute-start.4 = (f32[416,128]{1,0:T(8,128)S(1)}, f32[416,128]{1,0:T(8,128)S(1)}, u32[]{:S(2)}, u32[]{:S(2)}) collective-permute-start(f32[416,128]{1,0:T(8,128)S(1)} %get-tuple-element.18.own), channel_id=1, source_target_pairs={{0,16},{1,17},{2,18},{3,19},{4,20},{5,21},{6,22},{7,23},{8,24},{9,... | collective-permute-start | bytes 638984 | tf_op jit(solution)/shard_map/ppermute | solution.py:97
  128.9 1.0 copy-start.1
  128.9 1.0 slice-start
  132.7 0.9 slice-start.4
  132.7 1.0 slice-start.6
  133.8 0.8 slice-start.3
  133.8 0.9 slice-start.5
  134.8 3.9 %collective-permute-start.5 = (f32[1152,128]{1,0:T(8,128)S(1)}, f32[1152,128]{1,0:T(8,128)S(1)}, u32[]{:S(2)}, u32[]{:S(2)}) collective-permute-start(f32[1152,128]{1,0:T(8,128)S(1)} %pad_maximum_fusion.13), channel_id=1, source_target_pairs={{0,1},{1,0},{2,3},{3,2},{4,5},{5,4},{6,7},{7,6},{8,9},{9,8},{10,11... | collective-permute-start | bytes 1769480 | tf_op jit(solution)/shard_map/ppermute | solution.py:97
  164.3 6.8 %collective-permute-start.6 = (f32[80,128]{1,0:T(8,128)S(1)}, f32[80,128]{1,0:T(8,128)S(1)}, u32[]{:S(2)}, u32[]{:S(2)}) collective-permute-start(f32[80,128]{1,0:T(8,128)S(1)} %reduce_sum.19), channel_id=1, source_target_pairs={{0,32},{32,0},{64,96},{96,64},{128,160},{160,128},{192,224},{224,1... | collective-permute-start | bytes 122888 | tf_op jit(solution)/shard_map/ppermute | solution.py:97
  197.2 8.1 %collective-permute-start.7 = (f32[1632,128]{1,0:T(8,128)S(1)}, f32[1632,128]{1,0:T(8,128)S(1)}, u32[]{:S(2)}, u32[]{:S(2)}) collective-permute-start(f32[1632,128]{1,0:T(8,128)S(1)} %pad_maximum_fusion.4), channel_id=1, source_target_pairs={{0,1},{1,0},{2,3},{3,2},{4,5},{5,4},{6,7},{7,6},{8,9},{9,8},{10,11... | collective-permute-start | bytes 2506760 | tf_op jit(solution)/shard_map/ppermute | solution.py:97
  208.6 12.6 %collective-permute-start.8 = (f32[336,128]{1,0:T(8,128)S(1)}, f32[336,128]{1,0:T(8,128)S(1)}, u32[]{:S(2)}, u32[]{:S(2)}) collective-permute-start(f32[336,128]{1,0:T(8,128)S(1)} %constant_dynamic-slice_fusion.1), channel_id=1, source_target_pairs={{0,64},{32,96},{64,0},{96,32},{128,192},{160,224},{192,128},{224,1... | collective-permute-start | bytes 516104 | tf_op jit(solution)/shard_map/ppermute | solution.py:97
  235.2 7.5 %collective-permute-start.9 = (f32[320,128]{1,0:T(8,128)S(1)}, f32[320,128]{1,0:T(8,128)S(1)}, u32[]{:S(2)}, u32[]{:S(2)}) collective-permute-start(f32[320,128]{1,0:T(8,128)S(1)} %get-tuple-element.63), channel_id=1, source_target_pairs={{0,128},{32,160},{64,192},{96,224},{128,0},{160,32},{192,64},{224,... | collective-permute-start | bytes 491528 | tf_op jit(solution)/shard_map/ppermute | solution.py:97
  247.5 7.4 %collective-permute-start.10 = (f32[192,128]{1,0:T(8,128)S(1)}, f32[192,128]{1,0:T(8,128)S(1)}, u32[]{:S(2)}, u32[]{:S(2)}) collective-permute-start(f32[192,128]{1,0:T(8,128)S(1)} %get-tuple-element.24.own), channel_id=1, source_target_pairs={{0,256},{32,288},{64,320},{96,352},{128,384},{160,416},{192,448},{... | collective-permute-start | bytes 294920 | tf_op jit(solution)/shard_map/ppermute | solution.py:97
  (5 other events, 3.6 us)

commit v3 on v0

v3 whole, which is shorter than its diff:
```python
import functools

import jax
import jax.numpy as jnp
from jax import lax
from jax.experimental import pallas as pl
from jax.experimental.pallas import tpu as pltpu
from jax.sharding import PartitionSpec as P

VMEM_BYTES = 40 * 2**20


def split(value):
    high = value.astype(jnp.bfloat16)
    low = (value - high.astype(jnp.float32)).astype(jnp.bfloat16)
    return high, low


def dot_split(a, b):
    def part(x, y):
        return jnp.dot(x, y, preferred_element_type=jnp.float32)

    return part(a[0], b[0]) + (part(a[0], b[1]) + part(a[1], b[0]))


def kdot(a, b):
    return dot_split(split(a), split(b))


def inverse_of(error):
    total = jnp.eye(error.shape[0], dtype=jnp.float32) + error
    power = error
    for step in range(6):
        parts = split(power)
        power = dot_split(parts, parts)
        total = total + kdot(total, power)
    return total


def solve_own(gram_own, gram_sib, proj_own, proj_sib):
    inverse = inverse_of(kdot(gram_own, gram_sib))
    return kdot(proj_sib - kdot(proj_own, gram_sib), inverse)


def solve_node(own, sib, ops_own, ops_sib, sums):
    rank = own.shape[1]
    width = own.shape[0] - rank
    gram_own, proj_own = own[:rank], own[rank:]
    z = solve_own(gram_own, sib[:rank], proj_own, sib[rank:])
    z_sib = proj_own - kdot(z, gram_own)
    z_both = split(jnp.concatenate([z, z_sib], axis=1))
    node = []
    for j in range(ops_own.shape[0] // rank):
        at = slice(j * rank, (j + 1) * rank)
        left = split(jnp.concatenate([ops_own[at], ops_sib[at]], axis=0))
        node.append(sums[j * width : (j + 1) * width] - dot_split(z_both, left))
    return z, jnp.concatenate(node, axis=0)


def put_rows(out, base, size, start, value):
    at, rows = 0, value.shape[0]
    while at < rows:
        i, r = divmod(start + at, size)
        n = min(size - r, rows - at)
        out[i, base + r : base + r + n] = value[at : at + n]
        at += n


def get_rows(ref, base, size):
    return jnp.concatenate([ref[i, pl.ds(base, size)] for i in range(ref.shape[0])], axis=0)


def bit_of(axis, bit):
    return (lax.axis_index(axis) >> bit) & 1


def times8(value, rows):
    return pl.multiple_of(value * rows, 8)


def project_pair(carried, v, keep, give, low, up, shares):
    rank = v.shape[1]
    parts = split(carried)
    low[...] = dot_split(parts, split(v[0]))
    up[...] = dot_split(parts, split(v[1]))
    shared = 2 * rank
    rest = (carried.shape[0] - shared) // 2
    size_both = (shared + rest + rank) // shares
    size_sums = (rank + rest) // shares
    core = bit_of("gy", 0)
    for out, side in ((keep, core), (give, 1 - core)):
        half = pl.ds(shared + times8(side, rest), rest)
        put_rows(out, 0, size_both, 0, low[:shared])
        put_rows(out, 0, size_both, shared, low[half])
        put_rows(out, 0, size_both, shared + rest, up[:rank])
        put_rows(out, size_both, size_sums, 0, up[rank:shared])
        put_rows(out, size_both, size_sums, rank, up[half])


def start_kernel(shares, u, v, y, carried, keep, give, low, up):
    levels, _, rank = u.shape
    for j in range(levels):
        carried[j * rank : (j + 1) * rank] = u[j].T
    carried[levels * rank :] = y[...].T
    project_pair(carried[...], v, keep, give, low, up, shares)


def lower_node_kernel(bit, n_both, rest, pieces, z_out, node_out):
    side = bit_of("gy", bit)
    rank = z_out.shape[1]
    if n_both is None:
        top = 2 * rank + rest
        own = pieces[side, :top]
        sib = pieces[1 - side, :top]
        ops_own = pieces[side, top : top + rank]
        ops_sib = pieces[1 - side, top : top + rank]
        sums = pieces[0, top + rank :] + pieces[1, top + rank :]
    else:
        top = 2 * rank + rest
        own = get_rows(pieces, times8(side, n_both), n_both)
        sib = get_rows(pieces, times8(1 - side, n_both), n_both)
        own, ops_own = own[:top], own[top:]
        sib, ops_sib = sib[:top], sib[top:]
        sums = get_rows(pieces, 2 * n_both, pieces.shape[1] - 2 * n_both)
    z, node = solve_node(own, sib, ops_own, ops_sib, sums)
    z_out[...] = z
    node_out[...] = node


def lower_leaf_kernel(bit, pair, z_low, out):
    side = bit_of("gy", bit)
    rank = pair.shape[2]
    rest = z_low.shape[0] - rank
    own, sib = pair[side], pair[1 - side]
    out[:rest] = z_low[rank:]
    out[rest:] = solve_own(own[:rank], sib[:rank], own[rank:], sib[rank:])


def advanced(carried, z_low, halves):
    rank = z_low.shape[1]
    rest = halves.shape[1] // 2
    left = carried[:rank]
    next_left = carried[rank : 2 * rank] - kdot(z_low[:rank], left)
    z_rest = jnp.concatenate(
        [
            jnp.concatenate([halves[c, :rest], halves[c, rest:]], axis=1) for c in range(2)
        ],
        axis=0,
    )
    return carried[2 * rank :] - kdot(z_rest, jnp.concatenate([left, next_left], axis=0))


def next_pair_kernel(shares, carried, z_low, halves, v, new, keep, give, low, up):
    value = advanced(carried, z_low, halves)
    new[...] = value
    project_pair(value, v, keep, give, low, up, shares)


def upper_kernel(shares, carried, z_low, halves, v, new, keep, give, both, sums):
    value = advanced(carried, z_low, halves)
    new[...] = value
    rank = v.shape[1]
    count, width = v.shape[0], value.shape[0]
    parts = split(value)
    both[:width] = dot_split(parts, split(v[0]))
    for j in range(1, count):
        rows = dot_split(parts, split(v[j]))
        both[width + (j - 1) * rank : width + j * rank] = rows[:rank]
        sums[(j - 1) * (width - rank) : j * (width - rank)] = rows[rank:]
    half_both, half_sums = both.shape[0] // 2, sums.shape[0] // 2
    core = bit_of("gy", 0)
    for out, side in ((keep, core), (give, 1 - core)):
        put_rows(out, 0, half_both // shares, 0, both[pl.ds(times8(side, half_both), half_both)])
        put_rows(
            out,
            half_both // shares,
            half_sums // shares,
            0,
            sums[pl.ds(times8(side, half_sums), half_sums)],
        )


def updated(carried, z):
    rank = z.shape[1]
    return carried[rank:] - kdot(z, carried[:rank])


def top_node_kernel(width, n_both, n_sums, mine, other, carried, new, node_out, quarter):
    rank = carried.shape[1]
    core = bit_of("gy", 0)
    side = bit_of("gx", 0)
    halves = []
    for c in range(2):
        take = core == c
        halves.append(
            [
                jnp.where(take, get_rows(mine, base, size), get_rows(other, base, size))
                for base, size in (
                    (times8(side, n_both), n_both),
                    (times8(1 - side, n_both), n_both),
                    (2 * n_both, n_sums),
                )
            ]
        )
    own, sib, sums = [jnp.concatenate([a, b], axis=0) for a, b in zip(*halves)]
    z, node = solve_node(own[:width], sib[:width], own[width:], sib[width:], sums)
    node_out[...] = node
    rows = quarter.shape[0]
    at = lax.axis_index("gy") & 3
    quarter[...] = node_out[pl.ds(times8(at, rows), rows)]
    new[...] = updated(carried, z)


def upper_node_kernel(count, own, sib, carried, new, node_out, *part):
    rank = carried.shape[1]
    width = own.shape[0] // count

    def rows(ref, j, low, high):
        return ref[j * width + low : j * width + high]

    ops_own = jnp.concatenate([rows(own, j, 0, rank) for j in range(1, count)], axis=0)
    ops_sib = jnp.concatenate([rows(sib, j, 0, rank) for j in range(1, count)], axis=0)
    sums = jnp.concatenate(
        [rows(own, j, rank, width) + rows(sib, j, rank, width) for j in range(1, count)], axis=0
    )
    z, node = solve_node(own[:width], sib[:width], ops_own, ops_sib, sums)
    node_out[...] = node
    if part:
        n = part[0].shape[0]
        part[0][...] = node_out[pl.ds(times8(bit_of("gy", 0), n), n)]
    new[...] = updated(carried, z)


def last_kernel(axis, bit, pair, carried, out):
    side = bit_of(axis, bit)
    rank = carried.shape[1]
    own, sib = pair[side], pair[1 - side]
    z = solve_own(own[:rank], sib[:rank], own[rank:], sib[rank:])
    out[...] = updated(carried, z).T


def call(kernel, outs, *args, scratch=()):
    rows = sum(a.size // 128 for a in args)
    return pl.pallas_call(
        kernel,
        out_shape=[jax.ShapeDtypeStruct(o, jnp.float32) for o in outs],
        scratch_shapes=[pltpu.VMEM(s, jnp.float32) for s in scratch],
        compiler_params=pltpu.CompilerParams(vmem_limit_bytes=VMEM_BYTES),
        cost_estimate=pl.CostEstimate(
            flops=6 * 128 * 128 * (rows + 14 * 128),
            bytes_accessed=512 * rows,
            transcendentals=0,
        ),
    )(*args)


def bit_groups(count, bits):
    mask = sum(1 << b for b in bits)
    return [
        [
            base | sum(((i >> q) & 1) << b for q, b in enumerate(bits))
            for i in range(1 << len(bits))
        ]
        for base in range(count)
        if not base & mask
    ]


def swap_cores(value):
    return lax.ppermute(value, "gy", [(s, s ^ 1) for s in range(lax.axis_size("gy"))])


def pair_gather(value, axis, bit, tiled=False):
    groups = bit_groups(lax.axis_size(axis), [bit])
    return lax.all_gather(value, axis, axis_index_groups=groups, tiled=tiled)


def exchange(value, axis, bits):
    count = lax.axis_size(axis)
    return lax.all_to_all(value, axis, 0, 0, axis_index_groups=bit_groups(count, bits))


def to_all(value, axis, bits):
    return exchange(jnp.broadcast_to(value, (1 << len(bits),) + value.shape), axis, bits)


def pad_rows(value, rows):
    return jnp.pad(value, ((0, rows - value.shape[0]), (0, 0)))


def up8(value):
    return -(-value // 8) * 8


def shards(right_sides, factor_u, factor_v):
    levels, _, rank = factor_u.shape
    gy_bits = lax.axis_size("gy").bit_length() - 1
    near_chips = [1, 2]

    rows = levels * rank + right_sides.shape[1]
    rest = (rows - 2 * rank) // 2
    top = 2 * rank + rest
    sent = (1, top + rank + rank + rest, rank)
    carried, keep, give = call(
        functools.partial(start_kernel, 1),
        [(rows, rank), sent, sent],
        factor_u,
        factor_v[:2],
        right_sides,
        scratch=[(rows, rank)] * 2,
    )
    chip = (keep + swap_cores(give))[0]
    pieces = to_all(chip, "gy", [1])
    z_low, node = call(
        functools.partial(lower_node_kernel, 1, None, rest),
        [(rank + rest, rank), (rank + rest, rank)],
        pieces,
    )
    pair = pair_gather(node, "gy", 2)
    mine = call(functools.partial(lower_leaf_kernel, 2), [(2 * rest, rank)], pair, z_low)[0]
    halves = pair_gather(mine, "gy", 0)

    rows -= 2 * rank
    rest = (rows - 2 * rank) // 2
    top = 2 * rank + rest
    n_both, n_sums = (top + rank) // 4, (rank + rest) // 4
    sent = (4, n_both + n_sums, rank)
    carried, keep, give = call(
        functools.partial(next_pair_kernel, 4),
        [(rows, rank), sent, sent],
        carried,
        z_low,
        halves,
        factor_v[2:4],
        scratch=[(rows, rank)] * 2,
    )
    chip = keep + swap_cores(give)
    piece = exchange(chip, "gy", near_chips).sum(axis=0)
    pair = pair_gather(piece, "gy", 3)
    share = jnp.concatenate(
        [pair[0, :n_both], pair[1, :n_both], pair[0, n_both:] + pair[1, n_both:]], axis=0
    )
    pieces = to_all(share, "gy", near_chips)
    z_low, node = call(
        functools.partial(lower_node_kernel, 3, n_both, rest),
        [(rank + rest, rank), (rank + rest, rank)],
        pieces,
    )
    pair = pair_gather(node, "gy", 4)
    mine = call(functools.partial(lower_leaf_kernel, 4), [(2 * rest, rank)], pair, z_low)[0]
    halves = pair_gather(mine, "gy", 0)

    rows -= 2 * rank
    level = gy_bits - 1
    count = levels - level
    all_both = rows + (count - 1) * rank
    all_sums = (count - 1) * (rows - rank)
    n_both, n_sums = all_both // 8, all_sums // 8
    sent = (4, n_both + n_sums, rank)
    carried, keep, give = call(
        functools.partial(upper_kernel, 4),
        [(rows, rank), sent, sent],
        carried,
        z_low,
        halves,
        factor_v[level:],
        scratch=[(all_both, rank), (all_sums, rank)],
    )
    chip = keep + swap_cores(give)
    piece = exchange(chip, "gy", near_chips).sum(axis=0)
    s_both, s_sums = up8(-(-n_both // 8)), up8(-(-n_sums // 8))
    sent = jnp.concatenate(
        [
            pad_rows(piece[:n_both], 8 * s_both).reshape(8, s_both, rank),
            pad_rows(piece[n_both:], 8 * s_sums).reshape(8, s_sums, rank),
        ],
        axis=1,
    )
    far = [3, 4, 5]
    sides = exchange(sent, ("gx", "gy"), far)
    sides = sides.reshape((2, 4) + sides.shape[1:]).sum(axis=1)
    share = jnp.concatenate(
        [sides[0, :s_both], sides[1, :s_both], sides[0, s_both:] + sides[1, s_both:]], axis=0
    )
    pieces = to_all(share, ("gx", "gy"), far)
    share = jnp.concatenate(
        [
            pieces[:, :s_both].reshape(-1, rank)[:n_both],
            pieces[:, s_both : 2 * s_both].reshape(-1, rank)[:n_both],
            pieces[:, 2 * s_both :].reshape(-1, rank)[:n_sums],
        ],
        axis=0,
    )
    mine = to_all(share, "gy", near_chips)
    other = swap_cores(mine)
    carried, node, part = call(
        functools.partial(top_node_kernel, rows, n_both, n_sums),
        [(rows - rank, rank), (all_sums, rank), (all_sums // 4, rank)],
        mine,
        other,
        carried,
    )

    gx = lax.axis_index("gx")

    def of_sibling(value, bit):
        pair = pair_gather(value, "gx", bit)
        return lax.dynamic_index_in_dim(pair, 1 - ((gx >> bit) & 1), 0, keepdims=False)

    quads = bit_groups(lax.axis_size("gy"), [0, 1])
    near = lax.all_gather(of_sibling(part, 1), "gy", axis_index_groups=quads, tiled=True)
    rows, count = rows - rank, count - 1
    out_rows = (count - 1) * (rows - rank)
    carried, node, part = call(
        functools.partial(upper_node_kernel, count),
        [(rows - rank, rank), (out_rows, rank), (out_rows // 2, rank)],
        node,
        near,
        carried,
    )
    near = pair_gather(of_sibling(part, 2), "gy", 0, tiled=True)
    rows, count = rows - rank, count - 1
    out_rows = (count - 1) * (rows - rank)
    carried, node = call(
        functools.partial(upper_node_kernel, count),
        [(rows - rank, rank), (out_rows, rank)],
        node,
        near,
        carried,
    )
    pair = pair_gather(node, "gx", 3)
    return call(functools.partial(last_kernel, "gx", 3), [right_sides.shape], pair, carried)[0]


def solution(mesh):
    placed = (P(("gx", "gy"), None), P(None, ("gx", "gy"), None), P(None, ("gx", "gy"), None))
    return jax.shard_map(
        shards, mesh=mesh, in_specs=placed, out_specs=P(("gx", "gy"), None), check_vma=False
    )
```

time: 544 us -> 227 us (0.42)
  the two profiles are of different devices: /device:TPU:28 before, /device:TPU:1 now
where the time goes in v3:
time: 227 us
  blocking collectives  158 us (70%)
  starting transfers between devices  23.6 us (10%)
  Pallas kernels  21.3 us (9%)
  waiting for transfers between devices  18.5 us (8%)
  local copies, waits for them, and re-layouts  4.84 us (2%)
    all_to_all x6, blocking collectives, exchange(): lax.all_to_all(value, axis, 0, 0, axis_index_groups=bit_groups(count, bits))  82.1 us
    all_gather x9, blocking collectives, pair_gather(): return lax.all_gather(value, axis, axis_index_groups=groups, tiled=tiled)  66.4 us
    pallas_call x11, Pallas kernels, call(): pl.pallas_call(kernel, out_shape=[jax.ShapeDtypeStruct(o, jnp.float32) fo...  21.3 us
    ppermute x4, starting transfers between devices, swap_cores(): lax.ppermute(value, 'gy', [(s, s ^ 1) for s in range(lax.axis_size('gy'))])  20.1 us
    all_to_all x1, waiting for transfers between devices, exchange(): lax.all_to_all(value, axis, 0, 0, axis_index_groups=bit_groups(count, bits))  11.6 us
    all_gather x1, blocking collectives, shards(): lax.all_gather(of_sibling(part, 1), 'gy', axis_index_groups=quads, tiled=...  9.27 us
    ppermute x4, waiting for transfers between devices, swap_cores(): lax.ppermute(value, 'gy', [(s, s ^ 1) for s in range(lax.axis_size('gy'))])  6.88 us
  transfers between devices with their start and end apart: 5, of which 5 were waited for; matrix products, arithmetic and copies ran while one was open for 0% of the time, Pallas kernels for 0%

profile of v3, /device:TPU:1, one launch (start us, length us, event | category | flops | bytes accessed | tf_op | source)
XLA Modules:
  0.0 226.8 jit_solution(15348991522971160922)
XLA Ops:
  3.7 8.8 %collective-permute-start = (f32[1,1344,128]{2,1,0:T(8,128)S(1)}, f32[1,1344,128]{2,1,0:T(8,128)S(1)}, u32[]{:S(2)}, u32[]{:S(2)}) collective-permute-start(f32[1,1344,128]{2,1,0:T(8,128)S(1)} %get-tuple-element.28), channel_id=1, source_target_pairs={{0,1},{1,0},{2,3},{3,2},{4,5},{5,4},{6,7},{7,6},{8,9},{9,8},{10,11... | collective-permute-start | bytes 2064392 | tf_op jit(solution)/shard_map/ppermute | solution.py:270
  14.4 19.3 %all_to_all.35.pieces = f32[2,1344,128]{2,1,0:T(8,128)S(1)} all-to-all(f32[2,1344,128]{2,1,0:T(8,128)S(1)} %broadcast_in_dim.12), channel_id=1, replica_groups={{0,2},{1,3},{4,6},{5,7},{8,10},{9,11},{12,14},{13,15},{16,18},{17,19},{..., dimensions={0} | all-to-all | bytes 2752512 | tf_op jit(solution)/shard_map/all_to_all | solution.py:280
  33.7 2.4 %shard_map.38 = (f32[544,128]{1,0:T(8,128)S(1)}, f32[544,128]{1,0:T(8,128)S(1)}) custom-call(f32[2,1344,128]{2,1,0:T(8,128)S(1)} %all_to_all.35.pieces), custom_call_target="tpu_custom_call" | custom-call | flops 440401920 | bytes 1376256 | tf_op jit(solution)/shard_map/pallas_call | solution.py:244
  36.2 7.6 %all-gather = f32[1088,128]{1,0:T(8,128)S(1)} all-gather(f32[544,128]{1,0:T(8,128)S(1)} %get-tuple-element.30), channel_id=2, replica_groups={{0,4},{1,5},{2,6},{3,7},{8,12},{9,13},{10,14},{11,15},{16,20},{17,21},{..., dimensions={0}, use_global_device_ids=true | all-gather | bytes 835584 | tf_op jit(solution)/shard_map/all_gather | solution.py:275
  45.5 4.2 %all-gather.1 = f32[1664,128]{1,0:T(8,128)S(1)} all-gather(f32[832,128]{1,0:T(8,128)S(1)} %shard_map.39), channel_id=3, replica_groups={{0,1},{2,3},{4,5},{6,7},{8,9},{10,11},{12,13},{14,15},{16,17},{18,19},{..., dimensions={0}, use_global_device_ids=true | all-gather | bytes 1277952 | tf_op jit(solution)/shard_map/all_gather | solution.py:275
  55.3 10.9 %all_to_all.36 = f32[4,272,128]{2,1,0:T(8,128)S(1)} all-to-all(f32[4,272,128]{2,1,0:T(8,128)S(1)} %add.34), channel_id=1, replica_groups={{0,2,4,6},{1,3,5,7},{8,10,12,14},{9,11,13,15},{16,18,20,22},{17,19,21,2..., dimensions={0} | all-to-all | bytes 1114112 | tf_op jit(solution)/shard_map/all_to_all | solution.py:280
  66.2 9.2 %all-gather.2 = f32[544,128]{1,0:T(8,128)S(1)} all-gather(f32[272,128]{1,0:T(8,128)S(1)} %reduce_sum.27), channel_id=4, replica_groups={{0,8},{1,9},{2,10},{3,11},{4,12},{5,13},{6,14},{7,15},{16,24},{17,25},{..., dimensions={0}, use_global_device_ids=true | all-gather | bytes 417792 | tf_op jit(solution)/shard_map/all_gather | solution.py:275
  76.5 3.5 %all-to-all-start.2 = ((f32[4,440,128]{2,1,0:T(8,128)}), f32[4,440,128]{2,1,0:T(8,128)S(1)}, u32[]{:S(2)}, u32[]{:S(2)}) async-start(f32[4,440,128]{2,1,0:T(8,128)} %broadcast_in_dim.13), calls=%async_computation.2 | async-start | bytes 1802240 | tf_op jit(solution)/shard_map/all_to_all | solution.py:280
  80.0 11.6 %all-to-all-done.2.pieces = f32[4,440,128]{2,1,0:T(8,128)S(1)} async-done(((f32[4,440,128]{2,1,0:T(8,128)}), f32[4,440,128]{2,1,0:T(8,128)S(1)}, u32[]{:S(2)}, u32[]{:S(2)}) %all-to-all-start.2) | async-done | bytes 901152 | tf_op jit(solution)/shard_map/all_to_all | solution.py:280
  91.7 2.3 %shard_map.41 = (f32[416,128]{1,0:T(8,128)S(1)}, f32[416,128]{1,0:T(8,128)S(1)}) custom-call(f32[4,440,128]{2,1,0:T(8,128)S(1)} %all-to-all-done.2.pieces), custom_call_target="tpu_custom_call" | custom-call | flops 349175808 | bytes 901120 | tf_op jit(solution)/shard_map/pallas_call | solution.py:244
  93.9 10.6 %all-gather.3 = f32[832,128]{1,0:T(8,128)S(1)} all-gather(f32[416,128]{1,0:T(8,128)S(1)} %get-tuple-element.35), channel_id=5, replica_groups={{0,16},{1,17},{2,18},{3,19},{4,20},{5,21},{6,22},{7,23},{8,24},{9,25},{..., dimensions={0}, use_global_device_ids=true | all-gather | bytes 638976 | tf_op jit(solution)/shard_map/all_gather | solution.py:275
  106.2 5.8 %all-gather.4 = f32[1152,128]{1,0:T(8,128)S(1)} all-gather(f32[576,128]{1,0:T(8,128)S(1)} %shard_map.42), channel_id=6, replica_groups={{0,1},{2,3},{4,5},{6,7},{8,9},{10,11},{12,13},{14,15},{16,17},{18,19},{..., dimensions={0}, use_global_device_ids=true | all-gather | bytes 884736 | tf_op jit(solution)/shard_map/all_gather | solution.py:275
  117.6 13.3 %all_to_all.37 = f32[4,288,128]{2,1,0:T(8,128)S(1)} all-to-all(f32[4,288,128]{2,1,0:T(8,128)S(1)} %add.37), channel_id=1, replica_groups={{0,2,4,6},{1,3,5,7},{8,10,12,14},{9,11,13,15},{16,18,20,22},{17,19,21,2..., dimensions={0} | all-to-all | bytes 1179648 | tf_op jit(solution)/shard_map/all_to_all | solution.py:280
  131.0 14.6 %all_to_all.38 = f32[8,40,128]{2,1,0:T(8,128)S(1)} all-to-all(f32[8,40,128]{2,1,0:T(8,128)S(1)} %pad_maximum_fusion.2), channel_id=1, replica_groups={{0,8,16,24,32,40,48,56},{1,9,17,25,33,41,49,57},{2,10,18,26,34,42,50,58..., dimensions={0} | all-to-all | bytes 327680 | tf_op jit(solution)/shard_map/all_to_all | solution.py:280
  145.7 11.8 %all_to_all.39 = f32[8,56,128]{2,1,0:T(8,128)S(1)} all-to-all(f32[8,56,128]{2,1,0:T(8,128)S(1)} %broadcast_in_dim.14), channel_id=1, replica_groups={{0,8,16,24,32,40,48,56},{1,9,17,25,33,41,49,57},{2,10,18,26,34,42,50,58..., dimensions={0} | all-to-all | bytes 458752 | tf_op jit(solution)/shard_map/all_to_all | solution.py:280
  157.7 12.2 %all_to_all.40.mine = f32[4,408,128]{2,1,0:T(8,128)S(1)} all-to-all(f32[4,408,128]{2,1,0:T(8,128)S(1)} %broadcast_in_dim.15), channel_id=1, replica_groups={{0,2,4,6},{1,3,5,7},{8,10,12,14},{9,11,13,15},{16,18,20,22},{17,19,21,2..., dimensions={0} | all-to-all | bytes 1671168 | tf_op jit(solution)/shard_map/all_to_all | solution.py:280
  169.9 6.8 %collective-permute-start.3 = (f32[4,408,128]{2,1,0:T(8,128)S(1)}, f32[4,408,128]{2,1,0:T(8,128)S(1)}, u32[]{:S(2)}, u32[]{:S(2)}) collective-permute-start(f32[4,408,128]{2,1,0:T(8,128)S(1)} %all_to_all.40.mine), channel_id=1, source_target_pairs={{0,1},{1,0},{2,3},{3,2},{4,5},{5,4},{6,7},{7,6},{8,9},{9,8},{10,11... | collective-permute-start | bytes 2506760 | tf_op jit(solution)/shard_map/ppermute | solution.py:270
  178.6 2.8 %shard_map.44 = (f32[448,128]{1,0:T(8,128)S(1)}, f32[1344,128]{1,0:T(8,128)S(1)}, f32[336,128]{1,0:T(8,128)S(1)}) custom-call(f32[4,408,128]{2,1,0:T(8,128)S(1)} %all_to_all.40.mine, f32[4,408,128]{2,1,0:T(8,128)S(1)} %collective-permute-done.3.other, f32[576,128]{1,0:T(8,128)S(1)} %get-tuple-element.38.carried), custom_call_target="tpu_custom_call" | custom-call | flops 553648128 | bytes 1966080 | tf_op jit(solution)/shard_map/pallas_call | solution.py:244
  181.4 13.8 %all-gather.5 = f32[672,128]{1,0:T(8,128)S(1)} all-gather(f32[336,128]{1,0:T(8,128)S(1)} %get-tuple-element.40), channel_id=7, replica_groups={{0,64},{32,96},{128,192},{160,224},{256,320},{288,352},{384,448},{416,4..., dimensions={0}, use_global_device_ids=true | all-gather | bytes 516096 | tf_op jit(solution)/shard_map/all_gather | solution.py:275
  195.3 9.3 %all-gather.6 = f32[1,1344,128]{2,1,0:T(8,128)S(1)} all-gather(f32[1,336,128]{2,1,0:T(8,128)S(1)} %constant_dynamic-slice_fusion.1), channel_id=8, replica_groups={{0,1,2,3},{4,5,6,7},{8,9,10,11},{12,13,14,15},{16,17,18,19},{20,21,22,2..., dimensions={1}, use_global_device_ids=true | all-gather | bytes 860160 | tf_op jit(solution)/shard_map/all_gather | solution.py:411
  204.6 2.4 %shard_map.45 = (f32[320,128]{1,0:T(8,128)S(1)}, f32[640,128]{1,0:T(8,128)S(1)}, f32[320,128]{1,0:T(8,128)S(1)}) custom-call(f32[1344,128]{1,0:T(8,128)S(1)} %get-tuple-element.39.own, f32[1344,128]{1,0:T(8,128)S(1)} %bitcast.33, f32[448,128]{1,0:T(8,128)S(1)} %get-tuple-element.41.carried), custom_call_target="tpu_custom_call" | custom-call | flops 484442112 | bytes 1605632 | tf_op jit(solution)/shard_map/pallas_call | solution.py:244
  207.0 6.3 %all-gather.7 = f32[640,128]{1,0:T(8,128)S(1)} all-gather(f32[320,128]{1,0:T(8,128)S(1)} %get-tuple-element.43), channel_id=9, replica_groups={{0,128},{32,160},{64,192},{96,224},{256,384},{288,416},{320,448},{352,4..., dimensions={0}, use_global_device_ids=true | all-gather | bytes 491520 | tf_op jit(solution)/shard_map/all_gather | solution.py:275
  213.3 2.6 %all-gather.8 = f32[1,640,128]{2,1,0:T(8,128)S(1)} all-gather(f32[1,320,128]{2,1,0:T(8,128)S(1)} %constant_dynamic-slice_fusion), channel_id=10, replica_groups={{0,1},{2,3},{4,5},{6,7},{8,9},{10,11},{12,13},{14,15},{16,17},{18,19},{..., dimensions={1}, use_global_device_ids=true | all-gather | bytes 491520 | tf_op jit(solution)/shard_map/all_gather | solution.py:275
  218.0 6.2 %all-gather.9 = f32[384,128]{1,0:T(8,128)S(1)} all-gather(f32[192,128]{1,0:T(8,128)S(1)} %get-tuple-element.45), channel_id=11, replica_groups={{0,256},{32,288},{64,320},{96,352},{128,384},{160,416},{192,448},{224,4..., dimensions={0}, use_global_device_ids=true | all-gather | bytes 294912 | tf_op jit(solution)/shard_map/all_gather | solution.py:275
  (50 shorter events, 28.1 us)
Async XLA Ops:
  1.8 1.0 copy-start
  3.7 10.5 %collective-permute-start = (f32[1,1344,128]{2,1,0:T(8,128)S(1)}, f32[1,1344,128]{2,1,0:T(8,128)S(1)}, u32[]{:S(2)}, u32[]{:S(2)}) collective-permute-start(f32[1,1344,128]{2,1,0:T(8,128)S(1)} %get-tuple-element.28), channel_id=1, source_target_pairs={{0,1},{1,0},{2,3},{3,2},{4,5},{5,4},{6,7},{7,6},{8,9},{9,8},{10,11... | collective-permute-start | bytes 2064392 | tf_op jit(solution)/shard_map/ppermute | solution.py:270
  51.4 3.9 %collective-permute-start.1 = (f32[4,272,128]{2,1,0:T(8,128)S(1)}, f32[4,272,128]{2,1,0:T(8,128)S(1)}, u32[]{:S(2)}, u32[]{:S(2)}) collective-permute-start(f32[4,272,128]{2,1,0:T(8,128)S(1)} %get-tuple-element.33), channel_id=1, source_target_pairs={{0,1},{1,0},{2,3},{3,2},{4,5},{5,4},{6,7},{7,6},{8,9},{9,8},{10,11... | collective-permute-start | bytes 1671176 | tf_op jit(solution)/shard_map/ppermute | solution.py:270
  75.5 4.5 %copy-start.1 = (f32[8,128,128]{2,1,0:T(8,128)S(1)}, f32[8,128,128]{2,1,0:T(8,128)}, u32[]{:S(2)}) copy-start(f32[8,128,128]{2,1,0:T(8,128)} %param.5) | copy-start | bytes 1572868
  76.5 15.2 %all-to-all-start.2 = ((f32[4,440,128]{2,1,0:T(8,128)}), f32[4,440,128]{2,1,0:T(8,128)S(1)}, u32[]{:S(2)}, u32[]{:S(2)}) async-start(f32[4,440,128]{2,1,0:T(8,128)} %broadcast_in_dim.13), calls=%async_computation.2 | async-start | bytes 1802240 | tf_op jit(solution)/shard_map/all_to_all | solution.py:280
  113.6 3.9 %collective-permute-start.2 = (f32[4,288,128]{2,1,0:T(8,128)S(1)}, f32[4,288,128]{2,1,0:T(8,128)S(1)}, u32[]{:S(2)}, u32[]{:S(2)}) collective-permute-start(f32[4,288,128]{2,1,0:T(8,128)S(1)} %get-tuple-element.37), channel_id=1, source_target_pairs={{0,1},{1,0},{2,3},{3,2},{4,5},{5,4},{6,7},{7,6},{8,9},{9,8},{10,11... | collective-permute-start | bytes 1769480 | tf_op jit(solution)/shard_map/ppermute | solution.py:270
  117.6 13.3 %copy-start.2 = (pred[128]{0:T(512)(128)(4,1)S(1)}, pred[128]{0:T(512)(128)(4,1)}, u32[]{:S(2)}) copy-start(pred[128]{0:T(512)(128)(4,1)} %constant.20.clone.1) | copy-start | bytes 388
  169.9 8.7 %collective-permute-start.3 = (f32[4,408,128]{2,1,0:T(8,128)S(1)}, f32[4,408,128]{2,1,0:T(8,128)S(1)}, u32[]{:S(2)}, u32[]{:S(2)}) collective-permute-start(f32[4,408,128]{2,1,0:T(8,128)S(1)} %all_to_all.40.mine), channel_id=1, source_target_pairs={{0,1},{1,0},{2,3},{3,2},{4,5},{5,4},{6,7},{7,6},{8,9},{9,8},{10,11... | collective-permute-start | bytes 2506760 | tf_op jit(solution)/shard_map/ppermute | solution.py:270

commit v4 on v3

v4 whole, which is shorter than its diff:
```python
import functools

import jax
import jax.numpy as jnp
from jax import lax
from jax.experimental import pallas as pl
from jax.experimental.pallas import tpu as pltpu
from jax.sharding import PartitionSpec as P

VMEM_BYTES = 40 * 2**20


def split(value):
    high = value.astype(jnp.bfloat16)
    low = (value - high.astype(jnp.float32)).astype(jnp.bfloat16)
    return high, low


def dot_split(a, b):
    def part(x, y):
        return jnp.dot(x, y, preferred_element_type=jnp.float32)

    return part(a[0], b[0]) + (part(a[0], b[1]) + part(a[1], b[0]))


def kdot(a, b):
    return dot_split(split(a), split(b))


def inverse_of(error):
    total = jnp.eye(error.shape[0], dtype=jnp.float32) + error
    power = error
    for step in range(6):
        parts = split(power)
        power = dot_split(parts, parts)
        total = total + kdot(total, power)
    return total


def solve_own(gram_own, gram_sib, proj_own, proj_sib):
    inverse = inverse_of(kdot(gram_own, gram_sib))
    return kdot(proj_sib - kdot(proj_own, gram_sib), inverse)


def solve_node(own, sib, ops_own, ops_sib, sums):
    rank = own.shape[1]
    width = own.shape[0] - rank
    gram_own, proj_own = own[:rank], own[rank:]
    z = solve_own(gram_own, sib[:rank], proj_own, sib[rank:])
    z_sib = proj_own - kdot(z, gram_own)
    z_both = split(jnp.concatenate([z, z_sib], axis=1))
    node = []
    for j in range(ops_own.shape[0] // rank):
        at = slice(j * rank, (j + 1) * rank)
        left = split(jnp.concatenate([ops_own[at], ops_sib[at]], axis=0))
        node.append(sums[j * width : (j + 1) * width] - dot_split(z_both, left))
    return z, jnp.concatenate(node, axis=0)


def put_rows(out, base, size, start, value):
    at, rows = 0, value.shape[0]
    while at < rows:
        i, r = divmod(start + at, size)
        n = min(size - r, rows - at)
        out[i, base + r : base + r + n] = value[at : at + n]
        at += n


def get_rows(ref, base, size):
    return jnp.concatenate([ref[i, pl.ds(base, size)] for i in range(ref.shape[0])], axis=0)


def bit_of(axis, bit):
    return (lax.axis_index(axis) >> bit) & 1


def times8(value, rows):
    return pl.multiple_of(value * rows, 8)


def start_kernel(u, v, y, carried, keep, give, low, up):
    levels, _, rank = u.shape
    for j in range(levels):
        carried[j * rank : (j + 1) * rank] = u[j].T
    carried[levels * rank :] = y[...]
    parts = split(carried[...])
    low[...] = dot_split(parts, split(v[0]))
    up[...] = dot_split(parts, split(v[1]))
    shared = 2 * rank
    rest = (carried.shape[0] - shared) // 2
    core = bit_of("gy", 0)
    for out, side in ((keep, core), (give, 1 - core)):
        half = pl.ds(shared + times8(side, rest), rest)
        out[:shared] = low[:shared]
        out[shared : shared + rest] = low[half]
        out[shared + rest : 2 * shared + rest] = up[:shared]
        out[2 * shared + rest :] = up[half]


def lower_node_kernel(bit, top, pieces, z_out, node_out):
    side = bit_of("gy", bit)
    rank = z_out.shape[1]
    ops = slice(top, top + rank)
    z, node = solve_node(
        pieces[side, :top],
        pieces[1 - side, :top],
        pieces[side, ops],
        pieces[1 - side, ops],
        pieces[0, top + rank :] + pieces[1, top + rank :],
    )
    z_out[...] = z
    node_out[...] = node


def lower_leaf_kernel(bit, pair, z_low, out):
    side = bit_of("gy", bit)
    rank = pair.shape[2]
    rest = z_low.shape[0] - rank
    own, sib = pair[side], pair[1 - side]
    out[:rest] = z_low[rank:]
    out[rest:] = solve_own(own[:rank], sib[:rank], own[rank:], sib[rank:])


def advanced(carried, z_low, halves):
    rank = z_low.shape[1]
    rest = halves.shape[1] // 2
    left = carried[:rank]
    next_left = carried[rank : 2 * rank] - kdot(z_low[:rank], left)
    z_rest = jnp.concatenate(
        [
            jnp.concatenate([halves[c, :rest], halves[c, rest:]], axis=1) for c in range(2)
        ],
        axis=0,
    )
    return carried[2 * rank :] - kdot(z_rest, jnp.concatenate([left, next_left], axis=0))


def upper_kernel(shares, carried, z_low, halves, v, new, keep, give, both, sums):
    value = advanced(carried, z_low, halves)
    new[...] = value
    rank = v.shape[1]
    count, width = v.shape[0], value.shape[0]
    parts = split(value)
    both[:width] = dot_split(parts, split(v[0]))
    for j in range(1, count):
        rows = dot_split(parts, split(v[j]))
        both[width + (j - 1) * rank : width + j * rank] = rows[:rank]
        sums[(j - 1) * (width - rank) : j * (width - rank)] = rows[rank:]
    half_both, half_sums = both.shape[0] // 2, sums.shape[0] // 2
    core = bit_of("gy", 0)
    for out, side in ((keep, core), (give, 1 - core)):
        put_rows(out, 0, half_both // shares, 0, both[pl.ds(times8(side, half_both), half_both)])
        put_rows(
            out,
            half_both // shares,
            half_sums // shares,
            0,
            sums[pl.ds(times8(side, half_sums), half_sums)],
        )


def updated(carried, z):
    rank = z.shape[1]
    return carried[rank:] - kdot(z, carried[:rank])


def share_kernel(n_both, pair, out):
    rows = [pair[0, :n_both], pair[1, :n_both], pair[0, n_both:] + pair[1, n_both:]]
    value = jnp.concatenate(rows, axis=0)
    for i in range(out.shape[0]):
        out[i] = value


def joined(mine, other):
    take = bit_of("gy", 0) == 0
    return jnp.concatenate([jnp.where(take, mine, other), jnp.where(take, other, mine)], axis=0)


def put_part(node_out, part):
    n = part.shape[0]
    gy = lax.axis_index("gy")
    part[...] = node_out[pl.ds(times8((gy & 1) * 4 + ((gy >> 1) & 3), n), n)]


def top_node_kernel(bit, width, n_both, n_sums, mine, other, carried, new, node_out, part):
    side = bit_of("gy", bit)
    own, sib, sums = [
        joined(get_rows(mine, base, size), get_rows(other, base, size))
        for base, size in (
            (times8(side, n_both), n_both),
            (times8(1 - side, n_both), n_both),
            (2 * n_both, n_sums),
        )
    ]
    z, node = solve_node(own[:width], sib[:width], own[width:], sib[width:], sums)
    node_out[...] = node
    put_part(node_out, part)
    new[...] = updated(carried, z)


def children_rows(own, sib, count):
    rank = own.shape[1]
    width = own.shape[0] // count
    at = [slice(j * width, j * width + rank) for j in range(1, count)]
    rest = [slice(j * width + rank, (j + 1) * width) for j in range(1, count)]
    return (
        own[:width],
        sib[:width],
        jnp.concatenate([own[s] for s in at], axis=0),
        jnp.concatenate([sib[s] for s in at], axis=0),
        jnp.concatenate([own[s] + sib[s] for s in rest], axis=0),
    )


def halves_node_kernel(count, own, mine, other, carried, new, node_out, part):
    shape = (-1, own.shape[1])
    sib = joined(mine[...].reshape(shape), other[...].reshape(shape))
    z, node = solve_node(*children_rows(own[...], sib, count))
    node_out[...] = node
    put_part(node_out, part)
    new[...] = updated(carried, z)


def upper_node_kernel(count, own, sib, carried, new, node_out, *part):
    z, node = solve_node(*children_rows(own[...], sib[...], count))
    node_out[...] = node
    if part:
        n = part[0].shape[0]
        part[0][...] = node_out[pl.ds(times8(bit_of("gy", 0), n), n)]
    new[...] = updated(carried, z)


def last_kernel(axis, bit, pair, carried, out):
    side = bit_of(axis, bit)
    rank = carried.shape[1]
    own, sib = pair[side], pair[1 - side]
    z = solve_own(own[:rank], sib[:rank], own[rank:], sib[rank:])
    out[...] = updated(carried, z)


def call(kernel, outs, *args, scratch=()):
    rows = sum(a.size // 128 for a in args)
    return pl.pallas_call(
        kernel,
        out_shape=[jax.ShapeDtypeStruct(o, jnp.float32) for o in outs],
        scratch_shapes=[pltpu.VMEM(s, jnp.float32) for s in scratch],
        compiler_params=pltpu.CompilerParams(vmem_limit_bytes=VMEM_BYTES),
        cost_estimate=pl.CostEstimate(
            flops=6 * 128 * 128 * (rows + 14 * 128),
            bytes_accessed=512 * rows,
            transcendentals=0,
        ),
    )(*args)


def bit_groups(count, bits):
    mask = sum(1 << b for b in bits)
    return [
        [
            base | sum(((i >> q) & 1) << b for q, b in enumerate(bits))
            for i in range(1 << len(bits))
        ]
        for base in range(count)
        if not base & mask
    ]


def swap_cores(value):
    return lax.ppermute(value, "gy", [(s, s ^ 1) for s in range(lax.axis_size("gy"))])


def pair_gather(value, axis, bit, tiled=False):
    groups = bit_groups(lax.axis_size(axis), [bit])
    return lax.all_gather(value, axis, axis_index_groups=groups, tiled=tiled)


def exchange(value, axis, bits):
    count = lax.axis_size(axis)
    return lax.all_to_all(value, axis, 0, 0, axis_index_groups=bit_groups(count, bits))


def to_all(value, axis, bits):
    return exchange(jnp.broadcast_to(value, (1 << len(bits),) + value.shape), axis, bits)


def shards(right_sides, factor_u, factor_v):
    levels, _, rank = factor_u.shape
    gx = lax.axis_index("gx")
    near_chips = [1, 2]

    rows = levels * rank + right_sides.shape[1]
    rest = (rows - 2 * rank) // 2
    sent = (4 * rank + 2 * rest, rank)
    carried, keep, give = call(
        start_kernel,
        [(rows, rank), sent, sent],
        factor_u,
        factor_v[:2],
        right_sides.T,
        scratch=[(rows, rank)] * 2,
    )
    pieces = to_all(keep + swap_cores(give), "gy", [1])
    z_low, node = call(
        functools.partial(lower_node_kernel, 1, 2 * rank + rest),
        [(rank + rest, rank), (rank + rest, rank)],
        pieces,
    )
    pair = pair_gather(node, "gy", 2)
    mine = call(functools.partial(lower_leaf_kernel, 2), [(2 * rest, rank)], pair, z_low)[0]
    halves = pair_gather(mine, "gy", 0)

    level = 2
    rows -= level * rank
    count = levels - level
    all_both = rows + (count - 1) * rank
    all_sums = (count - 1) * (rows - rank)
    n_both, n_sums = all_both // 8, all_sums // 8
    sent = (4, n_both + n_sums, rank)
    carried, keep, give = call(
        functools.partial(upper_kernel, 4),
        [(rows, rank), sent, sent],
        carried,
        z_low,
        halves,
        factor_v[level:],
        scratch=[(all_both, rank), (all_sums, rank)],
    )
    piece = exchange(keep + swap_cores(give), "gy", near_chips).sum(axis=0)
    share = call(
        functools.partial(share_kernel, n_both),
        [(4, 2 * n_both + n_sums, rank)],
        pair_gather(piece, "gy", 3),
    )[0]
    mine = exchange(share, "gy", near_chips)
    other = swap_cores(mine)
    carried, node, part = call(
        functools.partial(top_node_kernel, 3, rows, n_both, n_sums),
        [(rows - rank, rank), (all_sums, rank), (all_sums // 8, rank)],
        mine,
        other,
        carried,
    )

    def of_sibling(value, axis, bit):
        pair = pair_gather(value, axis, bit)
        return lax.dynamic_index_in_dim(pair, 1 - bit_of(axis, bit), 0, keepdims=False)

    for axis, bit in (("gy", 4), ("gx", 0), ("gx", 1), ("gx", 2)):
        rows, count = rows - rank, count - 1
        out_rows = (count - 1) * (rows - rank)
        if count > 2:
            mine = to_all(of_sibling(part, axis, bit), "gy", near_chips)
            outs = [(rows - rank, rank), (out_rows, rank)]
            if count > 3:
                carried, node, part = call(
                    functools.partial(halves_node_kernel, count),
                    outs + [(out_rows // 8, rank)],
                    node,
                    mine,
                    swap_cores(mine),
                    carried,
                )
            else:
                near = pair_gather(mine.reshape(-1, rank), "gy", 0, tiled=True)
                carried, node, part = call(
                    functools.partial(upper_node_kernel, count),
                    outs + [(out_rows // 2, rank)],
                    node,
                    near,
                    carried,
                )
        else:
            near = pair_gather(of_sibling(part, axis, bit), "gy", 0, tiled=True)
            carried, node = call(
                functools.partial(upper_node_kernel, count),
                [(rows - rank, rank), (out_rows, rank)],
                node,
                near,
                carried,
            )
    pair = pair_gather(node, "gx", 3)
    shape = right_sides.shape[::-1]
    return call(functools.partial(last_kernel, "gx", 3), [shape], pair, carried)[0].T


def solution(mesh):
    placed = (P(("gx", "gy"), None), P(None, ("gx", "gy"), None), P(None, ("gx", "gy"), None))
    return jax.shard_map(
        shards, mesh=mesh, in_specs=placed, out_specs=P(("gx", "gy"), None), check_vma=False
    )
```

time: 227 us -> 251 us (1.11)
  waiting for transfers between devices: 18.5 us -> 32.9 us
  blocking collectives: 158 us -> 150 us
  starting transfers between devices: 23.6 us -> 29.9 us
  local copies, waits for them, and re-layouts: 4.84 us -> 10.8 us
  Pallas kernels: 21.3 us -> 25.7 us
    all_gather x9 -> x10, blocking collectives: 66.4 us -> 84.3 us  [pair_gather(): return lax.all_gather(value, axis, axis_index_groups=groups, tiled=tiled)]
    all_to_all x6 -> x4, blocking collectives: 82.1 us -> 66 us  [exchange(): lax.all_to_all(value, axis, 0, 0, axis_index_groups=bit_groups(count, bits))]
    all_to_all x1 -> x2, waiting for transfers between devices: 11.6 us -> 21.8 us  [exchange(): lax.all_to_all(value, axis, 0, 0, axis_index_groups=bit_groups(count, bits))]
    all_gather x1 -> x0, blocking collectives: 9.27 us -> none  [shards(): lax.all_gather(of_sibling(part, 1), 'gy', axis_index_groups=quads, tiled=...]
    unnamed x7 -> x22, local copies, waits for them, and re-layouts: 1.9 us -> 7.73 us
    pallas_call x11, Pallas kernels: 21.3 us -> 25.7 us  [call(): pl.pallas_call(kernel, out_shape=[jax.ShapeDtypeStruct(o, jnp.float32) fo...]
    ppermute x4 -> x5, waiting for transfers between devices: 6.88 us -> 11.1 us  [swap_cores(): lax.ppermute(value, 'gy', [(s, s ^ 1) for s in range(lax.axis_size('gy'))])]
    all_to_all x1 -> x2, starting transfers between devices: 3.5 us -> 7.22 us  [exchange(): lax.all_to_all(value, axis, 0, 0, axis_index_groups=bit_groups(count, bits))]
  transfers between devices with their start and end apart: 5 -> 7, of which waited for: 5 -> 7; matrix products, arithmetic and copies ran while one was open for 0% -> 0% of each run, Pallas kernels for 0% -> 0%
where the time goes in v4:
time: 251 us; the launch traced here: 250 us
  blocking collectives  150 us (60%)
  waiting for transfers between devices  32.9 us (13%)
  starting transfers between devices  29.9 us (12%)
  Pallas kernels  25.7 us (10%)
  local copies, waits for them, and re-layouts  10.8 us (4%)
    all_gather x10, blocking collectives, pair_gather(): return lax.all_gather(value, axis, axis_index_groups=groups, tiled=tiled)  84.3 us
    all_to_all x4, blocking collectives, exchange(): lax.all_to_all(value, axis, 0, 0, axis_index_groups=bit_groups(count, bits))  66 us
    pallas_call x11, Pallas kernels, call(): pl.pallas_call(kernel, out_shape=[jax.ShapeDtypeStruct(o, jnp.float32) fo...  25.7 us
    ppermute x5, starting transfers between devices, swap_cores(): lax.ppermute(value, 'gy', [(s, s ^ 1) for s in range(lax.axis_size('gy'))])  22.6 us
    all_to_all x2, waiting for transfers between devices, exchange(): lax.all_to_all(value, axis, 0, 0, axis_index_groups=bit_groups(count, bits))  21.8 us
    ppermute x5, waiting for transfers between devices, swap_cores(): lax.ppermute(value, 'gy', [(s, s ^ 1) for s in range(lax.axis_size('gy'))])  11.1 us
    unnamed x22, local copies, waits for them, and re-layouts  7.73 us
    all_to_all x2, starting transfers between devices, exchange(): lax.all_to_all(value, axis, 0, 0, axis_index_groups=bit_groups(count, bits))  7.22 us
  transfers between devices with their start and end apart: 7, of which 7 were waited for; matrix products, arithmetic and copies ran while one was open for 0% of the time, Pallas kernels for 0%

profile of v4, /device:TPU:1, one launch (start us, length us, event | category | flops | bytes accessed | tf_op | source)
XLA Modules:
  0.0 250.1 jit_solution(15990775874807410658)
XLA Ops:
  3.5 8.8 %collective-permute-start = (f32[1344,128]{1,0:T(8,128)S(1)}, f32[1344,128]{1,0:T(8,128)S(1)}, u32[]{:S(2)}, u32[]{:S(2)}) collective-permute-start(f32[1344,128]{1,0:T(8,128)S(1)} %get-tuple-element.29), channel_id=1, source_target_pairs={{0,1},{1,0},{2,3},{3,2},{4,5},{5,4},{6,7},{7,6},{8,9},{9,8},{10,11... | collective-permute-start | bytes 2064392 | tf_op jit(solution)/shard_map/ppermute | solution.py:269
  15.3 3.8 %all-to-all-start = ((f32[2,1344,128]{2,1,0:T(8,128)}), f32[2,1344,128]{2,1,0:T(8,128)S(1)}, u32[]{:S(2)}, u32[]{:S(2)}) async-start(f32[2,1344,128]{2,1,0:T(8,128)} %broadcast_in_dim.12), calls=%async_computation | async-start | bytes 2752512 | tf_op jit(solution)/shard_map/all_to_all | solution.py:279
  19.1 16.8 %all-to-all-done.pieces = f32[2,1344,128]{2,1,0:T(8,128)S(1)} async-done(((f32[2,1344,128]{2,1,0:T(8,128)}), f32[2,1344,128]{2,1,0:T(8,128)S(1)}, u32[]{:S(2)}, u32[]{:S(2)}) %all-to-all-start) | async-done | bytes 1376288 | tf_op jit(solution)/shard_map/all_to_all | solution.py:279
  38.3 7.6 %all-gather = f32[1088,128]{1,0:T(8,128)S(1)} all-gather(f32[544,128]{1,0:T(8,128)S(1)} %get-tuple-element.31), channel_id=2, replica_groups={{0,4},{1,5},{2,6},{3,7},{8,12},{9,13},{10,14},{11,15},{16,20},{17,21},{..., dimensions={0}, use_global_device_ids=true | all-gather | bytes 835584 | tf_op jit(solution)/shard_map/all_gather | solution.py:274
  47.7 4.2 %all-gather.1 = f32[1664,128]{1,0:T(8,128)S(1)} all-gather(f32[832,128]{1,0:T(8,128)S(1)} %shard_map.39), channel_id=3, replica_groups={{0,1},{2,3},{4,5},{6,7},{8,9},{10,11},{12,13},{14,15},{16,17},{18,19},{..., dimensions={0}, use_global_device_ids=true | all-gather | bytes 1277952 | tf_op jit(solution)/shard_map/all_gather | solution.py:274
  59.5 18.6 %all_to_all.30 = f32[4,624,128]{2,1,0:T(8,128)S(1)} all-to-all(f32[4,624,128]{2,1,0:T(8,128)S(1)} %add.27), channel_id=1, replica_groups={{0,2,4,6},{1,3,5,7},{8,10,12,14},{9,11,13,15},{16,18,20,22},{17,19,21,2..., dimensions={0} | all-to-all | bytes 2555904 | tf_op jit(solution)/shard_map/all_to_all | solution.py:279
  78.2 17.1 %all-gather.2 = f32[1248,128]{1,0:T(8,128)S(1)} all-gather(f32[624,128]{1,0:T(8,128)S(1)} %reduce_sum.9), channel_id=4, replica_groups={{0,8},{1,9},{2,10},{3,11},{4,12},{5,13},{6,14},{7,15},{16,24},{17,25},{..., dimensions={0}, use_global_device_ids=true | all-gather | bytes 958464 | tf_op jit(solution)/shard_map/all_gather | solution.py:274
  95.4 22.2 %all_to_all.31.mine = f32[4,808,128]{2,1,0:T(8,128)S(1)} all-to-all(f32[4,808,128]{2,1,0:T(8,128)S(1)} %shard_map.41), channel_id=1, replica_groups={{0,2,4,6},{1,3,5,7},{8,10,12,14},{9,11,13,15},{16,18,20,22},{17,19,21,2..., dimensions={0} | all-to-all | bytes 3309568 | tf_op jit(solution)/shard_map/all_to_all | solution.py:279
  117.6 4.1 %collective-permute-start.2 = (f32[4,808,128]{2,1,0:T(8,128)S(1)}, f32[4,808,128]{2,1,0:T(8,128)S(1)}, u32[]{:S(2)}, u32[]{:S(2)}) collective-permute-start(f32[4,808,128]{2,1,0:T(8,128)S(1)} %all_to_all.31.mine), channel_id=1, source_target_pairs={{0,1},{1,0},{2,3},{3,2},{4,5},{5,4},{6,7},{7,6},{8,9},{9,8},{10,11... | collective-permute-start | bytes 4964360 | tf_op jit(solution)/shard_map/ppermute | solution.py:269
  121.7 3.1 %collective-permute-done.2.other = f32[4,808,128]{2,1,0:T(8,128)S(1)} collective-permute-done((f32[4,808,128]{2,1,0:T(8,128)S(1)}, f32[4,808,128]{2,1,0:T(8,128)S(1)}, u32[]{:S(2)}, u32[]{:S(2)}) %collective-permute-start.2) | collective-permute-done | bytes 1654816 | tf_op jit(solution)/shard_map/ppermute | solution.py:269
  128.5 4.0 %shard_map.42 = (f32[704,128]{1,0:T(8,128)S(1)}, f32[3520,128]{1,0:T(8,128)S(1)}, f32[440,128]{1,0:T(8,128)S(1)}) custom-call(f32[4,808,128]{2,1,0:T(8,128)S(1)} %all_to_all.31.mine, f32[4,808,128]{2,1,0:T(8,128)S(1)} %copy-done.1, f32[832,128]{1,0:T(8,128)S(1)} %copy-done.5), custom_call_target="tpu_custom_call" | custom-call | flops 893386752 | bytes 3735552 | tf_op jit(solution)/shard_map/pallas_call | solution.py:243
  132.5 16.2 %all-gather.3 = f32[880,128]{1,0:T(8,128)S(1)} all-gather(f32[440,128]{1,0:T(8,128)S(1)} %get-tuple-element.36), channel_id=5, replica_groups={{0,16},{1,17},{2,18},{3,19},{4,20},{5,21},{6,22},{7,23},{8,24},{9,25},{..., dimensions={0}, use_global_device_ids=true | all-gather | bytes 675840 | tf_op jit(solution)/shard_map/all_gather | solution.py:274
  148.8 14.3 %all_to_all.32.mine = f32[4,440,128]{2,1,0:T(8,128)S(1)} all-to-all(f32[4,440,128]{2,1,0:T(8,128)S(1)} %broadcast_in_dim.13), channel_id=1, replica_groups={{0,2,4,6},{1,3,5,7},{8,10,12,14},{9,11,13,15},{16,18,20,22},{17,19,21,2..., dimensions={0} | all-to-all | bytes 1802240 | tf_op jit(solution)/shard_map/all_to_all | solution.py:279
  163.1 3.6 %collective-permute-start.3 = (f32[4,440,128]{2,1,0:T(8,128)S(1)}, f32[4,440,128]{2,1,0:T(8,128)}, u32[]{:S(2)}, u32[]{:S(2)}) collective-permute-start(f32[4,440,128]{2,1,0:T(8,128)S(1)} %all_to_all.32.mine), channel_id=1, source_target_pairs={{0,1},{1,0},{2,3},{3,2},{4,5},{5,4},{6,7},{7,6},{8,9},{9,8},{10,11... | collective-permute-start | bytes 2703368 | tf_op jit(solution)/shard_map/ppermute | solution.py:269
  169.8 4.5 %shard_map.43 = (f32[576,128]{1,0:T(8,128)S(1)}, f32[2304,128]{1,0:T(8,128)S(1)}, f32[288,128]{1,0:T(8,128)S(1)}) custom-call(f32[3520,128]{1,0:T(8,128)S(1)} %get-tuple-element.35.own, f32[4,440,128]{2,1,0:T(8,128)S(1)} %all_to_all.32.mine, f32[4,440,128]{2,1,0:T(8,128)} %collective-permute-done.3.other, f32[704,128]{1,0:T(8,128)S(1)} %copy-done.7), custom_call_target="tpu_custom_call" | custom-call | flops 937426944 | bytes 3964928 | tf_op jit(solution)/shard_map/pallas_call | solution.py:243
  174.4 10.2 %all-gather.4 = f32[576,128]{1,0:T(8,128)S(1)} all-gather(f32[288,128]{1,0:T(8,128)S(1)} %get-tuple-element.39), channel_id=6, replica_groups={{0,32},{64,96},{128,160},{192,224},{256,288},{320,352},{384,416},{448,4..., dimensions={0}, use_global_device_ids=true | all-gather | bytes 442368 | tf_op jit(solution)/shard_map/all_gather | solution.py:274
  184.7 10.9 %all_to_all.33.mine = f32[4,288,128]{2,1,0:T(8,128)S(1)} all-to-all(f32[4,288,128]{2,1,0:T(8,128)S(1)} %broadcast_in_dim.14), channel_id=1, replica_groups={{0,2,4,6},{1,3,5,7},{8,10,12,14},{9,11,13,15},{16,18,20,22},{17,19,21,2..., dimensions={0} | all-to-all | bytes 1179648 | tf_op jit(solution)/shard_map/all_to_all | solution.py:279
  195.6 3.9 %collective-permute-start.4 = (f32[4,288,128]{2,1,0:T(8,128)S(1)}, f32[4,288,128]{2,1,0:T(8,128)S(1)}, u32[]{:S(2)}, u32[]{:S(2)}) collective-permute-start(f32[4,288,128]{2,1,0:T(8,128)S(1)} %all_to_all.33.mine), channel_id=1, source_target_pairs={{0,1},{1,0},{2,3},{3,2},{4,5},{5,4},{6,7},{7,6},{8,9},{9,8},{10,11... | collective-permute-start | bytes 1769480 | tf_op jit(solution)/shard_map/ppermute | solution.py:269
  205.0 8.3 %all-gather.5 = f32[336,128]{1,0:T(8,128)S(1)} all-gather(f32[168,128]{1,0:T(8,128)S(1)} %get-tuple-element.42), channel_id=7, replica_groups={{0,64},{32,96},{128,192},{160,224},{256,320},{288,352},{384,448},{416,4..., dimensions={0}, use_global_device_ids=true | all-gather | bytes 258048 | tf_op jit(solution)/shard_map/all_gather | solution.py:274
  214.1 3.5 %all-to-all-start.5 = ((f32[4,168,128]{2,1,0:T(8,128)}), f32[4,168,128]{2,1,0:T(8,128)S(1)}, u32[]{:S(2)}, u32[]{:S(2)}) async-start(f32[4,168,128]{2,1,0:T(8,128)} %broadcast_in_dim.15), calls=%async_computation.5 | async-start | bytes 688128 | tf_op jit(solution)/shard_map/all_to_all | solution.py:279
  217.5 5.0 %all-to-all-done.5 = f32[4,168,128]{2,1,0:T(8,128)S(1)} async-done(((f32[4,168,128]{2,1,0:T(8,128)}), f32[4,168,128]{2,1,0:T(8,128)S(1)}, u32[]{:S(2)}, u32[]{:S(2)}) %all-to-all-start.5) | async-done | bytes 344096 | tf_op jit(solution)/shard_map/all_to_all | solution.py:279
  222.5 5.6 %all_gather.66.sib = f32[1344,128]{1,0:T(8,128)S(1)} all-gather(f32[672,128]{1,0:T(8,128)S(1)} %bitcast.24), channel_id=1, replica_groups={{0,1},{2,3},{4,5},{6,7},{8,9},{10,11},{12,13},{14,15},{16,17},{18,19},{..., dimensions={0}, use_global_device_ids=true | all-gather | bytes 1032192 | tf_op jit(solution)/shard_map/all_gather | solution.py:274
  230.5 6.1 %all-gather.6 = f32[640,128]{1,0:T(8,128)S(1)} all-gather(f32[320,128]{1,0:T(8,128)S(1)} %get-tuple-element.45), channel_id=8, replica_groups={{0,128},{32,160},{64,192},{96,224},{256,384},{288,416},{320,448},{352,4..., dimensions={0}, use_global_device_ids=true | all-gather | bytes 491520 | tf_op jit(solution)/shard_map/all_gather | solution.py:274
  241.5 6.2 %all-gather.8 = f32[384,128]{1,0:T(8,128)S(1)} all-gather(f32[192,128]{1,0:T(8,128)S(1)} %get-tuple-element.47), channel_id=10, replica_groups={{0,256},{32,288},{64,320},{96,352},{128,384},{160,416},{192,448},{224,4..., dimensions={0}, use_global_device_ids=true | all-gather | bytes 294912 | tf_op jit(solution)/shard_map/all_gather | solution.py:274
  (50 shorter events, 41.5 us)
Async XLA Ops:
  0.9 1.0 copy-start.8
  2.0 0.8 copy-start.9
  3.5 10.5 %collective-permute-start = (f32[1344,128]{1,0:T(8,128)S(1)}, f32[1344,128]{1,0:T(8,128)S(1)}, u32[]{:S(2)}, u32[]{:S(2)}) collective-permute-start(f32[1344,128]{1,0:T(8,128)S(1)} %get-tuple-element.29), channel_id=1, source_target_pairs={{0,1},{1,0},{2,3},{3,2},{4,5},{5,4},{6,7},{7,6},{8,9},{9,8},{10,11... | collective-permute-start | bytes 2064392 | tf_op jit(solution)/shard_map/ppermute | solution.py:269
  15.3 3.8 %copy-start.10 = (f32[8,128,128]{2,1,0:T(8,128)S(1)}, f32[8,128,128]{2,1,0:T(8,128)}, u32[]{:S(2)}) copy-start(f32[8,128,128]{2,1,0:T(8,128)} %param.5) | copy-start | bytes 1572868
  15.3 20.6 %all-to-all-start = ((f32[2,1344,128]{2,1,0:T(8,128)}), f32[2,1344,128]{2,1,0:T(8,128)S(1)}, u32[]{:S(2)}, u32[]{:S(2)}) async-start(f32[2,1344,128]{2,1,0:T(8,128)} %broadcast_in_dim.12), calls=%async_computation | async-start | bytes 2752512 | tf_op jit(solution)/shard_map/all_to_all | solution.py:279
  54.5 5.1 %copy-start.4 = (f32[832,128]{1,0:T(8,128)}, f32[832,128]{1,0:T(8,128)S(1)}, u32[]{:S(2)}) copy-start(f32[832,128]{1,0:T(8,128)S(1)} %get-tuple-element.34.carried) | copy-start | bytes 1277956
  54.5 4.9 %collective-permute-start.1 = (f32[4,624,128]{2,1,0:T(8,128)S(1)}, f32[4,624,128]{2,1,0:T(8,128)S(1)}, u32[]{:S(2)}, u32[]{:S(2)}) collective-permute-start(f32[4,624,128]{2,1,0:T(8,128)S(1)} %get-tuple-element.33), channel_id=1, source_target_pairs={{0,1},{1,0},{2,3},{3,2},{4,5},{5,4},{6,7},{7,6},{8,9},{9,8},{10,11... | collective-permute-start | bytes 3833864 | tf_op jit(solution)/shard_map/ppermute | solution.py:269
  117.6 7.2 %collective-permute-start.2 = (f32[4,808,128]{2,1,0:T(8,128)S(1)}, f32[4,808,128]{2,1,0:T(8,128)S(1)}, u32[]{:S(2)}, u32[]{:S(2)}) collective-permute-start(f32[4,808,128]{2,1,0:T(8,128)S(1)} %all_to_all.31.mine), channel_id=1, source_target_pairs={{0,1},{1,0},{2,3},{3,2},{4,5},{5,4},{6,7},{7,6},{8,9},{9,8},{10,11... | collective-permute-start | bytes 4964360 | tf_op jit(solution)/shard_map/ppermute | solution.py:269
  124.9 1.2 copy-start
  126.1 1.4 copy-start.1
  127.5 1.0 copy-start.5
  132.5 30.6 %copy-start.6 = (f32[704,128]{1,0:T(8,128)}, f32[704,128]{1,0:T(8,128)S(1)}, u32[]{:S(2)}) copy-start(f32[704,128]{1,0:T(8,128)S(1)} %get-tuple-element.37.carried) | copy-start | bytes 1081348
  163.1 5.8 %collective-permute-start.3 = (f32[4,440,128]{2,1,0:T(8,128)S(1)}, f32[4,440,128]{2,1,0:T(8,128)}, u32[]{:S(2)}, u32[]{:S(2)}) collective-permute-start(f32[4,440,128]{2,1,0:T(8,128)S(1)} %all_to_all.32.mine), channel_id=1, source_target_pairs={{0,1},{1,0},{2,3},{3,2},{4,5},{5,4},{6,7},{7,6},{8,9},{9,8},{10,11... | collective-permute-start | bytes 2703368 | tf_op jit(solution)/shard_map/ppermute | solution.py:269
  168.8 1.0 copy-start.7
  174.3 10.3 %copy-start.2 = (f32[2304,128]{1,0:T(8,128)}, f32[2304,128]{1,0:T(8,128)S(1)}, u32[]{:S(2)}) copy-start(f32[2304,128]{1,0:T(8,128)S(1)} %get-tuple-element.38.own) | copy-start | bytes 3538948
  195.6 5.4 %collective-permute-start.4 = (f32[4,288,128]{2,1,0:T(8,128)S(1)}, f32[4,288,128]{2,1,0:T(8,128)S(1)}, u32[]{:S(2)}, u32[]{:S(2)}) collective-permute-start(f32[4,288,128]{2,1,0:T(8,128)S(1)} %all_to_all.33.mine), channel_id=1, source_target_pairs={{0,1},{1,0},{2,3},{3,2},{4,5},{5,4},{6,7},{7,6},{8,9},{9,8},{10,11... | collective-permute-start | bytes 1769480 | tf_op jit(solution)/shard_map/ppermute | solution.py:269
  200.9 1.3 copy-start.3
  214.1 8.4 %all-to-all-start.5 = ((f32[4,168,128]{2,1,0:T(8,128)}), f32[4,168,128]{2,1,0:T(8,128)S(1)}, u32[]{:S(2)}, u32[]{:S(2)}) async-start(f32[4,168,128]{2,1,0:T(8,128)} %broadcast_in_dim.15), calls=%async_computation.5 | async-start | bytes 688128 | tf_op jit(solution)/shard_map/all_to_all | solution.py:279

commit v5 on v3

v5 whole, which is shorter than its diff:
```python
import functools

import jax
import jax.numpy as jnp
from jax import lax
from jax.experimental import pallas as pl
from jax.experimental.pallas import tpu as pltpu
from jax.sharding import PartitionSpec as P

VMEM_BYTES = 40 * 2**20


def split(value):
    high = value.astype(jnp.bfloat16)
    low = (value - high.astype(jnp.float32)).astype(jnp.bfloat16)
    return high, low


def dot_split(a, b):
    def part(x, y):
        return jnp.dot(x, y, preferred_element_type=jnp.float32)

    return part(a[0], b[0]) + (part(a[0], b[1]) + part(a[1], b[0]))


def kdot(a, b):
    return dot_split(split(a), split(b))


def inverse_of(error):
    total = jnp.eye(error.shape[0], dtype=jnp.float32) + error
    power = error
    for step in range(6):
        parts = split(power)
        power = dot_split(parts, parts)
        total = total + kdot(total, power)
    return total


def solve_own(gram_own, gram_sib, proj_own, proj_sib):
    inverse = inverse_of(kdot(gram_own, gram_sib))
    return kdot(proj_sib - kdot(proj_own, gram_sib), inverse)


def solve_node(own, sib, ops_own, ops_sib, sums):
    rank = own.shape[1]
    width = own.shape[0] - rank
    gram_own, proj_own = own[:rank], own[rank:]
    z = solve_own(gram_own, sib[:rank], proj_own, sib[rank:])
    z_sib = proj_own - kdot(z, gram_own)
    z_both = split(jnp.concatenate([z, z_sib], axis=1))
    node = []
    for j in range(ops_own.shape[0] // rank):
        at = slice(j * rank, (j + 1) * rank)
        left = split(jnp.concatenate([ops_own[at], ops_sib[at]], axis=0))
        node.append(sums[j * width : (j + 1) * width] - dot_split(z_both, left))
    return z, jnp.concatenate(node, axis=0)


def put_rows(out, base, size, start, value):
    at, rows = 0, value.shape[0]
    while at < rows:
        i, r = divmod(start + at, size)
        n = min(size - r, rows - at)
        out[i, base + r : base + r + n] = value[at : at + n]
        at += n


def get_rows(ref, base, size):
    return jnp.concatenate([ref[i, pl.ds(base, size)] for i in range(ref.shape[0])], axis=0)


def bit_of(axis, bit):
    return (lax.axis_index(axis) >> bit) & 1


def times8(value, rows):
    return pl.multiple_of(value * rows, 8)


def pack_kernel(u, v, y, pack):
    levels, _, rank = u.shape
    first = levels * rank + y.shape[0]
    for j in range(levels):
        pack[j * rank : (j + 1) * rank] = u[j].T
        pack[first + j * rank : first + (j + 1) * rank] = v[j]
    pack[levels * rank : first] = y[...]


def first_pair_kernel(levels, mine, other, held, sent, next_v, top_v):
    rank = mine.shape[1]
    half = rank // 2
    core = bit_of("gy", 0)
    first = mine.shape[0] - levels * rank
    last = first - levels * rank
    held[: 2 * rank, :rank] = mine[: 2 * rank]
    held[: 2 * rank, rank:] = other[: 2 * rank]
    for j in range(2, levels + 1):
        n = half if j < levels else last // 2
        at = pl.ds(j * rank + times8(core, n), n)
        to = slice(2 * rank + (j - 2) * half, 2 * rank + (j - 2) * half + n)
        held[to, :rank] = mine[at]
        held[to, rank:] = other[at]
    factors = [
        jnp.concatenate(
            [ref[first + j * rank : first + (j + 1) * rank] for ref in (mine, other)], axis=0
        )
        for j in range(levels)
    ]
    parts = split(held[...])
    rows = held.shape[0]
    for j in range(2):
        value = dot_split(parts, split(factors[j]))
        sent[0, j * rows : (j + 1) * rows] = value
        sent[1, j * rows : (j + 1) * rows] = value
    for j in range(2, 4):
        next_v[j - 2] = factors[j]
    for j in range(4, levels):
        top_v[j - 4] = factors[j]


def lower_node_kernel(bit, n_both, rest, pieces, z_out, node_out):
    side = bit_of("gy", bit)
    rank = z_out.shape[1]
    top = 2 * rank + rest
    if n_both is None:
        own = pieces[side, :top]
        sib = pieces[1 - side, :top]
        ops_own = pieces[side, top : top + rank]
        ops_sib = pieces[1 - side, top : top + rank]
        sums = pieces[0, top + rank :] + pieces[1, top + rank :]
    else:
        own = get_rows(pieces, times8(side, n_both), n_both)
        sib = get_rows(pieces, times8(1 - side, n_both), n_both)
        own, ops_own = own[:top], own[top:]
        sib, ops_sib = sib[:top], sib[top:]
        sums = get_rows(pieces, 2 * n_both, pieces.shape[1] - 2 * n_both)
    z, node = solve_node(own, sib, ops_own, ops_sib, sums)
    z_out[...] = z
    node_out[...] = node


def after_pair(bit, pair, z_low, held):
    side = bit_of("gy", bit)
    rank = pair.shape[2]
    own, sib = pair[side], pair[1 - side]
    z_up = solve_own(own[:rank], sib[:rank], own[rank:], sib[rank:])
    left = held[:rank]
    next_left = held[rank : 2 * rank] - kdot(z_low[:rank], left)
    z_both = jnp.concatenate([z_low[rank:], z_up], axis=1)
    return held[2 * rank :] - kdot(z_both, jnp.concatenate([left, next_left], axis=0))


def between_kernel(bit, pair, z_low, held, rest, halves):
    value = after_pair(bit, pair, z_low, held)
    rest[...] = value
    halves[...] = value[: halves.shape[0]]


def second_pair_kernel(shares, rest, gathered, v, held, sent):
    rank = v.shape[2]
    half = rank // 2
    core = bit_of("gy", 0)
    parts = []
    for c in range(2):
        value = gathered[c]
        turned = jnp.concatenate([value[:, rank:], value[:, :rank]], axis=1)
        parts.append(jnp.where(core == c, value, turned))
    for j in range(2):
        for c in range(2):
            at = j * rank + c * half
            held[at : at + half] = parts[c][j * half : (j + 1) * half]
    held[2 * rank :] = rest[rank:]
    rows = held.shape[0]
    value = split(held[...])
    low = dot_split(value, split(v[0]))
    up = dot_split(value, split(v[1]))
    n_both = (rows + rank) // shares
    put_rows(sent, 0, n_both, 0, low)
    put_rows(sent, 0, n_both, rows, up[:rank])
    put_rows(sent, n_both, (rows - rank) // shares, 0, up[rank:])


def upper_kernel(bit, shares, pair, z_low, held, v, mine, other, sent):
    value = after_pair(bit, pair, z_low, held)
    rank = v.shape[2]
    half = rank // 2
    mine[...] = value[:, :rank]
    other[...] = value[:, rank:]
    count, width = v.shape[0], value.shape[0]
    n_both = (width + (count - 1) * half) // shares
    n_sums = (count - 1) * (width - half) // shares
    parts = split(value)
    put_rows(sent, 0, n_both, 0, dot_split(parts, split(v[0])))
    for j in range(1, count):
        rows = dot_split(parts, split(v[j]))
        put_rows(sent, 0, n_both, width + (j - 1) * half, rows[:half])
        put_rows(sent, n_both, n_sums, (j - 1) * (width - half), rows[half:])


def share_kernel(n_both, pair, out):
    rows = [pair[0, :n_both], pair[1, :n_both], pair[0, n_both:] + pair[1, n_both:]]
    value = jnp.concatenate(rows, axis=0)
    for i in range(out.shape[0]):
        out[i] = value


def interleaved(first, second, block):
    out, at, rows = [], 0, first.shape[0]
    while at < rows:
        n = min(block, rows - at)
        out += [first[at : at + n], second[at : at + n]]
        at += n
    return jnp.concatenate(out, axis=0)


def updated(carried, z):
    rank = z.shape[1]
    return carried[rank:] - kdot(z, carried[:rank])


def top_node_kernel(count, n_both, n_sums, gathered, swapped, held, new, node_out, quarter):
    rank = held.shape[1]
    half = rank // 2
    width = held.shape[0]
    core = bit_of("gy", 0)
    side = bit_of("gx", 0)
    shares, size = gathered.shape[0], gathered.shape[1]

    def rows_of(base, n):
        here = get_rows(gathered, base, n)
        there = jnp.concatenate(
            [swapped[pl.ds(pl.multiple_of(i * size + base, 8), n)] for i in range(shares)], axis=0
        )
        return jnp.where(core == 0, here, there), jnp.where(core == 0, there, here)

    def child(which):
        first, second = rows_of(times8(which, n_both), n_both)
        ops = interleaved(first[width:], second[width:], half)
        return interleaved(first[:width], second[:width], half), ops

    own, ops_own = child(side)
    sib, ops_sib = child(1 - side)
    first, second = rows_of(2 * n_both, n_sums)
    w = width - half
    sums = jnp.concatenate(
        [
            interleaved(first[j * w : (j + 1) * w], second[j * w : (j + 1) * w], half)
            for j in range(count - 1)
        ],
        axis=0,
    )
    z, node = solve_node(own, sib, ops_own, ops_sib, sums)
    node_out[...] = node
    n = quarter.shape[0]
    quarter[...] = node_out[pl.ds(times8(lax.axis_index("gy") & 3, n), n)]
    here, there = held[...], swapped[shares * size :]
    carried = interleaved(
        jnp.where(core == 0, here, there), jnp.where(core == 0, there, here), half
    )
    new[...] = updated(carried, z)


def children_rows(own, sib, count):
    rank = own.shape[1]
    width = own.shape[0] // count
    at = [slice(j * width, j * width + rank) for j in range(1, count)]
    rest = [slice(j * width + rank, (j + 1) * width) for j in range(1, count)]
    return (
        own[:width],
        sib[:width],
        jnp.concatenate([own[s] for s in at], axis=0),
        jnp.concatenate([sib[s] for s in at], axis=0),
        jnp.concatenate([own[s] + sib[s] for s in rest], axis=0),
    )


def upper_node_kernel(count, bit, own, sib, carried, new, node_out):
    value = sib[...] if bit is None else sib[1 - bit_of("gx", bit)]
    z, node = solve_node(*children_rows(own[...], value, count))
    node_out[...] = node
    new[...] = updated(carried, z)


def last_kernel(axis, bit, pair, carried, out):
    side = bit_of(axis, bit)
    rank = carried.shape[1]
    own, sib = pair[side], pair[1 - side]
    z = solve_own(own[:rank], sib[:rank], own[rank:], sib[rank:])
    out[...] = updated(carried, z)


def call(kernel, outs, *args, scratch=()):
    rows = sum(a.size // 128 for a in args)
    return pl.pallas_call(
        kernel,
        out_shape=[jax.ShapeDtypeStruct(o, jnp.float32) for o in outs],
        scratch_shapes=[pltpu.VMEM(s, jnp.float32) for s in scratch],
        compiler_params=pltpu.CompilerParams(vmem_limit_bytes=VMEM_BYTES),
        cost_estimate=pl.CostEstimate(
            flops=6 * 128 * 128 * (rows + 14 * 128),
            bytes_accessed=512 * rows,
            transcendentals=0,
        ),
    )(*args)


def bit_groups(count, bits):
    mask = sum(1 << b for b in bits)
    return [
        [
            base | sum(((i >> q) & 1) << b for q, b in enumerate(bits))
            for i in range(1 << len(bits))
        ]
        for base in range(count)
        if not base & mask
    ]


def swap_cores(value):
    return lax.ppermute(value, "gy", [(s, s ^ 1) for s in range(lax.axis_size("gy"))])


def pair_gather(value, axis, bit, tiled=False):
    groups = bit_groups(lax.axis_size(axis), [bit])
    return lax.all_gather(value, axis, axis_index_groups=groups, tiled=tiled)


def exchange(value, axis, bits):
    count = lax.axis_size(axis)
    return lax.all_to_all(value, axis, 0, 0, axis_index_groups=bit_groups(count, bits))


def to_all(value, axis, bits):
    return exchange(jnp.broadcast_to(value, (1 << len(bits),) + value.shape), axis, bits)


def pad_rows(value, rows):
    return jnp.pad(value, ((0, rows - value.shape[0]), (0, 0)))


def up8(value):
    return -(-value // 8) * 8


def shards(right_sides, factor_u, factor_v):
    levels, _, rank = factor_u.shape
    half = rank // 2
    near_chips = [1, 2]

    all_rows = levels * rank + right_sides.shape[1]
    pack = call(
        pack_kernel,
        [(all_rows + levels * rank, rank)],
        factor_u,
        factor_v,
        right_sides.T,
    )[0]
    rest = (all_rows - 2 * rank) // 2
    rows = 2 * rank + rest
    held, sent, next_v, top_v = call(
        functools.partial(first_pair_kernel, levels),
        [
            (rows, 2 * rank),
            (2, 2 * rows, rank),
            (2, 2 * rank, rank),
            (levels - 4, 2 * rank, rank),
        ],
        pack,
        swap_cores(pack),
    )
    z_low, node = call(
        functools.partial(lower_node_kernel, 1, None, rest),
        [(rank + rest, rank), (rank + rest, rank)],
        exchange(sent, "gy", [1]),
    )
    own_rest, halves = call(
        functools.partial(between_kernel, 2),
        [(rest, 2 * rank), (rank, 2 * rank)],
        pair_gather(node, "gy", 2),
        z_low,
        held,
    )

    rest -= rank
    rows = 2 * rank + rest
    n_both, n_sums = (rows + rank) // 4, (rows - rank) // 4
    held, sent = call(
        functools.partial(second_pair_kernel, 4),
        [(rows, 2 * rank), (4, n_both + n_sums, rank)],
        own_rest,
        pair_gather(halves, "gy", 0),
        next_v,
    )
    piece = exchange(sent, "gy", near_chips).sum(axis=0)
    share = call(
        functools.partial(share_kernel, n_both),
        [(4, 2 * n_both + n_sums, rank)],
        pair_gather(piece, "gy", 3),
    )[0]
    z_low, node = call(
        functools.partial(lower_node_kernel, 3, n_both, rest),
        [(rank + rest, rank), (rank + rest, rank)],
        exchange(share, "gy", near_chips),
    )

    count = levels - 4
    n_both = (rest + (count - 1) * half) // 4
    n_sums = (count - 1) * (rest - half) // 4
    mine, other, sent = call(
        functools.partial(upper_kernel, 4, 4),
        [(rest, rank), (rest, rank), (4, n_both + n_sums, rank)],
        pair_gather(node, "gy", 4),
        z_low,
        held,
        top_v,
    )
    piece = exchange(sent, "gy", near_chips).sum(axis=0)
    s_both, s_sums = up8(-(-n_both // 8)), up8(-(-n_sums // 8))
    sent = jnp.concatenate(
        [
            pad_rows(piece[:n_both], 8 * s_both).reshape(8, s_both, rank),
            pad_rows(piece[n_both:], 8 * s_sums).reshape(8, s_sums, rank),
        ],
        axis=1,
    )
    far = [3, 4, 5]
    sides = exchange(sent, ("gx", "gy"), far)
    sides = sides.reshape((2, 4) + sides.shape[1:]).sum(axis=1)
    share = jnp.concatenate(
        [sides[0, :s_both], sides[1, :s_both], sides[0, s_both:] + sides[1, s_both:]], axis=0
    )
    pieces = to_all(share, ("gx", "gy"), far)
    share = jnp.concatenate(
        [
            pieces[:, :s_both].reshape(-1, rank)[:n_both],
            pieces[:, s_both : 2 * s_both].reshape(-1, rank)[:n_both],
            pieces[:, 2 * s_both :].reshape(-1, rank)[:n_sums],
        ],
        axis=0,
    )
    gathered = to_all(share, "gy", near_chips)
    swapped = swap_cores(jnp.concatenate([gathered.reshape(-1, rank), other], axis=0))
    rows = 2 * rest
    out_rows = (count - 1) * (rows - rank)
    carried, node, part = call(
        functools.partial(top_node_kernel, count, n_both, n_sums),
        [(rows - rank, rank), (out_rows, rank), (out_rows // 4, rank)],
        gathered,
        swapped,
        mine,
    )

    pair = pair_gather(part, "gx", 1)
    part = lax.dynamic_index_in_dim(pair, 1 - bit_of("gx", 1), 0, keepdims=False)
    quads = bit_groups(lax.axis_size("gy"), [0, 1])
    near = lax.all_gather(part, "gy", axis_index_groups=quads, tiled=True)
    for bit in (None, 2):
        rows, count = rows - rank, count - 1
        carried, node = call(
            functools.partial(upper_node_kernel, count, bit),
            [(rows - rank, rank), ((count - 1) * (rows - rank), rank)],
            node,
            near,
            carried,
        )
        near = pair_gather(node, "gx", 2 if bit is None else 3)
    shape = right_sides.shape[::-1]
    return call(functools.partial(last_kernel, "gx", 3), [shape], near, carried)[0].T


def solution(mesh):
    placed = (P(("gx", "gy"), None), P(None, ("gx", "gy"), None), P(None, ("gx", "gy"), None))
    return jax.shard_map(
        shards, mesh=mesh, in_specs=placed, out_specs=P(("gx", "gy"), None), check_vma=False
    )
```

time: 227 us -> 212 us (0.934)
  waiting for transfers between devices: 18.5 us -> 4.48 us
  blocking collectives: 158 us -> 166 us
  starting transfers between devices: 23.6 us -> 16.4 us
    all_to_all x6 -> x7, blocking collectives: 82.1 us -> 96.5 us  [exchange(): lax.all_to_all(value, axis, 0, 0, axis_index_groups=bit_groups(count, bits))]
    all_to_all x1 -> x0, waiting for transfers between devices: 11.6 us -> none  [exchange(): lax.all_to_all(value, axis, 0, 0, axis_index_groups=bit_groups(count, bits))]
    all_gather x9 -> x7, blocking collectives: 66.4 us -> 57.5 us  [pair_gather(): return lax.all_gather(value, axis, axis_index_groups=groups, tiled=tiled)]
    ppermute x4 -> x2, starting transfers between devices: 20.1 us -> 16.4 us  [swap_cores(): lax.ppermute(value, 'gy', [(s, s ^ 1) for s in range(lax.axis_size('gy'))])]
    all_to_all x1 -> x0, starting transfers between devices: 3.5 us -> none  [exchange(): lax.all_to_all(value, axis, 0, 0, axis_index_groups=bit_groups(count, bits))]
    all_gather x1, blocking collectives: 9.27 us -> 11.9 us  [shards(): near = lax.all_gather(part, 'gy', axis_index_groups=quads, tiled=True)]
    ppermute x4 -> x2, waiting for transfers between devices: 6.88 us -> 4.48 us  [swap_cores(): lax.ppermute(value, 'gy', [(s, s ^ 1) for s in range(lax.axis_size('gy'))])]
    pallas_call x11 -> x12, Pallas kernels: 21.3 us -> 20.6 us  [call(): pl.pallas_call(kernel, out_shape=[jax.ShapeDtypeStruct(o, jnp.float32) fo...]
  transfers between devices with their start and end apart: 5 -> 2, of which waited for: 5 -> 2; matrix products, arithmetic and copies ran while one was open for 0% -> 0% of each run, Pallas kernels for 0% -> 0%
where the time goes in v5:
time: 212 us; the launch traced here: 211 us
  blocking collectives  166 us (78%)
  Pallas kernels  20.6 us (10%)
  starting transfers between devices  16.4 us (8%)
  waiting for transfers between devices  4.48 us (2%)
  local copies, waits for them, and re-layouts  2.98 us (1%)
    all_to_all x7, blocking collectives, exchange(): lax.all_to_all(value, axis, 0, 0, axis_index_groups=bit_groups(count, bits))  96.5 us
    all_gather x7, blocking collectives, pair_gather(): return lax.all_gather(value, axis, axis_index_groups=groups, tiled=tiled)  57.5 us
    pallas_call x12, Pallas kernels, call(): pl.pallas_call(kernel, out_shape=[jax.ShapeDtypeStruct(o, jnp.float32) fo...  20.6 us
    ppermute x2, starting transfers between devices, swap_cores(): lax.ppermute(value, 'gy', [(s, s ^ 1) for s in range(lax.axis_size('gy'))])  16.4 us
    all_gather x1, blocking collectives, shards(): near = lax.all_gather(part, 'gy', axis_index_groups=quads, tiled=True)  11.9 us
    ppermute x2, waiting for transfers between devices, swap_cores(): lax.ppermute(value, 'gy', [(s, s ^ 1) for s in range(lax.axis_size('gy'))])  4.48 us
  transfers between devices with their start and end apart: 2, of which 2 were waited for; matrix products, arithmetic and copies ran while one was open for 0% of the time, Pallas kernels for 0%

profile of v5, /device:TPU:1, one launch (start us, length us, event | category | flops | bytes accessed | tf_op | source)
XLA Modules:
  0.0 210.8 jit_solution(10724965667079395349)
XLA Ops:
  3.0 8.8 %collective-permute-start = (f32[2112,128]{1,0:T(8,128)S(1)}, f32[2112,128]{1,0:T(8,128)S(1)}, u32[]{:S(2)}, u32[]{:S(2)}) collective-permute-start(f32[2112,128]{1,0:T(8,128)S(1)} %shard_map.37.mine), channel_id=1, source_target_pairs={{0,1},{1,0},{2,3},{3,2},{4,5},{5,4},{6,7},{7,6},{8,9},{9,8},{10,11... | collective-permute-start | bytes 3244040 | tf_op jit(solution)/shard_map/ppermute | solution.py:321
  11.8 2.3 %collective-permute-done.other = f32[2112,128]{1,0:T(8,128)S(1)} collective-permute-done((f32[2112,128]{1,0:T(8,128)S(1)}, f32[2112,128]{1,0:T(8,128)S(1)}, u32[]{:S(2)}, u32[]{:S(2)}) %collective-permute-start) | collective-permute-done | bytes 1081376 | tf_op jit(solution)/shard_map/ppermute | solution.py:321
  14.9 19.3 %all_to_all.35.pieces = f32[2,1344,128]{2,1,0:T(8,128)S(1)} all-to-all(f32[2,1344,128]{2,1,0:T(8,128)S(1)} %get-tuple-element.27), channel_id=1, replica_groups={{0,2},{1,3},{4,6},{5,7},{8,10},{9,11},{12,14},{13,15},{16,18},{17,19},{..., dimensions={0} | all-to-all | bytes 2752512 | tf_op jit(solution)/shard_map/all_to_all | solution.py:331
  34.3 2.4 %shard_map.39 = (f32[544,128]{1,0:T(8,128)S(1)}, f32[544,128]{1,0:T(8,128)S(1)}) custom-call(f32[2,1344,128]{2,1,0:T(8,128)S(1)} %all_to_all.35.pieces), custom_call_target="tpu_custom_call" | custom-call | flops 440401920 | bytes 1376256 | tf_op jit(solution)/shard_map/pallas_call | solution.py:295
  36.7 7.6 %all-gather = f32[1088,128]{1,0:T(8,128)S(1)} all-gather(f32[544,128]{1,0:T(8,128)S(1)} %get-tuple-element.28), channel_id=2, replica_groups={{0,4},{1,5},{2,6},{3,7},{8,12},{9,13},{10,14},{11,15},{16,20},{17,21},{..., dimensions={0}, use_global_device_ids=true | all-gather | bytes 835584 | tf_op jit(solution)/shard_map/all_gather | solution.py:326
  46.5 3.7 %all-gather.1 = f32[256,256]{1,0:T(8,128)S(1)} all-gather(f32[128,256]{1,0:T(8,128)S(1)} %get-tuple-element.32), channel_id=3, replica_groups={{0,1},{2,3},{4,5},{6,7},{8,9},{10,11},{12,13},{14,15},{16,17},{18,19},{..., dimensions={0}, use_global_device_ids=true | all-gather | bytes 393216 | tf_op jit(solution)/shard_map/all_gather | solution.py:326
  50.8 10.9 %all_to_all.36 = f32[4,272,128]{2,1,0:T(8,128)S(1)} all-to-all(f32[4,272,128]{2,1,0:T(8,128)S(1)} %get-tuple-element.34), channel_id=1, replica_groups={{0,2,4,6},{1,3,5,7},{8,10,12,14},{9,11,13,15},{16,18,20,22},{17,19,21,2..., dimensions={0} | all-to-all | bytes 1114112 | tf_op jit(solution)/shard_map/all_to_all | solution.py:331
  61.7 9.3 %all-gather.2 = f32[544,128]{1,0:T(8,128)S(1)} all-gather(f32[272,128]{1,0:T(8,128)S(1)} %reduce_sum.27), channel_id=4, replica_groups={{0,8},{1,9},{2,10},{3,11},{4,12},{5,13},{6,14},{7,15},{16,24},{17,25},{..., dimensions={0}, use_global_device_ids=true | all-gather | bytes 417792 | tf_op jit(solution)/shard_map/all_gather | solution.py:326
  71.1 13.4 %all_to_all.37.pieces = f32[4,440,128]{2,1,0:T(8,128)S(1)} all-to-all(f32[4,440,128]{2,1,0:T(8,128)S(1)} %shard_map.42), channel_id=1, replica_groups={{0,2,4,6},{1,3,5,7},{8,10,12,14},{9,11,13,15},{16,18,20,22},{17,19,21,2..., dimensions={0} | all-to-all | bytes 1802240 | tf_op jit(solution)/shard_map/all_to_all | solution.py:331
  84.5 2.3 %shard_map.43 = (f32[416,128]{1,0:T(8,128)S(1)}, f32[416,128]{1,0:T(8,128)S(1)}) custom-call(f32[4,440,128]{2,1,0:T(8,128)S(1)} %all_to_all.37.pieces), custom_call_target="tpu_custom_call" | custom-call | flops 349175808 | bytes 901120 | tf_op jit(solution)/shard_map/pallas_call | solution.py:295
  86.8 9.7 %all-gather.3 = f32[832,128]{1,0:T(8,128)S(1)} all-gather(f32[416,128]{1,0:T(8,128)S(1)} %get-tuple-element.35), channel_id=5, replica_groups={{0,16},{1,17},{2,18},{3,19},{4,20},{5,21},{6,22},{7,23},{8,24},{9,25},{..., dimensions={0}, use_global_device_ids=true | all-gather | bytes 638976 | tf_op jit(solution)/shard_map/all_gather | solution.py:326
  96.5 2.5 %shard_map.44 = (f32[288,128]{1,0:T(8,128)S(1)}, f32[288,128]{1,0:T(8,128)S(1)}, f32[4,288,128]{2,1,0:T(8,128)S(1)}) custom-call(f32[2,416,128]{2,1,0:T(8,128)S(1)} %bitcast.29, f32[416,128]{1,0:T(8,128)S(1)} %get-tuple-element.36.z_low, f32[544,256]{1,0:T(8,128)S(1)} %get-tuple-element.37.held, f32[4,256,128]{2,1,0:T(8,128)S(1)} %get-tuple-element.38.v), custom_call_target="tpu_custom_call" | custom-call | flops 506462208 | bytes 1720320 | tf_op jit(solution)/shard_map/pallas_call | solution.py:295
  99.0 15.0 %all_to_all.38 = f32[4,288,128]{2,1,0:T(8,128)S(1)} all-to-all(f32[4,288,128]{2,1,0:T(8,128)S(1)} %get-tuple-element.39), channel_id=1, replica_groups={{0,2,4,6},{1,3,5,7},{8,10,12,14},{9,11,13,15},{16,18,20,22},{17,19,21,2..., dimensions={0} | all-to-all | bytes 1179648 | tf_op jit(solution)/shard_map/all_to_all | solution.py:331
  114.2 14.5 %all_to_all.39 = f32[8,40,128]{2,1,0:T(8,128)S(1)} all-to-all(f32[8,40,128]{2,1,0:T(8,128)S(1)} %pad_maximum_fusion.2), channel_id=1, replica_groups={{0,8,16,24,32,40,48,56},{1,9,17,25,33,41,49,57},{2,10,18,26,34,42,50,58..., dimensions={0} | all-to-all | bytes 327680 | tf_op jit(solution)/shard_map/all_to_all | solution.py:331
  128.7 12.0 %all_to_all.40 = f32[8,56,128]{2,1,0:T(8,128)S(1)} all-to-all(f32[8,56,128]{2,1,0:T(8,128)S(1)} %broadcast_in_dim.6), channel_id=1, replica_groups={{0,8,16,24,32,40,48,56},{1,9,17,25,33,41,49,57},{2,10,18,26,34,42,50,58..., dimensions={0} | all-to-all | bytes 458752 | tf_op jit(solution)/shard_map/all_to_all | solution.py:331
  140.9 11.4 %all_to_all.41.gathered = f32[4,408,128]{2,1,0:T(8,128)S(1)} all-to-all(f32[4,408,128]{2,1,0:T(8,128)S(1)} %broadcast_in_dim.7), channel_id=1, replica_groups={{0,2,4,6},{1,3,5,7},{8,10,12,14},{9,11,13,15},{16,18,20,22},{17,19,21,2..., dimensions={0} | all-to-all | bytes 1671168 | tf_op jit(solution)/shard_map/all_to_all | solution.py:331
  152.3 7.7 %collective-permute-start.1 = (f32[1920,128]{1,0:T(8,128)S(1)}, f32[1920,128]{1,0:T(8,128)S(1)}, u32[]{:S(2)}, u32[]{:S(2)}) collective-permute-start(f32[1920,128]{1,0:T(8,128)S(1)} %pad_maximum_fusion), channel_id=1, source_target_pairs={{0,1},{1,0},{2,3},{3,2},{4,5},{5,4},{6,7},{7,6},{8,9},{9,8},{10,11... | collective-permute-start | bytes 2949128 | tf_op jit(solution)/shard_map/ppermute | solution.py:321
  162.1 2.8 %shard_map.45 = (f32[448,128]{1,0:T(8,128)S(1)}, f32[1344,128]{1,0:T(8,128)S(1)}, f32[336,128]{1,0:T(8,128)S(1)}) custom-call(f32[4,408,128]{2,1,0:T(8,128)S(1)} %all_to_all.41.gathered, f32[1920,128]{1,0:T(8,128)S(1)} %collective-permute-done.1.swapped, f32[288,128]{1,0:T(8,128)S(1)} %get-tuple-element.41.held), custom_call_target="tpu_custom_call" | custom-call | flops 553648128 | bytes 1966080 | tf_op jit(solution)/shard_map/pallas_call | solution.py:295
  164.9 11.7 %all-gather.4 = f32[672,128]{1,0:T(8,128)S(1)} all-gather(f32[336,128]{1,0:T(8,128)S(1)} %get-tuple-element.43), channel_id=6, replica_groups={{0,64},{32,96},{128,192},{160,224},{256,320},{288,352},{384,448},{416,4..., dimensions={0}, use_global_device_ids=true | all-gather | bytes 516096 | tf_op jit(solution)/shard_map/all_gather | solution.py:326
  176.6 11.9 %all-gather.5 = f32[1,1344,128]{2,1,0:T(8,128)S(1)} all-gather(f32[1,336,128]{2,1,0:T(8,128)S(1)} %constant_dynamic-slice_fusion), channel_id=7, replica_groups={{0,1,2,3},{4,5,6,7},{8,9,10,11},{12,13,14,15},{16,17,18,19},{20,21,22,2..., dimensions={1}, use_global_device_ids=true | all-gather | bytes 860160 | tf_op jit(solution)/shard_map/all_gather | solution.py:457
  188.5 2.4 %shard_map.46 = (f32[320,128]{1,0:T(8,128)S(1)}, f32[640,128]{1,0:T(8,128)S(1)}) custom-call(f32[1344,128]{1,0:T(8,128)S(1)} %get-tuple-element.42.own, f32[1344,128]{1,0:T(8,128)S(1)} %bitcast.26, f32[448,128]{1,0:T(8,128)S(1)} %get-tuple-element.44.carried), custom_call_target="tpu_custom_call" | custom-call | flops 484442112 | bytes 1605632 | tf_op jit(solution)/shard_map/pallas_call | solution.py:295
  190.9 9.8 %all-gather.6 = f32[1280,128]{1,0:T(8,128)S(1)} all-gather(f32[640,128]{1,0:T(8,128)S(1)} %get-tuple-element.45.own), channel_id=8, replica_groups={{0,128},{32,160},{64,192},{96,224},{256,384},{288,416},{320,448},{352,4..., dimensions={0}, use_global_device_ids=true | all-gather | bytes 983040 | tf_op jit(solution)/shard_map/all_gather | solution.py:326
  202.8 5.6 %all-gather.7 = f32[384,128]{1,0:T(8,128)S(1)} all-gather(f32[192,128]{1,0:T(8,128)S(1)} %get-tuple-element.47), channel_id=9, replica_groups={{0,256},{32,288},{64,320},{96,352},{128,384},{160,416},{192,448},{224,4..., dimensions={0}, use_global_device_ids=true | all-gather | bytes 294912 | tf_op jit(solution)/shard_map/all_gather | solution.py:326
  208.4 2.4 %shard_map.48 = f32[64,128]{1,0:T(8,128)} custom-call(f32[2,192,128]{2,1,0:T(8,128)S(1)} %bitcast.31, f32[192,128]{1,0:T(8,128)S(1)} %get-tuple-element.48.carried), custom_call_target="tpu_custom_call" | custom-call | flops 232783872 | bytes 294912 | tf_op jit(solution)/shard_map/pallas_call | solution.py:295
  (34 shorter events, 11.2 us)
Async XLA Ops:
  0.0 1.0 copy-start
  1.0 1.0 copy-start.1
  2.1 0.8 copy-start.2
  3.0 11.1 %collective-permute-start = (f32[2112,128]{1,0:T(8,128)S(1)}, f32[2112,128]{1,0:T(8,128)S(1)}, u32[]{:S(2)}, u32[]{:S(2)}) collective-permute-start(f32[2112,128]{1,0:T(8,128)S(1)} %shard_map.37.mine), channel_id=1, source_target_pairs={{0,1},{1,0},{2,3},{3,2},{4,5},{5,4},{6,7},{7,6},{8,9},{9,8},{10,11... | collective-permute-start | bytes 3244040 | tf_op jit(solution)/shard_map/ppermute | solution.py:321
  99.0 15.1 %copy-start.3 = (pred[128]{0:T(512)(128)(4,1)S(1)}, pred[128]{0:T(512)(128)(4,1)}, u32[]{:S(2)}) copy-start(pred[128]{0:T(512)(128)(4,1)} %constant.14.clone.1) | copy-start | bytes 388
  152.3 9.8 %collective-permute-start.1 = (f32[1920,128]{1,0:T(8,128)S(1)}, f32[1920,128]{1,0:T(8,128)S(1)}, u32[]{:S(2)}, u32[]{:S(2)}) collective-permute-start(f32[1920,128]{1,0:T(8,128)S(1)} %pad_maximum_fusion), channel_id=1, source_target_pairs={{0,1},{1,0},{2,3},{3,2},{4,5},{5,4},{6,7},{7,6},{8,9},{9,8},{10,11... | collective-permute-start | bytes 2949128 | tf_op jit(solution)/shard_map/ppermute | solution.py:321

commit v6 on v5

v6 whole, which is shorter than its diff:
```python
import functools

import jax
import jax.numpy as jnp
from jax import lax
from jax.experimental import pallas as pl
from jax.experimental.pallas import tpu as pltpu
from jax.sharding import PartitionSpec as P

VMEM_BYTES = 40 * 2**20
ALL_VMEM_BYTES = 62_000_000


def split(value):
    high = value.astype(jnp.bfloat16)
    low = (value - high.astype(jnp.float32)).astype(jnp.bfloat16)
    return high, low


def dot_split(a, b):
    def part(x, y):
        return jnp.dot(x, y, preferred_element_type=jnp.float32)

    return part(a[0], b[0]) + (part(a[0], b[1]) + part(a[1], b[0]))


def kdot(a, b):
    return dot_split(split(a), split(b))


def solve_own(gram_own, gram_sib, proj_own, proj_sib):
    power = kdot(gram_own, gram_sib)
    right = proj_sib - kdot(proj_own, gram_sib)
    total = jnp.eye(power.shape[0], dtype=jnp.float32) + power
    for step in range(5):
        parts = split(power)
        power = dot_split(parts, parts)
        total = total + kdot(total, power)
    parts = split(power)
    power = dot_split(parts, parts)
    right = kdot(right, total)
    return right + kdot(right, power)


def solve_node(own, sib, ops_own, ops_sib, sums):
    rank = own.shape[1]
    width = own.shape[0] - rank
    gram_own, proj_own = own[:rank], own[rank:]
    z = solve_own(gram_own, sib[:rank], proj_own, sib[rank:])
    z_sib = proj_own - kdot(z, gram_own)
    z_both = split(jnp.concatenate([z, z_sib], axis=1))
    node = []
    for j in range(ops_own.shape[0] // rank):
        at = slice(j * rank, (j + 1) * rank)
        left = split(jnp.concatenate([ops_own[at], ops_sib[at]], axis=0))
        node.append(sums[j * width : (j + 1) * width] - dot_split(z_both, left))
    return z, jnp.concatenate(node, axis=0)


def put_rows(out, base, size, start, value):
    at, rows = 0, value.shape[0]
    while at < rows:
        i, r = divmod(start + at, size)
        n = min(size - r, rows - at)
        out[i, base + r : base + r + n] = value[at : at + n]
        at += n


def get_rows(ref, base, size):
    return jnp.concatenate([ref[i, pl.ds(base, size)] for i in range(ref.shape[0])], axis=0)


def bit_of(axis, bit):
    return (lax.axis_index(axis) >> bit) & 1


def times8(value, rows):
    return pl.multiple_of(value * rows, 8)


def pack_kernel(u, v, y, pack, u_held, sems):
    levels, _, rank = u.shape
    first = levels * rank + y.shape[0]
    copies = [pltpu.make_async_copy(u.at[j], u_held.at[j], sems.at[j]) for j in range(levels)]
    copies.append(
        pltpu.make_async_copy(y, pack.at[pl.ds(levels * rank, y.shape[0])], sems.at[levels])
    )
    for j in range(levels):
        rows = pl.ds(first + j * rank, rank)
        copies.append(pltpu.make_async_copy(v.at[j], pack.at[rows], sems.at[levels + 1 + j]))
    for copy in copies:
        copy.start()
    for j in range(levels):
        copies[j].wait()
        pack[j * rank : (j + 1) * rank] = u_held[j].T
    for copy in copies[levels:]:
        copy.wait()


def first_pair_kernel(levels, mine, other, held, sent, next_v, top_v):
    rank = mine.shape[1]
    half = rank // 2
    core = bit_of("gy", 0)
    first = mine.shape[0] - levels * rank
    last = first - levels * rank
    held[: 2 * rank, :rank] = mine[: 2 * rank]
    held[: 2 * rank, rank:] = other[: 2 * rank]
    for j in range(2, levels + 1):
        n = half if j < levels else last // 2
        at = pl.ds(j * rank + times8(core, n), n)
        to = slice(2 * rank + (j - 2) * half, 2 * rank + (j - 2) * half + n)
        held[to, :rank] = mine[at]
        held[to, rank:] = other[at]
    factors = [
        jnp.concatenate(
            [ref[first + j * rank : first + (j + 1) * rank] for ref in (mine, other)], axis=0
        )
        for j in range(levels)
    ]
    parts = split(held[...])
    rows = held.shape[0]
    for j in range(2):
        value = dot_split(parts, split(factors[j]))
        sent[0, j * rows : (j + 1) * rows] = value
        sent[1, j * rows : (j + 1) * rows] = value
    for j in range(2, 4):
        next_v[j - 2] = factors[j]
    for j in range(4, levels):
        top_v[j - 4] = factors[j]


def first_node_kernel(bit, top, pieces, z_out, node_out):
    side = bit_of("gy", bit)
    rank = z_out.shape[1]
    ops = slice(top, top + rank)
    z, node = solve_node(
        pieces[side, :top],
        pieces[1 - side, :top],
        pieces[side, ops],
        pieces[1 - side, ops],
        pieces[0, top + rank :] + pieces[1, top + rank :],
    )
    z_out[...] = z
    node_out[...] = node


def after_pair(bit, pair, z_low, held):
    side = bit_of("gy", bit)
    rank = pair.shape[2]
    own, sib = pair[side], pair[1 - side]
    z_up = solve_own(own[:rank], sib[:rank], own[rank:], sib[rank:])
    left = held[:rank]
    next_left = held[rank : 2 * rank] - kdot(z_low[:rank], left)
    z_both = jnp.concatenate([z_low[rank:], z_up], axis=1)
    return held[2 * rank :] - kdot(z_both, jnp.concatenate([left, next_left], axis=0))


def between_kernel(bit, shares, pair, z_low, held, v, rest, sent):
    value = after_pair(bit, pair, z_low, held)
    rest[...] = value
    rows = value.shape[0]
    half = v.shape[2] // 2
    parts = split(value)
    low = dot_split(parts, split(v[0]))
    up = dot_split(parts, split(v[1]))
    n_both = (rows + half) // shares
    put_rows(sent, 0, n_both, 0, low)
    put_rows(sent, 0, n_both, rows, up[:half])
    put_rows(sent, n_both, (rows - half) // shares, 0, up[half:])


def second_shared_kernel(n_both, n_sums, rows, pieces, rest, out):
    rank = out.shape[1]
    half = rank // 2
    for c in range(2):
        both = get_rows(pieces, c * n_both, n_both)
        out[3 * half * c : 3 * half * c + rank] = both[:rank]
        out[3 * half * c + rank : 3 * half * (c + 1)] = both[rows:]
    out[6 * half : 7 * half] = get_rows(pieces, 2 * n_both, n_sums)[:half]
    out[7 * half : 9 * half] = rest[:rank, :rank]
    out[9 * half : 11 * half] = rest[:rank, rank:]


def both_cores(ref, at, n):
    return [ref[c, pl.ds(at, n)] for c in range(2)]


def full_rows(ref, at, n):
    return jnp.concatenate(both_cores(ref, at, n), axis=0)


def second_node_kernel(bit, n_both, n_sums, rows, pieces, shared, z_out, node_out):
    side = bit_of("gy", bit)
    rank = z_out.shape[1]
    half = rank // 2
    children = []
    for which in (side, 1 - side):
        at = times8(which, 3 * half)
        both = get_rows(pieces, times8(which, n_both), n_both)
        children.append(
            (
                jnp.concatenate(
                    [
                        full_rows(shared, at, half),
                        full_rows(shared, at + half, half),
                        both[rank:rows],
                    ],
                    axis=0,
                ),
                full_rows(shared, at + rank, half),
            )
        )
    (own, ops_own), (sib, ops_sib) = children
    sums = get_rows(pieces, 2 * n_both, n_sums)
    sums = jnp.concatenate([full_rows(shared, 6 * half, half), sums[half:]], axis=0)
    z, node = solve_node(own, sib, ops_own, ops_sib, sums)
    z_out[...] = z
    node_out[...] = node


def upper_kernel(bit, shares, pair, z_low, shared, rest, v, mine, other, sent):
    rank = v.shape[2]
    half = rank // 2
    core = bit_of("gy", 0)
    factors = []
    for c in range(2):
        a, b = shared[c, 7 * half : 9 * half], shared[c, 9 * half : 11 * half]
        here = core == c
        factors.append(
            jnp.concatenate([jnp.where(here, a, b), jnp.where(here, b, a)], axis=1)
        )
    held = jnp.concatenate(
        [factors[0][:half], factors[1][:half], factors[0][half:], factors[1][half:], rest[rank:]],
        axis=0,
    )
    value = after_pair(bit, pair, z_low, held)
    mine[...] = value[:, :rank]
    other[...] = value[:, rank:]
    count, width = v.shape[0], value.shape[0]
    n_both = (width + (count - 1) * half) // shares
    n_sums = (count - 1) * (width - half) // shares
    parts = split(value)
    put_rows(sent, 0, n_both, 0, dot_split(parts, split(v[0])))
    for j in range(1, count):
        rows = dot_split(parts, split(v[j]))
        put_rows(sent, 0, n_both, width + (j - 1) * half, rows[:half])
        put_rows(sent, n_both, n_sums, (j - 1) * (width - half), rows[half:])


def share_kernel(n_both, pair, out):
    rows = [pair[0, :n_both], pair[1, :n_both], pair[0, n_both:] + pair[1, n_both:]]
    value = jnp.concatenate(rows, axis=0)
    for i in range(out.shape[0]):
        out[i] = value


def interleaved(first, second, block):
    out, at, rows = [], 0, first.shape[0]
    while at < rows:
        n = min(block, rows - at)
        out += [first[at : at + n], second[at : at + n]]
        at += n
    return jnp.concatenate(out, axis=0)


def updated(carried, z):
    rank = z.shape[1]
    return carried[rank:] - kdot(z, carried[:rank])


def top_shared_kernel(n_both, width, gathered, other, out):
    half = out.shape[1] // 2
    n = half + 4 * n_both - width
    for c in range(2):
        both = get_rows(gathered, c * n_both, n_both)
        out[n * c : n * c + half] = both[:half]
        out[n * c + half : n * (c + 1)] = both[width:]
    out[2 * n :] = other[...]


def child_rows(shared, at, half, count, projections):
    own = jnp.concatenate([full_rows(shared, at, half), projections], axis=0)
    ops = [full_rows(shared, at + half * j, half) for j in range(1, count)]
    return own, jnp.concatenate(ops, axis=0)


def top_node_kernel(count, n_both, n_sums, gathered, shared, held, z_out, node_out, part, carried):
    rank = held.shape[1]
    half = rank // 2
    width = held.shape[0]
    core = bit_of("gy", 0)
    side = bit_of("gx", 0)
    children = []
    for which in (side, 1 - side):
        both = get_rows(gathered, times8(which, n_both), n_both)
        at = times8(which, half * count)
        children.append(child_rows(shared, at, half, count, both[half:width]))
    (own, ops_own), (sib, ops_sib) = children
    sums = get_rows(gathered, 2 * n_both, n_sums)
    z, node = solve_node(own, sib, ops_own, ops_sib, sums)
    z_out[...] = z
    node_out[...] = node
    n = part.shape[0]
    part[...] = node_out[pl.ds(times8((lax.axis_index("gy") >> 1) & 3, n), n)]
    swapped = [shared[c, 2 * half * count :] for c in range(2)]
    halves = [jnp.where(core == c, held[...], swapped[c]) for c in range(2)]
    carried[...] = interleaved(halves[0], halves[1], half)


def sibling_kernel(bit, pair, out):
    value = pair[1 - bit_of("gx", bit)]
    for i in range(out.shape[0]):
        out[i] = value


def upper_shared_kernel(count, bit, own, sib, out):
    half = out.shape[1] // 2
    width = own.shape[0] // count
    value = sib[...].reshape(own.shape) if bit is None else sib[1 - bit_of("gx", bit)]
    for j in range(count):
        at = slice(j * width, j * width + half)
        out[j * half : (j + 1) * half] = own[at]
        out[(count + j) * half : (count + j + 1) * half] = value[at]


def upper_node_kernel(count, bit, own, sib, shared, z_out, node_out):
    half = own.shape[1] // 2
    width = own.shape[0] // count
    here = own[...]
    there = sib[...].reshape(own.shape) if bit is None else sib[1 - bit_of("gx", bit)]
    rows_own, ops_own = child_rows(shared, 0, half, count, here[half:width])
    rows_sib, ops_sib = child_rows(shared, half * count, half, count, there[half:width])
    sums = jnp.concatenate(
        [
            here[j * width + half : (j + 1) * width] + there[j * width + half : (j + 1) * width]
            for j in range(1, count)
        ],
        axis=0,
    )
    z, node = solve_node(rows_own, rows_sib, ops_own, ops_sib, sums)
    z_out[...] = z
    node_out[...] = node


def last_kernel(bit, sizes, gathered, carried, out):
    rank = carried.shape[1]
    half = rank // 2
    side = bit_of("gx", bit)
    n = half + out.shape[0] // 2

    def child(which):
        return interleaved(*both_cores(gathered, times8(which, n), n), half)

    value, at = carried[...], 2 * n
    for size in sizes:
        value = updated(value, interleaved(*both_cores(gathered, at, size), half))
        at += size
    own, sib = child(side), child(1 - side)
    z = solve_own(own[:rank], sib[:rank], own[rank:], sib[rank:])
    out[...] = updated(value, z)


def call(kernel, outs, *args, vmem_bytes=VMEM_BYTES, **options):
    rows = sum(a.size // 128 for a in args)
    return pl.pallas_call(
        kernel,
        out_shape=[jax.ShapeDtypeStruct(o, jnp.float32) for o in outs],
        compiler_params=pltpu.CompilerParams(vmem_limit_bytes=vmem_bytes),
        cost_estimate=pl.CostEstimate(
            flops=6 * 128 * 128 * (rows + 14 * 128),
            bytes_accessed=512 * rows,
            transcendentals=0,
        ),
        **options,
    )(*args)


def bit_groups(count, bits):
    mask = sum(1 << b for b in bits)
    return [
        [
            base | sum(((i >> q) & 1) << b for q, b in enumerate(bits))
            for i in range(1 << len(bits))
        ]
        for base in range(count)
        if not base & mask
    ]


def swap_cores(value):
    return lax.ppermute(value, "gy", [(s, s ^ 1) for s in range(lax.axis_size("gy"))])


def pair_gather(value, axis, bit, tiled=False):
    groups = bit_groups(lax.axis_size(axis), [bit])
    return lax.all_gather(value, axis, axis_index_groups=groups, tiled=tiled)


def exchange(value, axis, bits):
    count = lax.axis_size(axis)
    return lax.all_to_all(value, axis, 0, 0, axis_index_groups=bit_groups(count, bits))


def to_all(value, axis, bits):
    return exchange(jnp.broadcast_to(value, (1 << len(bits),) + value.shape), axis, bits)


def pad_rows(value, rows):
    return jnp.pad(value, ((0, rows - value.shape[0]), (0, 0)))


def up8(value):
    return -(-value // 8) * 8


def shards(right_sides, factor_u, factor_v):
    levels, _, rank = factor_u.shape
    half = rank // 2
    near_chips = [1, 2]

    all_rows = levels * rank + right_sides.shape[1]
    pack = call(
        pack_kernel,
        [(all_rows + levels * rank, rank)],
        factor_u,
        factor_v,
        right_sides.T,
        vmem_bytes=ALL_VMEM_BYTES,
        in_specs=[pl.BlockSpec(memory_space=pltpu.HBM)] * 3,
        scratch_shapes=[
            pltpu.VMEM(factor_u.shape, jnp.float32),
            pltpu.SemaphoreType.DMA((2 * levels + 1,)),
        ],
    )[0]
    rest = (all_rows - 2 * rank) // 2
    rows = 2 * rank + rest
    held, sent, next_v, top_v = call(
        functools.partial(first_pair_kernel, levels),
        [
            (rows, 2 * rank),
            (2, 2 * rows, rank),
            (2, 2 * rank, rank),
            (levels - 4, 2 * rank, rank),
        ],
        pack,
        swap_cores(pack),
    )
    z_low, node = call(
        functools.partial(first_node_kernel, 1, rows),
        [(rank + rest, rank), (rank + rest, rank)],
        exchange(sent, "gy", [1]),
    )

    rows = rest
    rest -= rank
    n_both, n_sums = (rows + half) // 4, (rows - half) // 4
    held, sent = call(
        functools.partial(between_kernel, 2, 4),
        [(rows, 2 * rank), (4, n_both + n_sums, rank)],
        pair_gather(node, "gy", 2),
        z_low,
        held,
        next_v,
    )
    piece = exchange(sent, "gy", near_chips).sum(axis=0)
    share = call(
        functools.partial(share_kernel, n_both),
        [(4, 2 * n_both + n_sums, rank)],
        pair_gather(piece, "gy", 3),
    )[0]
    pieces = exchange(share, "gy", near_chips)
    shared = call(
        functools.partial(second_shared_kernel, n_both, n_sums, rows),
        [(11 * half, rank)],
        pieces,
        held,
    )[0]
    shared = pair_gather(shared, "gy", 0)
    z_low, node = call(
        functools.partial(second_node_kernel, 3, n_both, n_sums, rows),
        [(rank + rest, rank), (rank + rest, rank)],
        pieces,
        shared,
    )

    count = levels - 4
    n_both = (rest + (count - 1) * half) // 4
    n_sums = (count - 1) * (rest - half) // 4
    mine, other, sent = call(
        functools.partial(upper_kernel, 4, 4),
        [(rest, rank), (rest, rank), (4, n_both + n_sums, rank)],
        pair_gather(node, "gy", 4),
        z_low,
        shared,
        held,
        top_v,
    )
    piece = exchange(sent, "gy", near_chips).sum(axis=0)
    s_both, s_sums = up8(-(-n_both // 8)), up8(-(-n_sums // 8))
    sent = jnp.concatenate(
        [
            pad_rows(piece[:n_both], 8 * s_both).reshape(8, s_both, rank),
            pad_rows(piece[n_both:], 8 * s_sums).reshape(8, s_sums, rank),
        ],
        axis=1,
    )
    far = [3, 4, 5]
    sides = exchange(sent, ("gx", "gy"), far)
    sides = sides.reshape((2, 4) + sides.shape[1:]).sum(axis=1)
    share = jnp.concatenate(
        [sides[0, :s_both], sides[1, :s_both], sides[0, s_both:] + sides[1, s_both:]], axis=0
    )
    pieces = to_all(share, ("gx", "gy"), far)
    share = jnp.concatenate(
        [
            pieces[:, :s_both].reshape(-1, rank)[:n_both],
            pieces[:, s_both : 2 * s_both].reshape(-1, rank)[:n_both],
            pieces[:, 2 * s_both :].reshape(-1, rank)[:n_sums],
        ],
        axis=0,
    )
    gathered = to_all(share, "gy", near_chips)
    shared = call(
        functools.partial(top_shared_kernel, n_both, rest),
        [(2 * count * half + rest, rank)],
        gathered,
        other,
    )[0]
    width = rest - half
    z, node, part, carried = call(
        functools.partial(top_node_kernel, count, n_both, n_sums),
        [
            (width, rank),
            ((count - 1) * width, rank),
            ((count - 1) * width // 4, rank),
            (2 * rest, rank),
        ],
        gathered,
        pair_gather(shared, "gy", 0),
        mine,
    )
    solved = [z]

    for bit in (1, 2):
        count -= 1
        pair = pair_gather(part, "gx", bit)
        if bit == 1:
            near = call(functools.partial(sibling_kernel, bit), [(4,) + part.shape], pair)[0]
            near, pick = exchange(near, "gy", near_chips), None
        else:
            near, pick = pair, bit
        shared = call(
            functools.partial(upper_shared_kernel, count, pick),
            [(2 * count * half, rank)],
            node,
            near,
        )[0]
        width -= half
        z, node = call(
            functools.partial(upper_node_kernel, count, pick),
            [(width, rank), ((count - 1) * width, rank)],
            node,
            near,
            pair_gather(shared, "gy", 0),
        )
        part = node
        solved.append(z)

    pair = pair_gather(node, "gx", 3)
    gathered = pair_gather(jnp.concatenate([pair.reshape(-1, rank)] + solved, axis=0), "gy", 0)
    return call(
        functools.partial(last_kernel, 3, [v.shape[0] for v in solved]),
        [right_sides.shape[::-1]],
        gathered,
        carried,
    )[0].T


def solution(mesh):
    placed = (P(("gx", "gy"), None), P(None, ("gx", "gy"), None), P(None, ("gx", "gy"), None))
    return jax.shard_map(
        shards, mesh=mesh, in_specs=placed, out_specs=P(("gx", "gy"), None), check_vma=False
    )
```

time: 212 us -> 205 us (0.967)
  starting transfers between devices: 16.4 us -> 8.79 us
  Pallas kernels: 20.6 us -> 23.1 us
    all_gather x7 -> x11, blocking collectives: 57.5 us -> 74.6 us  [pair_gather(): return lax.all_gather(value, axis, axis_index_groups=groups, tiled=tiled)]
    all_gather x1 -> x0, blocking collectives: 11.9 us -> none  [shards(): near = lax.all_gather(part, 'gy', axis_index_groups=quads, tiled=True)]
    ppermute x2 -> x1, starting transfers between devices: 16.4 us -> 8.79 us  [swap_cores(): lax.ppermute(value, 'gy', [(s, s ^ 1) for s in range(lax.axis_size('gy'))])]
    all_to_all x7 -> x8, blocking collectives: 96.5 us -> 93.5 us  [exchange(): lax.all_to_all(value, axis, 0, 0, axis_index_groups=bit_groups(count, bits))]
    pallas_call x12 -> x16, Pallas kernels: 20.6 us -> 23.1 us  [call(): pl.pallas_call(kernel, out_shape=[jax.ShapeDtypeStruct(o, jnp.float32) fo...]
    ppermute x2 -> x1, waiting for transfers between devices: 4.48 us -> 2.52 us  [swap_cores(): lax.ppermute(value, 'gy', [(s, s ^ 1) for s in range(lax.axis_size('gy'))])]
  transfers between devices with their start and end apart: 2 -> 1, of which waited for: 2 -> 1; matrix products, arithmetic and copies ran while one was open for 0% -> 0% of each run, Pallas kernels for 0% -> 0%
where the time goes in v6:
time: 205 us; the launch traced here: 204 us
  blocking collectives  168 us (82%)
  Pallas kernels  23.1 us (11%)
  starting transfers between devices  8.79 us (4%)
  waiting for transfers between devices  2.52 us (1%)
    all_to_all x8, blocking collectives, exchange(): lax.all_to_all(value, axis, 0, 0, axis_index_groups=bit_groups(count, bits))  93.5 us
    all_gather x11, blocking collectives, pair_gather(): return lax.all_gather(value, axis, axis_index_groups=groups, tiled=tiled)  74.6 us
    pallas_call x16, Pallas kernels, call(): pl.pallas_call(kernel, out_shape=[jax.ShapeDtypeStruct(o, jnp.float32) fo...  23.1 us
    ppermute x1, starting transfers between devices, swap_cores(): lax.ppermute(value, 'gy', [(s, s ^ 1) for s in range(lax.axis_size('gy'))])  8.79 us
  transfers between devices with their start and end apart: 1, of which 1 were waited for; matrix products, arithmetic and copies ran while one was open for 0% of the time, Pallas kernels for 0%

profile of v6, /device:TPU:1, one launch (start us, length us, event | category | flops | bytes accessed | tf_op | source)
XLA Modules:
  0.0 204.2 jit_solution(15023574882040807865)
XLA Ops:
  0.0 2.8 %shard_map.37.mine = f32[2112,128]{1,0:T(8,128)} custom-call(f32[8,128,128]{2,1,0:T(8,128)} %u.1, f32[8,128,128]{2,1,0:T(8,128)} %v.1, f32[64,128]{1,0:T(8,128)} %bitcast.42), custom_call_target="tpu_custom_call" | custom-call | flops 383778816 | bytes 1081344 | tf_op jit(solution)/shard_map/pallas_call | solution.py:365
  2.8 8.8 %collective-permute-start = (f32[2112,128]{1,0:T(8,128)}, f32[2112,128]{1,0:T(8,128)S(1)}, u32[]{:S(2)}, u32[]{:S(2)}) collective-permute-start(f32[2112,128]{1,0:T(8,128)} %shard_map.37.mine), channel_id=1, source_target_pairs={{0,1},{1,0},{2,3},{3,2},{4,5},{5,4},{6,7},{7,6},{8,9},{9,8},{10,11... | collective-permute-start | bytes 3244040 | tf_op jit(solution)/shard_map/ppermute | solution.py:391
  16.1 19.3 %all_to_all.40.pieces = f32[2,1344,128]{2,1,0:T(8,128)S(1)} all-to-all(f32[2,1344,128]{2,1,0:T(8,128)S(1)} %get-tuple-element.26), channel_id=1, replica_groups={{0,2},{1,3},{4,6},{5,7},{8,10},{9,11},{12,14},{13,15},{16,18},{17,19},{..., dimensions={0} | all-to-all | bytes 2752512 | tf_op jit(solution)/shard_map/all_to_all | solution.py:401
  35.5 2.6 %shard_map.39 = (f32[544,128]{1,0:T(8,128)S(1)}, f32[544,128]{1,0:T(8,128)S(1)}) custom-call(f32[2,1344,128]{2,1,0:T(8,128)S(1)} %all_to_all.40.pieces), custom_call_target="tpu_custom_call" | custom-call | flops 440401920 | bytes 1376256 | tf_op jit(solution)/shard_map/pallas_call | solution.py:365
  38.1 7.6 %all-gather = f32[1088,128]{1,0:T(8,128)S(1)} all-gather(f32[544,128]{1,0:T(8,128)S(1)} %get-tuple-element.27), channel_id=2, replica_groups={{0,4},{1,5},{2,6},{3,7},{8,12},{9,13},{10,14},{11,15},{16,20},{17,21},{..., dimensions={0}, use_global_device_ids=true | all-gather | bytes 835584 | tf_op jit(solution)/shard_map/all_gather | solution.py:396
  48.3 8.1 %all_to_all.41 = f32[4,208,128]{2,1,0:T(8,128)S(1)} all-to-all(f32[4,208,128]{2,1,0:T(8,128)S(1)} %get-tuple-element.31), channel_id=1, replica_groups={{0,2,4,6},{1,3,5,7},{8,10,12,14},{9,11,13,15},{16,18,20,22},{17,19,21,2..., dimensions={0} | all-to-all | bytes 851968 | tf_op jit(solution)/shard_map/all_to_all | solution.py:401
  56.4 6.3 %all-gather.1 = f32[416,128]{1,0:T(8,128)S(1)} all-gather(f32[208,128]{1,0:T(8,128)S(1)} %reduce_sum.27), channel_id=3, replica_groups={{0,8},{1,9},{2,10},{3,11},{4,12},{5,13},{6,14},{7,15},{16,24},{17,25},{..., dimensions={0}, use_global_device_ids=true | all-gather | bytes 319488 | tf_op jit(solution)/shard_map/all_gather | solution.py:396
  62.7 9.5 %all_to_all.42.pieces = f32[4,328,128]{2,1,0:T(8,128)S(1)} all-to-all(f32[4,328,128]{2,1,0:T(8,128)S(1)} %shard_map.41), channel_id=1, replica_groups={{0,2,4,6},{1,3,5,7},{8,10,12,14},{9,11,13,15},{16,18,20,22},{17,19,21,2..., dimensions={0} | all-to-all | bytes 1343488 | tf_op jit(solution)/shard_map/all_to_all | solution.py:401
  72.2 7.5 %all-gather.2 = f32[1408,128]{1,0:T(8,128)S(1)} all-gather(f32[704,128]{1,0:T(8,128)S(1)} %shard_map.42), channel_id=4, replica_groups={{0,1},{2,3},{4,5},{6,7},{8,9},{10,11},{12,13},{14,15},{16,17},{18,19},{..., dimensions={0}, use_global_device_ids=true | all-gather | bytes 1081344 | tf_op jit(solution)/shard_map/all_gather | solution.py:396
  82.1 13.9 %all-gather.3 = f32[832,128]{1,0:T(8,128)S(1)} all-gather(f32[416,128]{1,0:T(8,128)S(1)} %get-tuple-element.33), channel_id=5, replica_groups={{0,16},{1,17},{2,18},{3,19},{4,20},{5,21},{6,22},{7,23},{8,24},{9,25},{..., dimensions={0}, use_global_device_ids=true | all-gather | bytes 638976 | tf_op jit(solution)/shard_map/all_gather | solution.py:396
  96.1 2.6 %shard_map.44 = (f32[288,128]{1,0:T(8,128)S(1)}, f32[288,128]{1,0:T(8,128)S(1)}, f32[4,288,128]{2,1,0:T(8,128)S(1)}) custom-call(f32[2,416,128]{2,1,0:T(8,128)S(1)} %bitcast.27, f32[416,128]{1,0:T(8,128)S(1)} %get-tuple-element.34.z_low, f32[2,704,128]{2,1,0:T(8,128)S(1)} %bitcast.26, f32[416,256]{1,0:T(8,128)S(1)} %get-tuple-element.32.rest, ...), custom_call_target="tpu_custom_call" | custom-call | flops 619708416 | bytes 2310144 | tf_op jit(solution)/shard_map/pallas_call | solution.py:365
  98.7 11.3 %all_to_all.43 = f32[4,288,128]{2,1,0:T(8,128)S(1)} all-to-all(f32[4,288,128]{2,1,0:T(8,128)S(1)} %get-tuple-element.36), channel_id=1, replica_groups={{0,2,4,6},{1,3,5,7},{8,10,12,14},{9,11,13,15},{16,18,20,22},{17,19,21,2..., dimensions={0} | all-to-all | bytes 1179648 | tf_op jit(solution)/shard_map/all_to_all | solution.py:401
  110.2 13.2 %all_to_all.44 = f32[8,40,128]{2,1,0:T(8,128)S(1)} all-to-all(f32[8,40,128]{2,1,0:T(8,128)S(1)} %pad_maximum_fusion.2), channel_id=1, replica_groups={{0,8,16,24,32,40,48,56},{1,9,17,25,33,41,49,57},{2,10,18,26,34,42,50,58..., dimensions={0} | all-to-all | bytes 327680 | tf_op jit(solution)/shard_map/all_to_all | solution.py:401
  123.5 11.8 %all_to_all.45 = f32[8,56,128]{2,1,0:T(8,128)S(1)} all-to-all(f32[8,56,128]{2,1,0:T(8,128)S(1)} %broadcast_in_dim.6), channel_id=1, replica_groups={{0,8,16,24,32,40,48,56},{1,9,17,25,33,41,49,57},{2,10,18,26,34,42,50,58..., dimensions={0} | all-to-all | bytes 458752 | tf_op jit(solution)/shard_map/all_to_all | solution.py:401
  135.5 11.1 %all_to_all.46.gathered = f32[4,408,128]{2,1,0:T(8,128)S(1)} all-to-all(f32[4,408,128]{2,1,0:T(8,128)S(1)} %broadcast_in_dim.7), channel_id=1, replica_groups={{0,2,4,6},{1,3,5,7},{8,10,12,14},{9,11,13,15},{16,18,20,22},{17,19,21,2..., dimensions={0} | all-to-all | bytes 1671168 | tf_op jit(solution)/shard_map/all_to_all | solution.py:401
  146.7 8.0 %all-gather.4 = f32[1600,128]{1,0:T(8,128)S(1)} all-gather(f32[800,128]{1,0:T(8,128)S(1)} %shard_map.45), channel_id=6, replica_groups={{0,1},{2,3},{4,5},{6,7},{8,9},{10,11},{12,13},{14,15},{16,17},{18,19},{..., dimensions={0}, use_global_device_ids=true | all-gather | bytes 1228800 | tf_op jit(solution)/shard_map/all_gather | solution.py:396
  157.0 9.8 %all-gather.5 = f32[336,128]{1,0:T(8,128)S(1)} all-gather(f32[168,128]{1,0:T(8,128)S(1)} %get-tuple-element.40), channel_id=7, replica_groups={{0,64},{32,96},{128,192},{160,224},{256,320},{288,352},{384,448},{416,4..., dimensions={0}, use_global_device_ids=true | all-gather | bytes 258048 | tf_op jit(solution)/shard_map/all_gather | solution.py:396
  166.8 9.1 %all_to_all.47.sib = f32[4,168,128]{2,1,0:T(8,128)S(1)} all-to-all(f32[4,168,128]{2,1,0:T(8,128)S(1)} %shard_map.47), channel_id=1, replica_groups={{0,2,4,6},{1,3,5,7},{8,10,12,14},{9,11,13,15},{16,18,20,22},{17,19,21,2..., dimensions={0} | all-to-all | bytes 688128 | tf_op jit(solution)/shard_map/all_to_all | solution.py:401
  175.9 3.9 %all-gather.6 = f32[768,128]{1,0:T(8,128)S(1)} all-gather(f32[384,128]{1,0:T(8,128)S(1)} %shard_map.48), channel_id=8, replica_groups={{0,1},{2,3},{4,5},{6,7},{8,9},{10,11},{12,13},{14,15},{16,17},{18,19},{..., dimensions={0}, use_global_device_ids=true | all-gather | bytes 589824 | tf_op jit(solution)/shard_map/all_gather | solution.py:396
  181.9 6.1 %all-gather.7 = f32[640,128]{1,0:T(8,128)S(1)} all-gather(f32[320,128]{1,0:T(8,128)S(1)} %get-tuple-element.41.own), channel_id=9, replica_groups={{0,128},{32,160},{64,192},{96,224},{256,384},{288,416},{320,448},{352,4..., dimensions={0}, use_global_device_ids=true | all-gather | bytes 491520 | tf_op jit(solution)/shard_map/all_gather | solution.py:396
  188.0 2.8 %all-gather.8 = f32[512,128]{1,0:T(8,128)S(1)} all-gather(f32[256,128]{1,0:T(8,128)S(1)} %shard_map.50), channel_id=10, replica_groups={{0,1},{2,3},{4,5},{6,7},{8,9},{10,11},{12,13},{14,15},{16,17},{18,19},{..., dimensions={0}, use_global_device_ids=true | all-gather | bytes 393216 | tf_op jit(solution)/shard_map/all_gather | solution.py:396
  192.8 5.1 %all-gather.9 = f32[192,128]{1,0:T(8,128)S(1)} all-gather(f32[96,128]{1,0:T(8,128)S(1)} %get-tuple-element.42), channel_id=11, replica_groups={{0,256},{32,288},{64,320},{96,352},{128,384},{160,416},{192,448},{224,4..., dimensions={0}, use_global_device_ids=true | all-gather | bytes 147456 | tf_op jit(solution)/shard_map/all_gather | solution.py:396
  197.9 3.4 %all-gather.10 = f32[1344,128]{1,0:T(8,128)S(1)} all-gather(f32[672,128]{1,0:T(8,128)S(1)} %pad_maximum_fusion), channel_id=12, replica_groups={{0,1},{2,3},{4,5},{6,7},{8,9},{10,11},{12,13},{14,15},{16,17},{18,19},{..., dimensions={0}, use_global_device_ids=true | all-gather | bytes 1032192 | tf_op jit(solution)/shard_map/all_gather | solution.py:396
  201.4 2.9 %shard_map.52 = f32[64,128]{1,0:T(8,128)} custom-call(f32[2,672,128]{2,1,0:T(8,128)S(1)} %bitcast.30, f32[576,128]{1,0:T(8,128)S(1)} %get-tuple-element.46.carried), custom_call_target="tpu_custom_call" | custom-call | flops 364904448 | bytes 983040 | tf_op jit(solution)/shard_map/pallas_call | solution.py:365
  (35 shorter events, 16.3 us)
Async XLA Ops:
  2.8 11.3 %collective-permute-start = (f32[2112,128]{1,0:T(8,128)}, f32[2112,128]{1,0:T(8,128)S(1)}, u32[]{:S(2)}, u32[]{:S(2)}) collective-permute-start(f32[2112,128]{1,0:T(8,128)} %shard_map.37.mine), channel_id=1, source_target_pairs={{0,1},{1,0},{2,3},{3,2},{4,5},{5,4},{6,7},{7,6},{8,9},{9,8},{10,11... | collective-permute-start | bytes 3244040 | tf_op jit(solution)/shard_map/ppermute | solution.py:391
  14.1 1.2 copy-start
  98.7 11.4 %copy-start.1 = (pred[128]{0:T(512)(128)(4,1)S(1)}, pred[128]{0:T(512)(128)(4,1)}, u32[]{:S(2)}) copy-start(pred[128]{0:T(512)(128)(4,1)} %constant.4.clone.1) | copy-start | bytes 388

commit v7 on v6

--- a/solution.py
+++ b/solution.py
@@ -8,7 +8,6 @@
 from jax.sharding import PartitionSpec as P
 
 VMEM_BYTES = 40 * 2**20
-ALL_VMEM_BYTES = 62_000_000
 
 
 def split(value):
@@ -28,18 +27,19 @@
     return dot_split(split(a), split(b))
 
 
-def solve_own(gram_own, gram_sib, proj_own, proj_sib):
-    power = kdot(gram_own, gram_sib)
-    right = proj_sib - kdot(proj_own, gram_sib)
-    total = jnp.eye(power.shape[0], dtype=jnp.float32) + power
-    for step in range(5):
+def inverse_of(error):
+    total = jnp.eye(error.shape[0], dtype=jnp.float32) + error
+    power = error
+    for step in range(6):
         parts = split(power)
         power = dot_split(parts, parts)
         total = total + kdot(total, power)
-    parts = split(power)
-    power = dot_split(parts, parts)
-    right = kdot(right, total)
-    return right + kdot(right, power)
+    return total
+
+
+def solve_own(gram_own, gram_sib, proj_own, proj_sib):
+    inverse = inverse_of(kdot(gram_own, gram_sib))
+    return kdot(proj_sib - kdot(proj_own, gram_sib), inverse)
 
 
 def solve_node(own, sib, ops_own, ops_sib, sums):
@@ -78,76 +78,49 @@
     return pl.multiple_of(value * rows, 8)
 
 
-def pack_kernel(u, v, y, pack, u_held, sems):
+def first_pair_kernel(u, u_other, v, v_other, held, low, up, next_v, top_v):
     levels, _, rank = u.shape
-    first = levels * rank + y.shape[0]
-    copies = [pltpu.make_async_copy(u.at[j], u_held.at[j], sems.at[j]) for j in range(levels)]
-    copies.append(
-        pltpu.make_async_copy(y, pack.at[pl.ds(levels * rank, y.shape[0])], sems.at[levels])
-    )
-    for j in range(levels):
-        rows = pl.ds(first + j * rank, rank)
-        copies.append(pltpu.make_async_copy(v.at[j], pack.at[rows], sems.at[levels + 1 + j]))
-    for copy in copies:
-        copy.start()
-    for j in range(levels):
-        copies[j].wait()
-        pack[j * rank : (j + 1) * rank] = u_held[j].T
-    for copy in copies[levels:]:
-        copy.wait()
-
-
-def first_pair_kernel(levels, mine, other, held, sent, next_v, top_v):
-    rank = mine.shape[1]
-    half = rank // 2
-    core = bit_of("gy", 0)
-    first = mine.shape[0] - levels * rank
-    last = first - levels * rank
-    held[: 2 * rank, :rank] = mine[: 2 * rank]
-    held[: 2 * rank, rank:] = other[: 2 * rank]
-    for j in range(2, levels + 1):
-        n = half if j < levels else last // 2
-        at = pl.ds(j * rank + times8(core, n), n)
-        to = slice(2 * rank + (j - 2) * half, 2 * rank + (j - 2) * half + n)
-        held[to, :rank] = mine[at]
-        held[to, rank:] = other[at]
+    half = rank // 2
+    first = bit_of("gy", 0) == 0
+    last = (v.shape[0] - levels * rank) // 2
+    lanes = (slice(0, rank), slice(rank, 2 * rank))
+    for lane, w in zip(lanes, (u, u_other)):
+        for j in range(levels):
+            value = w[j].T
+            if j < 2:
+                held[j * rank : (j + 1) * rank, lane] = value
+            else:
+                at = 2 * rank + (j - 2) * half
+                held[at : at + half, lane] = jnp.where(first, value[:half], value[half:])
+    rows = pl.ds(levels * rank + times8(bit_of("gy", 0), last), last)
+    for lane, ref in zip(lanes, (v, v_other)):
+        held[held.shape[0] - last :, lane] = ref[rows]
     factors = [
-        jnp.concatenate(
-            [ref[first + j * rank : first + (j + 1) * rank] for ref in (mine, other)], axis=0
-        )
+        jnp.concatenate([ref[j * rank : (j + 1) * rank] for ref in (v, v_other)], axis=0)
         for j in range(levels)
     ]
     parts = split(held[...])
-    rows = held.shape[0]
-    for j in range(2):
-        value = dot_split(parts, split(factors[j]))
-        sent[0, j * rows : (j + 1) * rows] = value
-        sent[1, j * rows : (j + 1) * rows] = value
+    low[...] = dot_split(parts, split(factors[0]))
+    up[...] = dot_split(parts, split(factors[1]))
     for j in range(2, 4):
         next_v[j - 2] = factors[j]
     for j in range(4, levels):
         top_v[j - 4] = factors[j]
 
 
-def first_node_kernel(bit, top, pieces, z_out, node_out):
+def first_node_kernel(bit, pair, up, z_out, out):
     side = bit_of("gy", bit)
-    rank = z_out.shape[1]
-    ops = slice(top, top + rank)
-    z, node = solve_node(
-        pieces[side, :top],
-        pieces[1 - side, :top],
-        pieces[side, ops],
-        pieces[1 - side, ops],
-        pieces[0, top + rank :] + pieces[1, top + rank :],
-    )
+    rank = up.shape[1]
+    own, sib = pair[side], pair[1 - side]
+    z = solve_own(own[:rank], sib[:rank], own[rank:], sib[rank:])
     z_out[...] = z
-    node_out[...] = node
-
-
-def after_pair(bit, pair, z_low, held):
-    side = bit_of("gy", bit)
-    rank = pair.shape[2]
-    own, sib = pair[side], pair[1 - side]
+    value = up[rank:] - kdot(z, up[:rank])
+    for i in range(out.shape[0]):
+        out[i] = value
+
+
+def after_pair(own, sib, z_low, held):
+    rank = own.shape[1]
     z_up = solve_own(own[:rank], sib[:rank], own[rank:], sib[rank:])
     left = held[:rank]
     next_left = held[rank : 2 * rank] - kdot(z_low[:rank], left)
@@ -155,8 +128,10 @@
     return held[2 * rank :] - kdot(z_both, jnp.concatenate([left, next_left], axis=0))
 
 
-def between_kernel(bit, shares, pair, z_low, held, v, rest, sent):
-    value = after_pair(bit, pair, z_low, held)
+def between_kernel(bit, shares, parts, z_low, held, v, rest, sent):
+    side = bit_of("gy", bit)
+    own, sib = [parts[2 * c] + parts[2 * c + 1] for c in (side, 1 - side)]
+    value = after_pair(own, sib, z_low, held)
     rest[...] = value
     rows = value.shape[0]
     half = v.shape[2] // 2
@@ -233,7 +208,8 @@
         [factors[0][:half], factors[1][:half], factors[0][half:], factors[1][half:], rest[rank:]],
         axis=0,
     )
-    value = after_pair(bit, pair, z_low, held)
+    side = bit_of("gy", bit)
+    value = after_pair(pair[side], pair[1 - side], z_low, held)
     mine[...] = value[:, :rank]
     other[...] = value[:, rank:]
     count, width = v.shape[0], value.shape[0]
@@ -360,18 +336,17 @@
     out[...] = updated(value, z)
 
 
-def call(kernel, outs, *args, vmem_bytes=VMEM_BYTES, **options):
+def call(kernel, outs, *args):
     rows = sum(a.size // 128 for a in args)
     return pl.pallas_call(
         kernel,
         out_shape=[jax.ShapeDtypeStruct(o, jnp.float32) for o in outs],
-        compiler_params=pltpu.CompilerParams(vmem_limit_bytes=vmem_bytes),
+        compiler_params=pltpu.CompilerParams(vmem_limit_bytes=VMEM_BYTES),
         cost_estimate=pl.CostEstimate(
             flops=6 * 128 * 128 * (rows + 14 * 128),
             bytes_accessed=512 * rows,
             transcendentals=0,
         ),
-        **options,
     )(*args)
 
 
@@ -418,37 +393,28 @@
     half = rank // 2
     near_chips = [1, 2]
 
-    all_rows = levels * rank + right_sides.shape[1]
-    pack = call(
-        pack_kernel,
-        [(all_rows + levels * rank, rank)],
-        factor_u,
-        factor_v,
-        right_sides.T,
-        vmem_bytes=ALL_VMEM_BYTES,
-        in_specs=[pl.BlockSpec(memory_space=pltpu.HBM)] * 3,
-        scratch_shapes=[
-            pltpu.VMEM(factor_u.shape, jnp.float32),
-            pltpu.SemaphoreType.DMA((2 * levels + 1,)),
-        ],
-    )[0]
-    rest = (all_rows - 2 * rank) // 2
+    factors = jnp.concatenate([factor_v.reshape(-1, rank), right_sides.T], axis=0)
+    rest = ((levels - 2) * rank + right_sides.shape[1]) // 2
     rows = 2 * rank + rest
-    held, sent, next_v, top_v = call(
-        functools.partial(first_pair_kernel, levels),
+    held, low, up, next_v, top_v = call(
+        first_pair_kernel,
         [
             (rows, 2 * rank),
-            (2, 2 * rows, rank),
+            (rows, rank),
+            (rows, rank),
             (2, 2 * rank, rank),
             (levels - 4, 2 * rank, rank),
         ],
-        pack,
-        swap_cores(pack),
+        factor_u,
+        swap_cores(factor_u),
+        factors,
+        swap_cores(factors),
     )
     z_low, node = call(
-        functools.partial(first_node_kernel, 1, rows),
-        [(rank + rest, rank), (rank + rest, rank)],
-        exchange(sent, "gy", [1]),
+        functools.partial(first_node_kernel, 1),
+        [(rank + rest, rank), (4, rank + rest, rank)],
+        pair_gather(low, "gy", 1),
+        up,
     )
 
     rows = rest
@@ -457,7 +423,7 @@
     held, sent = call(
         functools.partial(between_kernel, 2, 4),
         [(rows, 2 * rank), (4, n_both + n_sums, rank)],
-        pair_gather(node, "gy", 2),
+        exchange(node, "gy", near_chips),
         z_low,
         held,
         next_v,

time: 205 us -> 202 us (0.985)
  Pallas kernels: 23.1 us -> 19.5 us
    pallas_call x16 -> x15, Pallas kernels: 23.1 us -> 19.5 us  [call(): pl.pallas_call(kernel, out_shape=[jax.ShapeDtypeStruct(o, jnp.float32) fo...]
    ppermute x1 -> x2, starting transfers between devices: 8.79 us -> 10.7 us  [swap_cores(): lax.ppermute(value, 'gy', [(s, s ^ 1) for s in range(lax.axis_size('gy'))])]
  transfers between devices with their start and end apart: 1 -> 2, of which waited for: 1 -> 1; matrix products, arithmetic and copies ran while one was open for 0% -> 0% of each run, Pallas kernels for 0% -> 0%
where the time goes in v7:
time: 202 us
  blocking collectives  168 us (83%)
  Pallas kernels  19.5 us (10%)
  starting transfers between devices  10.7 us (5%)
    all_to_all x8, blocking collectives, exchange(): lax.all_to_all(value, axis, 0, 0, axis_index_groups=bit_groups(count, bits))  91.6 us
    all_gather x11, blocking collectives, pair_gather(): return lax.all_gather(value, axis, axis_index_groups=groups, tiled=tiled)  76.3 us
    pallas_call x15, Pallas kernels, call(): pl.pallas_call(kernel, out_shape=[jax.ShapeDtypeStruct(o, jnp.float32) fo...  19.5 us
    ppermute x2, starting transfers between devices, swap_cores(): lax.ppermute(value, 'gy', [(s, s ^ 1) for s in range(lax.axis_size('gy'))])  10.7 us
  transfers between devices with their start and end apart: 2, of which 1 were waited for; matrix products, arithmetic and copies ran while one was open for 0% of the time, Pallas kernels for 0%

profile of v7, /device:TPU:1, one launch (start us, length us, event | category | flops | bytes accessed | tf_op | source)
XLA Modules:
  0.0 201.7 jit_solution(5852526790610467287)
XLA Ops:
  1.2 8.8 %collective-permute-start.1 = (f32[1088,128]{1,0:T(8,128)S(1)}, f32[1088,128]{1,0:T(8,128)S(1)}, u32[]{:S(2)}, u32[]{:S(2)}) collective-permute-start(f32[1088,128]{1,0:T(8,128)S(1)} %pad_maximum_fusion.v), channel_id=1, source_target_pairs={{0,1},{1,0},{2,3},{3,2},{4,5},{5,4},{6,7},{7,6},{8,9},{9,8},{10,11... | collective-permute-start | bytes 1671176 | tf_op jit(solution)/shard_map/ppermute | solution.py:366
  14.7 10.2 %all-gather = f32[1344,128]{1,0:T(8,128)S(1)} all-gather(f32[672,128]{1,0:T(8,128)S(1)} %get-tuple-element.27), channel_id=2, replica_groups={{0,2},{1,3},{4,6},{5,7},{8,10},{9,11},{12,14},{13,15},{16,18},{17,19},{..., dimensions={0}, use_global_device_ids=true | all-gather | bytes 1032192 | tf_op jit(solution)/shard_map/all_gather | solution.py:371
  27.0 16.3 %all_to_all.40.parts = f32[4,544,128]{2,1,0:T(8,128)S(1)} all-to-all(f32[4,544,128]{2,1,0:T(8,128)S(1)} %get-tuple-element.29), channel_id=1, replica_groups={{0,2,4,6},{1,3,5,7},{8,10,12,14},{9,11,13,15},{16,18,20,22},{17,19,21,2..., dimensions={0} | all-to-all | bytes 2228224 | tf_op jit(solution)/shard_map/all_to_all | solution.py:376
  43.3 2.4 %shard_map.39 = (f32[416,256]{1,0:T(8,128)S(1)}, f32[4,208,128]{2,1,0:T(8,128)S(1)}) custom-call(f32[4,544,128]{2,1,0:T(8,128)S(1)} %all_to_all.40.parts, f32[544,128]{1,0:T(8,128)S(1)} %get-tuple-element.30.z_low, f32[672,256]{1,0:T(8,128)S(1)} %get-tuple-element.31.held, f32[2,256,128]{2,1,0:T(8,128)S(1)} %get-tuple-element.32.v), custom_call_target="tpu_custom_call" | custom-call | flops 625999872 | bytes 2342912 | tf_op jit(solution)/shard_map/pallas_call | solution.py:341
  45.8 8.1 %all_to_all.41 = f32[4,208,128]{2,1,0:T(8,128)S(1)} all-to-all(f32[4,208,128]{2,1,0:T(8,128)S(1)} %get-tuple-element.33), channel_id=1, replica_groups={{0,2,4,6},{1,3,5,7},{8,10,12,14},{9,11,13,15},{16,18,20,22},{17,19,21,2..., dimensions={0} | all-to-all | bytes 851968 | tf_op jit(solution)/shard_map/all_to_all | solution.py:376
  53.9 6.3 %all-gather.1 = f32[416,128]{1,0:T(8,128)S(1)} all-gather(f32[208,128]{1,0:T(8,128)S(1)} %reduce_sum.27), channel_id=3, replica_groups={{0,8},{1,9},{2,10},{3,11},{4,12},{5,13},{6,14},{7,15},{16,24},{17,25},{..., dimensions={0}, use_global_device_ids=true | all-gather | bytes 319488 | tf_op jit(solution)/shard_map/all_gather | solution.py:371
  60.2 9.5 %all_to_all.42.pieces = f32[4,328,128]{2,1,0:T(8,128)S(1)} all-to-all(f32[4,328,128]{2,1,0:T(8,128)S(1)} %shard_map.40), channel_id=1, replica_groups={{0,2,4,6},{1,3,5,7},{8,10,12,14},{9,11,13,15},{16,18,20,22},{17,19,21,2..., dimensions={0} | all-to-all | bytes 1343488 | tf_op jit(solution)/shard_map/all_to_all | solution.py:376
  69.7 7.4 %all-gather.2 = f32[1408,128]{1,0:T(8,128)S(1)} all-gather(f32[704,128]{1,0:T(8,128)S(1)} %shard_map.41), channel_id=4, replica_groups={{0,1},{2,3},{4,5},{6,7},{8,9},{10,11},{12,13},{14,15},{16,17},{18,19},{..., dimensions={0}, use_global_device_ids=true | all-gather | bytes 1081344 | tf_op jit(solution)/shard_map/all_gather | solution.py:371
  77.1 2.3 %shard_map.42 = (f32[416,128]{1,0:T(8,128)S(1)}, f32[416,128]{1,0:T(8,128)S(1)}) custom-call(f32[4,328,128]{2,1,0:T(8,128)S(1)} %all_to_all.42.pieces, f32[2,704,128]{2,1,0:T(8,128)S(1)} %bitcast.26), custom_call_target="tpu_custom_call" | custom-call | flops 443547648 | bytes 1392640 | tf_op jit(solution)/shard_map/pallas_call | solution.py:341
  79.4 14.9 %all-gather.3 = f32[832,128]{1,0:T(8,128)S(1)} all-gather(f32[416,128]{1,0:T(8,128)S(1)} %get-tuple-element.35), channel_id=5, replica_groups={{0,16},{1,17},{2,18},{3,19},{4,20},{5,21},{6,22},{7,23},{8,24},{9,25},{..., dimensions={0}, use_global_device_ids=true | all-gather | bytes 638976 | tf_op jit(solution)/shard_map/all_gather | solution.py:371
  94.3 2.5 %shard_map.43 = (f32[288,128]{1,0:T(8,128)S(1)}, f32[288,128]{1,0:T(8,128)S(1)}, f32[4,288,128]{2,1,0:T(8,128)S(1)}) custom-call(f32[2,416,128]{2,1,0:T(8,128)S(1)} %bitcast.28, f32[416,128]{1,0:T(8,128)S(1)} %get-tuple-element.36.z_low, f32[2,704,128]{2,1,0:T(8,128)S(1)} %bitcast.27, f32[416,256]{1,0:T(8,128)S(1)} %get-tuple-element.34.rest, ...), custom_call_target="tpu_custom_call" | custom-call | flops 619708416 | bytes 2310144 | tf_op jit(solution)/shard_map/pallas_call | solution.py:341
  96.8 10.9 %all_to_all.43 = f32[4,288,128]{2,1,0:T(8,128)S(1)} all-to-all(f32[4,288,128]{2,1,0:T(8,128)S(1)} %get-tuple-element.38), channel_id=1, replica_groups={{0,2,4,6},{1,3,5,7},{8,10,12,14},{9,11,13,15},{16,18,20,22},{17,19,21,2..., dimensions={0} | all-to-all | bytes 1179648 | tf_op jit(solution)/shard_map/all_to_all | solution.py:376
  107.9 14.5 %all_to_all.44 = f32[8,40,128]{2,1,0:T(8,128)S(1)} all-to-all(f32[8,40,128]{2,1,0:T(8,128)S(1)} %pad_maximum_fusion.3), channel_id=1, replica_groups={{0,8,16,24,32,40,48,56},{1,9,17,25,33,41,49,57},{2,10,18,26,34,42,50,58..., dimensions={0} | all-to-all | bytes 327680 | tf_op jit(solution)/shard_map/all_to_all | solution.py:376
  122.4 11.7 %all_to_all.45 = f32[8,56,128]{2,1,0:T(8,128)S(1)} all-to-all(f32[8,56,128]{2,1,0:T(8,128)S(1)} %broadcast_in_dim.6), channel_id=1, replica_groups={{0,8,16,24,32,40,48,56},{1,9,17,25,33,41,49,57},{2,10,18,26,34,42,50,58..., dimensions={0} | all-to-all | bytes 458752 | tf_op jit(solution)/shard_map/all_to_all | solution.py:376
  134.2 11.4 %all_to_all.46.gathered = f32[4,408,128]{2,1,0:T(8,128)S(1)} all-to-all(f32[4,408,128]{2,1,0:T(8,128)S(1)} %broadcast_in_dim.7), channel_id=1, replica_groups={{0,2,4,6},{1,3,5,7},{8,10,12,14},{9,11,13,15},{16,18,20,22},{17,19,21,2..., dimensions={0} | all-to-all | bytes 1671168 | tf_op jit(solution)/shard_map/all_to_all | solution.py:376
  145.6 7.7 %all-gather.4 = f32[1600,128]{1,0:T(8,128)S(1)} all-gather(f32[800,128]{1,0:T(8,128)S(1)} %shard_map.44), channel_id=6, replica_groups={{0,1},{2,3},{4,5},{6,7},{8,9},{10,11},{12,13},{14,15},{16,17},{18,19},{..., dimensions={0}, use_global_device_ids=true | all-gather | bytes 1228800 | tf_op jit(solution)/shard_map/all_gather | solution.py:371
  155.6 8.4 %all-gather.5 = f32[336,128]{1,0:T(8,128)S(1)} all-gather(f32[168,128]{1,0:T(8,128)S(1)} %get-tuple-element.42), channel_id=7, replica_groups={{0,64},{32,96},{128,192},{160,224},{256,320},{288,352},{384,448},{416,4..., dimensions={0}, use_global_device_ids=true | all-gather | bytes 258048 | tf_op jit(solution)/shard_map/all_gather | solution.py:371
  164.0 9.3 %all_to_all.47.sib = f32[4,168,128]{2,1,0:T(8,128)S(1)} all-to-all(f32[4,168,128]{2,1,0:T(8,128)S(1)} %shard_map.46), channel_id=1, replica_groups={{0,2,4,6},{1,3,5,7},{8,10,12,14},{9,11,13,15},{16,18,20,22},{17,19,21,2..., dimensions={0} | all-to-all | bytes 688128 | tf_op jit(solution)/shard_map/all_to_all | solution.py:376
  173.3 3.9 %all-gather.6 = f32[768,128]{1,0:T(8,128)S(1)} all-gather(f32[384,128]{1,0:T(8,128)S(1)} %shard_map.47), channel_id=8, replica_groups={{0,1},{2,3},{4,5},{6,7},{8,9},{10,11},{12,13},{14,15},{16,17},{18,19},{..., dimensions={0}, use_global_device_ids=true | all-gather | bytes 589824 | tf_op jit(solution)/shard_map/all_gather | solution.py:371
  179.3 6.1 %all-gather.7 = f32[640,128]{1,0:T(8,128)S(1)} all-gather(f32[320,128]{1,0:T(8,128)S(1)} %get-tuple-element.43.own), channel_id=9, replica_groups={{0,128},{32,160},{64,192},{96,224},{256,384},{288,416},{320,448},{352,4..., dimensions={0}, use_global_device_ids=true | all-gather | bytes 491520 | tf_op jit(solution)/shard_map/all_gather | solution.py:371
  185.4 2.8 %all-gather.8 = f32[512,128]{1,0:T(8,128)S(1)} all-gather(f32[256,128]{1,0:T(8,128)S(1)} %shard_map.49), channel_id=10, replica_groups={{0,1},{2,3},{4,5},{6,7},{8,9},{10,11},{12,13},{14,15},{16,17},{18,19},{..., dimensions={0}, use_global_device_ids=true | all-gather | bytes 393216 | tf_op jit(solution)/shard_map/all_gather | solution.py:371
  190.2 5.1 %all-gather.9 = f32[192,128]{1,0:T(8,128)S(1)} all-gather(f32[96,128]{1,0:T(8,128)S(1)} %get-tuple-element.44), channel_id=11, replica_groups={{0,256},{32,288},{64,320},{96,352},{128,384},{160,416},{192,448},{224,4..., dimensions={0}, use_global_device_ids=true | all-gather | bytes 147456 | tf_op jit(solution)/shard_map/all_gather | solution.py:371
  195.4 3.4 %all-gather.10 = f32[1344,128]{1,0:T(8,128)S(1)} all-gather(f32[672,128]{1,0:T(8,128)S(1)} %pad_maximum_fusion.1), channel_id=12, replica_groups={{0,1},{2,3},{4,5},{6,7},{8,9},{10,11},{12,13},{14,15},{16,17},{18,19},{..., dimensions={0}, use_global_device_ids=true | all-gather | bytes 1032192 | tf_op jit(solution)/shard_map/all_gather | solution.py:371
  198.8 2.9 %shard_map.51 = f32[64,128]{1,0:T(8,128)} custom-call(f32[2,672,128]{2,1,0:T(8,128)S(1)} %bitcast.32, f32[576,128]{1,0:T(8,128)S(1)} %get-tuple-element.48.carried), custom_call_target="tpu_custom_call" | custom-call | flops 364904448 | bytes 983040 | tf_op jit(solution)/shard_map/pallas_call | solution.py:341
  (37 shorter events, 14.7 us)
Async XLA Ops:
  0.0 10.0 %copy-start = (f32[8,128,128]{2,1,0:T(8,128)S(1)}, f32[8,128,128]{2,1,0:T(8,128)}, u32[]{:S(2)}) copy-start(f32[8,128,128]{2,1,0:T(8,128)} %u.1) | copy-start | bytes 1572868
  1.2 12.6 %collective-permute-start.1 = (f32[1088,128]{1,0:T(8,128)S(1)}, f32[1088,128]{1,0:T(8,128)S(1)}, u32[]{:S(2)}, u32[]{:S(2)}) collective-permute-start(f32[1088,128]{1,0:T(8,128)S(1)} %pad_maximum_fusion.v), channel_id=1, source_target_pairs={{0,1},{1,0},{2,3},{3,2},{4,5},{5,4},{6,7},{7,6},{8,9},{9,8},{10,11... | collective-permute-start | bytes 1671176 | tf_op jit(solution)/shard_map/ppermute | solution.py:366
  10.0 3.8 %collective-permute-start = (f32[8,128,128]{2,1,0:T(8,128)S(1)}, f32[8,128,128]{2,1,0:T(8,128)S(1)}, u32[]{:S(2)}, u32[]{:S(2)}) collective-permute-start(f32[8,128,128]{2,1,0:T(8,128)S(1)} %copy-done), channel_id=1, source_target_pairs={{0,1},{1,0},{2,3},{3,2},{4,5},{5,4},{6,7},{7,6},{8,9},{9,8},{10,11... | collective-permute-start | bytes 1572872 | tf_op jit(solution)/shard_map/ppermute | solution.py:366
  96.8 11.0 %copy-start.1 = (pred[128]{0:T(512)(128)(4,1)S(1)}, pred[128]{0:T(512)(128)(4,1)}, u32[]{:S(2)}) copy-start(pred[128]{0:T(512)(128)(4,1)} %constant.4.clone.1) | copy-start | bytes 388

commit v8 on v7

--- a/solution.py
+++ b/solution.py
@@ -45,15 +45,16 @@
 def solve_node(own, sib, ops_own, ops_sib, sums):
     rank = own.shape[1]
     width = own.shape[0] - rank
-    gram_own, proj_own = own[:rank], own[rank:]
-    z = solve_own(gram_own, sib[:rank], proj_own, sib[rank:])
-    z_sib = proj_own - kdot(z, gram_own)
-    z_both = split(jnp.concatenate([z, z_sib], axis=1))
-    node = []
+    gram_own, proj_own = split(own[:rank]), split(own[rank:])
+    base, lefts = [], []
     for j in range(ops_own.shape[0] // rank):
         at = slice(j * rank, (j + 1) * rank)
-        left = split(jnp.concatenate([ops_own[at], ops_sib[at]], axis=0))
-        node.append(sums[j * width : (j + 1) * width] - dot_split(z_both, left))
+        op_sib = split(ops_sib[at])
+        base.append(sums[j * width : (j + 1) * width] - dot_split(proj_own, op_sib))
+        lefts.append(split(ops_own[at] - dot_split(gram_own, op_sib)))
+    z = solve_own(own[:rank], sib[:rank], own[rank:], sib[rank:])
+    parts = split(z)
+    node = [b - dot_split(parts, left) for b, left in zip(base, lefts)]
     return z, jnp.concatenate(node, axis=0)
 
 
@@ -78,26 +79,25 @@
     return pl.multiple_of(value * rows, 8)
 
 
-def first_pair_kernel(u, u_other, v, v_other, held, low, up, next_v, top_v):
-    levels, _, rank = u.shape
+def first_pair_kernel(levels, mine, other, held, low, up, next_v, top_v):
+    rank = mine.shape[1]
     half = rank // 2
-    first = bit_of("gy", 0) == 0
-    last = (v.shape[0] - levels * rank) // 2
-    lanes = (slice(0, rank), slice(rank, 2 * rank))
-    for lane, w in zip(lanes, (u, u_other)):
+    core = bit_of("gy", 0)
+    last = (mine.shape[0] - 2 * levels * rank) // 2
+    rows = pl.ds(2 * levels * rank + times8(core, last), last)
+    for c, ref in enumerate((mine, other)):
+        lane = slice(c * rank, (c + 1) * rank)
         for j in range(levels):
-            value = w[j].T
+            value = ref[j * rank : (j + 1) * rank].T
             if j < 2:
                 held[j * rank : (j + 1) * rank, lane] = value
             else:
                 at = 2 * rank + (j - 2) * half
-                held[at : at + half, lane] = jnp.where(first, value[:half], value[half:])
-    rows = pl.ds(levels * rank + times8(bit_of("gy", 0), last), last)
-    for lane, ref in zip(lanes, (v, v_other)):
+                held[at : at + half, lane] = jnp.where(core == 0, value[:half], value[half:])
         held[held.shape[0] - last :, lane] = ref[rows]
     factors = [
-        jnp.concatenate([ref[j * rank : (j + 1) * rank] for ref in (v, v_other)], axis=0)
-        for j in range(levels)
+        jnp.concatenate([ref[j * rank : (j + 1) * rank] for ref in (mine, other)], axis=0)
+        for j in range(levels, 2 * levels)
     ]
     parts = split(held[...])
     low[...] = dot_split(parts, split(factors[0]))
@@ -289,21 +289,21 @@
         out[i] = value
 
 
-def upper_shared_kernel(count, bit, own, sib, out):
+def quarter_shared_kernel(count, own, sib, z, out):
     half = out.shape[1] // 2
     width = own.shape[0] // count
-    value = sib[...].reshape(own.shape) if bit is None else sib[1 - bit_of("gx", bit)]
+    value = sib[...].reshape(own.shape)
     for j in range(count):
         at = slice(j * width, j * width + half)
         out[j * half : (j + 1) * half] = own[at]
         out[(count + j) * half : (count + j + 1) * half] = value[at]
-
-
-def upper_node_kernel(count, bit, own, sib, shared, z_out, node_out):
+    out[2 * count * half :] = z[...]
+
+
+def quarter_node_kernel(count, own, sib, shared, carried, z_out, node_out, new):
     half = own.shape[1] // 2
     width = own.shape[0] // count
-    here = own[...]
-    there = sib[...].reshape(own.shape) if bit is None else sib[1 - bit_of("gx", bit)]
+    here, there = own[...], sib[...].reshape(own.shape)
     rows_own, ops_own = child_rows(shared, 0, half, count, here[half:width])
     rows_sib, ops_sib = child_rows(shared, half * count, half, count, there[half:width])
     sums = jnp.concatenate(
@@ -316,24 +316,46 @@
     z, node = solve_node(rows_own, rows_sib, ops_own, ops_sib, sums)
     z_out[...] = z
     node_out[...] = node
-
-
-def last_kernel(bit, sizes, gathered, carried, out):
+    below = both_cores(shared, 2 * count * half, shared.shape[1] - 2 * count * half)
+    new[...] = updated(carried, interleaved(*below, half))
+
+
+def whole_shared_kernel(bit, own, pair, z, out):
+    rows = own.shape[0]
+    out[:rows] = own[...]
+    out[rows : 2 * rows] = pair[1 - bit_of("gx", bit)]
+    out[2 * rows :] = z[...]
+
+
+def whole_node_kernel(count, rows, shared, carried, node_out, new):
+    half = carried.shape[1] // 2
+    rank = 2 * half
+    width = rows // count
+
+    def child(at):
+        return [
+            interleaved(*both_cores(shared, at + j * width, width), half) for j in range(count)
+        ]
+
+    own, sib = child(0), child(rows)
+    z, node = solve_node(
+        own[0],
+        sib[0],
+        jnp.concatenate([v[:rank] for v in own[1:]], axis=0),
+        jnp.concatenate([v[:rank] for v in sib[1:]], axis=0),
+        jnp.concatenate([v[rank:] + w[rank:] for v, w in zip(own[1:], sib[1:])], axis=0),
+    )
+    node_out[...] = node
+    below = both_cores(shared, 2 * rows, shared.shape[1] - 2 * rows)
+    new[...] = updated(updated(carried, interleaved(*below, half)), z)
+
+
+def last_kernel(bit, pair, carried, out):
+    side = bit_of("gx", bit)
     rank = carried.shape[1]
-    half = rank // 2
-    side = bit_of("gx", bit)
-    n = half + out.shape[0] // 2
-
-    def child(which):
-        return interleaved(*both_cores(gathered, times8(which, n), n), half)
-
-    value, at = carried[...], 2 * n
-    for size in sizes:
-        value = updated(value, interleaved(*both_cores(gathered, at, size), half))
-        at += size
-    own, sib = child(side), child(1 - side)
+    own, sib = pair[side], pair[1 - side]
     z = solve_own(own[:rank], sib[:rank], own[rank:], sib[rank:])
-    out[...] = updated(value, z)
+    out[...] = updated(carried, z)
 
 
 def call(kernel, outs, *args):
@@ -376,28 +398,18 @@
     return lax.all_to_all(value, axis, 0, 0, axis_index_groups=bit_groups(count, bits))
 
 
-def to_all(value, axis, bits):
-    return exchange(jnp.broadcast_to(value, (1 << len(bits),) + value.shape), axis, bits)
-
-
-def pad_rows(value, rows):
-    return jnp.pad(value, ((0, rows - value.shape[0]), (0, 0)))
-
-
-def up8(value):
-    return -(-value // 8) * 8
-
-
 def shards(right_sides, factor_u, factor_v):
     levels, _, rank = factor_u.shape
     half = rank // 2
     near_chips = [1, 2]
 
-    factors = jnp.concatenate([factor_v.reshape(-1, rank), right_sides.T], axis=0)
+    packed = jnp.concatenate(
+        [factor_u.reshape(-1, rank), factor_v.reshape(-1, rank), right_sides.T], axis=0
+    )
     rest = ((levels - 2) * rank + right_sides.shape[1]) // 2
     rows = 2 * rank + rest
     held, low, up, next_v, top_v = call(
-        first_pair_kernel,
+        functools.partial(first_pair_kernel, levels),
         [
             (rows, 2 * rank),
             (rows, rank),
@@ -405,10 +417,8 @@
             (2, 2 * rank, rank),
             (levels - 4, 2 * rank, rank),
         ],
-        factor_u,
-        swap_cores(factor_u),
-        factors,
-        swap_cores(factors),
+        packed,
+        swap_cores(packed),
     )
     z_low, node = call(
         functools.partial(first_node_kernel, 1),
@@ -462,30 +472,15 @@
         top_v,
     )
     piece = exchange(sent, "gy", near_chips).sum(axis=0)
-    s_both, s_sums = up8(-(-n_both // 8)), up8(-(-n_sums // 8))
-    sent = jnp.concatenate(
-        [
-            pad_rows(piece[:n_both], 8 * s_both).reshape(8, s_both, rank),
-            pad_rows(piece[n_both:], 8 * s_sums).reshape(8, s_sums, rank),
-        ],
-        axis=1,
-    )
-    far = [3, 4, 5]
-    sides = exchange(sent, ("gx", "gy"), far)
-    sides = sides.reshape((2, 4) + sides.shape[1:]).sum(axis=1)
-    share = jnp.concatenate(
-        [sides[0, :s_both], sides[1, :s_both], sides[0, s_both:] + sides[1, s_both:]], axis=0
-    )
-    pieces = to_all(share, ("gx", "gy"), far)
-    share = jnp.concatenate(
-        [
-            pieces[:, :s_both].reshape(-1, rank)[:n_both],
-            pieces[:, s_both : 2 * s_both].reshape(-1, rank)[:n_both],
-            pieces[:, 2 * s_both :].reshape(-1, rank)[:n_sums],
-        ],
-        axis=0,
-    )
-    gathered = to_all(share, "gy", near_chips)
+    for bit in (3, 4):
+        pair = pair_gather(piece, "gy", bit)
+        piece = pair[0] + pair[1]
+    share = call(
+        functools.partial(share_kernel, n_both),
+        [(4, 2 * n_both + n_sums, rank)],
+        pair_gather(piece, "gx", 0),
+    )[0]
+    gathered = exchange(share, "gy", near_chips)
     shared = call(
         functools.partial(top_shared_kernel, n_both, rest),
         [(2 * count * half + rest, rank)],
@@ -505,39 +500,51 @@
         pair_gather(shared, "gy", 0),
         mine,
     )
-    solved = [z]
-
-    for bit in (1, 2):
-        count -= 1
-        pair = pair_gather(part, "gx", bit)
-        if bit == 1:
-            near = call(functools.partial(sibling_kernel, bit), [(4,) + part.shape], pair)[0]
-            near, pick = exchange(near, "gy", near_chips), None
-        else:
-            near, pick = pair, bit
-        shared = call(
-            functools.partial(upper_shared_kernel, count, pick),
-            [(2 * count * half, rank)],
-            node,
-            near,
-        )[0]
-        width -= half
-        z, node = call(
-            functools.partial(upper_node_kernel, count, pick),
-            [(width, rank), ((count - 1) * width, rank)],
-            node,
-            near,
-            pair_gather(shared, "gy", 0),
-        )
-        part = node
-        solved.append(z)
-
-    pair = pair_gather(node, "gx", 3)
-    gathered = pair_gather(jnp.concatenate([pair.reshape(-1, rank)] + solved, axis=0), "gy", 0)
+
+    count -= 1
+    rows = 2 * rest
+    near = call(
+        functools.partial(sibling_kernel, 1), [(4,) + part.shape], pair_gather(part, "gx", 1)
+    )[0]
+    near = exchange(near, "gy", near_chips)
+    shared = call(
+        functools.partial(quarter_shared_kernel, count),
+        [(2 * count * half + width, rank)],
+        node,
+        near,
+        z,
+    )[0]
+    width -= half
+    rows -= rank
+    z, node, carried = call(
+        functools.partial(quarter_node_kernel, count),
+        [(width, rank), ((count - 1) * width, rank), (rows, rank)],
+        node,
+        near,
+        pair_gather(shared, "gy", 0),
+        carried,
+    )
+
+    count -= 1
+    shared = call(
+        functools.partial(whole_shared_kernel, 2),
+        [(2 * node.shape[0] + width, rank)],
+        node,
+        pair_gather(node, "gx", 2),
+        z,
+    )[0]
+    rows -= 2 * rank
+    node, carried = call(
+        functools.partial(whole_node_kernel, count, node.shape[0]),
+        [((count - 1) * rows, rank), (rows, rank)],
+        pair_gather(shared, "gy", 0),
+        carried,
+    )
+
     return call(
-        functools.partial(last_kernel, 3, [v.shape[0] for v in solved]),
+        functools.partial(last_kernel, 3),
         [right_sides.shape[::-1]],
-        gathered,
+        pair_gather(node, "gx", 3),
         carried,
     )[0].T
 

time: 202 us -> 201 us (level)
    all_gather x11 -> x13, blocking collectives: 76.3 us -> 105 us  [pair_gather(): return lax.all_gather(value, axis, axis_index_groups=groups, tiled=tiled)]
    all_to_all x8 -> x6, blocking collectives: 91.6 us -> 64.7 us  [exchange(): lax.all_to_all(value, axis, 0, 0, axis_index_groups=bit_groups(count, bits))]
    ppermute x2 -> x1, starting transfers between devices: 10.7 us -> 8.79 us  [swap_cores(): lax.ppermute(value, 'gy', [(s, s ^ 1) for s in range(lax.axis_size('gy'))])]
    pallas_call x15 -> x16, Pallas kernels: 19.5 us -> 18.9 us  [call(): pl.pallas_call(kernel, out_shape=[jax.ShapeDtypeStruct(o, jnp.float32) fo...]
  transfers between devices with their start and end apart: 2 -> 1, of which waited for: 1 -> 1; matrix products, arithmetic and copies ran while one was open for 0% -> 0% of each run, Pallas kernels for 0% -> 0%
where the time goes in v8:
time: 201 us
  blocking collectives  169 us (84%)
  Pallas kernels  18.9 us (9%)
  starting transfers between devices  8.79 us (4%)
  waiting for transfers between devices  2.31 us (1%)
    all_gather x13, blocking collectives, pair_gather(): return lax.all_gather(value, axis, axis_index_groups=groups, tiled=tiled)  105 us
    all_to_all x6, blocking collectives, exchange(): lax.all_to_all(value, axis, 0, 0, axis_index_groups=bit_groups(count, bits))  64.7 us
    pallas_call x16, Pallas kernels, call(): pl.pallas_call(kernel, out_shape=[jax.ShapeDtypeStruct(o, jnp.float32) fo...  18.9 us
    ppermute x1, starting transfers between devices, swap_cores(): lax.ppermute(value, 'gy', [(s, s ^ 1) for s in range(lax.axis_size('gy'))])  8.79 us
  transfers between devices with their start and end apart: 1, of which 1 were waited for; matrix products, arithmetic and copies ran while one was open for 0% of the time, Pallas kernels for 0%

profile of v8, /device:TPU:1, one launch (start us, length us, event | category | flops | bytes accessed | tf_op | source)
XLA Modules:
  0.0 201.0 jit_solution(13916369580739019885)
XLA Ops:
  1.3 8.8 %collective-permute-start = (f32[2112,128]{1,0:T(8,128)S(1)}, f32[2112,128]{1,0:T(8,128)S(1)}, u32[]{:S(2)}, u32[]{:S(2)}) collective-permute-start(f32[2112,128]{1,0:T(8,128)S(1)} %pad_maximum_fusion.mine), channel_id=1, source_target_pairs={{0,1},{1,0},{2,3},{3,2},{4,5},{5,4},{6,7},{7,6},{8,9},{9,8},{10,11... | collective-permute-start | bytes 3244040 | tf_op jit(solution)/shard_map/ppermute | solution.py:388
  10.1 2.3 %collective-permute-done.other = f32[2112,128]{1,0:T(8,128)S(1)} collective-permute-done((f32[2112,128]{1,0:T(8,128)S(1)}, f32[2112,128]{1,0:T(8,128)S(1)}, u32[]{:S(2)}, u32[]{:S(2)}) %collective-permute-start) | collective-permute-done | bytes 1081376 | tf_op jit(solution)/shard_map/ppermute | solution.py:388
  13.3 9.9 %all-gather = f32[1344,128]{1,0:T(8,128)S(1)} all-gather(f32[672,128]{1,0:T(8,128)S(1)} %get-tuple-element.28), channel_id=2, replica_groups={{0,2},{1,3},{4,6},{5,7},{8,10},{9,11},{12,14},{13,15},{16,18},{17,19},{..., dimensions={0}, use_global_device_ids=true | all-gather | bytes 1032192 | tf_op jit(solution)/shard_map/all_gather | solution.py:393
  25.4 15.8 %all_to_all.30.parts = f32[4,544,128]{2,1,0:T(8,128)S(1)} all-to-all(f32[4,544,128]{2,1,0:T(8,128)S(1)} %get-tuple-element.30), channel_id=1, replica_groups={{0,2,4,6},{1,3,5,7},{8,10,12,14},{9,11,13,15},{16,18,20,22},{17,19,21,2..., dimensions={0} | all-to-all | bytes 2228224 | tf_op jit(solution)/shard_map/all_to_all | solution.py:398
  41.1 2.4 %shard_map.39 = (f32[416,256]{1,0:T(8,128)S(1)}, f32[4,208,128]{2,1,0:T(8,128)S(1)}) custom-call(f32[4,544,128]{2,1,0:T(8,128)S(1)} %all_to_all.30.parts, f32[544,128]{1,0:T(8,128)S(1)} %get-tuple-element.31.z_low, f32[672,256]{1,0:T(8,128)S(1)} %get-tuple-element.32.held, f32[2,256,128]{2,1,0:T(8,128)S(1)} %get-tuple-element.33.v), custom_call_target="tpu_custom_call" | custom-call | flops 625999872 | bytes 2342912 | tf_op jit(solution)/shard_map/pallas_call | solution.py:363
  43.6 8.1 %all_to_all.31 = f32[4,208,128]{2,1,0:T(8,128)S(1)} all-to-all(f32[4,208,128]{2,1,0:T(8,128)S(1)} %get-tuple-element.34), channel_id=1, replica_groups={{0,2,4,6},{1,3,5,7},{8,10,12,14},{9,11,13,15},{16,18,20,22},{17,19,21,2..., dimensions={0} | all-to-all | bytes 851968 | tf_op jit(solution)/shard_map/all_to_all | solution.py:398
  51.7 6.3 %all-gather.1 = f32[416,128]{1,0:T(8,128)S(1)} all-gather(f32[208,128]{1,0:T(8,128)S(1)} %reduce_sum.18), channel_id=3, replica_groups={{0,8},{1,9},{2,10},{3,11},{4,12},{5,13},{6,14},{7,15},{16,24},{17,25},{..., dimensions={0}, use_global_device_ids=true | all-gather | bytes 319488 | tf_op jit(solution)/shard_map/all_gather | solution.py:393
  58.1 9.5 %all_to_all.32.pieces = f32[4,328,128]{2,1,0:T(8,128)S(1)} all-to-all(f32[4,328,128]{2,1,0:T(8,128)S(1)} %shard_map.40), channel_id=1, replica_groups={{0,2,4,6},{1,3,5,7},{8,10,12,14},{9,11,13,15},{16,18,20,22},{17,19,21,2..., dimensions={0} | all-to-all | bytes 1343488 | tf_op jit(solution)/shard_map/all_to_all | solution.py:398
  67.5 8.0 %all-gather.2 = f32[1408,128]{1,0:T(8,128)S(1)} all-gather(f32[704,128]{1,0:T(8,128)S(1)} %shard_map.41), channel_id=4, replica_groups={{0,1},{2,3},{4,5},{6,7},{8,9},{10,11},{12,13},{14,15},{16,17},{18,19},{..., dimensions={0}, use_global_device_ids=true | all-gather | bytes 1081344 | tf_op jit(solution)/shard_map/all_gather | solution.py:393
  77.6 15.0 %all-gather.3 = f32[832,128]{1,0:T(8,128)S(1)} all-gather(f32[416,128]{1,0:T(8,128)S(1)} %get-tuple-element.36), channel_id=5, replica_groups={{0,16},{1,17},{2,18},{3,19},{4,20},{5,21},{6,22},{7,23},{8,24},{9,25},{..., dimensions={0}, use_global_device_ids=true | all-gather | bytes 638976 | tf_op jit(solution)/shard_map/all_gather | solution.py:393
  92.6 2.5 %shard_map.43 = (f32[288,128]{1,0:T(8,128)S(1)}, f32[288,128]{1,0:T(8,128)S(1)}, f32[4,288,128]{2,1,0:T(8,128)S(1)}) custom-call(f32[2,416,128]{2,1,0:T(8,128)S(1)} %bitcast.18, f32[416,128]{1,0:T(8,128)S(1)} %get-tuple-element.37.z_low, f32[2,704,128]{2,1,0:T(8,128)S(1)} %bitcast.17, f32[416,256]{1,0:T(8,128)S(1)} %get-tuple-element.35.rest, ...), custom_call_target="tpu_custom_call" | custom-call | flops 619708416 | bytes 2310144 | tf_op jit(solution)/shard_map/pallas_call | solution.py:363
  95.1 10.9 %all_to_all.33 = f32[4,288,128]{2,1,0:T(8,128)S(1)} all-to-all(f32[4,288,128]{2,1,0:T(8,128)S(1)} %get-tuple-element.39), channel_id=1, replica_groups={{0,2,4,6},{1,3,5,7},{8,10,12,14},{9,11,13,15},{16,18,20,22},{17,19,21,2..., dimensions={0} | all-to-all | bytes 1179648 | tf_op jit(solution)/shard_map/all_to_all | solution.py:398
  106.0 9.4 %all-gather.4 = f32[576,128]{1,0:T(8,128)S(1)} all-gather(f32[288,128]{1,0:T(8,128)S(1)} %reduce_sum.19), channel_id=6, replica_groups={{0,8},{1,9},{2,10},{3,11},{4,12},{5,13},{6,14},{7,15},{16,24},{17,25},{..., dimensions={0}, use_global_device_ids=true | all-gather | bytes 442368 | tf_op jit(solution)/shard_map/all_gather | solution.py:393
  115.4 10.6 %all-gather.11 = f32[576,128]{1,0:T(8,128)S(1)} all-gather(f32[288,128]{1,0:T(8,128)S(1)} %slice_add_fusion.1), channel_id=13, replica_groups={{0,16},{1,17},{2,18},{3,19},{4,20},{5,21},{6,22},{7,23},{8,24},{9,25},{..., dimensions={0}, use_global_device_ids=true | all-gather | bytes 442368 | tf_op jit(solution)/shard_map/all_gather | solution.py:393
  126.0 9.5 %all_gather.85.pair = f32[2,288,128]{2,1,0:T(8,128)S(1)} all-gather(f32[1,288,128]{2,1,0:T(8,128)S(1)} %fusion), channel_id=1, replica_groups={{0,32},{64,96},{128,160},{192,224},{256,288},{320,352},{384,416},{448,4..., dimensions={0}, use_global_device_ids=true | all-gather | bytes 442368 | tf_op jit(solution)/shard_map/all_gather | solution.py:393
  135.6 12.9 %all_to_all.34.gathered = f32[4,408,128]{2,1,0:T(8,128)S(1)} all-to-all(f32[4,408,128]{2,1,0:T(8,128)S(1)} %shard_map.44), channel_id=1, replica_groups={{0,2,4,6},{1,3,5,7},{8,10,12,14},{9,11,13,15},{16,18,20,22},{17,19,21,2..., dimensions={0} | all-to-all | bytes 1671168 | tf_op jit(solution)/shard_map/all_to_all | solution.py:398
  148.5 4.5 %all-gather.5 = f32[1600,128]{1,0:T(8,128)S(1)} all-gather(f32[800,128]{1,0:T(8,128)S(1)} %shard_map.45), channel_id=7, replica_groups={{0,1},{2,3},{4,5},{6,7},{8,9},{10,11},{12,13},{14,15},{16,17},{18,19},{..., dimensions={0}, use_global_device_ids=true | all-gather | bytes 1228800 | tf_op jit(solution)/shard_map/all_gather | solution.py:393
  155.3 11.0 %all-gather.6 = f32[336,128]{1,0:T(8,128)S(1)} all-gather(f32[168,128]{1,0:T(8,128)S(1)} %get-tuple-element.43), channel_id=8, replica_groups={{0,64},{32,96},{128,192},{160,224},{256,320},{288,352},{384,448},{416,4..., dimensions={0}, use_global_device_ids=true | all-gather | bytes 258048 | tf_op jit(solution)/shard_map/all_gather | solution.py:393
  166.2 7.5 %all_to_all.35.sib = f32[4,168,128]{2,1,0:T(8,128)S(1)} all-to-all(f32[4,168,128]{2,1,0:T(8,128)S(1)} %shard_map.47), channel_id=1, replica_groups={{0,2,4,6},{1,3,5,7},{8,10,12,14},{9,11,13,15},{16,18,20,22},{17,19,21,2..., dimensions={0} | all-to-all | bytes 688128 | tf_op jit(solution)/shard_map/all_to_all | solution.py:398
  173.8 5.1 %all-gather.7 = f32[1216,128]{1,0:T(8,128)S(1)} all-gather(f32[608,128]{1,0:T(8,128)S(1)} %shard_map.48), channel_id=9, replica_groups={{0,1},{2,3},{4,5},{6,7},{8,9},{10,11},{12,13},{14,15},{16,17},{18,19},{..., dimensions={0}, use_global_device_ids=true | all-gather | bytes 933888 | tf_op jit(solution)/shard_map/all_gather | solution.py:393
  180.9 6.1 %all-gather.8 = f32[640,128]{1,0:T(8,128)S(1)} all-gather(f32[320,128]{1,0:T(8,128)S(1)} %get-tuple-element.46.own), channel_id=10, replica_groups={{0,128},{32,160},{64,192},{96,224},{256,384},{288,416},{320,448},{352,4..., dimensions={0}, use_global_device_ids=true | all-gather | bytes 491520 | tf_op jit(solution)/shard_map/all_gather | solution.py:393
  187.1 3.2 %all-gather.9 = f32[1600,128]{1,0:T(8,128)S(1)} all-gather(f32[800,128]{1,0:T(8,128)S(1)} %shard_map.50), channel_id=11, replica_groups={{0,1},{2,3},{4,5},{6,7},{8,9},{10,11},{12,13},{14,15},{16,17},{18,19},{..., dimensions={0}, use_global_device_ids=true | all-gather | bytes 1228800 | tf_op jit(solution)/shard_map/all_gather | solution.py:393
  192.3 6.3 %all-gather.10 = f32[384,128]{1,0:T(8,128)S(1)} all-gather(f32[192,128]{1,0:T(8,128)S(1)} %get-tuple-element.49), channel_id=12, replica_groups={{0,256},{32,288},{64,320},{96,352},{128,384},{160,416},{192,448},{224,4..., dimensions={0}, use_global_device_ids=true | all-gather | bytes 294912 | tf_op jit(solution)/shard_map/all_gather | solution.py:393
  198.6 2.4 %shard_map.52 = f32[64,128]{1,0:T(8,128)} custom-call(f32[2,192,128]{2,1,0:T(8,128)S(1)} %bitcast.25, f32[192,128]{1,0:T(8,128)S(1)} %get-tuple-element.50.carried), custom_call_target="tpu_custom_call" | custom-call | flops 232783872 | bytes 294912 | tf_op jit(solution)/shard_map/pallas_call | solution.py:363
  (18 shorter events, 13.0 us)
Async XLA Ops:
  1.3 11.1 %collective-permute-start = (f32[2112,128]{1,0:T(8,128)S(1)}, f32[2112,128]{1,0:T(8,128)S(1)}, u32[]{:S(2)}, u32[]{:S(2)}) collective-permute-start(f32[2112,128]{1,0:T(8,128)S(1)} %pad_maximum_fusion.mine), channel_id=1, source_target_pairs={{0,1},{1,0},{2,3},{3,2},{4,5},{5,4},{6,7},{7,6},{8,9},{9,8},{10,11... | collective-permute-start | bytes 3244040 | tf_op jit(solution)/shard_map/ppermute | solution.py:388

commit v9 on v8

--- a/solution.py
+++ b/solution.py
@@ -114,9 +114,7 @@
     own, sib = pair[side], pair[1 - side]
     z = solve_own(own[:rank], sib[:rank], own[rank:], sib[rank:])
     z_out[...] = z
-    value = up[rank:] - kdot(z, up[:rank])
-    for i in range(out.shape[0]):
-        out[i] = value
+    out[...] = up[rank:] - kdot(z, up[:rank])
 
 
 def after_pair(own, sib, z_low, held):
@@ -128,10 +126,9 @@
     return held[2 * rank :] - kdot(z_both, jnp.concatenate([left, next_left], axis=0))
 
 
-def between_kernel(bit, shares, parts, z_low, held, v, rest, sent):
+def between_kernel(bit, shares, pair, z_low, held, v, rest, sent):
     side = bit_of("gy", bit)
-    own, sib = [parts[2 * c] + parts[2 * c + 1] for c in (side, 1 - side)]
-    value = after_pair(own, sib, z_low, held)
+    value = after_pair(pair[side], pair[1 - side], z_low, held)
     rest[...] = value
     rows = value.shape[0]
     half = v.shape[2] // 2
@@ -398,6 +395,18 @@
     return lax.all_to_all(value, axis, 0, 0, axis_index_groups=bit_groups(count, bits))
 
 
+def to_all(value, axis, bits):
+    return exchange(jnp.broadcast_to(value, (1 << len(bits),) + value.shape), axis, bits)
+
+
+def pad_rows(value, rows):
+    return jnp.pad(value, ((0, rows - value.shape[0]), (0, 0)))
+
+
+def up8(value):
+    return -(-value // 8) * 8
+
+
 def shards(right_sides, factor_u, factor_v):
     levels, _, rank = factor_u.shape
     half = rank // 2
@@ -422,10 +431,12 @@
     )
     z_low, node = call(
         functools.partial(first_node_kernel, 1),
-        [(rank + rest, rank), (4, rank + rest, rank)],
+        [(rank + rest, rank), (rank + rest, rank)],
         pair_gather(low, "gy", 1),
         up,
     )
+    pair = pair_gather(node, "gy", 1)
+    pair = pair_gather(pair[0] + pair[1], "gy", 2)
 
     rows = rest
     rest -= rank
@@ -433,7 +444,7 @@
     held, sent = call(
         functools.partial(between_kernel, 2, 4),
         [(rows, 2 * rank), (4, n_both + n_sums, rank)],
-        exchange(node, "gy", near_chips),
+        pair,
         z_low,
         held,
         next_v,
@@ -472,15 +483,30 @@
         top_v,
     )
     piece = exchange(sent, "gy", near_chips).sum(axis=0)
-    for bit in (3, 4):
-        pair = pair_gather(piece, "gy", bit)
-        piece = pair[0] + pair[1]
-    share = call(
-        functools.partial(share_kernel, n_both),
-        [(4, 2 * n_both + n_sums, rank)],
-        pair_gather(piece, "gx", 0),
-    )[0]
-    gathered = exchange(share, "gy", near_chips)
+    s_both, s_sums = up8(-(-n_both // 8)), up8(-(-n_sums // 8))
+    sent = jnp.concatenate(
+        [
+            pad_rows(piece[:n_both], 8 * s_both).reshape(8, s_both, rank),
+            pad_rows(piece[n_both:], 8 * s_sums).reshape(8, s_sums, rank),
+        ],
+        axis=1,
+    )
+    far = [3, 4, 5]
+    sides = exchange(sent, ("gx", "gy"), far)
+    sides = sides.reshape((2, 4) + sides.shape[1:]).sum(axis=1)
+    share = jnp.concatenate(
+        [sides[0, :s_both], sides[1, :s_both], sides[0, s_both:] + sides[1, s_both:]], axis=0
+    )
+    pieces = to_all(share, ("gx", "gy"), far)
+    share = jnp.concatenate(
+        [
+            pieces[:, :s_both].reshape(-1, rank)[:n_both],
+            pieces[:, s_both : 2 * s_both].reshape(-1, rank)[:n_both],
+            pieces[:, 2 * s_both :].reshape(-1, rank)[:n_sums],
+        ],
+        axis=0,
+    )
+    gathered = to_all(share, "gy", near_chips)
     shared = call(
         functools.partial(top_shared_kernel, n_both, rest),
         [(2 * count * half + rest, rank)],

time: 201 us -> 198 us (0.985)
  blocking collectives: 169 us -> 165 us
    all_gather x13 -> x12, blocking collectives: 105 us -> 90.7 us  [pair_gather(): return lax.all_gather(value, axis, axis_index_groups=groups, tiled=tiled)]
    all_to_all x6 -> x7, blocking collectives: 64.7 us -> 74.8 us  [exchange(): lax.all_to_all(value, axis, 0, 0, axis_index_groups=bit_groups(count, bits))]
    pallas_call x16 -> x15, Pallas kernels: 18.9 us -> 18.9 us  [call(): pl.pallas_call(kernel, out_shape=[jax.ShapeDtypeStruct(o, jnp.float32) fo...]
where the time goes in v9:
time: 198 us; the launch traced here: 197 us
  blocking collectives  165 us (83%)
  Pallas kernels  18.9 us (10%)
  starting transfers between devices  8.79 us (4%)
  waiting for transfers between devices  2.31 us (1%)
    all_gather x12, blocking collectives, pair_gather(): return lax.all_gather(value, axis, axis_index_groups=groups, tiled=tiled)  90.7 us
    all_to_all x7, blocking collectives, exchange(): lax.all_to_all(value, axis, 0, 0, axis_index_groups=bit_groups(count, bits))  74.8 us
    pallas_call x15, Pallas kernels, call(): pl.pallas_call(kernel, out_shape=[jax.ShapeDtypeStruct(o, jnp.float32) fo...  18.9 us
    ppermute x1, starting transfers between devices, swap_cores(): lax.ppermute(value, 'gy', [(s, s ^ 1) for s in range(lax.axis_size('gy'))])  8.79 us
  transfers between devices with their start and end apart: 1, of which 1 were waited for; matrix products, arithmetic and copies ran while one was open for 0% of the time, Pallas kernels for 0%

profile of v9, /device:TPU:1, one launch (start us, length us, event | category | flops | bytes accessed | tf_op | source)
XLA Modules:
  0.0 197.3 jit_solution(11678355871564334541)
XLA Ops:
  1.3 8.8 %collective-permute-start = (f32[2112,128]{1,0:T(8,128)S(1)}, f32[2112,128]{1,0:T(8,128)S(1)}, u32[]{:S(2)}, u32[]{:S(2)}) collective-permute-start(f32[2112,128]{1,0:T(8,128)S(1)} %pad_maximum_fusion.mine), channel_id=1, source_target_pairs={{0,1},{1,0},{2,3},{3,2},{4,5},{5,4},{6,7},{7,6},{8,9},{9,8},{10,11... | collective-permute-start | bytes 3244040 | tf_op jit(solution)/shard_map/ppermute | solution.py:385
  10.1 2.3 %collective-permute-done.other = f32[2112,128]{1,0:T(8,128)S(1)} collective-permute-done((f32[2112,128]{1,0:T(8,128)S(1)}, f32[2112,128]{1,0:T(8,128)S(1)}, u32[]{:S(2)}, u32[]{:S(2)}) %collective-permute-start) | collective-permute-done | bytes 1081376 | tf_op jit(solution)/shard_map/ppermute | solution.py:385
  13.3 9.9 %all-gather = f32[1344,128]{1,0:T(8,128)S(1)} all-gather(f32[672,128]{1,0:T(8,128)S(1)} %get-tuple-element.28), channel_id=2, replica_groups={{0,2},{1,3},{4,6},{5,7},{8,10},{9,11},{12,14},{13,15},{16,18},{17,19},{..., dimensions={0}, use_global_device_ids=true | all-gather | bytes 1032192 | tf_op jit(solution)/shard_map/all_gather | solution.py:390
  25.3 7.6 %all-gather.1 = f32[1088,128]{1,0:T(8,128)S(1)} all-gather(f32[544,128]{1,0:T(8,128)S(1)} %get-tuple-element.30), channel_id=3, replica_groups={{0,2},{1,3},{4,6},{5,7},{8,10},{9,11},{12,14},{13,15},{16,18},{17,19},{..., dimensions={0}, use_global_device_ids=true | all-gather | bytes 835584 | tf_op jit(solution)/shard_map/all_gather | solution.py:390
  33.0 6.7 %all-gather.11 = f32[1088,128]{1,0:T(8,128)S(1)} all-gather(f32[544,128]{1,0:T(8,128)S(1)} %slice_add_fusion), channel_id=13, replica_groups={{0,4},{1,5},{2,6},{3,7},{8,12},{9,13},{10,14},{11,15},{16,20},{17,21},{..., dimensions={0}, use_global_device_ids=true | all-gather | bytes 835584 | tf_op jit(solution)/shard_map/all_gather | solution.py:390
  39.7 2.5 %shard_map.39 = (f32[416,256]{1,0:T(8,128)S(1)}, f32[4,208,128]{2,1,0:T(8,128)S(1)}) custom-call(f32[2,544,128]{2,1,0:T(8,128)S(1)} %bitcast.36, f32[544,128]{1,0:T(8,128)S(1)} %get-tuple-element.31.z_low, f32[672,256]{1,0:T(8,128)S(1)} %get-tuple-element.32.held, f32[2,256,128]{2,1,0:T(8,128)S(1)} %get-tuple-element.33.v), custom_call_target="tpu_custom_call" | custom-call | flops 519045120 | bytes 1785856 | tf_op jit(solution)/shard_map/pallas_call | solution.py:360
  42.2 8.1 %all_to_all.35 = f32[4,208,128]{2,1,0:T(8,128)S(1)} all-to-all(f32[4,208,128]{2,1,0:T(8,128)S(1)} %get-tuple-element.34), channel_id=1, replica_groups={{0,2,4,6},{1,3,5,7},{8,10,12,14},{9,11,13,15},{16,18,20,22},{17,19,21,2..., dimensions={0} | all-to-all | bytes 851968 | tf_op jit(solution)/shard_map/all_to_all | solution.py:395
  50.3 6.3 %all-gather.2 = f32[416,128]{1,0:T(8,128)S(1)} all-gather(f32[208,128]{1,0:T(8,128)S(1)} %reduce_sum.27), channel_id=4, replica_groups={{0,8},{1,9},{2,10},{3,11},{4,12},{5,13},{6,14},{7,15},{16,24},{17,25},{..., dimensions={0}, use_global_device_ids=true | all-gather | bytes 319488 | tf_op jit(solution)/shard_map/all_gather | solution.py:390
  56.6 9.5 %all_to_all.36.pieces = f32[4,328,128]{2,1,0:T(8,128)S(1)} all-to-all(f32[4,328,128]{2,1,0:T(8,128)S(1)} %shard_map.40), channel_id=1, replica_groups={{0,2,4,6},{1,3,5,7},{8,10,12,14},{9,11,13,15},{16,18,20,22},{17,19,21,2..., dimensions={0} | all-to-all | bytes 1343488 | tf_op jit(solution)/shard_map/all_to_all | solution.py:395
  66.1 8.4 %all-gather.3 = f32[1408,128]{1,0:T(8,128)S(1)} all-gather(f32[704,128]{1,0:T(8,128)S(1)} %shard_map.41), channel_id=5, replica_groups={{0,1},{2,3},{4,5},{6,7},{8,9},{10,11},{12,13},{14,15},{16,17},{18,19},{..., dimensions={0}, use_global_device_ids=true | all-gather | bytes 1081344 | tf_op jit(solution)/shard_map/all_gather | solution.py:390
  76.6 15.4 %all-gather.4 = f32[832,128]{1,0:T(8,128)S(1)} all-gather(f32[416,128]{1,0:T(8,128)S(1)} %get-tuple-element.36), channel_id=6, replica_groups={{0,16},{1,17},{2,18},{3,19},{4,20},{5,21},{6,22},{7,23},{8,24},{9,25},{..., dimensions={0}, use_global_device_ids=true | all-gather | bytes 638976 | tf_op jit(solution)/shard_map/all_gather | solution.py:390
  92.0 2.5 %shard_map.43 = (f32[288,128]{1,0:T(8,128)S(1)}, f32[288,128]{1,0:T(8,128)S(1)}, f32[4,288,128]{2,1,0:T(8,128)S(1)}) custom-call(f32[2,416,128]{2,1,0:T(8,128)S(1)} %bitcast.30, f32[416,128]{1,0:T(8,128)S(1)} %get-tuple-element.37.z_low, f32[2,704,128]{2,1,0:T(8,128)S(1)} %bitcast.29, f32[416,256]{1,0:T(8,128)S(1)} %get-tuple-element.35.rest, ...), custom_call_target="tpu_custom_call" | custom-call | flops 619708416 | bytes 2310144 | tf_op jit(solution)/shard_map/pallas_call | solution.py:360
  94.5 10.9 %all_to_all.37 = f32[4,288,128]{2,1,0:T(8,128)S(1)} all-to-all(f32[4,288,128]{2,1,0:T(8,128)S(1)} %get-tuple-element.39), channel_id=1, replica_groups={{0,2,4,6},{1,3,5,7},{8,10,12,14},{9,11,13,15},{16,18,20,22},{17,19,21,2..., dimensions={0} | all-to-all | bytes 1179648 | tf_op jit(solution)/shard_map/all_to_all | solution.py:395
  105.6 13.6 %all_to_all.38 = f32[8,40,128]{2,1,0:T(8,128)S(1)} all-to-all(f32[8,40,128]{2,1,0:T(8,128)S(1)} %pad_maximum_fusion.2), channel_id=1, replica_groups={{0,8,16,24,32,40,48,56},{1,9,17,25,33,41,49,57},{2,10,18,26,34,42,50,58..., dimensions={0} | all-to-all | bytes 327680 | tf_op jit(solution)/shard_map/all_to_all | solution.py:395
  119.3 11.7 %all_to_all.39 = f32[8,56,128]{2,1,0:T(8,128)S(1)} all-to-all(f32[8,56,128]{2,1,0:T(8,128)S(1)} %broadcast_in_dim.6), channel_id=1, replica_groups={{0,8,16,24,32,40,48,56},{1,9,17,25,33,41,49,57},{2,10,18,26,34,42,50,58..., dimensions={0} | all-to-all | bytes 458752 | tf_op jit(solution)/shard_map/all_to_all | solution.py:395
  131.1 11.6 %all_to_all.40.gathered = f32[4,408,128]{2,1,0:T(8,128)S(1)} all-to-all(f32[4,408,128]{2,1,0:T(8,128)S(1)} %broadcast_in_dim.7), channel_id=1, replica_groups={{0,2,4,6},{1,3,5,7},{8,10,12,14},{9,11,13,15},{16,18,20,22},{17,19,21,2..., dimensions={0} | all-to-all | bytes 1671168 | tf_op jit(solution)/shard_map/all_to_all | solution.py:395
  142.7 7.7 %all-gather.5 = f32[1600,128]{1,0:T(8,128)S(1)} all-gather(f32[800,128]{1,0:T(8,128)S(1)} %shard_map.44), channel_id=7, replica_groups={{0,1},{2,3},{4,5},{6,7},{8,9},{10,11},{12,13},{14,15},{16,17},{18,19},{..., dimensions={0}, use_global_device_ids=true | all-gather | bytes 1228800 | tf_op jit(solution)/shard_map/all_gather | solution.py:390
  152.6 9.3 %all-gather.6 = f32[336,128]{1,0:T(8,128)S(1)} all-gather(f32[168,128]{1,0:T(8,128)S(1)} %get-tuple-element.43), channel_id=8, replica_groups={{0,64},{32,96},{128,192},{160,224},{256,320},{288,352},{384,448},{416,4..., dimensions={0}, use_global_device_ids=true | all-gather | bytes 258048 | tf_op jit(solution)/shard_map/all_gather | solution.py:390
  161.9 9.4 %all_to_all.41.sib = f32[4,168,128]{2,1,0:T(8,128)S(1)} all-to-all(f32[4,168,128]{2,1,0:T(8,128)S(1)} %shard_map.46), channel_id=1, replica_groups={{0,2,4,6},{1,3,5,7},{8,10,12,14},{9,11,13,15},{16,18,20,22},{17,19,21,2..., dimensions={0} | all-to-all | bytes 688128 | tf_op jit(solution)/shard_map/all_to_all | solution.py:395
  171.4 3.8 %all-gather.7 = f32[1216,128]{1,0:T(8,128)S(1)} all-gather(f32[608,128]{1,0:T(8,128)S(1)} %shard_map.47), channel_id=9, replica_groups={{0,1},{2,3},{4,5},{6,7},{8,9},{10,11},{12,13},{14,15},{16,17},{18,19},{..., dimensions={0}, use_global_device_ids=true | all-gather | bytes 933888 | tf_op jit(solution)/shard_map/all_gather | solution.py:390
  177.3 6.1 %all-gather.8 = f32[640,128]{1,0:T(8,128)S(1)} all-gather(f32[320,128]{1,0:T(8,128)S(1)} %get-tuple-element.46.own), channel_id=10, replica_groups={{0,128},{32,160},{64,192},{96,224},{256,384},{288,416},{320,448},{352,4..., dimensions={0}, use_global_device_ids=true | all-gather | bytes 491520 | tf_op jit(solution)/shard_map/all_gather | solution.py:390
  183.4 3.2 %all-gather.9 = f32[1600,128]{1,0:T(8,128)S(1)} all-gather(f32[800,128]{1,0:T(8,128)S(1)} %shard_map.49), channel_id=11, replica_groups={{0,1},{2,3},{4,5},{6,7},{8,9},{10,11},{12,13},{14,15},{16,17},{18,19},{..., dimensions={0}, use_global_device_ids=true | all-gather | bytes 1228800 | tf_op jit(solution)/shard_map/all_gather | solution.py:390
  188.7 6.2 %all-gather.10 = f32[384,128]{1,0:T(8,128)S(1)} all-gather(f32[192,128]{1,0:T(8,128)S(1)} %get-tuple-element.49), channel_id=12, replica_groups={{0,256},{32,288},{64,320},{96,352},{128,384},{160,416},{192,448},{224,4..., dimensions={0}, use_global_device_ids=true | all-gather | bytes 294912 | tf_op jit(solution)/shard_map/all_gather | solution.py:390
  194.9 2.4 %shard_map.51 = f32[64,128]{1,0:T(8,128)} custom-call(f32[2,192,128]{2,1,0:T(8,128)S(1)} %bitcast.38, f32[192,128]{1,0:T(8,128)S(1)} %get-tuple-element.50.carried), custom_call_target="tpu_custom_call" | custom-call | flops 232783872 | bytes 294912 | tf_op jit(solution)/shard_map/pallas_call | solution.py:360
  (33 shorter events, 13.2 us)
Async XLA Ops:
  1.3 11.1 %collective-permute-start = (f32[2112,128]{1,0:T(8,128)S(1)}, f32[2112,128]{1,0:T(8,128)S(1)}, u32[]{:S(2)}, u32[]{:S(2)}) collective-permute-start(f32[2112,128]{1,0:T(8,128)S(1)} %pad_maximum_fusion.mine), channel_id=1, source_target_pairs={{0,1},{1,0},{2,3},{3,2},{4,5},{5,4},{6,7},{7,6},{8,9},{9,8},{10,11... | collective-permute-start | bytes 3244040 | tf_op jit(solution)/shard_map/ppermute | solution.py:385
  94.5 11.0 %copy-start = (pred[128]{0:T(512)(128)(4,1)S(1)}, pred[128]{0:T(512)(128)(4,1)}, u32[]{:S(2)}) copy-start(pred[128]{0:T(512)(128)(4,1)} %constant.4.clone.1) | copy-start | bytes 388

commit v10 on v9

--- a/solution.py
+++ b/solution.py
@@ -190,7 +190,7 @@
     node_out[...] = node
 
 
-def upper_kernel(bit, shares, pair, z_low, shared, rest, v, mine, other, sent):
+def upper_kernel(bit, s_both, pair, z_low, shared, rest, v, mine, other, sent):
     rank = v.shape[2]
     half = rank // 2
     core = bit_of("gy", 0)
@@ -210,14 +210,23 @@
     mine[...] = value[:, :rank]
     other[...] = value[:, rank:]
     count, width = v.shape[0], value.shape[0]
-    n_both = (width + (count - 1) * half) // shares
-    n_sums = (count - 1) * (width - half) // shares
     parts = split(value)
-    put_rows(sent, 0, n_both, 0, dot_split(parts, split(v[0])))
-    for j in range(1, count):
-        rows = dot_split(parts, split(v[j]))
-        put_rows(sent, 0, n_both, width + (j - 1) * half, rows[:half])
-        put_rows(sent, n_both, n_sums, (j - 1) * (width - half), rows[half:])
+    rows = [dot_split(parts, split(v[j])) for j in range(count)]
+    both = jnp.concatenate([rows[0]] + [r[:half] for r in rows[1:]], axis=0)
+    sums = jnp.concatenate([r[half:] for r in rows[1:]], axis=0)
+    far = sent.shape[0] // 4
+    for value, base, size in ((both, 0, s_both), (sums, s_both, sent.shape[1] - s_both)):
+        n = value.shape[0] // 4
+        for c in range(4):
+            for f in range(far):
+                at, end = min(f * size, n), min((f + 1) * size, n)
+                to = base + end - at
+                if end > at:
+                    sent[4 * f + c, base:to] = value[c * n + at : c * n + end]
+                if to < base + size:
+                    sent[4 * f + c, to : base + size] = jnp.zeros(
+                        (base + size - to, rank), jnp.float32
+                    )
 
 
 def share_kernel(n_both, pair, out):
@@ -399,10 +408,6 @@
     return exchange(jnp.broadcast_to(value, (1 << len(bits),) + value.shape), axis, bits)
 
 
-def pad_rows(value, rows):
-    return jnp.pad(value, ((0, rows - value.shape[0]), (0, 0)))
-
-
 def up8(value):
     return -(-value // 8) * 8
 
@@ -473,27 +478,19 @@
     count = levels - 4
     n_both = (rest + (count - 1) * half) // 4
     n_sums = (count - 1) * (rest - half) // 4
+    s_both, s_sums = up8(-(-n_both // 8)), up8(-(-n_sums // 8))
     mine, other, sent = call(
-        functools.partial(upper_kernel, 4, 4),
-        [(rest, rank), (rest, rank), (4, n_both + n_sums, rank)],
+        functools.partial(upper_kernel, 4, s_both),
+        [(rest, rank), (rest, rank), (32, s_both + s_sums, rank)],
         pair_gather(node, "gy", 4),
         z_low,
         shared,
         held,
         top_v,
     )
-    piece = exchange(sent, "gy", near_chips).sum(axis=0)
-    s_both, s_sums = up8(-(-n_both // 8)), up8(-(-n_sums // 8))
-    sent = jnp.concatenate(
-        [
-            pad_rows(piece[:n_both], 8 * s_both).reshape(8, s_both, rank),
-            pad_rows(piece[n_both:], 8 * s_sums).reshape(8, s_sums, rank),
-        ],
-        axis=1,
-    )
     far = [3, 4, 5]
-    sides = exchange(sent, ("gx", "gy"), far)
-    sides = sides.reshape((2, 4) + sides.shape[1:]).sum(axis=1)
+    sides = exchange(sent, ("gx", "gy"), near_chips + far)
+    sides = sides.reshape((2, 16) + sides.shape[1:]).sum(axis=1)
     share = jnp.concatenate(
         [sides[0, :s_both], sides[1, :s_both], sides[0, s_both:] + sides[1, s_both:]], axis=0
     )

time: 198 us -> 197 us (level)
    all_to_all x7 -> x6, blocking collectives: 74.8 us -> 74.3 us  [exchange(): lax.all_to_all(value, axis, 0, 0, axis_index_groups=bit_groups(count, bits))]
where the time goes in v10:
time: 197 us
  blocking collectives  165 us (84%)
  Pallas kernels  18.9 us (10%)
  starting transfers between devices  8.79 us (4%)
  waiting for transfers between devices  2.31 us (1%)
    all_gather x12, blocking collectives, pair_gather(): return lax.all_gather(value, axis, axis_index_groups=groups, tiled=tiled)  90.7 us
    all_to_all x6, blocking collectives, exchange(): lax.all_to_all(value, axis, 0, 0, axis_index_groups=bit_groups(count, bits))  74.3 us
    pallas_call x15, Pallas kernels, call(): pl.pallas_call(kernel, out_shape=[jax.ShapeDtypeStruct(o, jnp.float32) fo...  18.9 us
    ppermute x1, starting transfers between devices, swap_cores(): lax.ppermute(value, 'gy', [(s, s ^ 1) for s in range(lax.axis_size('gy'))])  8.79 us
  transfers between devices with their start and end apart: 1, of which 1 were waited for; matrix products, arithmetic and copies ran while one was open for 0% of the time, Pallas kernels for 0%

profile of v10, /device:TPU:1, one launch (start us, length us, event | category | flops | bytes accessed | tf_op | source)
XLA Modules:
  0.0 196.7 jit_solution(10941560818951387400)
XLA Ops:
  1.3 8.8 %collective-permute-start = (f32[2112,128]{1,0:T(8,128)S(1)}, f32[2112,128]{1,0:T(8,128)S(1)}, u32[]{:S(2)}, u32[]{:S(2)}) collective-permute-start(f32[2112,128]{1,0:T(8,128)S(1)} %pad_maximum_fusion.mine), channel_id=1, source_target_pairs={{0,1},{1,0},{2,3},{3,2},{4,5},{5,4},{6,7},{7,6},{8,9},{9,8},{10,11... | collective-permute-start | bytes 3244040 | tf_op jit(solution)/shard_map/ppermute | solution.py:394
  10.1 2.3 %collective-permute-done.other = f32[2112,128]{1,0:T(8,128)S(1)} collective-permute-done((f32[2112,128]{1,0:T(8,128)S(1)}, f32[2112,128]{1,0:T(8,128)S(1)}, u32[]{:S(2)}, u32[]{:S(2)}) %collective-permute-start) | collective-permute-done | bytes 1081376 | tf_op jit(solution)/shard_map/ppermute | solution.py:394
  13.3 9.9 %all-gather = f32[1344,128]{1,0:T(8,128)S(1)} all-gather(f32[672,128]{1,0:T(8,128)S(1)} %get-tuple-element.28), channel_id=2, replica_groups={{0,2},{1,3},{4,6},{5,7},{8,10},{9,11},{12,14},{13,15},{16,18},{17,19},{..., dimensions={0}, use_global_device_ids=true | all-gather | bytes 1032192 | tf_op jit(solution)/shard_map/all_gather | solution.py:399
  25.3 7.6 %all-gather.1 = f32[1088,128]{1,0:T(8,128)S(1)} all-gather(f32[544,128]{1,0:T(8,128)S(1)} %get-tuple-element.30), channel_id=3, replica_groups={{0,2},{1,3},{4,6},{5,7},{8,10},{9,11},{12,14},{13,15},{16,18},{17,19},{..., dimensions={0}, use_global_device_ids=true | all-gather | bytes 835584 | tf_op jit(solution)/shard_map/all_gather | solution.py:399
  33.0 6.7 %all-gather.11 = f32[1088,128]{1,0:T(8,128)S(1)} all-gather(f32[544,128]{1,0:T(8,128)S(1)} %slice_add_fusion), channel_id=13, replica_groups={{0,4},{1,5},{2,6},{3,7},{8,12},{9,13},{10,14},{11,15},{16,20},{17,21},{..., dimensions={0}, use_global_device_ids=true | all-gather | bytes 835584 | tf_op jit(solution)/shard_map/all_gather | solution.py:399
  39.7 2.5 %shard_map.39 = (f32[416,256]{1,0:T(8,128)S(1)}, f32[4,208,128]{2,1,0:T(8,128)S(1)}) custom-call(f32[2,544,128]{2,1,0:T(8,128)S(1)} %bitcast.34, f32[544,128]{1,0:T(8,128)S(1)} %get-tuple-element.31.z_low, f32[672,256]{1,0:T(8,128)S(1)} %get-tuple-element.32.held, f32[2,256,128]{2,1,0:T(8,128)S(1)} %get-tuple-element.33.v), custom_call_target="tpu_custom_call" | custom-call | flops 519045120 | bytes 1785856 | tf_op jit(solution)/shard_map/pallas_call | solution.py:369
  42.2 8.1 %all_to_all.30 = f32[4,208,128]{2,1,0:T(8,128)S(1)} all-to-all(f32[4,208,128]{2,1,0:T(8,128)S(1)} %get-tuple-element.34), channel_id=1, replica_groups={{0,2,4,6},{1,3,5,7},{8,10,12,14},{9,11,13,15},{16,18,20,22},{17,19,21,2..., dimensions={0} | all-to-all | bytes 851968 | tf_op jit(solution)/shard_map/all_to_all | solution.py:404
  50.3 6.3 %all-gather.2 = f32[416,128]{1,0:T(8,128)S(1)} all-gather(f32[208,128]{1,0:T(8,128)S(1)} %reduce_sum.18), channel_id=4, replica_groups={{0,8},{1,9},{2,10},{3,11},{4,12},{5,13},{6,14},{7,15},{16,24},{17,25},{..., dimensions={0}, use_global_device_ids=true | all-gather | bytes 319488 | tf_op jit(solution)/shard_map/all_gather | solution.py:399
  56.6 9.5 %all_to_all.31.pieces = f32[4,328,128]{2,1,0:T(8,128)S(1)} all-to-all(f32[4,328,128]{2,1,0:T(8,128)S(1)} %shard_map.40), channel_id=1, replica_groups={{0,2,4,6},{1,3,5,7},{8,10,12,14},{9,11,13,15},{16,18,20,22},{17,19,21,2..., dimensions={0} | all-to-all | bytes 1343488 | tf_op jit(solution)/shard_map/all_to_all | solution.py:404
  66.1 8.4 %all-gather.3 = f32[1408,128]{1,0:T(8,128)S(1)} all-gather(f32[704,128]{1,0:T(8,128)S(1)} %shard_map.41), channel_id=5, replica_groups={{0,1},{2,3},{4,5},{6,7},{8,9},{10,11},{12,13},{14,15},{16,17},{18,19},{..., dimensions={0}, use_global_device_ids=true | all-gather | bytes 1081344 | tf_op jit(solution)/shard_map/all_gather | solution.py:399
  76.6 15.4 %all-gather.4 = f32[832,128]{1,0:T(8,128)S(1)} all-gather(f32[416,128]{1,0:T(8,128)S(1)} %get-tuple-element.36), channel_id=6, replica_groups={{0,16},{1,17},{2,18},{3,19},{4,20},{5,21},{6,22},{7,23},{8,24},{9,25},{..., dimensions={0}, use_global_device_ids=true | all-gather | bytes 638976 | tf_op jit(solution)/shard_map/all_gather | solution.py:399
  92.0 2.5 %shard_map.43 = (f32[288,128]{1,0:T(8,128)S(1)}, f32[288,128]{1,0:T(8,128)S(1)}, f32[32,40,128]{2,1,0:T(8,128)S(1)}) custom-call(f32[2,416,128]{2,1,0:T(8,128)S(1)} %bitcast.28, f32[416,128]{1,0:T(8,128)S(1)} %get-tuple-element.37.z_low, f32[2,704,128]{2,1,0:T(8,128)S(1)} %bitcast.27, f32[416,256]{1,0:T(8,128)S(1)} %get-tuple-element.35.rest, ...), custom_call_target="tpu_custom_call" | custom-call | flops 619708416 | bytes 2310144 | tf_op jit(solution)/shard_map/pallas_call | solution.py:369
  94.5 24.2 %all_to_all.32 = f32[32,40,128]{2,1,0:T(8,128)S(1)} all-to-all(f32[32,40,128]{2,1,0:T(8,128)S(1)} %get-tuple-element.39), channel_id=1, replica_groups={{0,2,4,6,8,10,12,14,16,18,20,22,24,26,28,30,32,34,36,38,40,42,44,46,48,..., dimensions={0} | all-to-all | bytes 1310720 | tf_op jit(solution)/shard_map/all_to_all | solution.py:404
  118.8 13.7 %all_to_all.33 = f32[8,56,128]{2,1,0:T(8,128)S(1)} all-to-all(f32[8,56,128]{2,1,0:T(8,128)S(1)} %broadcast_in_dim.6), channel_id=1, replica_groups={{0,8,16,24,32,40,48,56},{1,9,17,25,33,41,49,57},{2,10,18,26,34,42,50,58..., dimensions={0} | all-to-all | bytes 458752 | tf_op jit(solution)/shard_map/all_to_all | solution.py:404
  132.6 10.3 %all_to_all.34.gathered = f32[4,408,128]{2,1,0:T(8,128)S(1)} all-to-all(f32[4,408,128]{2,1,0:T(8,128)S(1)} %broadcast_in_dim.7), channel_id=1, replica_groups={{0,2,4,6},{1,3,5,7},{8,10,12,14},{9,11,13,15},{16,18,20,22},{17,19,21,2..., dimensions={0} | all-to-all | bytes 1671168 | tf_op jit(solution)/shard_map/all_to_all | solution.py:404
  142.9 7.2 %all-gather.5 = f32[1600,128]{1,0:T(8,128)S(1)} all-gather(f32[800,128]{1,0:T(8,128)S(1)} %shard_map.44), channel_id=7, replica_groups={{0,1},{2,3},{4,5},{6,7},{8,9},{10,11},{12,13},{14,15},{16,17},{18,19},{..., dimensions={0}, use_global_device_ids=true | all-gather | bytes 1228800 | tf_op jit(solution)/shard_map/all_gather | solution.py:399
  150.1 2.2 %shard_map.45 = (f32[224,128]{1,0:T(8,128)S(1)}, f32[672,128]{1,0:T(8,128)S(1)}, f32[168,128]{1,0:T(8,128)S(1)}, f32[576,128]{1,0:T(8,128)S(1)}) custom-call(f32[4,408,128]{2,1,0:T(8,128)S(1)} %all_to_all.34.gathered, f32[2,800,128]{2,1,0:T(8,128)S(1)} %bitcast.30, f32[288,128]{1,0:T(8,128)S(1)} %get-tuple-element.41.held), custom_call_target="tpu_custom_call" | custom-call | flops 522190848 | bytes 1802240 | tf_op jit(solution)/shard_map/pallas_call | solution.py:369
  152.3 9.3 %all-gather.6 = f32[336,128]{1,0:T(8,128)S(1)} all-gather(f32[168,128]{1,0:T(8,128)S(1)} %get-tuple-element.43), channel_id=8, replica_groups={{0,64},{32,96},{128,192},{160,224},{256,320},{288,352},{384,448},{416,4..., dimensions={0}, use_global_device_ids=true | all-gather | bytes 258048 | tf_op jit(solution)/shard_map/all_gather | solution.py:399
  161.6 8.7 %all_to_all.35.sib = f32[4,168,128]{2,1,0:T(8,128)S(1)} all-to-all(f32[4,168,128]{2,1,0:T(8,128)S(1)} %shard_map.46), channel_id=1, replica_groups={{0,2,4,6},{1,3,5,7},{8,10,12,14},{9,11,13,15},{16,18,20,22},{17,19,21,2..., dimensions={0} | all-to-all | bytes 688128 | tf_op jit(solution)/shard_map/all_to_all | solution.py:404
  170.3 4.4 %all-gather.7 = f32[1216,128]{1,0:T(8,128)S(1)} all-gather(f32[608,128]{1,0:T(8,128)S(1)} %shard_map.47), channel_id=9, replica_groups={{0,1},{2,3},{4,5},{6,7},{8,9},{10,11},{12,13},{14,15},{16,17},{18,19},{..., dimensions={0}, use_global_device_ids=true | all-gather | bytes 933888 | tf_op jit(solution)/shard_map/all_gather | solution.py:399
  176.8 6.1 %all-gather.8 = f32[640,128]{1,0:T(8,128)S(1)} all-gather(f32[320,128]{1,0:T(8,128)S(1)} %get-tuple-element.46.own), channel_id=10, replica_groups={{0,128},{32,160},{64,192},{96,224},{256,384},{288,416},{320,448},{352,4..., dimensions={0}, use_global_device_ids=true | all-gather | bytes 491520 | tf_op jit(solution)/shard_map/all_gather | solution.py:399
  182.9 3.2 %all-gather.9 = f32[1600,128]{1,0:T(8,128)S(1)} all-gather(f32[800,128]{1,0:T(8,128)S(1)} %shard_map.49), channel_id=11, replica_groups={{0,1},{2,3},{4,5},{6,7},{8,9},{10,11},{12,13},{14,15},{16,17},{18,19},{..., dimensions={0}, use_global_device_ids=true | all-gather | bytes 1228800 | tf_op jit(solution)/shard_map/all_gather | solution.py:399
  188.1 6.2 %all-gather.10 = f32[384,128]{1,0:T(8,128)S(1)} all-gather(f32[192,128]{1,0:T(8,128)S(1)} %get-tuple-element.49), channel_id=12, replica_groups={{0,256},{32,288},{64,320},{96,352},{128,384},{160,416},{192,448},{224,4..., dimensions={0}, use_global_device_ids=true | all-gather | bytes 294912 | tf_op jit(solution)/shard_map/all_gather | solution.py:399
  194.3 2.4 %shard_map.51 = f32[64,128]{1,0:T(8,128)} custom-call(f32[2,192,128]{2,1,0:T(8,128)S(1)} %bitcast.36, f32[192,128]{1,0:T(8,128)S(1)} %get-tuple-element.50.carried), custom_call_target="tpu_custom_call" | custom-call | flops 232783872 | bytes 294912 | tf_op jit(solution)/shard_map/pallas_call | solution.py:369
  (25 shorter events, 10.9 us)
Async XLA Ops:
  1.3 11.1 %collective-permute-start = (f32[2112,128]{1,0:T(8,128)S(1)}, f32[2112,128]{1,0:T(8,128)S(1)}, u32[]{:S(2)}, u32[]{:S(2)}) collective-permute-start(f32[2112,128]{1,0:T(8,128)S(1)} %pad_maximum_fusion.mine), channel_id=1, source_target_pairs={{0,1},{1,0},{2,3},{3,2},{4,5},{5,4},{6,7},{7,6},{8,9},{9,8},{10,11... | collective-permute-start | bytes 3244040 | tf_op jit(solution)/shard_map/ppermute | solution.py:394

commit v11 on v10

--- a/solution.py
+++ b/solution.py
@@ -283,7 +283,7 @@
     z_out[...] = z
     node_out[...] = node
     n = part.shape[0]
-    part[...] = node_out[pl.ds(times8((lax.axis_index("gy") >> 1) & 3, n), n)]
+    part[...] = node_out[pl.ds(times8(((lax.axis_index("gy") >> 1) & 3) ^ 1, n), n)]
     swapped = [shared[c, 2 * half * count :] for c in range(2)]
     halves = [jnp.where(core == c, held[...], swapped[c]) for c in range(2)]
     carried[...] = interleaved(halves[0], halves[1], half)
@@ -394,9 +394,10 @@
     return lax.ppermute(value, "gy", [(s, s ^ 1) for s in range(lax.axis_size("gy"))])
 
 
-def pair_gather(value, axis, bit, tiled=False):
-    groups = bit_groups(lax.axis_size(axis), [bit])
-    return lax.all_gather(value, axis, axis_index_groups=groups, tiled=tiled)
+def pair_gather(value, axis, bit, also=()):
+    mask = sum(1 << b for b in (bit, *also))
+    groups = [[d, d ^ mask] for d in range(lax.axis_size(axis)) if not (d >> bit) & 1]
+    return lax.all_gather(value, axis, axis_index_groups=groups)
 
 
 def exchange(value, axis, bits):
@@ -482,7 +483,7 @@
     mine, other, sent = call(
         functools.partial(upper_kernel, 4, s_both),
         [(rest, rank), (rest, rank), (32, s_both + s_sums, rank)],
-        pair_gather(node, "gy", 4),
+        pair_gather(node, "gy", 4, (2, 3)),
         z_low,
         shared,
         held,
@@ -527,7 +528,7 @@
     count -= 1
     rows = 2 * rest
     near = call(
-        functools.partial(sibling_kernel, 1), [(4,) + part.shape], pair_gather(part, "gx", 1)
+        functools.partial(sibling_kernel, 1), [(4,) + part.shape], pair_gather(part, ("gx", "gy"), 6, (5, 1))
     )[0]
     near = exchange(near, "gy", near_chips)
     shared = call(
@@ -567,7 +568,7 @@
     return call(
         functools.partial(last_kernel, 3),
         [right_sides.shape[::-1]],
-        pair_gather(node, "gx", 3),
+        pair_gather(node, "gx", 3, (2,)),
         carried,
     )[0].T
 

time: 197 us -> 194 us (0.985)
  blocking collectives: 165 us -> 162 us
    all_gather x12, blocking collectives: 90.7 us -> 87.3 us  [pair_gather(): return lax.all_gather(value, axis, axis_index_groups=groups)]
where the time goes in v11:
time: 194 us
  blocking collectives  162 us (84%)
  Pallas kernels  18.9 us (10%)
  starting transfers between devices  8.79 us (5%)
  waiting for transfers between devices  2.31 us (1%)
    all_gather x12, blocking collectives, pair_gather(): return lax.all_gather(value, axis, axis_index_groups=groups)  87.3 us
    all_to_all x6, blocking collectives, exchange(): lax.all_to_all(value, axis, 0, 0, axis_index_groups=bit_groups(count, bits))  74.9 us
    pallas_call x15, Pallas kernels, call(): pl.pallas_call(kernel, out_shape=[jax.ShapeDtypeStruct(o, jnp.float32) fo...  18.9 us
    ppermute x1, starting transfers between devices, swap_cores(): lax.ppermute(value, 'gy', [(s, s ^ 1) for s in range(lax.axis_size('gy'))])  8.79 us
  transfers between devices with their start and end apart: 1, of which 1 were waited for; matrix products, arithmetic and copies ran while one was open for 0% of the time, Pallas kernels for 0%

profile of v11, /device:TPU:1, one launch (start us, length us, event | category | flops | bytes accessed | tf_op | source)
XLA Modules:
  0.0 193.9 jit_solution(16330193408657787871)
XLA Ops:
  1.3 8.8 %collective-permute-start = (f32[2112,128]{1,0:T(8,128)S(1)}, f32[2112,128]{1,0:T(8,128)S(1)}, u32[]{:S(2)}, u32[]{:S(2)}) collective-permute-start(f32[2112,128]{1,0:T(8,128)S(1)} %pad_maximum_fusion.mine), channel_id=1, source_target_pairs={{0,1},{1,0},{2,3},{3,2},{4,5},{5,4},{6,7},{7,6},{8,9},{9,8},{10,11... | collective-permute-start | bytes 3244040 | tf_op jit(solution)/shard_map/ppermute | solution.py:394
  10.1 2.3 %collective-permute-done.other = f32[2112,128]{1,0:T(8,128)S(1)} collective-permute-done((f32[2112,128]{1,0:T(8,128)S(1)}, f32[2112,128]{1,0:T(8,128)S(1)}, u32[]{:S(2)}, u32[]{:S(2)}) %collective-permute-start) | collective-permute-done | bytes 1081376 | tf_op jit(solution)/shard_map/ppermute | solution.py:394
  13.3 9.9 %all-gather = f32[1344,128]{1,0:T(8,128)S(1)} all-gather(f32[672,128]{1,0:T(8,128)S(1)} %get-tuple-element.28), channel_id=2, replica_groups={{0,2},{1,3},{4,6},{5,7},{8,10},{9,11},{12,14},{13,15},{16,18},{17,19},{..., dimensions={0}, use_global_device_ids=true | all-gather | bytes 1032192 | tf_op jit(solution)/shard_map/all_gather | solution.py:400
  25.3 7.6 %all-gather.1 = f32[1088,128]{1,0:T(8,128)S(1)} all-gather(f32[544,128]{1,0:T(8,128)S(1)} %get-tuple-element.30), channel_id=3, replica_groups={{0,2},{1,3},{4,6},{5,7},{8,10},{9,11},{12,14},{13,15},{16,18},{17,19},{..., dimensions={0}, use_global_device_ids=true | all-gather | bytes 835584 | tf_op jit(solution)/shard_map/all_gather | solution.py:400
  33.0 6.7 %all-gather.11 = f32[1088,128]{1,0:T(8,128)S(1)} all-gather(f32[544,128]{1,0:T(8,128)S(1)} %slice_add_fusion), channel_id=13, replica_groups={{0,4},{1,5},{2,6},{3,7},{8,12},{9,13},{10,14},{11,15},{16,20},{17,21},{..., dimensions={0}, use_global_device_ids=true | all-gather | bytes 835584 | tf_op jit(solution)/shard_map/all_gather | solution.py:400
  39.7 2.5 %shard_map.39 = (f32[416,256]{1,0:T(8,128)S(1)}, f32[4,208,128]{2,1,0:T(8,128)S(1)}) custom-call(f32[2,544,128]{2,1,0:T(8,128)S(1)} %bitcast.34, f32[544,128]{1,0:T(8,128)S(1)} %get-tuple-element.31.z_low, f32[672,256]{1,0:T(8,128)S(1)} %get-tuple-element.32.held, f32[2,256,128]{2,1,0:T(8,128)S(1)} %get-tuple-element.33.v), custom_call_target="tpu_custom_call" | custom-call | flops 519045120 | bytes 1785856 | tf_op jit(solution)/shard_map/pallas_call | solution.py:369
  42.2 8.1 %all_to_all.30 = f32[4,208,128]{2,1,0:T(8,128)S(1)} all-to-all(f32[4,208,128]{2,1,0:T(8,128)S(1)} %get-tuple-element.34), channel_id=1, replica_groups={{0,2,4,6},{1,3,5,7},{8,10,12,14},{9,11,13,15},{16,18,20,22},{17,19,21,2..., dimensions={0} | all-to-all | bytes 851968 | tf_op jit(solution)/shard_map/all_to_all | solution.py:405
  50.3 6.3 %all-gather.2 = f32[416,128]{1,0:T(8,128)S(1)} all-gather(f32[208,128]{1,0:T(8,128)S(1)} %reduce_sum.18), channel_id=4, replica_groups={{0,8},{1,9},{2,10},{3,11},{4,12},{5,13},{6,14},{7,15},{16,24},{17,25},{..., dimensions={0}, use_global_device_ids=true | all-gather | bytes 319488 | tf_op jit(solution)/shard_map/all_gather | solution.py:400
  56.6 9.5 %all_to_all.31.pieces = f32[4,328,128]{2,1,0:T(8,128)S(1)} all-to-all(f32[4,328,128]{2,1,0:T(8,128)S(1)} %shard_map.40), channel_id=1, replica_groups={{0,2,4,6},{1,3,5,7},{8,10,12,14},{9,11,13,15},{16,18,20,22},{17,19,21,2..., dimensions={0} | all-to-all | bytes 1343488 | tf_op jit(solution)/shard_map/all_to_all | solution.py:405
  66.1 8.4 %all-gather.3 = f32[1408,128]{1,0:T(8,128)S(1)} all-gather(f32[704,128]{1,0:T(8,128)S(1)} %shard_map.41), channel_id=5, replica_groups={{0,1},{2,3},{4,5},{6,7},{8,9},{10,11},{12,13},{14,15},{16,17},{18,19},{..., dimensions={0}, use_global_device_ids=true | all-gather | bytes 1081344 | tf_op jit(solution)/shard_map/all_gather | solution.py:400
  76.6 12.9 %all-gather.4 = f32[832,128]{1,0:T(8,128)S(1)} all-gather(f32[416,128]{1,0:T(8,128)S(1)} %get-tuple-element.36), channel_id=6, replica_groups={{0,28},{1,29},{2,30},{3,31},{4,24},{5,25},{6,26},{7,27},{8,20},{9,21},{..., dimensions={0}, use_global_device_ids=true | all-gather | bytes 638976 | tf_op jit(solution)/shard_map/all_gather | solution.py:400
  89.5 2.5 %shard_map.43 = (f32[288,128]{1,0:T(8,128)S(1)}, f32[288,128]{1,0:T(8,128)S(1)}, f32[32,40,128]{2,1,0:T(8,128)S(1)}) custom-call(f32[2,416,128]{2,1,0:T(8,128)S(1)} %bitcast.28, f32[416,128]{1,0:T(8,128)S(1)} %get-tuple-element.37.z_low, f32[2,704,128]{2,1,0:T(8,128)S(1)} %bitcast.27, f32[416,256]{1,0:T(8,128)S(1)} %get-tuple-element.35.rest, ...), custom_call_target="tpu_custom_call" | custom-call | flops 619708416 | bytes 2310144 | tf_op jit(solution)/shard_map/pallas_call | solution.py:369
  92.0 25.5 %all_to_all.32 = f32[32,40,128]{2,1,0:T(8,128)S(1)} all-to-all(f32[32,40,128]{2,1,0:T(8,128)S(1)} %get-tuple-element.39), channel_id=1, replica_groups={{0,2,4,6,8,10,12,14,16,18,20,22,24,26,28,30,32,34,36,38,40,42,44,46,48,..., dimensions={0} | all-to-all | bytes 1310720 | tf_op jit(solution)/shard_map/all_to_all | solution.py:405
  117.6 13.5 %all_to_all.33 = f32[8,56,128]{2,1,0:T(8,128)S(1)} all-to-all(f32[8,56,128]{2,1,0:T(8,128)S(1)} %broadcast_in_dim.6), channel_id=1, replica_groups={{0,8,16,24,32,40,48,56},{1,9,17,25,33,41,49,57},{2,10,18,26,34,42,50,58..., dimensions={0} | all-to-all | bytes 458752 | tf_op jit(solution)/shard_map/all_to_all | solution.py:405
  131.2 10.4 %all_to_all.34.gathered = f32[4,408,128]{2,1,0:T(8,128)S(1)} all-to-all(f32[4,408,128]{2,1,0:T(8,128)S(1)} %broadcast_in_dim.7), channel_id=1, replica_groups={{0,2,4,6},{1,3,5,7},{8,10,12,14},{9,11,13,15},{16,18,20,22},{17,19,21,2..., dimensions={0} | all-to-all | bytes 1671168 | tf_op jit(solution)/shard_map/all_to_all | solution.py:405
  141.7 7.5 %all-gather.5 = f32[1600,128]{1,0:T(8,128)S(1)} all-gather(f32[800,128]{1,0:T(8,128)S(1)} %shard_map.44), channel_id=7, replica_groups={{0,1},{2,3},{4,5},{6,7},{8,9},{10,11},{12,13},{14,15},{16,17},{18,19},{..., dimensions={0}, use_global_device_ids=true | all-gather | bytes 1228800 | tf_op jit(solution)/shard_map/all_gather | solution.py:400
  149.1 2.2 %shard_map.45 = (f32[224,128]{1,0:T(8,128)S(1)}, f32[672,128]{1,0:T(8,128)S(1)}, f32[168,128]{1,0:T(8,128)S(1)}, f32[576,128]{1,0:T(8,128)S(1)}) custom-call(f32[4,408,128]{2,1,0:T(8,128)S(1)} %all_to_all.34.gathered, f32[2,800,128]{2,1,0:T(8,128)S(1)} %bitcast.30, f32[288,128]{1,0:T(8,128)S(1)} %get-tuple-element.41.held), custom_call_target="tpu_custom_call" | custom-call | flops 522190848 | bytes 1802240 | tf_op jit(solution)/shard_map/pallas_call | solution.py:369
  151.3 8.8 %all-gather.6 = f32[336,128]{1,0:T(8,128)S(1)} all-gather(f32[168,128]{1,0:T(8,128)S(1)} %get-tuple-element.43), channel_id=8, replica_groups={{0,98},{1,99},{2,96},{3,97},{4,102},{5,103},{6,100},{7,101},{8,106},{9,..., dimensions={0}, use_global_device_ids=true | all-gather | bytes 258048 | tf_op jit(solution)/shard_map/all_gather | solution.py:400
  160.2 8.1 %all_to_all.35.sib = f32[4,168,128]{2,1,0:T(8,128)S(1)} all-to-all(f32[4,168,128]{2,1,0:T(8,128)S(1)} %shard_map.46), channel_id=1, replica_groups={{0,2,4,6},{1,3,5,7},{8,10,12,14},{9,11,13,15},{16,18,20,22},{17,19,21,2..., dimensions={0} | all-to-all | bytes 688128 | tf_op jit(solution)/shard_map/all_to_all | solution.py:405
  168.3 3.9 %all-gather.7 = f32[1216,128]{1,0:T(8,128)S(1)} all-gather(f32[608,128]{1,0:T(8,128)S(1)} %shard_map.47), channel_id=9, replica_groups={{0,1},{2,3},{4,5},{6,7},{8,9},{10,11},{12,13},{14,15},{16,17},{18,19},{..., dimensions={0}, use_global_device_ids=true | all-gather | bytes 933888 | tf_op jit(solution)/shard_map/all_gather | solution.py:400
  174.3 6.1 %all-gather.8 = f32[640,128]{1,0:T(8,128)S(1)} all-gather(f32[320,128]{1,0:T(8,128)S(1)} %get-tuple-element.46.own), channel_id=10, replica_groups={{0,128},{32,160},{64,192},{96,224},{256,384},{288,416},{320,448},{352,4..., dimensions={0}, use_global_device_ids=true | all-gather | bytes 491520 | tf_op jit(solution)/shard_map/all_gather | solution.py:400
  180.4 3.2 %all-gather.9 = f32[1600,128]{1,0:T(8,128)S(1)} all-gather(f32[800,128]{1,0:T(8,128)S(1)} %shard_map.49), channel_id=11, replica_groups={{0,1},{2,3},{4,5},{6,7},{8,9},{10,11},{12,13},{14,15},{16,17},{18,19},{..., dimensions={0}, use_global_device_ids=true | all-gather | bytes 1228800 | tf_op jit(solution)/shard_map/all_gather | solution.py:400
  185.6 5.9 %all-gather.10 = f32[384,128]{1,0:T(8,128)S(1)} all-gather(f32[192,128]{1,0:T(8,128)S(1)} %get-tuple-element.49), channel_id=12, replica_groups={{0,384},{32,416},{64,448},{96,480},{128,256},{160,288},{192,320},{224,3..., dimensions={0}, use_global_device_ids=true | all-gather | bytes 294912 | tf_op jit(solution)/shard_map/all_gather | solution.py:400
  191.5 2.4 %shard_map.51 = f32[64,128]{1,0:T(8,128)} custom-call(f32[2,192,128]{2,1,0:T(8,128)S(1)} %bitcast.36, f32[192,128]{1,0:T(8,128)S(1)} %get-tuple-element.50.carried), custom_call_target="tpu_custom_call" | custom-call | flops 232783872 | bytes 294912 | tf_op jit(solution)/shard_map/pallas_call | solution.py:369
  (25 shorter events, 10.9 us)
Async XLA Ops:
  1.3 11.1 %collective-permute-start = (f32[2112,128]{1,0:T(8,128)S(1)}, f32[2112,128]{1,0:T(8,128)S(1)}, u32[]{:S(2)}, u32[]{:S(2)}) collective-permute-start(f32[2112,128]{1,0:T(8,128)S(1)} %pad_maximum_fusion.mine), channel_id=1, source_target_pairs={{0,1},{1,0},{2,3},{3,2},{4,5},{5,4},{6,7},{7,6},{8,9},{9,8},{10,11... | collective-permute-start | bytes 3244040 | tf_op jit(solution)/shard_map/ppermute | solution.py:394

commit v12 on v11

--- a/solution.py
+++ b/solution.py
@@ -190,6 +190,16 @@
     node_out[...] = node
 
 
+def next_level_rows(rows, half):
+    both = jnp.concatenate([rows[0]] + [r[:half] for r in rows[1:]], axis=0)
+    return both, jnp.concatenate([r[half:] for r in rows[1:]], axis=0)
+
+
+def quarter(value, c):
+    n = value.shape[0] // 4
+    return value[c * n : (c + 1) * n]
+
+
 def upper_kernel(bit, s_both, pair, z_low, shared, rest, v, mine, other, sent):
     rank = v.shape[2]
     half = rank // 2
@@ -213,7 +223,11 @@
     parts = split(value)
     rows = [dot_split(parts, split(v[j])) for j in range(count)]
     both = jnp.concatenate([rows[0]] + [r[:half] for r in rows[1:]], axis=0)
-    sums = jnp.concatenate([r[half:] for r in rows[1:]], axis=0)
+    rest_rows = [r[half:] for r in rows[1:]]
+    next_both, next_sums = next_level_rows(rest_rows, half)
+    sums = jnp.concatenate(
+        [v for c in range(4) for v in (quarter(next_both, c), quarter(next_sums, c))], axis=0
+    )
     far = sent.shape[0] // 4
     for value, base, size in ((both, 0, s_both), (sums, s_both, sent.shape[1] - s_both)):
         n = value.shape[0] // 4
@@ -266,60 +280,45 @@
     return own, jnp.concatenate(ops, axis=0)
 
 
-def top_node_kernel(count, n_both, n_sums, gathered, shared, held, z_out, node_out, part, carried):
+def half_children(bit, count, n_both, width, gathered, shared):
+    half = gathered.shape[2] // 2
+    side = bit_of("gx", bit)
+    out = []
+    for which in (side, 1 - side):
+        both = get_rows(gathered, times8(which, n_both), n_both)
+        at = times8(which, half * count)
+        out.append(child_rows(shared, at, half, count, both[half:width]))
+    return out
+
+
+def top_node_kernel(count, n_both, gathered, shared, held, sums, z_out, part, carried, change):
     rank = held.shape[1]
     half = rank // 2
     width = held.shape[0]
     core = bit_of("gy", 0)
-    side = bit_of("gx", 0)
-    children = []
-    for which in (side, 1 - side):
-        both = get_rows(gathered, times8(which, n_both), n_both)
-        at = times8(which, half * count)
-        children.append(child_rows(shared, at, half, count, both[half:width]))
-    (own, ops_own), (sib, ops_sib) = children
-    sums = get_rows(gathered, 2 * n_both, n_sums)
-    z, node = solve_node(own, sib, ops_own, ops_sib, sums)
+    (own, ops_own), (sib, ops_sib) = half_children(0, count, n_both, width, gathered, shared)
+    nothing = jnp.zeros(change.shape, jnp.float32)
+    z, node = solve_node(own, sib, ops_own, ops_sib, nothing)
     z_out[...] = z
-    node_out[...] = node
-    n = part.shape[0]
-    part[...] = node_out[pl.ds(times8(((lax.axis_index("gy") >> 1) & 3) ^ 1, n), n)]
+    w = width - half
+    both, rest = next_level_rows([node[j * w : (j + 1) * w] for j in range(count - 1)], half)
+    change[: both.shape[0]] = both
+    change[both.shape[0] :] = rest
+    at = (lax.axis_index("gy") >> 1) & 3
+    n, m = both.shape[0] // 4, rest.shape[0] // 4
+    part[:n] = sums[:n] + change[pl.ds(times8(at, n), n)]
+    part[n:] = sums[n:] + change[pl.ds(both.shape[0] + times8(at, m), m)]
     swapped = [shared[c, 2 * half * count :] for c in range(2)]
     halves = [jnp.where(core == c, held[...], swapped[c]) for c in range(2)]
     carried[...] = interleaved(halves[0], halves[1], half)
 
 
-def sibling_kernel(bit, pair, out):
-    value = pair[1 - bit_of("gx", bit)]
-    for i in range(out.shape[0]):
-        out[i] = value
-
-
-def quarter_shared_kernel(count, own, sib, z, out):
-    half = out.shape[1] // 2
-    width = own.shape[0] // count
-    value = sib[...].reshape(own.shape)
-    for j in range(count):
-        at = slice(j * width, j * width + half)
-        out[j * half : (j + 1) * half] = own[at]
-        out[(count + j) * half : (count + j + 1) * half] = value[at]
-    out[2 * count * half :] = z[...]
-
-
-def quarter_node_kernel(count, own, sib, shared, carried, z_out, node_out, new):
-    half = own.shape[1] // 2
-    width = own.shape[0] // count
-    here, there = own[...], sib[...].reshape(own.shape)
-    rows_own, ops_own = child_rows(shared, 0, half, count, here[half:width])
-    rows_sib, ops_sib = child_rows(shared, half * count, half, count, there[half:width])
-    sums = jnp.concatenate(
-        [
-            here[j * width + half : (j + 1) * width] + there[j * width + half : (j + 1) * width]
-            for j in range(1, count)
-        ],
-        axis=0,
-    )
-    z, node = solve_node(rows_own, rows_sib, ops_own, ops_sib, sums)
+def quarter_node_kernel(count, n_both, gathered, shared, carried, z_out, node_out, new):
+    half = gathered.shape[2] // 2
+    width = z_out.shape[0] + half
+    (own, ops_own), (sib, ops_sib) = half_children(1, count, n_both, width, gathered, shared)
+    sums = get_rows(gathered, 2 * n_both, gathered.shape[1] - 2 * n_both)
+    z, node = solve_node(own, sib, ops_own, ops_sib, sums)
     z_out[...] = z
     node_out[...] = node
     below = both_cores(shared, 2 * count * half, shared.shape[1] - 2 * count * half)
@@ -483,7 +482,7 @@
     mine, other, sent = call(
         functools.partial(upper_kernel, 4, s_both),
         [(rest, rank), (rest, rank), (32, s_both + s_sums, rank)],
-        pair_gather(node, "gy", 4, (2, 3)),
+        pair_gather(node, "gy", 4, (3,)),
         z_low,
         shared,
         held,
@@ -500,11 +499,11 @@
         [
             pieces[:, :s_both].reshape(-1, rank)[:n_both],
             pieces[:, s_both : 2 * s_both].reshape(-1, rank)[:n_both],
-            pieces[:, 2 * s_both :].reshape(-1, rank)[:n_sums],
         ],
         axis=0,
     )
     gathered = to_all(share, "gy", near_chips)
+    sums = pieces[:, 2 * s_both :].reshape(-1, rank)[:n_sums]
     shared = call(
         functools.partial(top_shared_kernel, n_both, rest),
         [(2 * count * half + rest, rank)],
@@ -512,39 +511,36 @@
         other,
     )[0]
     width = rest - half
-    z, node, part, carried = call(
-        functools.partial(top_node_kernel, count, n_both, n_sums),
-        [
-            (width, rank),
-            ((count - 1) * width, rank),
-            ((count - 1) * width // 4, rank),
-            (2 * rest, rank),
-        ],
+    rows = 2 * rest
+    z, part, carried, _ = call(
+        functools.partial(top_node_kernel, count, n_both),
+        [(width, rank), (n_sums, rank), (rows, rank), (4 * n_sums, rank)],
         gathered,
         pair_gather(shared, "gy", 0),
         mine,
+        sums,
     )
 
     count -= 1
-    rows = 2 * rest
-    near = call(
-        functools.partial(sibling_kernel, 1), [(4,) + part.shape], pair_gather(part, ("gx", "gy"), 6, (5, 1))
+    n_both = (width + (count - 1) * half) // 4
+    share = call(
+        functools.partial(share_kernel, n_both),
+        [(4, n_both + n_sums, rank)],
+        pair_gather(part, ("gx", "gy"), 6, (5,)),
     )[0]
-    near = exchange(near, "gy", near_chips)
+    gathered = exchange(share, "gy", near_chips)
     shared = call(
-        functools.partial(quarter_shared_kernel, count),
+        functools.partial(top_shared_kernel, n_both, width),
         [(2 * count * half + width, rank)],
-        node,
-        near,
+        gathered,
         z,
     )[0]
     width -= half
     rows -= rank
     z, node, carried = call(
-        functools.partial(quarter_node_kernel, count),
+        functools.partial(quarter_node_kernel, count, n_both),
         [(width, rank), ((count - 1) * width, rank), (rows, rank)],
-        node,
-        near,
+        gathered,
         pair_gather(shared, "gy", 0),
         carried,
     )

time: 194 us -> 197 us (1.015)
  blocking collectives: 162 us -> 154 us
  waiting for transfers between devices: 2.31 us -> 7.56 us
  starting transfers between devices: 8.79 us -> 12.3 us
    all_to_all x0 -> x1, waiting for transfers between devices: none -> 5.25 us  [exchange(): lax.all_to_all(value, axis, 0, 0, axis_index_groups=bit_groups(count, bits))]
    all_gather x12, blocking collectives: 87.3 us -> 82.4 us  [pair_gather(): return lax.all_gather(value, axis, axis_index_groups=groups)]
    all_to_all x0 -> x1, starting transfers between devices: none -> 3.47 us  [exchange(): lax.all_to_all(value, axis, 0, 0, axis_index_groups=bit_groups(count, bits))]
    all_to_all x6 -> x5, blocking collectives: 74.9 us -> 72.1 us  [exchange(): lax.all_to_all(value, axis, 0, 0, axis_index_groups=bit_groups(count, bits))]
  transfers between devices with their start and end apart: 1 -> 2, of which waited for: 1 -> 2; matrix products, arithmetic and copies ran while one was open for 0% -> 0% of each run, Pallas kernels for 0% -> 0%
where the time goes in v12:
time: 197 us; the launch traced here: 196 us
  blocking collectives  154 us (78%)
  Pallas kernels  19.6 us (10%)
  starting transfers between devices  12.3 us (6%)
  waiting for transfers between devices  7.56 us (4%)
    all_gather x12, blocking collectives, pair_gather(): return lax.all_gather(value, axis, axis_index_groups=groups)  82.4 us
    all_to_all x5, blocking collectives, exchange(): lax.all_to_all(value, axis, 0, 0, axis_index_groups=bit_groups(count, bits))  72.1 us
    pallas_call x15, Pallas kernels, call(): pl.pallas_call(kernel, out_shape=[jax.ShapeDtypeStruct(o, jnp.float32) fo...  19.6 us
    ppermute x1, starting transfers between devices, swap_cores(): lax.ppermute(value, 'gy', [(s, s ^ 1) for s in range(lax.axis_size('gy'))])  8.79 us
    all_to_all x1, waiting for transfers between devices, exchange(): lax.all_to_all(value, axis, 0, 0, axis_index_groups=bit_groups(count, bits))  5.25 us
  transfers between devices with their start and end apart: 2, of which 2 were waited for; matrix products, arithmetic and copies ran while one was open for 0% of the time, Pallas kernels for 0%

profile of v12, /device:TPU:1, one launch (start us, length us, event | category | flops | bytes accessed | tf_op | source)
XLA Modules:
  0.0 196.3 jit_solution(16558173153389463893)
XLA Ops:
  1.3 8.8 %collective-permute-start = (f32[2112,128]{1,0:T(8,128)S(1)}, f32[2112,128]{1,0:T(8,128)S(1)}, u32[]{:S(2)}, u32[]{:S(2)}) collective-permute-start(f32[2112,128]{1,0:T(8,128)S(1)} %pad_maximum_fusion.mine), channel_id=1, source_target_pairs={{0,1},{1,0},{2,3},{3,2},{4,5},{5,4},{6,7},{7,6},{8,9},{9,8},{10,11... | collective-permute-start | bytes 3244040 | tf_op jit(solution)/shard_map/ppermute | solution.py:393
  13.3 9.9 %all-gather = f32[1344,128]{1,0:T(8,128)S(1)} all-gather(f32[672,128]{1,0:T(8,128)S(1)} %get-tuple-element.27), channel_id=2, replica_groups={{0,2},{1,3},{4,6},{5,7},{8,10},{9,11},{12,14},{13,15},{16,18},{17,19},{..., dimensions={0}, use_global_device_ids=true | all-gather | bytes 1032192 | tf_op jit(solution)/shard_map/all_gather | solution.py:399
  25.3 7.6 %all-gather.1 = f32[1088,128]{1,0:T(8,128)S(1)} all-gather(f32[544,128]{1,0:T(8,128)S(1)} %get-tuple-element.29), channel_id=3, replica_groups={{0,2},{1,3},{4,6},{5,7},{8,10},{9,11},{12,14},{13,15},{16,18},{17,19},{..., dimensions={0}, use_global_device_ids=true | all-gather | bytes 835584 | tf_op jit(solution)/shard_map/all_gather | solution.py:399
  33.0 6.7 %all-gather.11 = f32[1088,128]{1,0:T(8,128)S(1)} all-gather(f32[544,128]{1,0:T(8,128)S(1)} %slice_add_fusion), channel_id=13, replica_groups={{0,4},{1,5},{2,6},{3,7},{8,12},{9,13},{10,14},{11,15},{16,20},{17,21},{..., dimensions={0}, use_global_device_ids=true | all-gather | bytes 835584 | tf_op jit(solution)/shard_map/all_gather | solution.py:399
  39.7 2.5 %shard_map.39 = (f32[416,256]{1,0:T(8,128)S(1)}, f32[4,208,128]{2,1,0:T(8,128)S(1)}) custom-call(f32[2,544,128]{2,1,0:T(8,128)S(1)} %bitcast.34, f32[544,128]{1,0:T(8,128)S(1)} %get-tuple-element.30.z_low, f32[672,256]{1,0:T(8,128)S(1)} %get-tuple-element.31.held, f32[2,256,128]{2,1,0:T(8,128)S(1)} %get-tuple-element.32.v), custom_call_target="tpu_custom_call" | custom-call | flops 519045120 | bytes 1785856 | tf_op jit(solution)/shard_map/pallas_call | solution.py:368
  42.2 8.1 %all_to_all.30 = f32[4,208,128]{2,1,0:T(8,128)S(1)} all-to-all(f32[4,208,128]{2,1,0:T(8,128)S(1)} %get-tuple-element.33), channel_id=1, replica_groups={{0,2,4,6},{1,3,5,7},{8,10,12,14},{9,11,13,15},{16,18,20,22},{17,19,21,2..., dimensions={0} | all-to-all | bytes 851968 | tf_op jit(solution)/shard_map/all_to_all | solution.py:404
  50.3 6.3 %all-gather.2 = f32[416,128]{1,0:T(8,128)S(1)} all-gather(f32[208,128]{1,0:T(8,128)S(1)} %reduce_sum.18), channel_id=4, replica_groups={{0,8},{1,9},{2,10},{3,11},{4,12},{5,13},{6,14},{7,15},{16,24},{17,25},{..., dimensions={0}, use_global_device_ids=true | all-gather | bytes 319488 | tf_op jit(solution)/shard_map/all_gather | solution.py:399
  56.6 9.5 %all_to_all.31.pieces = f32[4,328,128]{2,1,0:T(8,128)S(1)} all-to-all(f32[4,328,128]{2,1,0:T(8,128)S(1)} %shard_map.40), channel_id=1, replica_groups={{0,2,4,6},{1,3,5,7},{8,10,12,14},{9,11,13,15},{16,18,20,22},{17,19,21,2..., dimensions={0} | all-to-all | bytes 1343488 | tf_op jit(solution)/shard_map/all_to_all | solution.py:404
  66.1 8.4 %all-gather.3 = f32[1408,128]{1,0:T(8,128)S(1)} all-gather(f32[704,128]{1,0:T(8,128)S(1)} %shard_map.41), channel_id=5, replica_groups={{0,1},{2,3},{4,5},{6,7},{8,9},{10,11},{12,13},{14,15},{16,17},{18,19},{..., dimensions={0}, use_global_device_ids=true | all-gather | bytes 1081344 | tf_op jit(solution)/shard_map/all_gather | solution.py:399
  76.6 10.2 %all-gather.4 = f32[832,128]{1,0:T(8,128)S(1)} all-gather(f32[416,128]{1,0:T(8,128)S(1)} %get-tuple-element.35), channel_id=6, replica_groups={{0,24},{1,25},{2,26},{3,27},{4,28},{5,29},{6,30},{7,31},{8,16},{9,17},{..., dimensions={0}, use_global_device_ids=true | all-gather | bytes 638976 | tf_op jit(solution)/shard_map/all_gather | solution.py:399
  86.8 2.5 %shard_map.43 = (f32[288,128]{1,0:T(8,128)S(1)}, f32[288,128]{1,0:T(8,128)S(1)}, f32[32,40,128]{2,1,0:T(8,128)S(1)}) custom-call(f32[2,416,128]{2,1,0:T(8,128)S(1)} %bitcast.28, f32[416,128]{1,0:T(8,128)S(1)} %get-tuple-element.36.z_low, f32[2,704,128]{2,1,0:T(8,128)S(1)} %bitcast.27, f32[416,256]{1,0:T(8,128)S(1)} %get-tuple-element.34.rest, ...), custom_call_target="tpu_custom_call" | custom-call | flops 619708416 | bytes 2310144 | tf_op jit(solution)/shard_map/pallas_call | solution.py:368
  89.3 28.7 %all_to_all.32 = f32[32,40,128]{2,1,0:T(8,128)S(1)} all-to-all(f32[32,40,128]{2,1,0:T(8,128)S(1)} %get-tuple-element.38), channel_id=1, replica_groups={{0,2,4,6,8,10,12,14,16,18,20,22,24,26,28,30,32,34,36,38,40,42,44,46,48,..., dimensions={0} | all-to-all | bytes 1310720 | tf_op jit(solution)/shard_map/all_to_all | solution.py:404
  118.0 14.0 %all_to_all.33 = f32[8,56,128]{2,1,0:T(8,128)S(1)} all-to-all(f32[8,56,128]{2,1,0:T(8,128)S(1)} %broadcast_in_dim.6), channel_id=1, replica_groups={{0,8,16,24,32,40,48,56},{1,9,17,25,33,41,49,57},{2,10,18,26,34,42,50,58..., dimensions={0} | all-to-all | bytes 458752 | tf_op jit(solution)/shard_map/all_to_all | solution.py:404
  132.9 3.5 %all-to-all-start.4 = ((f32[4,240,128]{2,1,0:T(8,128)}), f32[4,240,128]{2,1,0:T(8,128)S(1)}, u32[]{:S(2)}, u32[]{:S(2)}) async-start(f32[4,240,128]{2,1,0:T(8,128)} %broadcast_in_dim.7), calls=%async_computation.4 | async-start | bytes 983040 | tf_op jit(solution)/shard_map/all_to_all | solution.py:404
  136.4 5.2 %all-to-all-done.4.gathered = f32[4,240,128]{2,1,0:T(8,128)S(1)} async-done(((f32[4,240,128]{2,1,0:T(8,128)}), f32[4,240,128]{2,1,0:T(8,128)S(1)}, u32[]{:S(2)}, u32[]{:S(2)}) %all-to-all-start.4) | async-done | bytes 491552 | tf_op jit(solution)/shard_map/all_to_all | solution.py:404
  141.7 6.5 %all-gather.5 = f32[1600,128]{1,0:T(8,128)S(1)} all-gather(f32[800,128]{1,0:T(8,128)S(1)} %shard_map.44), channel_id=7, replica_groups={{0,1},{2,3},{4,5},{6,7},{8,9},{10,11},{12,13},{14,15},{16,17},{18,19},{..., dimensions={0}, use_global_device_ids=true | all-gather | bytes 1228800 | tf_op jit(solution)/shard_map/all_gather | solution.py:399
  148.2 2.9 %shard_map.45 = (f32[224,128]{1,0:T(8,128)S(1)}, f32[168,128]{1,0:T(8,128)S(1)}, f32[576,128]{1,0:T(8,128)S(1)}, f32[672,128]{1,0:T(8,128)}) custom-call(f32[4,240,128]{2,1,0:T(8,128)S(1)} %all-to-all-done.4.gathered, f32[2,800,128]{2,1,0:T(8,128)S(1)} %bitcast.30, f32[288,128]{1,0:T(8,128)S(1)} %get-tuple-element.40.held, f32[168,128]{1,0:T(8,128)S(1)} %bitcast.38), custom_call_target="tpu_custom_call" | custom-call | flops 472645632 | bytes 1544192 | tf_op jit(solution)/shard_map/pallas_call | solution.py:368
  151.1 7.6 %all-gather.6 = f32[336,128]{1,0:T(8,128)S(1)} all-gather(f32[168,128]{1,0:T(8,128)S(1)} %get-tuple-element.41), channel_id=8, replica_groups={{0,96},{1,97},{2,98},{3,99},{4,100},{5,101},{6,102},{7,103},{8,104},{9,..., dimensions={0}, use_global_device_ids=true | all-gather | bytes 258048 | tf_op jit(solution)/shard_map/all_gather | solution.py:399
  158.7 11.8 %all_to_all.34.gathered = f32[4,256,128]{2,1,0:T(8,128)S(1)} all-to-all(f32[4,256,128]{2,1,0:T(8,128)S(1)} %shard_map.46), channel_id=1, replica_groups={{0,2,4,6},{1,3,5,7},{8,10,12,14},{9,11,13,15},{16,18,20,22},{17,19,21,2..., dimensions={0} | all-to-all | bytes 1048576 | tf_op jit(solution)/shard_map/all_to_all | solution.py:404
  170.5 4.0 %all-gather.7 = f32[1216,128]{1,0:T(8,128)S(1)} all-gather(f32[608,128]{1,0:T(8,128)S(1)} %shard_map.47), channel_id=9, replica_groups={{0,1},{2,3},{4,5},{6,7},{8,9},{10,11},{12,13},{14,15},{16,17},{18,19},{..., dimensions={0}, use_global_device_ids=true | all-gather | bytes 933888 | tf_op jit(solution)/shard_map/all_gather | solution.py:399
  176.7 6.1 %all-gather.8 = f32[640,128]{1,0:T(8,128)S(1)} all-gather(f32[320,128]{1,0:T(8,128)S(1)} %get-tuple-element.44.own), channel_id=10, replica_groups={{0,128},{32,160},{64,192},{96,224},{256,384},{288,416},{320,448},{352,4..., dimensions={0}, use_global_device_ids=true | all-gather | bytes 491520 | tf_op jit(solution)/shard_map/all_gather | solution.py:399
  182.8 3.2 %all-gather.9 = f32[1600,128]{1,0:T(8,128)S(1)} all-gather(f32[800,128]{1,0:T(8,128)S(1)} %shard_map.49), channel_id=11, replica_groups={{0,1},{2,3},{4,5},{6,7},{8,9},{10,11},{12,13},{14,15},{16,17},{18,19},{..., dimensions={0}, use_global_device_ids=true | all-gather | bytes 1228800 | tf_op jit(solution)/shard_map/all_gather | solution.py:399
  188.0 5.9 %all-gather.10 = f32[384,128]{1,0:T(8,128)S(1)} all-gather(f32[192,128]{1,0:T(8,128)S(1)} %get-tuple-element.47), channel_id=12, replica_groups={{0,384},{32,416},{64,448},{96,480},{128,256},{160,288},{192,320},{224,3..., dimensions={0}, use_global_device_ids=true | all-gather | bytes 294912 | tf_op jit(solution)/shard_map/all_gather | solution.py:399
  193.9 2.4 %shard_map.51 = f32[64,128]{1,0:T(8,128)} custom-call(f32[2,192,128]{2,1,0:T(8,128)S(1)} %bitcast.36, f32[192,128]{1,0:T(8,128)S(1)} %get-tuple-element.48.carried), custom_call_target="tpu_custom_call" | custom-call | flops 232783872 | bytes 294912 | tf_op jit(solution)/shard_map/pallas_call | solution.py:368
  (26 shorter events, 13.9 us)
Async XLA Ops:
  1.3 11.1 %collective-permute-start = (f32[2112,128]{1,0:T(8,128)S(1)}, f32[2112,128]{1,0:T(8,128)S(1)}, u32[]{:S(2)}, u32[]{:S(2)}) collective-permute-start(f32[2112,128]{1,0:T(8,128)S(1)} %pad_maximum_fusion.mine), channel_id=1, source_target_pairs={{0,1},{1,0},{2,3},{3,2},{4,5},{5,4},{6,7},{7,6},{8,9},{9,8},{10,11... | collective-permute-start | bytes 3244040 | tf_op jit(solution)/shard_map/ppermute | solution.py:393
  132.9 8.7 %all-to-all-start.4 = ((f32[4,240,128]{2,1,0:T(8,128)}), f32[4,240,128]{2,1,0:T(8,128)S(1)}, u32[]{:S(2)}, u32[]{:S(2)}) async-start(f32[4,240,128]{2,1,0:T(8,128)} %broadcast_in_dim.7), calls=%async_computation.4 | async-start | bytes 983040 | tf_op jit(solution)/shard_map/all_to_all | solution.py:404

commit v13 on v11

--- a/solution.py
+++ b/solution.py
@@ -283,7 +283,7 @@
     z_out[...] = z
     node_out[...] = node
     n = part.shape[0]
-    part[...] = node_out[pl.ds(times8(((lax.axis_index("gy") >> 1) & 3) ^ 1, n), n)]
+    part[...] = node_out[pl.ds(times8((lax.axis_index("gy") >> 1) & 3, n), n)]
     swapped = [shared[c, 2 * half * count :] for c in range(2)]
     halves = [jnp.where(core == c, held[...], swapped[c]) for c in range(2)]
     carried[...] = interleaved(halves[0], halves[1], half)
@@ -483,7 +483,7 @@
     mine, other, sent = call(
         functools.partial(upper_kernel, 4, s_both),
         [(rest, rank), (rest, rank), (32, s_both + s_sums, rank)],
-        pair_gather(node, "gy", 4, (2, 3)),
+        pair_gather(node, "gy", 4, (3,)),
         z_low,
         shared,
         held,
@@ -528,7 +528,7 @@
     count -= 1
     rows = 2 * rest
     near = call(
-        functools.partial(sibling_kernel, 1), [(4,) + part.shape], pair_gather(part, ("gx", "gy"), 6, (5, 1))
+        functools.partial(sibling_kernel, 1), [(4,) + part.shape], pair_gather(part, "gx", 1, (0,))
     )[0]
     near = exchange(near, "gy", near_chips)
     shared = call(

time: 194 us -> 195 us (level)
    all_to_all x6, blocking collectives: 74.9 us -> 78.6 us  [exchange(): lax.all_to_all(value, axis, 0, 0, axis_index_groups=bit_groups(count, bits))]
    all_gather x12, blocking collectives: 87.3 us -> 84.6 us  [pair_gather(): return lax.all_gather(value, axis, axis_index_groups=groups)]
where the time goes in v13:
time: 195 us
  blocking collectives  163 us (84%)
  Pallas kernels  18.9 us (10%)
  starting transfers between devices  8.79 us (5%)
  waiting for transfers between devices  2.31 us (1%)
    all_gather x12, blocking collectives, pair_gather(): return lax.all_gather(value, axis, axis_index_groups=groups)  84.6 us
    all_to_all x6, blocking collectives, exchange(): lax.all_to_all(value, axis, 0, 0, axis_index_groups=bit_groups(count, bits))  78.6 us
    pallas_call x15, Pallas kernels, call(): pl.pallas_call(kernel, out_shape=[jax.ShapeDtypeStruct(o, jnp.float32) fo...  18.9 us
    ppermute x1, starting transfers between devices, swap_cores(): lax.ppermute(value, 'gy', [(s, s ^ 1) for s in range(lax.axis_size('gy'))])  8.79 us
  transfers between devices with their start and end apart: 1, of which 1 were waited for; matrix products, arithmetic and copies ran while one was open for 0% of the time, Pallas kernels for 0%

profile of v13, /device:TPU:1, one launch (start us, length us, event | category | flops | bytes accessed | tf_op | source)
XLA Modules:
  0.0 194.8 jit_solution(13801809817649619369)
XLA Ops:
  1.3 8.8 %collective-permute-start = (f32[2112,128]{1,0:T(8,128)S(1)}, f32[2112,128]{1,0:T(8,128)S(1)}, u32[]{:S(2)}, u32[]{:S(2)}) collective-permute-start(f32[2112,128]{1,0:T(8,128)S(1)} %pad_maximum_fusion.mine), channel_id=1, source_target_pairs={{0,1},{1,0},{2,3},{3,2},{4,5},{5,4},{6,7},{7,6},{8,9},{9,8},{10,11... | collective-permute-start | bytes 3244040 | tf_op jit(solution)/shard_map/ppermute | solution.py:394
  10.1 2.3 %collective-permute-done.other = f32[2112,128]{1,0:T(8,128)S(1)} collective-permute-done((f32[2112,128]{1,0:T(8,128)S(1)}, f32[2112,128]{1,0:T(8,128)S(1)}, u32[]{:S(2)}, u32[]{:S(2)}) %collective-permute-start) | collective-permute-done | bytes 1081376 | tf_op jit(solution)/shard_map/ppermute | solution.py:394
  13.3 9.9 %all-gather = f32[1344,128]{1,0:T(8,128)S(1)} all-gather(f32[672,128]{1,0:T(8,128)S(1)} %get-tuple-element.28), channel_id=2, replica_groups={{0,2},{1,3},{4,6},{5,7},{8,10},{9,11},{12,14},{13,15},{16,18},{17,19},{..., dimensions={0}, use_global_device_ids=true | all-gather | bytes 1032192 | tf_op jit(solution)/shard_map/all_gather | solution.py:400
  25.3 7.6 %all-gather.1 = f32[1088,128]{1,0:T(8,128)S(1)} all-gather(f32[544,128]{1,0:T(8,128)S(1)} %get-tuple-element.30), channel_id=3, replica_groups={{0,2},{1,3},{4,6},{5,7},{8,10},{9,11},{12,14},{13,15},{16,18},{17,19},{..., dimensions={0}, use_global_device_ids=true | all-gather | bytes 835584 | tf_op jit(solution)/shard_map/all_gather | solution.py:400
  33.0 6.7 %all-gather.11 = f32[1088,128]{1,0:T(8,128)S(1)} all-gather(f32[544,128]{1,0:T(8,128)S(1)} %slice_add_fusion), channel_id=13, replica_groups={{0,4},{1,5},{2,6},{3,7},{8,12},{9,13},{10,14},{11,15},{16,20},{17,21},{..., dimensions={0}, use_global_device_ids=true | all-gather | bytes 835584 | tf_op jit(solution)/shard_map/all_gather | solution.py:400
  39.7 2.5 %shard_map.39 = (f32[416,256]{1,0:T(8,128)S(1)}, f32[4,208,128]{2,1,0:T(8,128)S(1)}) custom-call(f32[2,544,128]{2,1,0:T(8,128)S(1)} %bitcast.34, f32[544,128]{1,0:T(8,128)S(1)} %get-tuple-element.31.z_low, f32[672,256]{1,0:T(8,128)S(1)} %get-tuple-element.32.held, f32[2,256,128]{2,1,0:T(8,128)S(1)} %get-tuple-element.33.v), custom_call_target="tpu_custom_call" | custom-call | flops 519045120 | bytes 1785856 | tf_op jit(solution)/shard_map/pallas_call | solution.py:369
  42.2 8.1 %all_to_all.30 = f32[4,208,128]{2,1,0:T(8,128)S(1)} all-to-all(f32[4,208,128]{2,1,0:T(8,128)S(1)} %get-tuple-element.34), channel_id=1, replica_groups={{0,2,4,6},{1,3,5,7},{8,10,12,14},{9,11,13,15},{16,18,20,22},{17,19,21,2..., dimensions={0} | all-to-all | bytes 851968 | tf_op jit(solution)/shard_map/all_to_all | solution.py:405
  50.3 6.3 %all-gather.2 = f32[416,128]{1,0:T(8,128)S(1)} all-gather(f32[208,128]{1,0:T(8,128)S(1)} %reduce_sum.18), channel_id=4, replica_groups={{0,8},{1,9},{2,10},{3,11},{4,12},{5,13},{6,14},{7,15},{16,24},{17,25},{..., dimensions={0}, use_global_device_ids=true | all-gather | bytes 319488 | tf_op jit(solution)/shard_map/all_gather | solution.py:400
  56.6 9.5 %all_to_all.31.pieces = f32[4,328,128]{2,1,0:T(8,128)S(1)} all-to-all(f32[4,328,128]{2,1,0:T(8,128)S(1)} %shard_map.40), channel_id=1, replica_groups={{0,2,4,6},{1,3,5,7},{8,10,12,14},{9,11,13,15},{16,18,20,22},{17,19,21,2..., dimensions={0} | all-to-all | bytes 1343488 | tf_op jit(solution)/shard_map/all_to_all | solution.py:405
  66.1 8.4 %all-gather.3 = f32[1408,128]{1,0:T(8,128)S(1)} all-gather(f32[704,128]{1,0:T(8,128)S(1)} %shard_map.41), channel_id=5, replica_groups={{0,1},{2,3},{4,5},{6,7},{8,9},{10,11},{12,13},{14,15},{16,17},{18,19},{..., dimensions={0}, use_global_device_ids=true | all-gather | bytes 1081344 | tf_op jit(solution)/shard_map/all_gather | solution.py:400
  76.6 10.2 %all-gather.4 = f32[832,128]{1,0:T(8,128)S(1)} all-gather(f32[416,128]{1,0:T(8,128)S(1)} %get-tuple-element.36), channel_id=6, replica_groups={{0,24},{1,25},{2,26},{3,27},{4,28},{5,29},{6,30},{7,31},{8,16},{9,17},{..., dimensions={0}, use_global_device_ids=true | all-gather | bytes 638976 | tf_op jit(solution)/shard_map/all_gather | solution.py:400
  86.8 2.5 %shard_map.43 = (f32[288,128]{1,0:T(8,128)S(1)}, f32[288,128]{1,0:T(8,128)S(1)}, f32[32,40,128]{2,1,0:T(8,128)S(1)}) custom-call(f32[2,416,128]{2,1,0:T(8,128)S(1)} %bitcast.28, f32[416,128]{1,0:T(8,128)S(1)} %get-tuple-element.37.z_low, f32[2,704,128]{2,1,0:T(8,128)S(1)} %bitcast.27, f32[416,256]{1,0:T(8,128)S(1)} %get-tuple-element.35.rest, ...), custom_call_target="tpu_custom_call" | custom-call | flops 619708416 | bytes 2310144 | tf_op jit(solution)/shard_map/pallas_call | solution.py:369
  89.3 28.7 %all_to_all.32 = f32[32,40,128]{2,1,0:T(8,128)S(1)} all-to-all(f32[32,40,128]{2,1,0:T(8,128)S(1)} %get-tuple-element.39), channel_id=1, replica_groups={{0,2,4,6,8,10,12,14,16,18,20,22,24,26,28,30,32,34,36,38,40,42,44,46,48,..., dimensions={0} | all-to-all | bytes 1310720 | tf_op jit(solution)/shard_map/all_to_all | solution.py:405
  118.0 14.0 %all_to_all.33 = f32[8,56,128]{2,1,0:T(8,128)S(1)} all-to-all(f32[8,56,128]{2,1,0:T(8,128)S(1)} %broadcast_in_dim.6), channel_id=1, replica_groups={{0,8,16,24,32,40,48,56},{1,9,17,25,33,41,49,57},{2,10,18,26,34,42,50,58..., dimensions={0} | all-to-all | bytes 458752 | tf_op jit(solution)/shard_map/all_to_all | solution.py:405
  132.2 10.3 %all_to_all.34.gathered = f32[4,408,128]{2,1,0:T(8,128)S(1)} all-to-all(f32[4,408,128]{2,1,0:T(8,128)S(1)} %broadcast_in_dim.7), channel_id=1, replica_groups={{0,2,4,6},{1,3,5,7},{8,10,12,14},{9,11,13,15},{16,18,20,22},{17,19,21,2..., dimensions={0} | all-to-all | bytes 1671168 | tf_op jit(solution)/shard_map/all_to_all | solution.py:405
  142.5 7.2 %all-gather.5 = f32[1600,128]{1,0:T(8,128)S(1)} all-gather(f32[800,128]{1,0:T(8,128)S(1)} %shard_map.44), channel_id=7, replica_groups={{0,1},{2,3},{4,5},{6,7},{8,9},{10,11},{12,13},{14,15},{16,17},{18,19},{..., dimensions={0}, use_global_device_ids=true | all-gather | bytes 1228800 | tf_op jit(solution)/shard_map/all_gather | solution.py:400
  149.7 2.2 %shard_map.45 = (f32[224,128]{1,0:T(8,128)S(1)}, f32[672,128]{1,0:T(8,128)S(1)}, f32[168,128]{1,0:T(8,128)S(1)}, f32[576,128]{1,0:T(8,128)S(1)}) custom-call(f32[4,408,128]{2,1,0:T(8,128)S(1)} %all_to_all.34.gathered, f32[2,800,128]{2,1,0:T(8,128)S(1)} %bitcast.30, f32[288,128]{1,0:T(8,128)S(1)} %get-tuple-element.41.held), custom_call_target="tpu_custom_call" | custom-call | flops 522190848 | bytes 1802240 | tf_op jit(solution)/shard_map/pallas_call | solution.py:369
  151.9 9.2 %all-gather.6 = f32[336,128]{1,0:T(8,128)S(1)} all-gather(f32[168,128]{1,0:T(8,128)S(1)} %get-tuple-element.43), channel_id=8, replica_groups={{0,96},{32,64},{128,224},{160,192},{256,352},{288,320},{384,480},{416,4..., dimensions={0}, use_global_device_ids=true | all-gather | bytes 258048 | tf_op jit(solution)/shard_map/all_gather | solution.py:400
  161.1 8.0 %all_to_all.35.sib = f32[4,168,128]{2,1,0:T(8,128)S(1)} all-to-all(f32[4,168,128]{2,1,0:T(8,128)S(1)} %shard_map.46), channel_id=1, replica_groups={{0,2,4,6},{1,3,5,7},{8,10,12,14},{9,11,13,15},{16,18,20,22},{17,19,21,2..., dimensions={0} | all-to-all | bytes 688128 | tf_op jit(solution)/shard_map/all_to_all | solution.py:405
  169.2 3.9 %all-gather.7 = f32[1216,128]{1,0:T(8,128)S(1)} all-gather(f32[608,128]{1,0:T(8,128)S(1)} %shard_map.47), channel_id=9, replica_groups={{0,1},{2,3},{4,5},{6,7},{8,9},{10,11},{12,13},{14,15},{16,17},{18,19},{..., dimensions={0}, use_global_device_ids=true | all-gather | bytes 933888 | tf_op jit(solution)/shard_map/all_gather | solution.py:400
  175.1 6.1 %all-gather.8 = f32[640,128]{1,0:T(8,128)S(1)} all-gather(f32[320,128]{1,0:T(8,128)S(1)} %get-tuple-element.46.own), channel_id=10, replica_groups={{0,128},{32,160},{64,192},{96,224},{256,384},{288,416},{320,448},{352,4..., dimensions={0}, use_global_device_ids=true | all-gather | bytes 491520 | tf_op jit(solution)/shard_map/all_gather | solution.py:400
  181.3 3.2 %all-gather.9 = f32[1600,128]{1,0:T(8,128)S(1)} all-gather(f32[800,128]{1,0:T(8,128)S(1)} %shard_map.49), channel_id=11, replica_groups={{0,1},{2,3},{4,5},{6,7},{8,9},{10,11},{12,13},{14,15},{16,17},{18,19},{..., dimensions={0}, use_global_device_ids=true | all-gather | bytes 1228800 | tf_op jit(solution)/shard_map/all_gather | solution.py:400
  186.5 5.9 %all-gather.10 = f32[384,128]{1,0:T(8,128)S(1)} all-gather(f32[192,128]{1,0:T(8,128)S(1)} %get-tuple-element.49), channel_id=12, replica_groups={{0,384},{32,416},{64,448},{96,480},{128,256},{160,288},{192,320},{224,3..., dimensions={0}, use_global_device_ids=true | all-gather | bytes 294912 | tf_op jit(solution)/shard_map/all_gather | solution.py:400
  192.4 2.4 %shard_map.51 = f32[64,128]{1,0:T(8,128)} custom-call(f32[2,192,128]{2,1,0:T(8,128)S(1)} %bitcast.36, f32[192,128]{1,0:T(8,128)S(1)} %get-tuple-element.50.carried), custom_call_target="tpu_custom_call" | custom-call | flops 232783872 | bytes 294912 | tf_op jit(solution)/shard_map/pallas_call | solution.py:369
  (25 shorter events, 10.9 us)
Async XLA Ops:
  1.3 11.1 %collective-permute-start = (f32[2112,128]{1,0:T(8,128)S(1)}, f32[2112,128]{1,0:T(8,128)S(1)}, u32[]{:S(2)}, u32[]{:S(2)}) collective-permute-start(f32[2112,128]{1,0:T(8,128)S(1)} %pad_maximum_fusion.mine), channel_id=1, source_target_pairs={{0,1},{1,0},{2,3},{3,2},{4,5},{5,4},{6,7},{7,6},{8,9},{9,8},{10,11... | collective-permute-start | bytes 3244040 | tf_op jit(solution)/shard_map/ppermute | solution.py:394

commit v14 on v11

--- a/solution.py
+++ b/solution.py
@@ -418,9 +418,11 @@
     half = rank // 2
     near_chips = [1, 2]
 
-    packed = jnp.concatenate(
-        [factor_u.reshape(-1, rank), factor_v.reshape(-1, rank), right_sides.T], axis=0
-    )
+    n = levels * rank
+    packed = jnp.zeros((2 * n + right_sides.shape[1], rank), jnp.float32)
+    packed = packed.at[:n].set(factor_u.reshape(-1, rank))
+    packed = packed.at[n : 2 * n].set(factor_v.reshape(-1, rank))
+    packed = packed.at[2 * n :].set(right_sides.T)
     rest = ((levels - 2) * rank + right_sides.shape[1]) // 2
     rows = 2 * rank + rest
     held, low, up, next_v, top_v = call(
@@ -483,7 +485,7 @@
     mine, other, sent = call(
         functools.partial(upper_kernel, 4, s_both),
         [(rest, rank), (rest, rank), (32, s_both + s_sums, rank)],
-        pair_gather(node, "gy", 4, (2, 3)),
+        pair_gather(node, "gy", 4, (3,)),
         z_low,
         shared,
         held,

time: 194 us -> 195 us (level)
    all_to_all x6, blocking collectives: 74.9 us -> 78.6 us  [exchange(): lax.all_to_all(value, axis, 0, 0, axis_index_groups=bit_groups(count, bits))]
    all_gather x12, blocking collectives: 87.3 us -> 84.4 us  [pair_gather(): return lax.all_gather(value, axis, axis_index_groups=groups)]
where the time goes in v14:
time: 195 us
  blocking collectives  163 us (84%)
  Pallas kernels  18.9 us (10%)
  starting transfers between devices  8.79 us (5%)
  waiting for transfers between devices  2.31 us (1%)
    all_gather x12, blocking collectives, pair_gather(): return lax.all_gather(value, axis, axis_index_groups=groups)  84.4 us
    all_to_all x6, blocking collectives, exchange(): lax.all_to_all(value, axis, 0, 0, axis_index_groups=bit_groups(count, bits))  78.6 us
    pallas_call x15, Pallas kernels, call(): pl.pallas_call(kernel, out_shape=[jax.ShapeDtypeStruct(o, jnp.float32) fo...  18.9 us
    ppermute x1, starting transfers between devices, swap_cores(): lax.ppermute(value, 'gy', [(s, s ^ 1) for s in range(lax.axis_size('gy'))])  8.79 us
  transfers between devices with their start and end apart: 1, of which 1 were waited for; matrix products, arithmetic and copies ran while one was open for 0% of the time, Pallas kernels for 0%

profile of v14, /device:TPU:1, one launch (start us, length us, event | category | flops | bytes accessed | tf_op | source)
XLA Modules:
  0.0 194.6 jit_solution(18067313014761771433)
XLA Ops:
  1.3 8.8 %collective-permute-start = (f32[2112,128]{1,0:T(8,128)S(1)}, f32[2112,128]{1,0:T(8,128)S(1)}, u32[]{:S(2)}, u32[]{:S(2)}) collective-permute-start(f32[2112,128]{1,0:T(8,128)S(1)} %bitcast_dynamic-update-slice_fusion.mine), channel_id=1, source_target_pairs={{0,1},{1,0},{2,3},{3,2},{4,5},{5,4},{6,7},{7,6},{8,9},{9,8},{10,11... | collective-permute-start | bytes 3244040 | tf_op jit(solution)/shard_map/ppermute | solution.py:394
  10.1 2.3 %collective-permute-done.other = f32[2112,128]{1,0:T(8,128)S(1)} collective-permute-done((f32[2112,128]{1,0:T(8,128)S(1)}, f32[2112,128]{1,0:T(8,128)S(1)}, u32[]{:S(2)}, u32[]{:S(2)}) %collective-permute-start) | collective-permute-done | bytes 1081376 | tf_op jit(solution)/shard_map/ppermute | solution.py:394
  13.3 9.9 %all-gather = f32[1344,128]{1,0:T(8,128)S(1)} all-gather(f32[672,128]{1,0:T(8,128)S(1)} %get-tuple-element.64), channel_id=2, replica_groups={{0,2},{1,3},{4,6},{5,7},{8,10},{9,11},{12,14},{13,15},{16,18},{17,19},{..., dimensions={0}, use_global_device_ids=true | all-gather | bytes 1032192 | tf_op jit(solution)/shard_map/all_gather | solution.py:400
  25.3 7.6 %all-gather.1 = f32[1088,128]{1,0:T(8,128)S(1)} all-gather(f32[544,128]{1,0:T(8,128)S(1)} %get-tuple-element.66), channel_id=3, replica_groups={{0,2},{1,3},{4,6},{5,7},{8,10},{9,11},{12,14},{13,15},{16,18},{17,19},{..., dimensions={0}, use_global_device_ids=true | all-gather | bytes 835584 | tf_op jit(solution)/shard_map/all_gather | solution.py:400
  33.0 6.7 %all-gather.11 = f32[1088,128]{1,0:T(8,128)S(1)} all-gather(f32[544,128]{1,0:T(8,128)S(1)} %slice_add_fusion), channel_id=13, replica_groups={{0,4},{1,5},{2,6},{3,7},{8,12},{9,13},{10,14},{11,15},{16,20},{17,21},{..., dimensions={0}, use_global_device_ids=true | all-gather | bytes 835584 | tf_op jit(solution)/shard_map/all_gather | solution.py:400
  39.7 2.5 %shard_map.39 = (f32[416,256]{1,0:T(8,128)S(1)}, f32[4,208,128]{2,1,0:T(8,128)S(1)}) custom-call(f32[2,544,128]{2,1,0:T(8,128)S(1)} %bitcast.35, f32[544,128]{1,0:T(8,128)S(1)} %get-tuple-element.67.z_low, f32[672,256]{1,0:T(8,128)S(1)} %get-tuple-element.68.held, f32[2,256,128]{2,1,0:T(8,128)S(1)} %get-tuple-element.69.v), custom_call_target="tpu_custom_call" | custom-call | flops 519045120 | bytes 1785856 | tf_op jit(solution)/shard_map/pallas_call | solution.py:369
  42.1 8.1 %all_to_all.30 = f32[4,208,128]{2,1,0:T(8,128)S(1)} all-to-all(f32[4,208,128]{2,1,0:T(8,128)S(1)} %get-tuple-element.70), channel_id=1, replica_groups={{0,2,4,6},{1,3,5,7},{8,10,12,14},{9,11,13,15},{16,18,20,22},{17,19,21,2..., dimensions={0} | all-to-all | bytes 851968 | tf_op jit(solution)/shard_map/all_to_all | solution.py:405
  50.2 6.3 %all-gather.2 = f32[416,128]{1,0:T(8,128)S(1)} all-gather(f32[208,128]{1,0:T(8,128)S(1)} %reduce_sum.18), channel_id=4, replica_groups={{0,8},{1,9},{2,10},{3,11},{4,12},{5,13},{6,14},{7,15},{16,24},{17,25},{..., dimensions={0}, use_global_device_ids=true | all-gather | bytes 319488 | tf_op jit(solution)/shard_map/all_gather | solution.py:400
  56.6 9.5 %all_to_all.31.pieces = f32[4,328,128]{2,1,0:T(8,128)S(1)} all-to-all(f32[4,328,128]{2,1,0:T(8,128)S(1)} %shard_map.40), channel_id=1, replica_groups={{0,2,4,6},{1,3,5,7},{8,10,12,14},{9,11,13,15},{16,18,20,22},{17,19,21,2..., dimensions={0} | all-to-all | bytes 1343488 | tf_op jit(solution)/shard_map/all_to_all | solution.py:405
  66.0 8.4 %all-gather.3 = f32[1408,128]{1,0:T(8,128)S(1)} all-gather(f32[704,128]{1,0:T(8,128)S(1)} %shard_map.41), channel_id=5, replica_groups={{0,1},{2,3},{4,5},{6,7},{8,9},{10,11},{12,13},{14,15},{16,17},{18,19},{..., dimensions={0}, use_global_device_ids=true | all-gather | bytes 1081344 | tf_op jit(solution)/shard_map/all_gather | solution.py:400
  76.6 10.2 %all-gather.4 = f32[832,128]{1,0:T(8,128)S(1)} all-gather(f32[416,128]{1,0:T(8,128)S(1)} %get-tuple-element.72), channel_id=6, replica_groups={{0,24},{1,25},{2,26},{3,27},{4,28},{5,29},{6,30},{7,31},{8,16},{9,17},{..., dimensions={0}, use_global_device_ids=true | all-gather | bytes 638976 | tf_op jit(solution)/shard_map/all_gather | solution.py:400
  86.8 2.5 %shard_map.43 = (f32[288,128]{1,0:T(8,128)S(1)}, f32[288,128]{1,0:T(8,128)S(1)}, f32[32,40,128]{2,1,0:T(8,128)S(1)}) custom-call(f32[2,416,128]{2,1,0:T(8,128)S(1)} %bitcast.29, f32[416,128]{1,0:T(8,128)S(1)} %get-tuple-element.73.z_low, f32[2,704,128]{2,1,0:T(8,128)S(1)} %bitcast.28, f32[416,256]{1,0:T(8,128)S(1)} %get-tuple-element.71.rest, ...), custom_call_target="tpu_custom_call" | custom-call | flops 619708416 | bytes 2310144 | tf_op jit(solution)/shard_map/pallas_call | solution.py:369
  89.2 28.7 %all_to_all.32 = f32[32,40,128]{2,1,0:T(8,128)S(1)} all-to-all(f32[32,40,128]{2,1,0:T(8,128)S(1)} %get-tuple-element.75), channel_id=1, replica_groups={{0,2,4,6,8,10,12,14,16,18,20,22,24,26,28,30,32,34,36,38,40,42,44,46,48,..., dimensions={0} | all-to-all | bytes 1310720 | tf_op jit(solution)/shard_map/all_to_all | solution.py:405
  118.0 14.0 %all_to_all.33 = f32[8,56,128]{2,1,0:T(8,128)S(1)} all-to-all(f32[8,56,128]{2,1,0:T(8,128)S(1)} %broadcast_in_dim.7), channel_id=1, replica_groups={{0,8,16,24,32,40,48,56},{1,9,17,25,33,41,49,57},{2,10,18,26,34,42,50,58..., dimensions={0} | all-to-all | bytes 458752 | tf_op jit(solution)/shard_map/all_to_all | solution.py:405
  132.2 10.3 %all_to_all.34.gathered = f32[4,408,128]{2,1,0:T(8,128)S(1)} all-to-all(f32[4,408,128]{2,1,0:T(8,128)S(1)} %broadcast_in_dim.8), channel_id=1, replica_groups={{0,2,4,6},{1,3,5,7},{8,10,12,14},{9,11,13,15},{16,18,20,22},{17,19,21,2..., dimensions={0} | all-to-all | bytes 1671168 | tf_op jit(solution)/shard_map/all_to_all | solution.py:405
  142.5 7.2 %all-gather.5 = f32[1600,128]{1,0:T(8,128)S(1)} all-gather(f32[800,128]{1,0:T(8,128)S(1)} %shard_map.44), channel_id=7, replica_groups={{0,1},{2,3},{4,5},{6,7},{8,9},{10,11},{12,13},{14,15},{16,17},{18,19},{..., dimensions={0}, use_global_device_ids=true | all-gather | bytes 1228800 | tf_op jit(solution)/shard_map/all_gather | solution.py:400
  149.7 2.2 %shard_map.45 = (f32[224,128]{1,0:T(8,128)S(1)}, f32[672,128]{1,0:T(8,128)S(1)}, f32[168,128]{1,0:T(8,128)S(1)}, f32[576,128]{1,0:T(8,128)S(1)}) custom-call(f32[4,408,128]{2,1,0:T(8,128)S(1)} %all_to_all.34.gathered, f32[2,800,128]{2,1,0:T(8,128)S(1)} %bitcast.31, f32[288,128]{1,0:T(8,128)S(1)} %get-tuple-element.77.held), custom_call_target="tpu_custom_call" | custom-call | flops 522190848 | bytes 1802240 | tf_op jit(solution)/shard_map/pallas_call | solution.py:369
  151.9 9.0 %all-gather.6 = f32[336,128]{1,0:T(8,128)S(1)} all-gather(f32[168,128]{1,0:T(8,128)S(1)} %get-tuple-element.79), channel_id=8, replica_groups={{0,98},{1,99},{2,96},{3,97},{4,102},{5,103},{6,100},{7,101},{8,106},{9,..., dimensions={0}, use_global_device_ids=true | all-gather | bytes 258048 | tf_op jit(solution)/shard_map/all_gather | solution.py:400
  160.9 8.1 %all_to_all.35.sib = f32[4,168,128]{2,1,0:T(8,128)S(1)} all-to-all(f32[4,168,128]{2,1,0:T(8,128)S(1)} %shard_map.46), channel_id=1, replica_groups={{0,2,4,6},{1,3,5,7},{8,10,12,14},{9,11,13,15},{16,18,20,22},{17,19,21,2..., dimensions={0} | all-to-all | bytes 688128 | tf_op jit(solution)/shard_map/all_to_all | solution.py:405
  169.0 3.9 %all-gather.7 = f32[1216,128]{1,0:T(8,128)S(1)} all-gather(f32[608,128]{1,0:T(8,128)S(1)} %shard_map.47), channel_id=9, replica_groups={{0,1},{2,3},{4,5},{6,7},{8,9},{10,11},{12,13},{14,15},{16,17},{18,19},{..., dimensions={0}, use_global_device_ids=true | all-gather | bytes 933888 | tf_op jit(solution)/shard_map/all_gather | solution.py:400
  175.0 6.1 %all-gather.8 = f32[640,128]{1,0:T(8,128)S(1)} all-gather(f32[320,128]{1,0:T(8,128)S(1)} %get-tuple-element.82.own), channel_id=10, replica_groups={{0,128},{32,160},{64,192},{96,224},{256,384},{288,416},{320,448},{352,4..., dimensions={0}, use_global_device_ids=true | all-gather | bytes 491520 | tf_op jit(solution)/shard_map/all_gather | solution.py:400
  181.1 3.2 %all-gather.9 = f32[1600,128]{1,0:T(8,128)S(1)} all-gather(f32[800,128]{1,0:T(8,128)S(1)} %shard_map.49), channel_id=11, replica_groups={{0,1},{2,3},{4,5},{6,7},{8,9},{10,11},{12,13},{14,15},{16,17},{18,19},{..., dimensions={0}, use_global_device_ids=true | all-gather | bytes 1228800 | tf_op jit(solution)/shard_map/all_gather | solution.py:400
  186.3 5.9 %all-gather.10 = f32[384,128]{1,0:T(8,128)S(1)} all-gather(f32[192,128]{1,0:T(8,128)S(1)} %get-tuple-element.85), channel_id=12, replica_groups={{0,384},{32,416},{64,448},{96,480},{128,256},{160,288},{192,320},{224,3..., dimensions={0}, use_global_device_ids=true | all-gather | bytes 294912 | tf_op jit(solution)/shard_map/all_gather | solution.py:400
  192.2 2.4 %shard_map.51 = f32[64,128]{1,0:T(8,128)} custom-call(f32[2,192,128]{2,1,0:T(8,128)S(1)} %bitcast.37, f32[192,128]{1,0:T(8,128)S(1)} %get-tuple-element.86.carried), custom_call_target="tpu_custom_call" | custom-call | flops 232783872 | bytes 294912 | tf_op jit(solution)/shard_map/pallas_call | solution.py:369
  (31 shorter events, 10.8 us)
Async XLA Ops:
  0.0 1.2 copy-start
  0.0 1.2 copy-start.1
  1.3 11.1 %collective-permute-start = (f32[2112,128]{1,0:T(8,128)S(1)}, f32[2112,128]{1,0:T(8,128)S(1)}, u32[]{:S(2)}, u32[]{:S(2)}) collective-permute-start(f32[2112,128]{1,0:T(8,128)S(1)} %bitcast_dynamic-update-slice_fusion.mine), channel_id=1, source_target_pairs={{0,1},{1,0},{2,3},{3,2},{4,5},{5,4},{6,7},{7,6},{8,9},{9,8},{10,11... | collective-permute-start | bytes 3244040 | tf_op jit(solution)/shard_map/ppermute | solution.py:394

commit v15 on v9

--- a/solution.py
+++ b/solution.py
@@ -274,7 +274,7 @@
     z_out[...] = z
     node_out[...] = node
     n = part.shape[0]
-    part[...] = node_out[pl.ds(times8((lax.axis_index("gy") >> 1) & 3, n), n)]
+    part[...] = node_out[pl.ds(times8(((lax.axis_index("gy") >> 1) & 3) ^ 1, n), n)]
     swapped = [shared[c, 2 * half * count :] for c in range(2)]
     halves = [jnp.where(core == c, held[...], swapped[c]) for c in range(2)]
     carried[...] = interleaved(halves[0], halves[1], half)
@@ -385,9 +385,10 @@
     return lax.ppermute(value, "gy", [(s, s ^ 1) for s in range(lax.axis_size("gy"))])
 
 
-def pair_gather(value, axis, bit, tiled=False):
-    groups = bit_groups(lax.axis_size(axis), [bit])
-    return lax.all_gather(value, axis, axis_index_groups=groups, tiled=tiled)
+def pair_gather(value, axis, bit, also=()):
+    mask = sum(1 << b for b in (bit, *also))
+    groups = [[d, d ^ mask] for d in range(lax.axis_size(axis)) if not (d >> bit) & 1]
+    return lax.all_gather(value, axis, axis_index_groups=groups)
 
 
 def exchange(value, axis, bits):
@@ -476,7 +477,7 @@
     mine, other, sent = call(
         functools.partial(upper_kernel, 4, 4),
         [(rest, rank), (rest, rank), (4, n_both + n_sums, rank)],
-        pair_gather(node, "gy", 4),
+        pair_gather(node, "gy", 4, (3,)),
         z_low,
         shared,
         held,
@@ -530,7 +531,7 @@
     count -= 1
     rows = 2 * rest
     near = call(
-        functools.partial(sibling_kernel, 1), [(4,) + part.shape], pair_gather(part, "gx", 1)
+        functools.partial(sibling_kernel, 1), [(4,) + part.shape], pair_gather(part, ("gx", "gy"), 6, (5, 1))
     )[0]
     near = exchange(near, "gy", near_chips)
     shared = call(
@@ -570,7 +571,7 @@
     return call(
         functools.partial(last_kernel, 3),
         [right_sides.shape[::-1]],
-        pair_gather(node, "gx", 3),
+        pair_gather(node, "gx", 3, (2,)),
         carried,
     )[0].T
 

time: 198 us -> 194 us (0.980)
  blocking collectives: 165 us -> 162 us
    all_gather x12, blocking collectives: 90.7 us -> 82.9 us  [pair_gather(): return lax.all_gather(value, axis, axis_index_groups=groups)]
    all_to_all x7, blocking collectives: 74.8 us -> 79.1 us  [exchange(): lax.all_to_all(value, axis, 0, 0, axis_index_groups=bit_groups(count, bits))]
where the time goes in v15:
time: 194 us
  blocking collectives  162 us (84%)
  Pallas kernels  18.9 us (10%)
  starting transfers between devices  8.79 us (5%)
  waiting for transfers between devices  2.31 us (1%)
    all_gather x12, blocking collectives, pair_gather(): return lax.all_gather(value, axis, axis_index_groups=groups)  82.9 us
    all_to_all x7, blocking collectives, exchange(): lax.all_to_all(value, axis, 0, 0, axis_index_groups=bit_groups(count, bits))  79.1 us
    pallas_call x15, Pallas kernels, call(): pl.pallas_call(kernel, out_shape=[jax.ShapeDtypeStruct(o, jnp.float32) fo...  18.9 us
    ppermute x1, starting transfers between devices, swap_cores(): lax.ppermute(value, 'gy', [(s, s ^ 1) for s in range(lax.axis_size('gy'))])  8.79 us
  transfers between devices with their start and end apart: 1, of which 1 were waited for; matrix products, arithmetic and copies ran while one was open for 0% of the time, Pallas kernels for 0%

profile of v15, /device:TPU:1, one launch (start us, length us, event | category | flops | bytes accessed | tf_op | source)
XLA Modules:
  0.0 193.8 jit_solution(2953202151041550653)
XLA Ops:
  1.3 8.8 %collective-permute-start = (f32[2112,128]{1,0:T(8,128)S(1)}, f32[2112,128]{1,0:T(8,128)S(1)}, u32[]{:S(2)}, u32[]{:S(2)}) collective-permute-start(f32[2112,128]{1,0:T(8,128)S(1)} %pad_maximum_fusion.mine), channel_id=1, source_target_pairs={{0,1},{1,0},{2,3},{3,2},{4,5},{5,4},{6,7},{7,6},{8,9},{9,8},{10,11... | collective-permute-start | bytes 3244040 | tf_op jit(solution)/shard_map/ppermute | solution.py:385
  10.1 2.3 %collective-permute-done.other = f32[2112,128]{1,0:T(8,128)S(1)} collective-permute-done((f32[2112,128]{1,0:T(8,128)S(1)}, f32[2112,128]{1,0:T(8,128)S(1)}, u32[]{:S(2)}, u32[]{:S(2)}) %collective-permute-start) | collective-permute-done | bytes 1081376 | tf_op jit(solution)/shard_map/ppermute | solution.py:385
  13.3 9.9 %all-gather = f32[1344,128]{1,0:T(8,128)S(1)} all-gather(f32[672,128]{1,0:T(8,128)S(1)} %get-tuple-element.28), channel_id=2, replica_groups={{0,2},{1,3},{4,6},{5,7},{8,10},{9,11},{12,14},{13,15},{16,18},{17,19},{..., dimensions={0}, use_global_device_ids=true | all-gather | bytes 1032192 | tf_op jit(solution)/shard_map/all_gather | solution.py:391
  25.3 7.6 %all-gather.1 = f32[1088,128]{1,0:T(8,128)S(1)} all-gather(f32[544,128]{1,0:T(8,128)S(1)} %get-tuple-element.30), channel_id=3, replica_groups={{0,2},{1,3},{4,6},{5,7},{8,10},{9,11},{12,14},{13,15},{16,18},{17,19},{..., dimensions={0}, use_global_device_ids=true | all-gather | bytes 835584 | tf_op jit(solution)/shard_map/all_gather | solution.py:391
  33.0 6.7 %all-gather.11 = f32[1088,128]{1,0:T(8,128)S(1)} all-gather(f32[544,128]{1,0:T(8,128)S(1)} %slice_add_fusion), channel_id=13, replica_groups={{0,4},{1,5},{2,6},{3,7},{8,12},{9,13},{10,14},{11,15},{16,20},{17,21},{..., dimensions={0}, use_global_device_ids=true | all-gather | bytes 835584 | tf_op jit(solution)/shard_map/all_gather | solution.py:391
  39.7 2.5 %shard_map.39 = (f32[416,256]{1,0:T(8,128)S(1)}, f32[4,208,128]{2,1,0:T(8,128)S(1)}) custom-call(f32[2,544,128]{2,1,0:T(8,128)S(1)} %bitcast.36, f32[544,128]{1,0:T(8,128)S(1)} %get-tuple-element.31.z_low, f32[672,256]{1,0:T(8,128)S(1)} %get-tuple-element.32.held, f32[2,256,128]{2,1,0:T(8,128)S(1)} %get-tuple-element.33.v), custom_call_target="tpu_custom_call" | custom-call | flops 519045120 | bytes 1785856 | tf_op jit(solution)/shard_map/pallas_call | solution.py:360
  42.2 8.1 %all_to_all.35 = f32[4,208,128]{2,1,0:T(8,128)S(1)} all-to-all(f32[4,208,128]{2,1,0:T(8,128)S(1)} %get-tuple-element.34), channel_id=1, replica_groups={{0,2,4,6},{1,3,5,7},{8,10,12,14},{9,11,13,15},{16,18,20,22},{17,19,21,2..., dimensions={0} | all-to-all | bytes 851968 | tf_op jit(solution)/shard_map/all_to_all | solution.py:396
  50.3 6.3 %all-gather.2 = f32[416,128]{1,0:T(8,128)S(1)} all-gather(f32[208,128]{1,0:T(8,128)S(1)} %reduce_sum.27), channel_id=4, replica_groups={{0,8},{1,9},{2,10},{3,11},{4,12},{5,13},{6,14},{7,15},{16,24},{17,25},{..., dimensions={0}, use_global_device_ids=true | all-gather | bytes 319488 | tf_op jit(solution)/shard_map/all_gather | solution.py:391
  56.6 9.5 %all_to_all.36.pieces = f32[4,328,128]{2,1,0:T(8,128)S(1)} all-to-all(f32[4,328,128]{2,1,0:T(8,128)S(1)} %shard_map.40), channel_id=1, replica_groups={{0,2,4,6},{1,3,5,7},{8,10,12,14},{9,11,13,15},{16,18,20,22},{17,19,21,2..., dimensions={0} | all-to-all | bytes 1343488 | tf_op jit(solution)/shard_map/all_to_all | solution.py:396
  66.1 8.4 %all-gather.3 = f32[1408,128]{1,0:T(8,128)S(1)} all-gather(f32[704,128]{1,0:T(8,128)S(1)} %shard_map.41), channel_id=5, replica_groups={{0,1},{2,3},{4,5},{6,7},{8,9},{10,11},{12,13},{14,15},{16,17},{18,19},{..., dimensions={0}, use_global_device_ids=true | all-gather | bytes 1081344 | tf_op jit(solution)/shard_map/all_gather | solution.py:391
  76.6 10.2 %all-gather.4 = f32[832,128]{1,0:T(8,128)S(1)} all-gather(f32[416,128]{1,0:T(8,128)S(1)} %get-tuple-element.36), channel_id=6, replica_groups={{0,24},{1,25},{2,26},{3,27},{4,28},{5,29},{6,30},{7,31},{8,16},{9,17},{..., dimensions={0}, use_global_device_ids=true | all-gather | bytes 638976 | tf_op jit(solution)/shard_map/all_gather | solution.py:391
  86.8 2.5 %shard_map.43 = (f32[288,128]{1,0:T(8,128)S(1)}, f32[288,128]{1,0:T(8,128)S(1)}, f32[4,288,128]{2,1,0:T(8,128)S(1)}) custom-call(f32[2,416,128]{2,1,0:T(8,128)S(1)} %bitcast.30, f32[416,128]{1,0:T(8,128)S(1)} %get-tuple-element.37.z_low, f32[2,704,128]{2,1,0:T(8,128)S(1)} %bitcast.29, f32[416,256]{1,0:T(8,128)S(1)} %get-tuple-element.35.rest, ...), custom_call_target="tpu_custom_call" | custom-call | flops 619708416 | bytes 2310144 | tf_op jit(solution)/shard_map/pallas_call | solution.py:360
  89.3 12.8 %all_to_all.37 = f32[4,288,128]{2,1,0:T(8,128)S(1)} all-to-all(f32[4,288,128]{2,1,0:T(8,128)S(1)} %get-tuple-element.39), channel_id=1, replica_groups={{0,2,4,6},{1,3,5,7},{8,10,12,14},{9,11,13,15},{16,18,20,22},{17,19,21,2..., dimensions={0} | all-to-all | bytes 1179648 | tf_op jit(solution)/shard_map/all_to_all | solution.py:396
  102.3 16.2 %all_to_all.38 = f32[8,40,128]{2,1,0:T(8,128)S(1)} all-to-all(f32[8,40,128]{2,1,0:T(8,128)S(1)} %pad_maximum_fusion.2), channel_id=1, replica_groups={{0,8,16,24,32,40,48,56},{1,9,17,25,33,41,49,57},{2,10,18,26,34,42,50,58..., dimensions={0} | all-to-all | bytes 327680 | tf_op jit(solution)/shard_map/all_to_all | solution.py:396
  118.5 11.9 %all_to_all.39 = f32[8,56,128]{2,1,0:T(8,128)S(1)} all-to-all(f32[8,56,128]{2,1,0:T(8,128)S(1)} %broadcast_in_dim.6), channel_id=1, replica_groups={{0,8,16,24,32,40,48,56},{1,9,17,25,33,41,49,57},{2,10,18,26,34,42,50,58..., dimensions={0} | all-to-all | bytes 458752 | tf_op jit(solution)/shard_map/all_to_all | solution.py:396
  130.6 12.6 %all_to_all.40.gathered = f32[4,408,128]{2,1,0:T(8,128)S(1)} all-to-all(f32[4,408,128]{2,1,0:T(8,128)S(1)} %broadcast_in_dim.7), channel_id=1, replica_groups={{0,2,4,6},{1,3,5,7},{8,10,12,14},{9,11,13,15},{16,18,20,22},{17,19,21,2..., dimensions={0} | all-to-all | bytes 1671168 | tf_op jit(solution)/shard_map/all_to_all | solution.py:396
  143.2 6.6 %all-gather.5 = f32[1600,128]{1,0:T(8,128)S(1)} all-gather(f32[800,128]{1,0:T(8,128)S(1)} %shard_map.44), channel_id=7, replica_groups={{0,1},{2,3},{4,5},{6,7},{8,9},{10,11},{12,13},{14,15},{16,17},{18,19},{..., dimensions={0}, use_global_device_ids=true | all-gather | bytes 1228800 | tf_op jit(solution)/shard_map/all_gather | solution.py:391
  152.0 8.1 %all-gather.6 = f32[336,128]{1,0:T(8,128)S(1)} all-gather(f32[168,128]{1,0:T(8,128)S(1)} %get-tuple-element.43), channel_id=8, replica_groups={{0,98},{1,99},{2,96},{3,97},{4,102},{5,103},{6,100},{7,101},{8,106},{9,..., dimensions={0}, use_global_device_ids=true | all-gather | bytes 258048 | tf_op jit(solution)/shard_map/all_gather | solution.py:391
  160.1 8.0 %all_to_all.41.sib = f32[4,168,128]{2,1,0:T(8,128)S(1)} all-to-all(f32[4,168,128]{2,1,0:T(8,128)S(1)} %shard_map.46), channel_id=1, replica_groups={{0,2,4,6},{1,3,5,7},{8,10,12,14},{9,11,13,15},{16,18,20,22},{17,19,21,2..., dimensions={0} | all-to-all | bytes 688128 | tf_op jit(solution)/shard_map/all_to_all | solution.py:396
  168.2 3.9 %all-gather.7 = f32[1216,128]{1,0:T(8,128)S(1)} all-gather(f32[608,128]{1,0:T(8,128)S(1)} %shard_map.47), channel_id=9, replica_groups={{0,1},{2,3},{4,5},{6,7},{8,9},{10,11},{12,13},{14,15},{16,17},{18,19},{..., dimensions={0}, use_global_device_ids=true | all-gather | bytes 933888 | tf_op jit(solution)/shard_map/all_gather | solution.py:391
  174.2 6.1 %all-gather.8 = f32[640,128]{1,0:T(8,128)S(1)} all-gather(f32[320,128]{1,0:T(8,128)S(1)} %get-tuple-element.46.own), channel_id=10, replica_groups={{0,128},{32,160},{64,192},{96,224},{256,384},{288,416},{320,448},{352,4..., dimensions={0}, use_global_device_ids=true | all-gather | bytes 491520 | tf_op jit(solution)/shard_map/all_gather | solution.py:391
  180.3 3.2 %all-gather.9 = f32[1600,128]{1,0:T(8,128)S(1)} all-gather(f32[800,128]{1,0:T(8,128)S(1)} %shard_map.49), channel_id=11, replica_groups={{0,1},{2,3},{4,5},{6,7},{8,9},{10,11},{12,13},{14,15},{16,17},{18,19},{..., dimensions={0}, use_global_device_ids=true | all-gather | bytes 1228800 | tf_op jit(solution)/shard_map/all_gather | solution.py:391
  185.6 5.9 %all-gather.10 = f32[384,128]{1,0:T(8,128)S(1)} all-gather(f32[192,128]{1,0:T(8,128)S(1)} %get-tuple-element.49), channel_id=12, replica_groups={{0,384},{32,416},{64,448},{96,480},{128,256},{160,288},{192,320},{224,3..., dimensions={0}, use_global_device_ids=true | all-gather | bytes 294912 | tf_op jit(solution)/shard_map/all_gather | solution.py:391
  191.4 2.4 %shard_map.51 = f32[64,128]{1,0:T(8,128)} custom-call(f32[2,192,128]{2,1,0:T(8,128)S(1)} %bitcast.38, f32[192,128]{1,0:T(8,128)S(1)} %get-tuple-element.50.carried), custom_call_target="tpu_custom_call" | custom-call | flops 232783872 | bytes 294912 | tf_op jit(solution)/shard_map/pallas_call | solution.py:360
  (33 shorter events, 13.2 us)
Async XLA Ops:
  1.3 11.1 %collective-permute-start = (f32[2112,128]{1,0:T(8,128)S(1)}, f32[2112,128]{1,0:T(8,128)S(1)}, u32[]{:S(2)}, u32[]{:S(2)}) collective-permute-start(f32[2112,128]{1,0:T(8,128)S(1)} %pad_maximum_fusion.mine), channel_id=1, source_target_pairs={{0,1},{1,0},{2,3},{3,2},{4,5},{5,4},{6,7},{7,6},{8,9},{9,8},{10,11... | collective-permute-start | bytes 3244040 | tf_op jit(solution)/shard_map/ppermute | solution.py:385
  89.3 12.9 %copy-start = (pred[128]{0:T(512)(128)(4,1)S(1)}, pred[128]{0:T(512)(128)(4,1)}, u32[]{:S(2)}) copy-start(pred[128]{0:T(512)(128)(4,1)} %constant.4.clone.1) | copy-start | bytes 388

commit v16 on v15

--- a/solution.py
+++ b/solution.py
@@ -274,7 +274,7 @@
     z_out[...] = z
     node_out[...] = node
     n = part.shape[0]
-    part[...] = node_out[pl.ds(times8(((lax.axis_index("gy") >> 1) & 3) ^ 1, n), n)]
+    part[...] = node_out[pl.ds(times8((lax.axis_index("gy") >> 1) & 3, n), n)]
     swapped = [shared[c, 2 * half * count :] for c in range(2)]
     halves = [jnp.where(core == c, held[...], swapped[c]) for c in range(2)]
     carried[...] = interleaved(halves[0], halves[1], half)
@@ -531,7 +531,7 @@
     count -= 1
     rows = 2 * rest
     near = call(
-        functools.partial(sibling_kernel, 1), [(4,) + part.shape], pair_gather(part, ("gx", "gy"), 6, (5, 1))
+        functools.partial(sibling_kernel, 1), [(4,) + part.shape], pair_gather(part, "gx", 1, (0,))
     )[0]
     near = exchange(near, "gy", near_chips)
     shared = call(

time: 194 us -> 194 us (level)
  no operation moved by 1% of the time
where the time goes in v16:
time: 194 us
  blocking collectives  162 us (84%)
  Pallas kernels  18.9 us (10%)
  starting transfers between devices  8.79 us (5%)
  waiting for transfers between devices  2.31 us (1%)
    all_gather x12, blocking collectives, pair_gather(): return lax.all_gather(value, axis, axis_index_groups=groups)  83.1 us
    all_to_all x7, blocking collectives, exchange(): lax.all_to_all(value, axis, 0, 0, axis_index_groups=bit_groups(count, bits))  79.1 us
    pallas_call x15, Pallas kernels, call(): pl.pallas_call(kernel, out_shape=[jax.ShapeDtypeStruct(o, jnp.float32) fo...  18.9 us
    ppermute x1, starting transfers between devices, swap_cores(): lax.ppermute(value, 'gy', [(s, s ^ 1) for s in range(lax.axis_size('gy'))])  8.79 us
  transfers between devices with their start and end apart: 1, of which 1 were waited for; matrix products, arithmetic and copies ran while one was open for 0% of the time, Pallas kernels for 0%

profile of v16, /device:TPU:1, one launch (start us, length us, event | category | flops | bytes accessed | tf_op | source)
XLA Modules:
  0.0 194.0 jit_solution(18077978292296901707)
XLA Ops:
  1.3 8.8 %collective-permute-start = (f32[2112,128]{1,0:T(8,128)S(1)}, f32[2112,128]{1,0:T(8,128)S(1)}, u32[]{:S(2)}, u32[]{:S(2)}) collective-permute-start(f32[2112,128]{1,0:T(8,128)S(1)} %pad_maximum_fusion.mine), channel_id=1, source_target_pairs={{0,1},{1,0},{2,3},{3,2},{4,5},{5,4},{6,7},{7,6},{8,9},{9,8},{10,11... | collective-permute-start | bytes 3244040 | tf_op jit(solution)/shard_map/ppermute | solution.py:385
  10.1 2.3 %collective-permute-done.other = f32[2112,128]{1,0:T(8,128)S(1)} collective-permute-done((f32[2112,128]{1,0:T(8,128)S(1)}, f32[2112,128]{1,0:T(8,128)S(1)}, u32[]{:S(2)}, u32[]{:S(2)}) %collective-permute-start) | collective-permute-done | bytes 1081376 | tf_op jit(solution)/shard_map/ppermute | solution.py:385
  13.3 9.9 %all-gather = f32[1344,128]{1,0:T(8,128)S(1)} all-gather(f32[672,128]{1,0:T(8,128)S(1)} %get-tuple-element.28), channel_id=2, replica_groups={{0,2},{1,3},{4,6},{5,7},{8,10},{9,11},{12,14},{13,15},{16,18},{17,19},{..., dimensions={0}, use_global_device_ids=true | all-gather | bytes 1032192 | tf_op jit(solution)/shard_map/all_gather | solution.py:391
  25.3 7.6 %all-gather.1 = f32[1088,128]{1,0:T(8,128)S(1)} all-gather(f32[544,128]{1,0:T(8,128)S(1)} %get-tuple-element.30), channel_id=3, replica_groups={{0,2},{1,3},{4,6},{5,7},{8,10},{9,11},{12,14},{13,15},{16,18},{17,19},{..., dimensions={0}, use_global_device_ids=true | all-gather | bytes 835584 | tf_op jit(solution)/shard_map/all_gather | solution.py:391
  33.0 6.7 %all-gather.11 = f32[1088,128]{1,0:T(8,128)S(1)} all-gather(f32[544,128]{1,0:T(8,128)S(1)} %slice_add_fusion), channel_id=13, replica_groups={{0,4},{1,5},{2,6},{3,7},{8,12},{9,13},{10,14},{11,15},{16,20},{17,21},{..., dimensions={0}, use_global_device_ids=true | all-gather | bytes 835584 | tf_op jit(solution)/shard_map/all_gather | solution.py:391
  39.7 2.5 %shard_map.39 = (f32[416,256]{1,0:T(8,128)S(1)}, f32[4,208,128]{2,1,0:T(8,128)S(1)}) custom-call(f32[2,544,128]{2,1,0:T(8,128)S(1)} %bitcast.36, f32[544,128]{1,0:T(8,128)S(1)} %get-tuple-element.31.z_low, f32[672,256]{1,0:T(8,128)S(1)} %get-tuple-element.32.held, f32[2,256,128]{2,1,0:T(8,128)S(1)} %get-tuple-element.33.v), custom_call_target="tpu_custom_call" | custom-call | flops 519045120 | bytes 1785856 | tf_op jit(solution)/shard_map/pallas_call | solution.py:360
  42.2 8.1 %all_to_all.35 = f32[4,208,128]{2,1,0:T(8,128)S(1)} all-to-all(f32[4,208,128]{2,1,0:T(8,128)S(1)} %get-tuple-element.34), channel_id=1, replica_groups={{0,2,4,6},{1,3,5,7},{8,10,12,14},{9,11,13,15},{16,18,20,22},{17,19,21,2..., dimensions={0} | all-to-all | bytes 851968 | tf_op jit(solution)/shard_map/all_to_all | solution.py:396
  50.3 6.3 %all-gather.2 = f32[416,128]{1,0:T(8,128)S(1)} all-gather(f32[208,128]{1,0:T(8,128)S(1)} %reduce_sum.27), channel_id=4, replica_groups={{0,8},{1,9},{2,10},{3,11},{4,12},{5,13},{6,14},{7,15},{16,24},{17,25},{..., dimensions={0}, use_global_device_ids=true | all-gather | bytes 319488 | tf_op jit(solution)/shard_map/all_gather | solution.py:391
  56.6 9.5 %all_to_all.36.pieces = f32[4,328,128]{2,1,0:T(8,128)S(1)} all-to-all(f32[4,328,128]{2,1,0:T(8,128)S(1)} %shard_map.40), channel_id=1, replica_groups={{0,2,4,6},{1,3,5,7},{8,10,12,14},{9,11,13,15},{16,18,20,22},{17,19,21,2..., dimensions={0} | all-to-all | bytes 1343488 | tf_op jit(solution)/shard_map/all_to_all | solution.py:396
  66.1 8.4 %all-gather.3 = f32[1408,128]{1,0:T(8,128)S(1)} all-gather(f32[704,128]{1,0:T(8,128)S(1)} %shard_map.41), channel_id=5, replica_groups={{0,1},{2,3},{4,5},{6,7},{8,9},{10,11},{12,13},{14,15},{16,17},{18,19},{..., dimensions={0}, use_global_device_ids=true | all-gather | bytes 1081344 | tf_op jit(solution)/shard_map/all_gather | solution.py:391
  76.6 10.2 %all-gather.4 = f32[832,128]{1,0:T(8,128)S(1)} all-gather(f32[416,128]{1,0:T(8,128)S(1)} %get-tuple-element.36), channel_id=6, replica_groups={{0,24},{1,25},{2,26},{3,27},{4,28},{5,29},{6,30},{7,31},{8,16},{9,17},{..., dimensions={0}, use_global_device_ids=true | all-gather | bytes 638976 | tf_op jit(solution)/shard_map/all_gather | solution.py:391
  86.8 2.5 %shard_map.43 = (f32[288,128]{1,0:T(8,128)S(1)}, f32[288,128]{1,0:T(8,128)S(1)}, f32[4,288,128]{2,1,0:T(8,128)S(1)}) custom-call(f32[2,416,128]{2,1,0:T(8,128)S(1)} %bitcast.30, f32[416,128]{1,0:T(8,128)S(1)} %get-tuple-element.37.z_low, f32[2,704,128]{2,1,0:T(8,128)S(1)} %bitcast.29, f32[416,256]{1,0:T(8,128)S(1)} %get-tuple-element.35.rest, ...), custom_call_target="tpu_custom_call" | custom-call | flops 619708416 | bytes 2310144 | tf_op jit(solution)/shard_map/pallas_call | solution.py:360
  89.3 12.8 %all_to_all.37 = f32[4,288,128]{2,1,0:T(8,128)S(1)} all-to-all(f32[4,288,128]{2,1,0:T(8,128)S(1)} %get-tuple-element.39), channel_id=1, replica_groups={{0,2,4,6},{1,3,5,7},{8,10,12,14},{9,11,13,15},{16,18,20,22},{17,19,21,2..., dimensions={0} | all-to-all | bytes 1179648 | tf_op jit(solution)/shard_map/all_to_all | solution.py:396
  102.3 16.2 %all_to_all.38 = f32[8,40,128]{2,1,0:T(8,128)S(1)} all-to-all(f32[8,40,128]{2,1,0:T(8,128)S(1)} %pad_maximum_fusion.2), channel_id=1, replica_groups={{0,8,16,24,32,40,48,56},{1,9,17,25,33,41,49,57},{2,10,18,26,34,42,50,58..., dimensions={0} | all-to-all | bytes 327680 | tf_op jit(solution)/shard_map/all_to_all | solution.py:396
  118.5 11.9 %all_to_all.39 = f32[8,56,128]{2,1,0:T(8,128)S(1)} all-to-all(f32[8,56,128]{2,1,0:T(8,128)S(1)} %broadcast_in_dim.6), channel_id=1, replica_groups={{0,8,16,24,32,40,48,56},{1,9,17,25,33,41,49,57},{2,10,18,26,34,42,50,58..., dimensions={0} | all-to-all | bytes 458752 | tf_op jit(solution)/shard_map/all_to_all | solution.py:396
  130.6 12.6 %all_to_all.40.gathered = f32[4,408,128]{2,1,0:T(8,128)S(1)} all-to-all(f32[4,408,128]{2,1,0:T(8,128)S(1)} %broadcast_in_dim.7), channel_id=1, replica_groups={{0,2,4,6},{1,3,5,7},{8,10,12,14},{9,11,13,15},{16,18,20,22},{17,19,21,2..., dimensions={0} | all-to-all | bytes 1671168 | tf_op jit(solution)/shard_map/all_to_all | solution.py:396
  143.2 6.6 %all-gather.5 = f32[1600,128]{1,0:T(8,128)S(1)} all-gather(f32[800,128]{1,0:T(8,128)S(1)} %shard_map.44), channel_id=7, replica_groups={{0,1},{2,3},{4,5},{6,7},{8,9},{10,11},{12,13},{14,15},{16,17},{18,19},{..., dimensions={0}, use_global_device_ids=true | all-gather | bytes 1228800 | tf_op jit(solution)/shard_map/all_gather | solution.py:391
  152.0 8.2 %all-gather.6 = f32[336,128]{1,0:T(8,128)S(1)} all-gather(f32[168,128]{1,0:T(8,128)S(1)} %get-tuple-element.43), channel_id=8, replica_groups={{0,96},{32,64},{128,224},{160,192},{256,352},{288,320},{384,480},{416,4..., dimensions={0}, use_global_device_ids=true | all-gather | bytes 258048 | tf_op jit(solution)/shard_map/all_gather | solution.py:391
  160.3 8.1 %all_to_all.41.sib = f32[4,168,128]{2,1,0:T(8,128)S(1)} all-to-all(f32[4,168,128]{2,1,0:T(8,128)S(1)} %shard_map.46), channel_id=1, replica_groups={{0,2,4,6},{1,3,5,7},{8,10,12,14},{9,11,13,15},{16,18,20,22},{17,19,21,2..., dimensions={0} | all-to-all | bytes 688128 | tf_op jit(solution)/shard_map/all_to_all | solution.py:396
  168.4 3.9 %all-gather.7 = f32[1216,128]{1,0:T(8,128)S(1)} all-gather(f32[608,128]{1,0:T(8,128)S(1)} %shard_map.47), channel_id=9, replica_groups={{0,1},{2,3},{4,5},{6,7},{8,9},{10,11},{12,13},{14,15},{16,17},{18,19},{..., dimensions={0}, use_global_device_ids=true | all-gather | bytes 933888 | tf_op jit(solution)/shard_map/all_gather | solution.py:391
  174.3 6.1 %all-gather.8 = f32[640,128]{1,0:T(8,128)S(1)} all-gather(f32[320,128]{1,0:T(8,128)S(1)} %get-tuple-element.46.own), channel_id=10, replica_groups={{0,128},{32,160},{64,192},{96,224},{256,384},{288,416},{320,448},{352,4..., dimensions={0}, use_global_device_ids=true | all-gather | bytes 491520 | tf_op jit(solution)/shard_map/all_gather | solution.py:391
  180.5 3.2 %all-gather.9 = f32[1600,128]{1,0:T(8,128)S(1)} all-gather(f32[800,128]{1,0:T(8,128)S(1)} %shard_map.49), channel_id=11, replica_groups={{0,1},{2,3},{4,5},{6,7},{8,9},{10,11},{12,13},{14,15},{16,17},{18,19},{..., dimensions={0}, use_global_device_ids=true | all-gather | bytes 1228800 | tf_op jit(solution)/shard_map/all_gather | solution.py:391
  185.7 5.9 %all-gather.10 = f32[384,128]{1,0:T(8,128)S(1)} all-gather(f32[192,128]{1,0:T(8,128)S(1)} %get-tuple-element.49), channel_id=12, replica_groups={{0,384},{32,416},{64,448},{96,480},{128,256},{160,288},{192,320},{224,3..., dimensions={0}, use_global_device_ids=true | all-gather | bytes 294912 | tf_op jit(solution)/shard_map/all_gather | solution.py:391
  191.6 2.4 %shard_map.51 = f32[64,128]{1,0:T(8,128)} custom-call(f32[2,192,128]{2,1,0:T(8,128)S(1)} %bitcast.38, f32[192,128]{1,0:T(8,128)S(1)} %get-tuple-element.50.carried), custom_call_target="tpu_custom_call" | custom-call | flops 232783872 | bytes 294912 | tf_op jit(solution)/shard_map/pallas_call | solution.py:360
  (33 shorter events, 13.2 us)
Async XLA Ops:
  1.3 11.1 %collective-permute-start = (f32[2112,128]{1,0:T(8,128)S(1)}, f32[2112,128]{1,0:T(8,128)S(1)}, u32[]{:S(2)}, u32[]{:S(2)}) collective-permute-start(f32[2112,128]{1,0:T(8,128)S(1)} %pad_maximum_fusion.mine), channel_id=1, source_target_pairs={{0,1},{1,0},{2,3},{3,2},{4,5},{5,4},{6,7},{7,6},{8,9},{9,8},{10,11... | collective-permute-start | bytes 3244040 | tf_op jit(solution)/shard_map/ppermute | solution.py:385
  89.3 12.9 %copy-start = (pred[128]{0:T(512)(128)(4,1)S(1)}, pred[128]{0:T(512)(128)(4,1)}, u32[]{:S(2)}) copy-start(pred[128]{0:T(512)(128)(4,1)} %constant.4.clone.1) | copy-start | bytes 388
